TPU v7x, 32 devices: a whole 2x2x4 slice. The times are simulated.
32 devices in a mesh: tm: 4 (over x, core), contact: 8 (over z, y).
Axes of the slice: x: 2, y: 2, z: 4, core: 2. Of those that a mesh axis runs over, the one named last changes fastest.
Arguments:
- signal: bfloat16 [8, 512, 4096], P(None, 'contact', 'tm'), may hold values from -6 to 6
- fir_taps: bfloat16 [512, 129], P('contact'), may hold values from -0.5 to 0.5
- neighbours: int32 [512, 4], replicated, may hold values from 0 to 511, as said below
- live_mask: int32 [512], replicated, may hold values 0 or 1
- lap_coef: float32 [512], replicated, may hold values from 0.1 to 1
- w_query: bfloat16 [256, 256], replicated, may hold values from -8 to 8
- w_key: bfloat16 [256, 256], replicated, may hold values from -8 to 8
- w_value: bfloat16 [256, 256], replicated, may hold values from -0.375 to 0.375
- w_out: bfloat16 [256, 256], replicated, may hold values from -0.375 to 0.375
- cotangent: bfloat16 [8, 512, 4096], P(None, 'contact', 'tm'), may hold values from -6 to 6
Outputs:
- attended: bfloat16 [8, 512, 4096], P(None, 'contact', 'tm')
- weight_grads: float32 [4, 256, 256], replicated
Inputs may be any that keep to these rules, and one draw needn't show every extreme that they name: `neighbours`: entry [c, k] names a contact whose grid row (index // 16) differs from that of contact c by at most one and whose column (index % 16) differs by at most two.
All inputs are finite; a program needn't handle non-finite values.
Results may differ from a plain program's by a relative error of at most 0.011.
Values may be sent and summed in bfloat16 or wider, within the bound.
No kernel may reach another device: no remote copies, remote signals or barrier semaphores. Data moves between devices by JAX's collectives and lax.ppermute only.
A program may use at most 64 MiB of HBM per device.

v0:
```python
import jax
import jax.numpy as jnp
from jax import lax
from jax.sharding import PartitionSpec as P

GRID_COLS = 16
HEADS = 4


def from_behind(value, axis, by):
    count = lax.axis_size(axis)
    pairs = [(i, i + by) for i in range(count) if 0 <= i + by < count]
    return lax.ppermute(value, axis, pairs)


def extended_2(cells, sides, width):
    for axis, dim in sides:
        count = lax.axis_size(axis)
        ends = count - 1
        head = lax.slice_in_dim(cells, 0, width, axis=dim)
        tail = lax.slice_in_dim(cells, cells.shape[dim] - width, cells.shape[dim], axis=dim)
        cells = jnp.concatenate(
            [
                lax.ppermute(tail, axis, [(i, (i + 1) % count) for i in range(ends)]),
                cells,
                lax.ppermute(head, axis, [((i + 1) % count, i) for i in range(ends)]),
            ],
            axis=dim,
        )
    return cells


def contract(left, right, left_dim, right_dim):
    return lax.dot_general(
        left, right, (((left_dim,), (right_dim,)), ((), ())), preferred_element_type=jnp.float32
    )


def toeplitz(fir_taps):
    rim_width = fir_taps.shape[1] - 1
    source = jnp.arange(2 * rim_width, dtype=jnp.int32)[:, None]
    target = jnp.arange(rim_width, dtype=jnp.int32)[None, :]
    lag_table = target + rim_width - source
    inside = (lag_table >= 0) & (lag_table <= rim_width)
    picked = jnp.take(fir_taps, jnp.clip(lag_table, 0, rim_width), axis=1)
    return jnp.where(inside[None, :, :], picked, jnp.zeros_like(picked))


def laplace(field, centre, indices, nbr_alive, own_alive, coef):
    source_ids = jnp.arange(field.shape[-2], dtype=jnp.int32)
    counts = jnp.zeros((indices.shape[0], field.shape[-2]), jnp.float32)
    for slot_index in range(indices.shape[1]):
        hit = (indices[:, slot_index][:, None] == source_ids[None, :]).astype(jnp.float32)
        counts = counts + nbr_alive[:, slot_index][:, None] * hit
    alive_count = jnp.sum(nbr_alive, axis=1)
    beside = jnp.einsum(
        "cn,bnt->bct", counts.astype(jnp.bfloat16), field, preferred_element_type=jnp.float32
    )
    middle = centre.astype(jnp.float32)
    running = beside - alive_count[:, None] * middle
    return (own_alive[:, None] * (middle + coef[:, None] * running)).astype(jnp.bfloat16)


def one_head(query_head, key_head, value_head, back_head, key_alive, score_scale):
    scores = contract(query_head, key_head, 1, 1) * score_scale
    scores = jnp.where(key_alive[None, :] > 0, scores, -1e30)
    top_score = jnp.max(scores, axis=1, keepdims=True)
    raised = jnp.exp(scores - top_score)
    attn_prob = raised / jnp.sum(raised, axis=1, keepdims=True)
    prob_low = attn_prob.astype(jnp.bfloat16)
    head_out = jnp.dot(prob_low, value_head, preferred_element_type=jnp.float32).astype(
        jnp.bfloat16
    )
    grad_value = contract(prob_low, back_head, 0, 0).astype(jnp.bfloat16)
    grad_prob = contract(back_head, value_head, 1, 1)
    row_inner = jnp.sum(
        back_head.astype(jnp.float32) * head_out.astype(jnp.float32), axis=1, keepdims=True
    )
    grad_score = (attn_prob * (grad_prob - row_inner) * score_scale).astype(jnp.bfloat16)
    grad_query = jnp.dot(grad_score, key_head, preferred_element_type=jnp.float32).astype(
        jnp.bfloat16
    )
    grad_key = contract(grad_score, query_head, 0, 0).astype(jnp.bfloat16)
    return (head_out, grad_query, grad_key, grad_value)


def group_step(tokens, upstream, key_alive, w_query, w_key, w_value, w_out):
    as_float = tokens.astype(jnp.float32)
    normed = (
        as_float * lax.rsqrt(jnp.mean(as_float * as_float, axis=1, keepdims=True) + 1e-05)
    ).astype(jnp.bfloat16)
    query_rows = jnp.dot(normed, w_query, preferred_element_type=jnp.float32).astype(jnp.bfloat16)
    key_rows = jnp.dot(normed, w_key, preferred_element_type=jnp.float32).astype(jnp.bfloat16)
    value_rows = jnp.dot(normed, w_value, preferred_element_type=jnp.float32).astype(jnp.bfloat16)
    back_signal = contract(upstream, w_out, 1, 1).astype(jnp.bfloat16)
    head_size = w_query.shape[1] // HEADS
    score_scale = head_size ** (-0.5)
    head_results = []
    for head_index in range(HEADS):
        lower = head_index * head_size
        upper = lower + head_size
        head_results.append(
            one_head(
                query_rows[:, lower:upper],
                key_rows[:, lower:upper],
                value_rows[:, lower:upper],
                back_signal[:, lower:upper],
                key_alive,
                score_scale,
            )
        )
    mixed_heads = jnp.concatenate([entry[0] for entry in head_results], axis=1)
    grad_query = jnp.concatenate([entry[1] for entry in head_results], axis=1)
    grad_key = jnp.concatenate([entry[2] for entry in head_results], axis=1)
    grad_value = jnp.concatenate([entry[3] for entry in head_results], axis=1)
    attended = jnp.dot(mixed_heads, w_out, preferred_element_type=jnp.float32).astype(jnp.bfloat16)
    grad_stack = jnp.stack(
        [
            contract(normed, grad_query, 0, 0),
            contract(normed, grad_key, 0, 0),
            contract(normed, grad_value, 0, 0),
            contract(mixed_heads, upstream, 0, 0),
        ]
    )
    return (attended, grad_stack)


def to_groups(whole, patch_len):
    batch_size, contacts_here, slab_len = whole.shape
    patch_count = slab_len // patch_len
    shaped = whole.reshape(batch_size, contacts_here, patch_count, patch_len).transpose(0, 2, 1, 3)
    return shaped.reshape(batch_size * patch_count, contacts_here, patch_len)


def from_groups(grouped, batch_size):
    group_count, contacts_here, patch_len = grouped.shape
    patch_count = group_count // batch_size
    shaped = grouped.reshape(batch_size, patch_count, contacts_here, patch_len).transpose(
        0, 2, 1, 3
    )
    return shaped.reshape(batch_size, contacts_here, patch_count * patch_len)


def local(
    signal, fir_taps, neighbours, live_mask, lap_coef, w_query, w_key, w_value, w_out, cotangent
):
    batch_size, contacts_here, slab_len = signal.shape
    rim_width = fir_taps.shape[1] - 1
    patch_len = w_query.shape[0]
    patch_count = slab_len // patch_len
    prior_rim = from_behind(signal[:, :, slab_len - rim_width :], "tm", 1)
    extended = jnp.concatenate([prior_rim, signal], axis=2)
    blocks = extended.reshape(batch_size, contacts_here, slab_len // rim_width + 1, rim_width)
    windows = jnp.concatenate([blocks[:, :, :-1], blocks[:, :, 1:]], axis=3)
    filter_table = toeplitz(fir_taps)
    filtered = jnp.einsum(
        "bcjw,cwu->bcju", windows, filter_table, preferred_element_type=jnp.float32
    )
    filtered = filtered.reshape(batch_size, contacts_here, slab_len).astype(jnp.bfloat16)
    alive_f = live_mask.astype(jnp.float32)
    nbr_alive = jnp.take(alive_f, neighbours)
    first_contact = lax.axis_index("contact") * contacts_here
    padded = extended_2(filtered, (("contact", 1),), GRID_COLS)
    local_index = (
        lax.dynamic_slice_in_dim(neighbours, first_contact, contacts_here, 0)
        - first_contact
        + GRID_COLS
    )
    ready = laplace(
        padded,
        filtered,
        local_index,
        lax.dynamic_slice_in_dim(nbr_alive, first_contact, contacts_here, 0),
        lax.dynamic_slice_in_dim(alive_f, first_contact, contacts_here, 0),
        lax.dynamic_slice_in_dim(lap_coef, first_contact, contacts_here, 0),
    )
    grouped = to_groups(ready, patch_len)
    features, upstream = (
        lax.all_to_all(grouped, "contact", split_axis=0, concat_axis=1, tiled=True),
        lax.all_to_all(
            to_groups(cotangent, patch_len), "contact", split_axis=0, concat_axis=1, tiled=True
        ),
    )

    def run_group(running, inputs_pair):
        attended, grad_stack = group_step(
            inputs_pair[0], inputs_pair[1], alive_f, w_query, w_key, w_value, w_out
        )
        return (running + grad_stack, attended)

    running, attended_groups = lax.scan(
        run_group, jnp.zeros((4, patch_len, patch_len), jnp.float32), (features, upstream)
    )
    summed = lax.psum(running, ("tm", "contact"))
    returned = lax.all_to_all(attended_groups, "contact", split_axis=1, concat_axis=0, tiled=True)
    attended = from_groups(returned, batch_size)
    grad_scale = (batch_size * patch_count * lax.axis_size("tm") * neighbours.shape[0]) ** (-0.5)
    return (attended, summed * grad_scale)


def solution(mesh):
    in_specs = (
        P(None, "contact", "tm"),
        P("contact", None),
        P(),
        P(),
        P(),
        P(),
        P(),
        P(),
        P(),
        P(None, "contact", "tm"),
    )
    out_specs = (P(None, "contact", "tm"), P())
    return jax.shard_map(local, mesh=mesh, in_specs=in_specs, out_specs=out_specs, check_vma=False)
```

profile of v0, /device:TPU:0, one launch (start us, length us, event | category | flops | bytes accessed | tf_op | source)
XLA Modules:
  0.0 431.3 jit_solution(16537218032241431759)
XLA Ops:
  8.1 2.4 collective-permute-start
  10.5 1.3 fusion.159
  12.8 6.7 %all-to-all-start.1 = ((bf16[32,64,256]{2,1,0:T(8,128)(2,1)}), bf16[32,64,256]{2,1,0:T(8,128)(2,1)}, u32[]{:S(2)}, u32[]{:S(2)}) async-start(bf16[32,64,256]{2,1,0:T(8,128)(2,1)} %bitcast.20), calls=%async_computation.1 | async-start | bytes 2097152 | tf_op jit(solution)/shard_map/all_to_all | solution.py:180
  20.0 13.2 %gather_fusion.1 = f32[2048]{0:T(1024)S(1)} fusion(f32[512]{0:T(512)S(1)} %convert_element_type.145, s32[2048]{0:T(1024)S(1)} %broadcast_clamp_fusion), kind=kCustom, calls=%fused_computation.1 | custom fusion | bytes 24576 | tf_op jit(solution)/shard_map/jit(_take)/gather | solution.py:161
  33.8 114.2 %gather_fusion = bf16[32768,64]{1,0:T(8,128)(2,1)} fusion(bf16[64,129]{0,1:T(8,128)(2,1)S(1)} %copy.88, s32[32768]{0:T(1024)S(1)} %fusion.131), kind=kCustom, calls=%fused_computation | custom fusion | bytes 8519680 | tf_op jit(solution)/shard_map/jit(_take)/gather | solution.py:45
  148.0 10.1 %copy.89 = bf16[256,128,64]{1,0,2:T(8,128)(2,1)} copy(bf16[256,128,64]{2,1,0:T(8,128)(2,1)} %bitcast.175) | data formatting | bytes 8388608 | tf_op jit(solution)/shard_map/jit(_take)/gather | solution.py:45
  159.4 1.8 copy-done.1
  161.1 1.3 fusion.125
  163.6 3.9 collective-permute-start.1
  167.5 1.3 collective-permute-start.2
  169.8 9.8 %collective-permute-done.1 = bf16[8,16,1024]{2,1,0:T(8,128)(2,1)S(1)} collective-permute-done((bf16[8,16,1024]{2,1,0:T(8,128)(2,1)S(1)}, bf16[8,16,1024]{2,1,0:T(8,128)(2,1)S(1)}, u32[]{:S(2)}, u32[]{:S(2)}) %collective-permute-start.1) | collective-permute-done | bytes 262176 | tf_op jit(solution)/shard_map/ppermute | solution.py:24
  181.7 6.7 %all-to-all-start = ((bf16[32,64,256]{2,1,0:T(8,128)(2,1)}), bf16[32,64,256]{2,1,0:T(8,128)(2,1)S(1)}, u32[]{:S(2)}, u32[]{:S(2)}) async-start(bf16[32,64,256]{2,1,0:T(8,128)(2,1)} %bitcast.16), calls=%async_computation | async-start | bytes 2097152 | tf_op jit(solution)/shard_map/all_to_all | solution.py:179
  188.4 2.4 copy.99
  190.8 23.6 %all-to-all-done = bf16[32,64,256]{2,1,0:T(8,128)(2,1)S(1)} async-done(((bf16[32,64,256]{2,1,0:T(8,128)(2,1)}), bf16[32,64,256]{2,1,0:T(8,128)(2,1)S(1)}, u32[]{:S(2)}, u32[]{:S(2)}) %all-to-all-start) | async-done | bytes 1048608 | tf_op jit(solution)/shard_map/all_to_all | solution.py:179
  214.6 59.1 %while.13 = (s32[]{:T(128)}, f32[4,256,256]{2,1,0:T(8,128)S(1)}, bf16[4,512,256]{2,1,0:T(8,128)(2,1)}, bf16[4,512,256]{2,1,0:T(8,128)(2,1)S(1)}, f32[512]{0:T(51...) while((s32[]{:T(128)}, f32[4,256,256]{2,1,0:T(8,128)S(1)}, ...), condition=%wide.region_15.16_spmd.clone, body=%wide.region_1.15_spmd.clone.sunk | while | flops 1434971136 | bytes 43417780 | solution.py:191
  219.6 1.2 convolution_convert_fusion.46
  234.4 1.2 convolution_convert_fusion.46
  249.2 1.2 convolution_convert_fusion.46
  263.9 1.2 convolution_convert_fusion.46
  273.7 3.4 copy.100
  277.1 3.6 all-to-all-start.2
  281.4 139.2 %all-reduce.2.cloned.1.call-done = f32[4,256,256]{2,1,0:T(8,128)} async-done(((f32[4,256,256]{2,1,0:T(8,128)}), f32[4,256,256]{2,1,0:T(8,128)}) %all-reduce.2.cloned.1.call-update) | async-done | bytes 1048592 | tf_op jit(solution)/shard_map/psum | solution.py:194
  420.6 2.3 broadcast_multiply_fusion
  422.9 1.5 reshape.144
  (239 shorter events, 62.5 us)
Async XLA Ops:
  8.1 150.0 %collective-permute-start = (bf16[8,64,128]{2,1,0:T(8,128)(2,1)S(1)}, bf16[8,64,128]{2,1,0:T(8,128)(2,1)S(1)}, u32[]{:S(2)}, u32[]{:S(2)}) collective-permute-start(bf16[8,64,128]{2,1,0:T(8,128)(2,1)S(1)} %slice.111), channel_id=1, source_target_pairs={{0,8},{8,16},{16,24},{1,9},{9,17},{17,25},{2,10},{10,18},{18,26},{... | collective-permute-start | bytes 393224 | tf_op jit(solution)/shard_map/ppermute | solution.py:13
  11.7 7.9 %copy-start.9 = (s32[512]{0:T(512)S(1)}, s32[512]{0:T(512)}, u32[]{:S(2)}) copy-start(s32[512]{0:T(512)} %param.15) | copy-start | bytes 6148
  11.7 7.9 %copy-start.8 = (s32[512,4]{0,1:T(4,128)S(1)}, s32[512,4]{0,1:T(4,128)}, u32[]{:S(2)}) copy-start(s32[512,4]{0,1:T(4,128)} %param.14) | copy-start | bytes 24580
  12.8 168.9 %all-to-all-start.1 = ((bf16[32,64,256]{2,1,0:T(8,128)(2,1)}), bf16[32,64,256]{2,1,0:T(8,128)(2,1)}, u32[]{:S(2)}, u32[]{:S(2)}) async-start(bf16[32,64,256]{2,1,0:T(8,128)(2,1)} %bitcast.20), calls=%async_computation.1 | async-start | bytes 2097152 | tf_op jit(solution)/shard_map/all_to_all | solution.py:180
  20.0 13.7 %copy-start.7 = (bf16[64,129]{1,0:T(8,128)(2,1)S(1)}, bf16[64,129]{1,0:T(8,128)(2,1)}, u32[]{:S(2)}) copy-start(bf16[64,129]{1,0:T(8,128)(2,1)} %param.13) | copy-start | bytes 49540
  148.0 10.1 %copy-start.6 = (bf16[8,64,1024]{2,1,0:T(8,128)(2,1)S(1)}, bf16[8,64,1024]{2,1,0:T(8,128)(2,1)}, u32[]{:S(2)}) copy-start(bf16[8,64,1024]{2,1,0:T(8,128)(2,1)} %param.12) | copy-start | bytes 3145732
  159.0 2.2 copy-start.1
  163.6 16.0 %collective-permute-start.1 = (bf16[8,16,1024]{2,1,0:T(8,128)(2,1)S(1)}, bf16[8,16,1024]{2,1,0:T(8,128)(2,1)S(1)}, u32[]{:S(2)}, u32[]{:S(2)}) collective-permute-start(bf16[8,16,1024]{2,1,0:T(8,128)(2,1)S(1)} %get-tuple-element.135), channel_id=1, source_target_pairs={{0,1},{1,2},{2,3},{3,4},{4,5},{5,6},{6,7},{8,9},{9,10},{10,11},{11... | collective-permute-start | bytes 786440 | tf_op jit(solution)/shard_map/ppermute | solution.py:24
  167.5 12.0 %collective-permute-start.2 = (bf16[8,16,1024]{2,1,0:T(8,128)(2,1)S(1)}, bf16[8,16,1024]{2,1,0:T(8,128)(2,1)S(1)}, u32[]{:S(2)}, u32[]{:S(2)}) collective-permute-start(bf16[8,16,1024]{2,1,0:T(8,128)(2,1)S(1)} %get-tuple-element.136), channel_id=1, source_target_pairs={{1,0},{2,1},{3,2},{4,3},{5,4},{6,5},{7,6},{9,8},{10,9},{11,10},{12... | collective-permute-start | bytes 786440 | tf_op jit(solution)/shard_map/ppermute | solution.py:26
  181.7 32.7 %all-to-all-start = ((bf16[32,64,256]{2,1,0:T(8,128)(2,1)}), bf16[32,64,256]{2,1,0:T(8,128)(2,1)S(1)}, u32[]{:S(2)}, u32[]{:S(2)}) async-start(bf16[32,64,256]{2,1,0:T(8,128)(2,1)} %bitcast.16), calls=%async_computation | async-start | bytes 2097152 | tf_op jit(solution)/shard_map/all_to_all | solution.py:179
  188.4 26.1 %copy-start.2 = (bf16[256,256]{1,0:T(8,128)(2,1)S(1)}, bf16[256,256]{1,0:T(8,128)(2,1)}, u32[]{:S(2)}) copy-start(bf16[256,256]{1,0:T(8,128)(2,1)} %param.17) | copy-start | bytes 393220
  188.4 26.1 %copy-start.3 = (bf16[256,256]{1,0:T(8,128)(2,1)S(1)}, bf16[256,256]{1,0:T(8,128)(2,1)}, u32[]{:S(2)}) copy-start(bf16[256,256]{1,0:T(8,128)(2,1)} %param.18) | copy-start | bytes 393220
  188.4 26.1 %copy-start.4 = (bf16[256,256]{1,0:T(8,128)(2,1)S(1)}, bf16[256,256]{1,0:T(8,128)(2,1)}, u32[]{:S(2)}) copy-start(bf16[256,256]{1,0:T(8,128)(2,1)} %param.20) | copy-start | bytes 393220
  216.2 0.9 copy-start.5
  231.0 0.9 copy-start.5
  245.8 0.9 copy-start.5
  260.5 0.9 copy-start.5
  273.7 3.4 copy-start
  277.1 145.9 %all-to-all-start.2 = ((bf16[4,512,256]{2,0,1:T(4,128)(2,1)}), bf16[4,512,256]{2,0,1:T(4,128)(2,1)S(1)}, u32[]{:S(2)}, u32[]{:S(2)}) async-start(bf16[4,512,256]{2,0,1:T(4,128)(2,1)} %copy.100), calls=%async_computation.2 | async-start | bytes 2097152 | tf_op jit(solution)/shard_map/all_to_all | solution.py:195
  280.7 139.9 %all-reduce.2.cloned.1.call-start = ((), (), s32[]{:S(2)}) async-start(), calls=%async_computation.3 | async-start | bytes 2097152 | tf_op jit(solution)/shard_map/psum | solution.py:194
Sparse Core Ops, SparseCore 0:
  286.7 133.8 all-reduce.1
where the time goes:
time: 432 us; the launch traced here: 431 us
  waiting for transfers between devices  173 us (40%)
  local copies, waits for them, and re-layouts  153 us (35%)
  matrix products  52.3 us (12%)
  starting transfers between devices  24.6 us (6%)
  between operations  14.4 us (3%)
  other arithmetic  12.3 us (3%)
    psum x1, waiting for transfers between devices, local(): summed = lax.psum(running, ('tm', 'contact'))  139 us
    gather x2, local copies, waits for them, and re-layouts, toeplitz(): picked = jnp.take(fir_taps, jnp.clip(lag_table, 0, rim_width), axis=1)  124 us
    dot_general x84, matrix products, contract(): lax.dot_general(left, right, (((left_dim,), (right_dim,)), ((), ())), pre...  35.3 us
    all_to_all x1, waiting for transfers between devices, local(): lax.all_to_all(grouped, 'contact', split_axis=0, concat_axis=1, tiled=True)  23.6 us
    gather x2, local copies, waits for them, and re-layouts, local(): nbr_alive = jnp.take(alive_f, neighbours)  13.5 us
    ppermute x1, waiting for transfers between devices, extended_2(): lax.ppermute(tail, axis, [(i, (i + 1) % count) for i in range(ends)])  9.83 us
  transfers between devices with their start and end apart: 7, of which 3 were waited for; matrix products, arithmetic and copies ran while one was open for 35% of the time, Pallas kernels for 0%

commit v1 on v0

v1 whole, which is shorter than its diff:
```python
import functools

import jax
import jax.numpy as jnp
from jax import lax
from jax.experimental import pallas as pl
from jax.experimental.pallas import tpu as pltpu
from jax.sharding import PartitionSpec as P

HEADS = 4
F32 = jnp.float32
BF16 = jnp.bfloat16


def mm(left, right, left_dim=1, right_dim=0):
    return lax.dot_general(
        left, right, (((left_dim,), (right_dim,)), ((), ())), preferred_element_type=F32
    )


def filter_kernel(sig_ref, rim_ref, taps_ref, out_ref):
    batch, rows, slab = sig_ref.shape
    width = rim_ref.shape[2]
    blocks = slab // width
    signal = jnp.swapaxes(sig_ref[...].astype(F32), 0, 1)
    rim = jnp.swapaxes(rim_ref[...].astype(F32), 0, 1)
    results = []
    for row in range(rows):
        own = [signal[row, :, j * width : (j + 1) * width] for j in range(blocks)]
        current = jnp.concatenate(own, axis=0)
        before = jnp.concatenate([rim[row]] + own[:-1], axis=0)
        window = jnp.concatenate([before, current], axis=1).astype(BF16)
        spread = jnp.broadcast_to(taps_ref[row : row + 1, :], (width, 2 * width))
        rolled = pltpu.roll(spread, 0, 1, stride=1, stride_axis=0)
        table = jnp.concatenate([rolled[:, width:], rolled[:, :width]], axis=0).astype(BF16)
        product = mm(window, table)
        results.append(
            jnp.concatenate(
                [product[j * batch : (j + 1) * batch] for j in range(blocks)], axis=1
            )
        )
    out_ref[...] = jnp.swapaxes(jnp.stack(results, axis=0), 0, 1).astype(BF16)


def filter_all(signal, rim, taps):
    batch, contacts, slab = signal.shape
    width = rim.shape[2]
    rows = 16
    return pl.pallas_call(
        filter_kernel,
        grid=(contacts // rows,),
        in_specs=[
            pl.BlockSpec((batch, rows, slab), lambda i: (0, i, 0)),
            pl.BlockSpec((batch, rows, width), lambda i: (0, i, 0)),
            pl.BlockSpec((rows, 2 * width), lambda i: (i, 0)),
        ],
        out_specs=pl.BlockSpec((batch, rows, slab), lambda i: (0, i, 0)),
        out_shape=jax.ShapeDtypeStruct(signal.shape, BF16),
        compiler_params=pltpu.CompilerParams(vmem_limit_bytes=40 * 2**20),
        cost_estimate=pl.CostEstimate(
            flops=4 * batch * contacts * slab * width,
            bytes_accessed=4 * batch * contacts * slab,
            transcendentals=0,
        ),
        name="filter",
    )(signal, rim, taps)


def attend_kernel(
    feat_ref, up_ref, nbr_ref, live_row_ref, live_col_ref, coef_ref, wqkv_ref, wo_ref,
    out_ref, wg_ref, counts, alive_count, e_all, gs_all, v_blocks, k_blocks,
):
    contacts, width = feat_ref.shape
    head = width // HEADS
    scale = head ** (-0.5)
    step = pl.program_id(0)

    @pl.when(step == 0)
    def _():
        ids = lax.broadcasted_iota(jnp.int32, (contacts, contacts), 1)
        total = jnp.zeros((contacts, contacts), F32)
        for slot in range(nbr_ref.shape[1]):
            hit = nbr_ref[:, slot : slot + 1] == ids
            total = total + jnp.where(hit, live_row_ref[...], 0.0)
        counts[...] = total.astype(BF16)
        alive_count[...] = jnp.sum(total, axis=1, keepdims=True)
        wg_ref[...] = jnp.zeros_like(wg_ref)

    field = feat_ref[...]
    middle = field.astype(F32)
    beside = mm(counts[...], field)
    ready = live_col_ref[...] * (middle + coef_ref[...] * (beside - alive_count[...] * middle))
    ready = ready.astype(BF16).astype(F32)
    mean_square = jnp.mean(ready * ready, axis=1, keepdims=True)
    normed = (ready * lax.rsqrt(mean_square + 1e-05)).astype(BF16)
    upstream = up_ref[...]
    query = (mm(normed, wqkv_ref[:, :width]) * scale).astype(BF16)
    keys = mm(normed, wqkv_ref[:, width : 2 * width]).astype(BF16)
    value = mm(normed, wqkv_ref[:, 2 * width :]).astype(BF16)
    back = mm(upstream, wo_ref[...], 1, 1)
    lane_head = lax.broadcasted_iota(jnp.int32, (1, width), 1) // head
    masks = [(lane_head == h).astype(F32) for h in range(HEADS)]
    low_masks = [m.astype(BF16) for m in masks]
    bias = jnp.where(live_row_ref[...] > 0, 0.0, -1e30)
    inverse = jnp.zeros((contacts, width), F32)
    for h in range(HEADS):
        k_blocks[h * contacts : (h + 1) * contacts, :] = keys * low_masks[h]
        v_blocks[h * contacts : (h + 1) * contacts, :] = value * low_masks[h]
    for h in range(HEADS):
        scores = mm(query * low_masks[h], keys, 1, 1) + bias
        top = jnp.max(scores, axis=1, keepdims=True)
        raised = jnp.exp(scores - top)
        inverse = inverse + masks[h] * (1.0 / jnp.sum(raised, axis=1, keepdims=True))
        e_all[:, h * contacts : (h + 1) * contacts] = raised.astype(BF16)
    mixed = (mm(e_all[...], v_blocks[...]) * inverse).astype(BF16)
    out_ref[...] = mm(mixed, wo_ref[...]).astype(BF16)
    back_scaled = (back.astype(BF16).astype(F32) * inverse).astype(BF16)
    inner = back_scaled.astype(F32) * mixed.astype(F32)
    back_t = back_scaled.T
    query_t = query.T
    grad_value_t = []
    grad_key_t = []
    for h in range(HEADS):
        grad_prob = mm(back_scaled * low_masks[h], value, 1, 1)
        row_inner = jnp.sum(inner * masks[h], axis=1, keepdims=True)
        raised = e_all[:, h * contacts : (h + 1) * contacts]
        grad_score = (raised.astype(F32) * (grad_prob - row_inner)).astype(BF16)
        gs_all[:, h * contacts : (h + 1) * contacts] = grad_score
        grad_value_t.append(mm(back_t[h * head : (h + 1) * head], raised))
        grad_key_t.append(mm(query_t[h * head : (h + 1) * head], grad_score))
    grad_query = (mm(gs_all[...], k_blocks[...]) * scale).astype(BF16)
    grad_key_t = jnp.concatenate(grad_key_t, axis=0).astype(BF16)
    grad_value_t = jnp.concatenate(grad_value_t, axis=0).astype(BF16)
    wg_ref[0] += mm(normed.T, grad_query)
    wg_ref[1] += mm(grad_key_t, normed)
    wg_ref[2] += mm(grad_value_t, normed)
    wg_ref[3] += mm(mixed.T, upstream)

    @pl.when(step == pl.num_programs(0) - 1)
    def _():
        wg_ref[1] = wg_ref[1].T
        wg_ref[2] = wg_ref[2].T


def attend_all(features, upstream, neighbours, live_row, live_col, coef, w_qkv, w_out):
    contacts, span = features.shape
    width = w_out.shape[0]
    groups = span // width
    block = pl.BlockSpec((contacts, width), lambda i: (0, i))

    def whole(shape):
        return pl.BlockSpec(shape, lambda i: (0,) * len(shape))

    return pl.pallas_call(
        attend_kernel,
        grid=(groups,),
        in_specs=[
            block, block, whole(neighbours.shape), whole(live_row.shape), whole(live_col.shape),
            whole(coef.shape), whole(w_qkv.shape), whole(w_out.shape),
        ],
        out_specs=[block, whole((4, width, width))],
        out_shape=[
            jax.ShapeDtypeStruct(features.shape, BF16),
            jax.ShapeDtypeStruct((4, width, width), F32),
        ],
        scratch_shapes=[
            pltpu.VMEM((contacts, contacts), BF16),
            pltpu.VMEM((contacts, 1), F32),
            pltpu.VMEM((contacts, HEADS * contacts), BF16),
            pltpu.VMEM((contacts, HEADS * contacts), BF16),
            pltpu.VMEM((HEADS * contacts, width), BF16),
            pltpu.VMEM((HEADS * contacts, width), BF16),
        ],
        compiler_params=pltpu.CompilerParams(vmem_limit_bytes=48 * 2**20),
        cost_estimate=pl.CostEstimate(
            flops=groups * 4 * 10**9,
            bytes_accessed=6 * contacts * span,
            transcendentals=groups * HEADS * contacts * contacts,
        ),
        name="attend",
    )(features, upstream, neighbours, live_row, live_col, coef, w_qkv, w_out)


def exchange(value, axis):
    return lax.all_to_all(value, axis, split_axis=0, concat_axis=0, tiled=True)


def scatter_sum(value, axis):
    count = lax.axis_size(axis)
    parts = exchange(value.astype(BF16), axis)
    parts = parts.reshape((count, value.shape[0] // count) + value.shape[1:])
    return jnp.sum(parts.astype(F32), axis=0)


def gather(value, axis):
    count = lax.axis_size(axis)
    return exchange(jnp.concatenate([value] * count, axis=0), axis)


def local(
    signal, fir_taps, neighbours, live_mask, lap_coef, w_query, w_key, w_value, w_out, cotangent
):
    batch, contacts_here, slab = signal.shape
    rim_width = fir_taps.shape[1] - 1
    width = w_query.shape[0]
    tm_count = lax.axis_size("tm")
    count = lax.axis_size("contact")
    pieces = max(1, count // batch)

    def by_group(whole):
        if pieces == 1:
            return whole
        cut = whole.reshape(batch, contacts_here, pieces, slab // pieces)
        return cut.transpose(0, 2, 1, 3).reshape(batch * pieces, contacts_here, slab // pieces)

    def to_attend(whole):
        moved = lax.all_to_all(
            by_group(whole), "contact", split_axis=0, concat_axis=1, tiled=True
        )
        held = moved.shape[0]
        return moved.transpose(1, 0, 2).reshape(moved.shape[1], held * moved.shape[2])

    rim = lax.ppermute(
        signal[:, :, slab - rim_width :], "tm", [(i, i + 1) for i in range(tm_count - 1)]
    )
    upstream = to_attend(cotangent)
    taps = jnp.pad(fir_taps.astype(F32), ((0, 0), (0, 2 * rim_width - fir_taps.shape[1])))
    filtered = filter_all(signal, rim, taps)
    features = to_attend(filtered)
    alive = live_mask.astype(F32)
    attended, grads = attend_all(
        features, upstream, neighbours, alive[None, :], alive[:, None], lap_coef[:, None],
        jnp.concatenate([w_query, w_key, w_value], axis=1), w_out,
    )
    held = batch * pieces // count
    shaped = attended.reshape(attended.shape[0], held, slab // pieces).transpose(1, 0, 2)
    returned = lax.all_to_all(shaped, "contact", split_axis=1, concat_axis=0, tiled=True)
    if pieces > 1:
        returned = returned.reshape(batch, pieces, contacts_here, slab // pieces)
        returned = returned.transpose(0, 2, 1, 3).reshape(batch, contacts_here, slab)
    grad_scale = (batch * (slab // width) * tm_count * neighbours.shape[0]) ** (-0.5)
    part = scatter_sum(grads.reshape(4 * width, width), "tm")
    part = scatter_sum(part, "contact") * grad_scale
    summed = gather(gather(part.astype(BF16), "contact"), "tm")
    return (returned, summed.astype(F32).reshape(4, width, width))


def solution(mesh):
    in_specs = (
        P(None, "contact", "tm"),
        P("contact", None),
        P(),
        P(),
        P(),
        P(),
        P(),
        P(),
        P(),
        P(None, "contact", "tm"),
    )
    out_specs = (P(None, "contact", "tm"), P())
    return jax.shard_map(local, mesh=mesh, in_specs=in_specs, out_specs=out_specs, check_vma=False)
```

time: 432 us -> 176 us (0.41)
  local copies, waits for them, and re-layouts: 153 us -> 12.5 us
  waiting for transfers between devices: 173 us -> 67.4 us
  matrix products: 52.3 us -> 0 us
  blocking collectives: 0 us -> 31.9 us
  Pallas kernels: 0 us -> 31.1 us
  between operations: 14.4 us -> 0.86 us
    psum x1 -> x0, waiting for transfers between devices: 139 us -> none  [local(): summed = lax.psum(running, ('tm', 'contact'))]
    gather x4 -> x0, local copies, waits for them, and re-layouts: 138 us -> none  [the longest x2 124 us: toeplitz(): picked = jnp.take(fir_taps, jnp.clip(lag_table, 0, rim_width), axis=1)]
    dot_general x134 -> x0, matrix products: 52.3 us -> none  [the longest x84 35.3 us: contract(): lax.dot_general(left, right, (((left_dim,), (right_dim,)), ((), ())), pre...]
    all_to_all x3 -> x4, waiting for transfers between devices: 23.6 us -> 66.5 us  [the longest x2 42.2 us: to_attend(): lax.all_to_all(by_group(whole), 'contact', split_axis=0, concat_axis=1, t...]
    all_to_all x0 -> x3, blocking collectives: none -> 31.9 us  [exchange(): return lax.all_to_all(value, axis, split_axis=0, concat_axis=0, tiled=True)]
    pallas_call x0 -> x2, Pallas kernels: none -> 31.1 us  [the longest x1 27.7 us: attend_all(): pl.pallas_call(attend_kernel, grid=(groups,), in_specs=[block, block, who...]
    ppermute x3 -> x1, waiting for transfers between devices: 9.83 us -> 0.9 us  [local(): lax.ppermute(signal[:, :, slab - rim_width:], 'tm', [(i, i + 1) for i in...]
    unnamed x20 -> x29, local copies, waits for them, and re-layouts: 2 us -> 9.14 us
  transfers between devices with their start and end apart: 7 -> 5, of which waited for: 3 -> 4; matrix products, arithmetic and copies ran while one was open for 35% -> 9% of each run, Pallas kernels for 0% -> 2%
where the time goes in v1:
time: 176 us; the launch traced here: 175 us
  waiting for transfers between devices  67.4 us (38%)
  blocking collectives  31.9 us (18%)
  Pallas kernels  31.1 us (18%)
  starting transfers between devices  20.4 us (12%)
  local copies, waits for them, and re-layouts  12.5 us (7%)
  other arithmetic  10.9 us (6%)
    all_to_all x2, waiting for transfers between devices, to_attend(): lax.all_to_all(by_group(whole), 'contact', split_axis=0, concat_axis=1, t...  42.2 us
    all_to_all x3, blocking collectives, exchange(): return lax.all_to_all(value, axis, split_axis=0, concat_axis=0, tiled=True)  31.9 us
    pallas_call x1, Pallas kernels, attend_all(): pl.pallas_call(attend_kernel, grid=(groups,), in_specs=[block, block, who...  27.7 us
    all_to_all x1, waiting for transfers between devices, local(): lax.all_to_all(shaped, 'contact', split_axis=1, concat_axis=0, tiled=True)  24.3 us
    all_to_all x2, starting transfers between devices, to_attend(): lax.all_to_all(by_group(whole), 'contact', split_axis=0, concat_axis=1, t...  11 us
    unnamed x29, local copies, waits for them, and re-layouts  9.14 us
    unnamed x2, other arithmetic  6.79 us
    all_to_all x1, starting transfers between devices, exchange(): return lax.all_to_all(value, axis, split_axis=0, concat_axis=0, tiled=True)  4.31 us
  transfers between devices with their start and end apart: 5, of which 4 were waited for; matrix products, arithmetic and copies ran while one was open for 9% of the time, Pallas kernels for 2%

profile of v1, /device:TPU:0, one launch (start us, length us, event | category | flops | bytes accessed | tf_op | source)
XLA Modules:
  0.0 175.1 jit_solution(15667425323114558665)
XLA Ops:
  0.6 7.4 %all-to-all-start.1 = ((bf16[8,64,1024]{2,1,0:T(8,128)(2,1)}), bf16[8,64,1024]{2,1,0:T(8,128)(2,1)S(1)}, u32[]{:S(2)}, u32[]{:S(2)}) async-start(bf16[8,64,1024]{2,1,0:T(8,128)(2,1)} %param.19), calls=%async_computation.1 | async-start | bytes 2097152 | tf_op jit(solution)/shard_map/all_to_all | solution.py:217
  8.1 1.5 collective-permute-start
  10.6 3.3 %filter.1 = bf16[8,64,1024]{2,1,0:T(8,128)(2,1)} custom-call(bf16[8,64,1024]{2,1,0:T(8,128)(2,1)S(1)} %copy-done, bf16[8,64,128]{2,1,0:T(8,128)(2,1)S(1)} %collective-permute-done.rim_ref, f32[64,256]{1,0:T(8,128)S(1)} %pad_convert_fusion.taps_ref), custom_call_target="tpu_custom_call" | custom-call | flops 268435456 | bytes 2097152 | tf_op jit(solution)/shard_map/filter/pallas_call | solution.py:49
  13.9 19.9 %all-to-all-done.1 = bf16[8,64,1024]{2,1,0:T(8,128)(2,1)S(1)} async-done(((bf16[8,64,1024]{2,1,0:T(8,128)(2,1)}), bf16[8,64,1024]{2,1,0:T(8,128)(2,1)S(1)}, u32[]{:S(2)}, u32[]{:S(2)}) %all-to-all-start.1) | async-done | bytes 1048608 | tf_op jit(solution)/shard_map/all_to_all | solution.py:217
  33.8 3.6 %all-to-all-start = ((bf16[8,64,1024]{2,1,0:T(8,128)(2,1)}), bf16[8,64,1024]{2,1,0:T(8,128)(2,1)S(1)}, u32[]{:S(2)}, u32[]{:S(2)}) async-start(bf16[8,64,1024]{2,1,0:T(8,128)(2,1)} %filter.1), calls=%async_computation | async-start | bytes 2097152 | tf_op jit(solution)/shard_map/all_to_all | solution.py:217
  40.0 1.1 pad_maximum_fusion.1.wqkv_ref
  41.1 22.3 %all-to-all-done = bf16[8,64,1024]{2,1,0:T(8,128)(2,1)S(1)} async-done(((bf16[8,64,1024]{2,1,0:T(8,128)(2,1)}), bf16[8,64,1024]{2,1,0:T(8,128)(2,1)S(1)}, u32[]{:S(2)}, u32[]{:S(2)}) %all-to-all-start) | async-done | bytes 1048608 | tf_op jit(solution)/shard_map/all_to_all | solution.py:217
  63.4 0.9 copy-done.1
  64.3 0.9 copy-done.2
  65.3 0.9 copy-done.3
  66.2 0.9 copy-done.4
  67.1 27.7 %attend.1 = (bf16[512,1024]{1,0:T(8,128)(2,1)S(1)}, f32[4,256,256]{2,1,0:T(8,128)S(1)}) custom-call(bf16[512,1024]{1,0:T(8,128)(2,1)S(1)} %bitcast.17, bf16[512,1024]{1,0:T(8,128)(2,1)S(1)} %bitcast.16, s32[512,4]{1,0:T(8,128)S(1)} %copy-done.2, f32[1,512]{1,0:T(1,128)S(1)} %bitcast.19, f32[512,1]{1,0:T(8,128)S(1)} %copy-done.1, f32[512,1]{1,0:T(8,128)S(1)} %copy-done.3, ...), custom_call_target="tpu_custom_call" | custom-call | flops 16000000000 | bytes 3145728 | tf_op jit(solution)/shard_map/attend/pallas_call | solution.py:154
  95.0 11.4 %all_to_all.66 = bf16[4,256,256]{2,1,0:T(8,128)(2,1)S(1)} all-to-all(bf16[4,256,256]{2,1,0:T(8,128)(2,1)S(1)} %convert_element_type.23), channel_id=1, replica_groups=mesh['tm'=4,'contact'=8] {'tm'}, dimensions={0} | all-to-all | bytes 1048576 | tf_op jit(solution)/shard_map/all_to_all | solution.py:185
  106.4 10.8 %all_to_all.67 = bf16[8,32,256]{2,1,0:T(8,128)(2,1)S(1)} all-to-all(bf16[8,32,256]{2,1,0:T(8,128)(2,1)S(1)} %bitcast.24), channel_id=1, replica_groups=mesh['tm'=4,'contact'=8] {'contact'}, dimensions={0} | all-to-all | bytes 262144 | tf_op jit(solution)/shard_map/all_to_all | solution.py:185
  117.3 9.7 %all_to_all.68 = bf16[8,32,256]{2,1,0:T(8,128)(2,1)S(1)} all-to-all(bf16[8,32,256]{2,1,0:T(8,128)(2,1)S(1)} %bitcast.25), channel_id=1, replica_groups=mesh['tm'=4,'contact'=8] {'contact'}, dimensions={0} | all-to-all | bytes 262144 | tf_op jit(solution)/shard_map/all_to_all | solution.py:185
  127.9 4.3 %all-to-all-start.6 = ((bf16[4,256,256]{2,1,0:T(8,128)(2,1)}), bf16[4,256,256]{2,1,0:T(8,128)(2,1)}, u32[]{:S(2)}, u32[]{:S(2)}) async-start(bf16[4,256,256]{2,1,0:T(8,128)(2,1)} %bitcast.9), calls=%async_computation.6 | async-start | bytes 1048576 | tf_op jit(solution)/shard_map/all_to_all | solution.py:185
  132.2 1.6 copy.30
  134.4 6.8 %reduce.2 = bf16[512,1024]{1,0:T(8,128)(2,1)S(1)} reduce(bf16[512,1,1024]{2,1,0:T(2,128)(2,1)S(1)} %bitcast.21, bf16[]{:T(256)} %broadcast.2), dimensions={1}, to_apply=%bitcast.14.reduce_sub_computation | reduce | bytes 2097154
  141.1 1.6 reshape.29
  142.7 3.6 %all-to-all-start.2 = ((bf16[8,2,32768]{2,1,0:T(2,128)(2,1)}), bf16[8,2,32768]{2,1,0:T(2,128)(2,1)S(1)}, u32[]{:S(2)}, u32[]{:S(2)}) async-start(bf16[8,2,32768]{2,1,0:T(2,128)(2,1)} %reshape.29), calls=%async_computation.2 | async-start | bytes 2097152 | tf_op jit(solution)/shard_map/all_to_all | solution.py:237
  146.3 2.1 %convert_element_type.26 = f32[4,256,256]{2,1,0:T(8,128)} convert(bf16[4,256,256]{2,1,0:T(8,128)(2,1)} %all-to-all-done.6) | non-fusion elementwise | flops 262144 | bytes 1572864 | tf_op jit(solution)/shard_map/convert_element_type | solution.py:245
  148.4 24.3 %all-to-all-done.2 = bf16[8,2,32768]{2,1,0:T(2,128)(2,1)S(1)} async-done(((bf16[8,2,32768]{2,1,0:T(2,128)(2,1)}), bf16[8,2,32768]{2,1,0:T(2,128)(2,1)S(1)}, u32[]{:S(2)}, u32[]{:S(2)}) %all-to-all-start.2) | async-done | bytes 1048608 | tf_op jit(solution)/shard_map/all_to_all | solution.py:237
  172.7 1.0 reshape.30
  173.7 1.3 copy.28
  (35 shorter events, 5.1 us)
Async XLA Ops:
  0.6 7.4 %copy-start = (bf16[8,64,1024]{2,1,0:T(8,128)(2,1)S(1)}, bf16[8,64,1024]{2,1,0:T(8,128)(2,1)}, u32[]{:S(2)}) copy-start(bf16[8,64,1024]{2,1,0:T(8,128)(2,1)} %sig_ref.1) | copy-start | bytes 3145732
  0.6 9.0 %copy-start.5 = (bf16[64,129]{1,0:T(8,128)(2,1)S(1)}, bf16[64,129]{1,0:T(8,128)(2,1)}, u32[]{:S(2)}) copy-start(bf16[64,129]{1,0:T(8,128)(2,1)} %param.11) | copy-start | bytes 49540
  0.6 33.2 %all-to-all-start.1 = ((bf16[8,64,1024]{2,1,0:T(8,128)(2,1)}), bf16[8,64,1024]{2,1,0:T(8,128)(2,1)S(1)}, u32[]{:S(2)}, u32[]{:S(2)}) async-start(bf16[8,64,1024]{2,1,0:T(8,128)(2,1)} %param.19), calls=%async_computation.1 | async-start | bytes 2097152 | tf_op jit(solution)/shard_map/all_to_all | solution.py:217
  8.1 2.4 %collective-permute-start = (bf16[8,64,128]{2,1,0:T(8,128)(2,1)S(1)}, bf16[8,64,128]{2,1,0:T(8,128)(2,1)S(1)}, u32[]{:S(2)}, u32[]{:S(2)}) collective-permute-start(bf16[8,64,128]{2,1,0:T(8,128)(2,1)S(1)} %slice.3), channel_id=1, source_target_pairs={{0,8},{8,16},{16,24},{1,9},{9,17},{17,25},{2,10},{10,18},{18,26},{... | collective-permute-start | bytes 393224 | tf_op jit(solution)/shard_map/ppermute | solution.py:223
  9.6 27.8 %copy-start.8 = (s32[512]{0:T(512)S(1)}, s32[512]{0:T(512)}, u32[]{:S(2)}) copy-start(s32[512]{0:T(512)} %param.13) | copy-start | bytes 6148
  9.6 28.7 %copy-start.6 = (s32[512,4]{0,1:T(4,128)S(1)}, s32[512,4]{0,1:T(4,128)}, u32[]{:S(2)}) copy-start(s32[512,4]{0,1:T(4,128)} %param.12) | copy-start | bytes 24580
  9.6 29.5 %copy-start.7 = (f32[512]{0:T(512)S(1)}, f32[512]{0:T(512)}, u32[]{:S(2)}) copy-start(f32[512]{0:T(512)} %param.14) | copy-start | bytes 6148
  33.8 29.5 %all-to-all-start = ((bf16[8,64,1024]{2,1,0:T(8,128)(2,1)}), bf16[8,64,1024]{2,1,0:T(8,128)(2,1)S(1)}, u32[]{:S(2)}, u32[]{:S(2)}) async-start(bf16[8,64,1024]{2,1,0:T(8,128)(2,1)} %filter.1), calls=%async_computation | async-start | bytes 2097152 | tf_op jit(solution)/shard_map/all_to_all | solution.py:217
  63.4 1.0 copy-start.1
  64.3 0.9 copy-start.2
  65.3 0.9 copy-start.3
  66.2 0.9 copy-start.4
  127.9 14.8 %all-to-all-start.6 = ((bf16[4,256,256]{2,1,0:T(8,128)(2,1)}), bf16[4,256,256]{2,1,0:T(8,128)(2,1)}, u32[]{:S(2)}, u32[]{:S(2)}) async-start(bf16[4,256,256]{2,1,0:T(8,128)(2,1)} %bitcast.9), calls=%async_computation.6 | async-start | bytes 1048576 | tf_op jit(solution)/shard_map/all_to_all | solution.py:185
  142.7 30.0 %all-to-all-start.2 = ((bf16[8,2,32768]{2,1,0:T(2,128)(2,1)}), bf16[8,2,32768]{2,1,0:T(2,128)(2,1)S(1)}, u32[]{:S(2)}, u32[]{:S(2)}) async-start(bf16[8,2,32768]{2,1,0:T(2,128)(2,1)} %reshape.29), calls=%async_computation.2 | async-start | bytes 2097152 | tf_op jit(solution)/shard_map/all_to_all | solution.py:237

commit v2 on v1

v2 whole, which is shorter than its diff:
```python
import functools

import jax
import jax.numpy as jnp
from jax import lax
from jax.experimental import pallas as pl
from jax.experimental.pallas import tpu as pltpu
from jax.sharding import PartitionSpec as P

HEADS = 4
F32 = jnp.float32
BF16 = jnp.bfloat16


def mm(left, right, left_dim=1, right_dim=0):
    return lax.dot_general(
        left, right, (((left_dim,), (right_dim,)), ((), ())), preferred_element_type=F32
    )


def filter_kernel(sig_ref, rim_ref, taps_ref, out_ref):
    batch, rows, slab = sig_ref.shape
    width = rim_ref.shape[2]
    blocks = slab // width
    signal = jnp.swapaxes(sig_ref[...].astype(F32), 0, 1)
    rim = jnp.swapaxes(rim_ref[...].astype(F32), 0, 1)
    results = []
    for row in range(rows):
        own = [signal[row, :, j * width : (j + 1) * width] for j in range(blocks)]
        current = jnp.concatenate(own, axis=0)
        before = jnp.concatenate([rim[row]] + own[:-1], axis=0)
        window = jnp.concatenate([before, current], axis=1).astype(BF16)
        spread = jnp.broadcast_to(taps_ref[row : row + 1, :], (width, 2 * width))
        rolled = pltpu.roll(spread, 0, 1, stride=1, stride_axis=0)
        table = jnp.concatenate([rolled[:, width:], rolled[:, :width]], axis=0).astype(BF16)
        product = mm(window, table)
        results.append(
            jnp.concatenate(
                [product[j * batch : (j + 1) * batch] for j in range(blocks)], axis=1
            )
        )
    out_ref[...] = jnp.swapaxes(jnp.stack(results, axis=0), 0, 1).astype(BF16)


def filter_all(signal, rim, taps):
    batch, contacts, slab = signal.shape
    width = rim.shape[2]
    rows = 16
    return pl.pallas_call(
        filter_kernel,
        grid=(contacts // rows,),
        in_specs=[
            pl.BlockSpec((batch, rows, slab), lambda i: (0, i, 0)),
            pl.BlockSpec((batch, rows, width), lambda i: (0, i, 0)),
            pl.BlockSpec((rows, 2 * width), lambda i: (i, 0)),
        ],
        out_specs=pl.BlockSpec((batch, rows, slab), lambda i: (0, i, 0)),
        out_shape=jax.ShapeDtypeStruct(signal.shape, BF16),
        compiler_params=pltpu.CompilerParams(vmem_limit_bytes=40 * 2**20),
        cost_estimate=pl.CostEstimate(
            flops=4 * batch * contacts * slab * width,
            bytes_accessed=4 * batch * contacts * slab,
            transcendentals=0,
        ),
        name="filter",
    )(signal, rim, taps)


def head_masks(width):
    lane_head = lax.broadcasted_iota(jnp.int32, (1, width), 1) // (width // HEADS)
    return [(lane_head == h).astype(F32) for h in range(HEADS)]


def forward_kernel(
    feat_ref, small_ref, wqkv_ref, wo_ref,
    out_ref, prob_ref, value_ref, kblk_ref, query_t_ref, normed_ref, normed_t_ref, mixed_ref,
    mixed_t_ref, counts, columns, v_blocks,
):
    contacts, width = feat_ref.shape
    scale = (width // HEADS) ** (-0.5)
    slots = small_ref.shape[0] - 3

    @pl.when(pl.program_id(0) == 0)
    def _():
        small = small_ref[...]
        filler = jnp.zeros((128 - small.shape[0], contacts), F32)
        turned = jnp.concatenate([small, filler], axis=0).T
        ids = lax.broadcasted_iota(jnp.int32, (contacts, contacts), 1)
        total = jnp.zeros((contacts, contacts), F32)
        for slot in range(slots):
            hit = turned[:, slot + 2 : slot + 3].astype(jnp.int32) == ids
            total = total + jnp.where(hit, small[0:1], 0.0)
        counts[...] = total.astype(BF16)
        columns[:, 0:1] = turned[:, 0:1]
        columns[:, 1:2] = turned[:, 1:2]
        columns[:, 2:3] = jnp.sum(total, axis=1, keepdims=True)

    live = columns[:, 0:1]
    coef = columns[:, 1:2]
    field = feat_ref[...]
    middle = field.astype(F32)
    beside = mm(counts[...], field)
    ready = live * (middle + coef * (beside - columns[:, 2:3] * middle))
    ready = ready.astype(BF16).astype(F32)
    mean_square = jnp.mean(ready * ready, axis=1, keepdims=True)
    normed = (ready * lax.rsqrt(mean_square + 1e-05)).astype(BF16)
    query = (mm(normed, wqkv_ref[:, :width]) * scale).astype(BF16)
    keys = mm(normed, wqkv_ref[:, width : 2 * width]).astype(BF16)
    value = mm(normed, wqkv_ref[:, 2 * width :]).astype(BF16)
    masks = [m.astype(BF16) for m in head_masks(width)]
    bias = jnp.where(small_ref[0:1, :] > 0, 0.0, -1e30)
    for h in range(HEADS):
        kblk_ref[h * contacts : (h + 1) * contacts, :] = keys * masks[h]
        v_blocks[h * contacts : (h + 1) * contacts, :] = value * masks[h]
    for h in range(HEADS):
        scores = mm(query * masks[h], keys, 1, 1) + bias
        top = jnp.max(scores, axis=1, keepdims=True)
        raised = jnp.exp(scores - top)
        share = 1.0 / jnp.sum(raised, axis=1, keepdims=True)
        prob_ref[:, h * contacts : (h + 1) * contacts] = (raised * share).astype(BF16)
    mixed = mm(prob_ref[...], v_blocks[...]).astype(BF16)
    out_ref[...] = mm(mixed, wo_ref[...]).astype(BF16)
    value_ref[...] = value
    query_t_ref[...] = query.T
    normed_ref[...] = normed
    normed_t_ref[...] = normed.T
    mixed_ref[...] = mixed
    mixed_t_ref[...] = mixed.T


def backward_kernel(
    up_ref, prob_ref, value_ref, kblk_ref, query_t_ref, normed_ref, normed_t_ref, mixed_ref,
    mixed_t_ref, wo_ref, out_ref, total, gs_all,
):
    contacts, width = up_ref.shape
    head = width // HEADS
    scale = head ** (-0.5)
    step = pl.program_id(0)

    @pl.when(step == 0)
    def _():
        total[...] = jnp.zeros_like(total)

    upstream = up_ref[...]
    normed = normed_ref[...]
    value = value_ref[...]
    back = mm(upstream, wo_ref[...], 1, 1).astype(BF16)
    back_t = back.T
    inner = back.astype(F32) * mixed_ref[...].astype(F32)
    masks = head_masks(width)
    grad_value_t = []
    grad_key_t = []
    for h in range(HEADS):
        grad_prob = mm(back * masks[h].astype(BF16), value, 1, 1)
        row_inner = jnp.sum(inner * masks[h], axis=1, keepdims=True)
        prob = prob_ref[:, h * contacts : (h + 1) * contacts]
        grad_score = (prob.astype(F32) * (grad_prob - row_inner)).astype(BF16)
        gs_all[:, h * contacts : (h + 1) * contacts] = grad_score
        grad_value_t.append(mm(back_t[h * head : (h + 1) * head], prob))
        grad_key_t.append(mm(query_t_ref[h * head : (h + 1) * head, :], grad_score))
    grad_query = (mm(gs_all[...], kblk_ref[...]) * scale).astype(BF16)
    total[0] += mm(normed_t_ref[...], grad_query)
    total[1] += mm(jnp.concatenate(grad_key_t, axis=0).astype(BF16), normed)
    total[2] += mm(jnp.concatenate(grad_value_t, axis=0).astype(BF16), normed)
    total[3] += mm(mixed_t_ref[...], upstream)

    @pl.when(step == pl.num_programs(0) - 1)
    def _():
        out_ref[0] = total[0].astype(BF16)
        out_ref[1] = total[1].T.astype(BF16)
        out_ref[2] = total[2].T.astype(BF16)
        out_ref[3] = total[3].astype(BF16)


def whole(shape):
    return pl.BlockSpec(shape, lambda i: (0,) * len(shape))


def forward(features, small, w_qkv, w_out):
    contacts, span = features.shape
    width = w_out.shape[0]
    groups = span // width
    shapes = [
        (contacts, width), (contacts, HEADS * contacts), (contacts, width),
        (HEADS * contacts, width), (width, contacts), (contacts, width), (width, contacts),
        (contacts, width), (width, contacts),
    ]
    specs = [pl.BlockSpec(shape, lambda i: (0, i)) for shape in shapes]
    return pl.pallas_call(
        forward_kernel,
        grid=(groups,),
        in_specs=[specs[0], whole(small.shape), whole(w_qkv.shape), whole(w_out.shape)],
        out_specs=specs,
        out_shape=[
            jax.ShapeDtypeStruct((shape[0], groups * shape[1]), BF16) for shape in shapes
        ],
        scratch_shapes=[
            pltpu.VMEM((contacts, contacts), BF16),
            pltpu.VMEM((contacts, 128), F32),
            pltpu.VMEM((HEADS * contacts, width), BF16),
        ],
        compiler_params=pltpu.CompilerParams(vmem_limit_bytes=48 * 2**20),
        cost_estimate=pl.CostEstimate(
            flops=groups * 5 * 10**9,
            bytes_accessed=20 * contacts * span,
            transcendentals=groups * HEADS * contacts * contacts,
        ),
        name="forward",
    )(features, small, w_qkv, w_out)


def backward(upstream, kept, w_out):
    contacts, span = upstream.shape
    width = w_out.shape[0]
    groups = span // width
    inputs = [upstream] + list(kept)
    return pl.pallas_call(
        backward_kernel,
        grid=(groups,),
        in_specs=[
            pl.BlockSpec((item.shape[0], item.shape[1] // groups), lambda i: (0, i))
            for item in inputs
        ]
        + [whole(w_out.shape)],
        out_specs=whole((4, width, width)),
        out_shape=jax.ShapeDtypeStruct((4, width, width), BF16),
        scratch_shapes=[
            pltpu.VMEM((4, width, width), F32),
            pltpu.VMEM((contacts, HEADS * contacts), BF16),
        ],
        compiler_params=pltpu.CompilerParams(vmem_limit_bytes=48 * 2**20),
        cost_estimate=pl.CostEstimate(
            flops=groups * 5 * 10**9, bytes_accessed=20 * contacts * span, transcendentals=0
        ),
        name="backward",
    )(*inputs, w_out)


def exchange(value, axis):
    return lax.all_to_all(value, axis, split_axis=0, concat_axis=0, tiled=True)


def scatter_sum(value, axis):
    count = lax.axis_size(axis)
    parts = exchange(value.astype(BF16), axis)
    parts = parts.reshape((count, value.shape[0] // count) + value.shape[1:])
    return jnp.sum(parts.astype(F32), axis=0)


def gather(value, axis):
    count = lax.axis_size(axis)
    return exchange(jnp.concatenate([value] * count, axis=0), axis)


def local(
    signal, fir_taps, neighbours, live_mask, lap_coef, w_query, w_key, w_value, w_out, cotangent
):
    batch, contacts_here, slab = signal.shape
    rim_width = fir_taps.shape[1] - 1
    width = w_query.shape[0]
    tm_count = lax.axis_size("tm")
    count = lax.axis_size("contact")
    pieces = max(1, count // batch)

    def by_group(whole):
        if pieces == 1:
            return whole
        cut = whole.reshape(batch, contacts_here, pieces, slab // pieces)
        return cut.transpose(0, 2, 1, 3).reshape(batch * pieces, contacts_here, slab // pieces)

    def to_attend(whole):
        moved = lax.all_to_all(
            by_group(whole), "contact", split_axis=0, concat_axis=1, tiled=True
        )
        held = moved.shape[0]
        return moved.transpose(1, 0, 2).reshape(moved.shape[1], held * moved.shape[2])

    rim = lax.ppermute(
        signal[:, :, slab - rim_width :], "tm", [(i, i + 1) for i in range(tm_count - 1)]
    )
    taps = jnp.pad(fir_taps.astype(F32), ((0, 0), (0, 2 * rim_width - fir_taps.shape[1])))
    filtered = filter_all(signal, rim, taps)
    features = to_attend(filtered)
    cotangent, features = lax.optimization_barrier((cotangent, features))
    upstream = to_attend(cotangent)
    small = jnp.concatenate(
        [live_mask.astype(F32)[None], lap_coef[None], neighbours.T.astype(F32),
         jnp.zeros((1, neighbours.shape[0]), F32)],
        axis=0,
    )
    attended, *kept = forward(
        features, small, jnp.concatenate([w_query, w_key, w_value], axis=1), w_out
    )
    attended, upstream = lax.optimization_barrier((attended, upstream))
    held = batch * pieces // count
    shaped = attended.reshape(attended.shape[0], held, slab // pieces).transpose(1, 0, 2)
    shaped = shaped.reshape(held * count, contacts_here, slab // pieces)
    if held > 1:
        shaped = shaped.reshape(held, count, contacts_here, slab // pieces).transpose(1, 0, 2, 3)
        shaped = shaped.reshape(count * held, contacts_here, slab // pieces)
    returned = exchange(shaped, "contact")
    if pieces > 1:
        returned = returned.reshape(batch, pieces, contacts_here, slab // pieces)
        returned = returned.transpose(0, 2, 1, 3).reshape(batch, contacts_here, slab)
    grads = backward(upstream, kept, w_out)
    grad_scale = (batch * (slab // width) * tm_count * neighbours.shape[0]) ** (-0.5)
    part = scatter_sum(grads.reshape(4 * width, width), "tm")
    part = scatter_sum(part, "contact") * grad_scale
    summed = gather(gather(part.astype(BF16), "contact"), "tm")
    return (returned, summed.astype(F32).reshape(4, width, width))


def solution(mesh):
    in_specs = (
        P(None, "contact", "tm"),
        P("contact", None),
        P(),
        P(),
        P(),
        P(),
        P(),
        P(),
        P(),
        P(None, "contact", "tm"),
    )
    out_specs = (P(None, "contact", "tm"), P())
    return jax.shard_map(local, mesh=mesh, in_specs=in_specs, out_specs=out_specs, check_vma=False)
```

time: 176 us -> 169 us (0.960)
  waiting for transfers between devices: 67.4 us -> 52.3 us
  blocking collectives: 31.9 us -> 43 us
  Pallas kernels: 31.1 us -> 38.1 us
  other arithmetic: 10.9 us -> 5.16 us
  starting transfers between devices: 20.4 us -> 16.9 us
    all_to_all x1, waiting for transfers between devices: 0.01 us -> 24.6 us  [exchange(): return lax.all_to_all(value, axis, split_axis=0, concat_axis=0, tiled=True)]
    all_to_all x1 -> x0, waiting for transfers between devices: 24.3 us -> none  [local(): lax.all_to_all(shaped, 'contact', split_axis=1, concat_axis=0, tiled=True)]
    all_to_all x2, waiting for transfers between devices: 42.2 us -> 27.6 us  [to_attend(): lax.all_to_all(by_group(whole), 'contact', split_axis=0, concat_axis=1, t...]
    all_to_all x3 -> x4, blocking collectives: 31.9 us -> 43 us  [exchange(): return lax.all_to_all(value, axis, split_axis=0, concat_axis=0, tiled=True)]
    pallas_call x1 -> x2, Pallas kernels: 27.7 us -> 34.8 us  [the longest x1 18.2 us: forward(): pl.pallas_call(forward_kernel, grid=(groups,), in_specs=[specs[0], whole(...]
    unnamed x2 -> x1, other arithmetic: 6.79 us -> 0.01 us
    all_to_all x1 -> x0, starting transfers between devices: 3.56 us -> none  [local(): lax.all_to_all(shaped, 'contact', split_axis=1, concat_axis=0, tiled=True)]
    unnamed x29 -> x27, local copies, waits for them, and re-layouts: 9.14 us -> 10.7 us
  transfers between devices with their start and end apart: 5 -> 4, of which waited for: 4 -> 4; matrix products, arithmetic and copies ran while one was open for 9% -> 3% of each run, Pallas kernels for 2% -> 11%
where the time goes in v2:
time: 169 us; the launch traced here: 168 us
  waiting for transfers between devices  52.3 us (31%)
  blocking collectives  43 us (25%)
  Pallas kernels  38.1 us (23%)
  starting transfers between devices  16.9 us (10%)
  local copies, waits for them, and re-layouts  11.7 us (7%)
  other arithmetic  5.16 us (3%)
    all_to_all x4, blocking collectives, exchange(): return lax.all_to_all(value, axis, split_axis=0, concat_axis=0, tiled=True)  43 us
    all_to_all x2, waiting for transfers between devices, to_attend(): lax.all_to_all(by_group(whole), 'contact', split_axis=0, concat_axis=1, t...  27.6 us
    all_to_all x1, waiting for transfers between devices, exchange(): return lax.all_to_all(value, axis, split_axis=0, concat_axis=0, tiled=True)  24.6 us
    pallas_call x1, Pallas kernels, forward(): pl.pallas_call(forward_kernel, grid=(groups,), in_specs=[specs[0], whole(...  18.2 us
    pallas_call x1, Pallas kernels, backward(): pl.pallas_call(backward_kernel, grid=(groups,), in_specs=[pl.BlockSpec((i...  16.5 us
    all_to_all x2, starting transfers between devices, to_attend(): lax.all_to_all(by_group(whole), 'contact', split_axis=0, concat_axis=1, t...  10.9 us
    unnamed x27, local copies, waits for them, and re-layouts  10.7 us
    all_to_all x1, starting transfers between devices, exchange(): return lax.all_to_all(value, axis, split_axis=0, concat_axis=0, tiled=True)  3.56 us
  transfers between devices with their start and end apart: 4, of which 4 were waited for; matrix products, arithmetic and copies ran while one was open for 3% of the time, Pallas kernels for 11%

profile of v2, /device:TPU:0, one launch (start us, length us, event | category | flops | bytes accessed | tf_op | source)
XLA Modules:
  0.0 167.9 jit_solution(10248906689051639964)
XLA Ops:
  1.5 2.4 %collective-permute-start = (bf16[8,64,128]{2,1,0:T(8,128)(2,1)S(1)}, bf16[8,64,128]{2,1,0:T(8,128)(2,1)S(1)}, u32[]{:S(2)}, u32[]{:S(2)}) collective-permute-start(bf16[8,64,128]{2,1,0:T(8,128)(2,1)S(1)} %slice.3), channel_id=1, source_target_pairs={{0,8},{8,16},{16,24},{1,9},{9,17},{17,25},{2,10},{10,18},{18,26},{... | collective-permute-start | bytes 393224 | tf_op jit(solution)/shard_map/ppermute | solution.py:278
  4.9 1.2 copy-done
  6.1 3.3 %filter.1 = bf16[8,64,1024]{2,1,0:T(8,128)(2,1)} custom-call(bf16[8,64,1024]{2,1,0:T(8,128)(2,1)S(1)} %copy-done, bf16[8,64,128]{2,1,0:T(8,128)(2,1)S(1)} %collective-permute-done.rim_ref, f32[64,256]{1,0:T(8,128)S(1)} %pad_convert_fusion.taps_ref), custom_call_target="tpu_custom_call" | custom-call | flops 268435456 | bytes 2097152 | tf_op jit(solution)/shard_map/filter/pallas_call | solution.py:49
  9.5 6.7 %all-to-all-start = ((bf16[8,64,1024]{2,1,0:T(8,128)(2,1)}), bf16[8,64,1024]{2,1,0:T(8,128)(2,1)S(1)}, u32[]{:S(2)}, u32[]{:S(2)}) async-start(bf16[8,64,1024]{2,1,0:T(8,128)(2,1)} %filter.1), calls=%async_computation | async-start | bytes 2097152 | tf_op jit(solution)/shard_map/all_to_all | solution.py:272
  16.9 1.1 pad_maximum_fusion.1.wqkv_ref
  19.4 23.1 %all-to-all-done = bf16[8,64,1024]{2,1,0:T(8,128)(2,1)S(1)} async-done(((bf16[8,64,1024]{2,1,0:T(8,128)(2,1)}), bf16[8,64,1024]{2,1,0:T(8,128)(2,1)S(1)}, u32[]{:S(2)}, u32[]{:S(2)}) %all-to-all-start) | async-done | bytes 1048608 | tf_op jit(solution)/shard_map/all_to_all | solution.py:272
  42.5 1.0 copy-done.9
  43.5 4.3 %all-to-all-start.1 = ((bf16[8,64,1024]{2,1,0:T(8,128)(2,1)}), bf16[8,64,1024]{2,1,0:T(8,128)(2,1)S(1)}, u32[]{:S(2)}, u32[]{:S(2)}) async-start(bf16[8,64,1024]{2,1,0:T(8,128)(2,1)} %param.19), calls=%async_computation.1 | async-start | bytes 2097152 | tf_op jit(solution)/shard_map/all_to_all | solution.py:272
  48.7 18.2 %forward.1 = (bf16[512,1024]{1,0:T(8,128)(2,1)}, bf16[512,8192]{1,0:T(8,128)(2,1)}, bf16[512,1024]{1,0:T(8,128)(2,1)S(1)}, bf16[2048,1024]{1,0:T(8,128)(2,1)}, b...) custom-call(bf16[512,1024]{1,0:T(8,128)(2,1)} %bitcast.14, ...), custom_call_target="tpu_custom_call" | custom-call | flops 20000000000 | bytes 10485760 | tf_op jit(solution)/shard_map/forward/pallas_call | solution.py:189
  67.9 1.0 copy-done.5
  68.9 1.0 copy-done.7
  69.8 4.4 %all-to-all-done.1 = bf16[8,64,1024]{2,1,0:T(8,128)(2,1)S(1)} async-done(((bf16[8,64,1024]{2,1,0:T(8,128)(2,1)}), bf16[8,64,1024]{2,1,0:T(8,128)(2,1)S(1)}, u32[]{:S(2)}, u32[]{:S(2)}) %all-to-all-start.1) | async-done | bytes 1048608 | tf_op jit(solution)/shard_map/all_to_all | solution.py:272
  74.3 1.2 copy-done.4
  75.5 1.2 copy-done.6
  76.7 1.2 copy-done.8
  77.9 16.5 %backward.1 = bf16[4,256,256]{2,1,0:T(8,128)(2,1)S(1)} custom-call(bf16[512,1024]{1,0:T(8,128)(2,1)S(1)} %bitcast.12, bf16[512,8192]{1,0:T(8,128)(2,1)} %get-tuple-element.20.prob_ref, bf16[512,1024]{1,0:T(8,128)(2,1)S(1)} %get-tuple-element.21.value_ref, bf16[2048,1024]{1,0:T(8,128)(2,1)} %get-tuple-element.22.kblk_ref, bf16[256,2048]{1,0:T(8,128)(2,1)S(1)} %copy-done.4, ...), custom_call_target="tpu_custom_call" | custom-call | flops 20000000000 | bytes 10485760 | tf_op jit(solution)/shard_map/backward/pallas_call | solution.py:217
  94.5 11.2 %all_to_all.59 = bf16[4,256,256]{2,1,0:T(8,128)(2,1)S(1)} all-to-all(bf16[4,256,256]{2,1,0:T(8,128)(2,1)S(1)} %backward.1), channel_id=1, replica_groups=mesh['tm'=4,'contact'=8] {'tm'}, dimensions={0} | all-to-all | bytes 1048576 | tf_op jit(solution)/shard_map/all_to_all | solution.py:240
  105.8 10.8 %all_to_all.60 = bf16[8,32,256]{2,1,0:T(8,128)(2,1)S(1)} all-to-all(bf16[8,32,256]{2,1,0:T(8,128)(2,1)S(1)} %bitcast.16), channel_id=1, replica_groups=mesh['tm'=4,'contact'=8] {'contact'}, dimensions={0} | all-to-all | bytes 262144 | tf_op jit(solution)/shard_map/all_to_all | solution.py:240
  116.7 9.7 %all_to_all.61 = bf16[8,32,256]{2,1,0:T(8,128)(2,1)S(1)} all-to-all(bf16[8,32,256]{2,1,0:T(8,128)(2,1)S(1)} %bitcast.17), channel_id=1, replica_groups=mesh['tm'=4,'contact'=8] {'contact'}, dimensions={0} | all-to-all | bytes 262144 | tf_op jit(solution)/shard_map/all_to_all | solution.py:240
  126.5 11.2 %all_to_all.62 = bf16[4,256,256]{2,1,0:T(8,128)(2,1)S(1)} all-to-all(bf16[4,256,256]{2,1,0:T(8,128)(2,1)S(1)} %bitcast.13), channel_id=1, replica_groups=mesh['tm'=4,'contact'=8] {'tm'}, dimensions={0} | all-to-all | bytes 1048576 | tf_op jit(solution)/shard_map/all_to_all | solution.py:240
  137.7 3.6 %all-to-all-start.2 = ((bf16[8,64,1024]{2,1,0:T(8,128)(2,1)}), bf16[8,64,1024]{2,1,0:T(8,128)(2,1)S(1)}, u32[]{:S(2)}, u32[]{:S(2)}) async-start(bf16[8,64,1024]{2,1,0:T(8,128)(2,1)} %bitcast.5), calls=%async_computation.2 | async-start | bytes 2097152 | tf_op jit(solution)/shard_map/all_to_all | solution.py:240
  141.3 1.1 convert_element_type.29
  142.3 24.6 %all-to-all-done.2 = bf16[8,64,1024]{2,1,0:T(8,128)(2,1)S(1)} async-done(((bf16[8,64,1024]{2,1,0:T(8,128)(2,1)}), bf16[8,64,1024]{2,1,0:T(8,128)(2,1)S(1)}, u32[]{:S(2)}, u32[]{:S(2)}) %all-to-all-start.2) | async-done | bytes 1048608 | tf_op jit(solution)/shard_map/all_to_all | solution.py:240
  166.9 1.0 copy.20
  (31 shorter events, 6.1 us)
Async XLA Ops:
  1.5 3.3 %collective-permute-start = (bf16[8,64,128]{2,1,0:T(8,128)(2,1)S(1)}, bf16[8,64,128]{2,1,0:T(8,128)(2,1)S(1)}, u32[]{:S(2)}, u32[]{:S(2)}) collective-permute-start(bf16[8,64,128]{2,1,0:T(8,128)(2,1)S(1)} %slice.3), channel_id=1, source_target_pairs={{0,8},{8,16},{16,24},{1,9},{9,17},{17,25},{2,10},{10,18},{18,26},{... | collective-permute-start | bytes 393224 | tf_op jit(solution)/shard_map/ppermute | solution.py:278
  4.9 1.2 copy-start
  9.5 33.1 %all-to-all-start = ((bf16[8,64,1024]{2,1,0:T(8,128)(2,1)}), bf16[8,64,1024]{2,1,0:T(8,128)(2,1)S(1)}, u32[]{:S(2)}, u32[]{:S(2)}) async-start(bf16[8,64,1024]{2,1,0:T(8,128)(2,1)} %filter.1), calls=%async_computation | async-start | bytes 2097152 | tf_op jit(solution)/shard_map/all_to_all | solution.py:272
  42.5 1.0 copy-start.9
  43.5 30.8 %all-to-all-start.1 = ((bf16[8,64,1024]{2,1,0:T(8,128)(2,1)}), bf16[8,64,1024]{2,1,0:T(8,128)(2,1)S(1)}, u32[]{:S(2)}, u32[]{:S(2)}) async-start(bf16[8,64,1024]{2,1,0:T(8,128)(2,1)} %param.19), calls=%async_computation.1 | async-start | bytes 2097152 | tf_op jit(solution)/shard_map/all_to_all | solution.py:272
  47.8 0.9 copy-start.1
  48.7 25.6 %copy-start.2 = (bf16[256,256]{1,0:T(8,128)(2,1)S(1)}, bf16[256,256]{1,0:T(8,128)(2,1)}, u32[]{:S(2)}) copy-start(bf16[256,256]{1,0:T(8,128)(2,1)} %wo_ref.3) | copy-start | bytes 393220
  66.9 1.0 copy-start.3
  67.9 1.0 copy-start.5
  68.9 1.0 copy-start.7
  74.3 1.2 copy-start.4
  75.5 1.2 copy-start.6
  76.7 1.2 copy-start.8
  137.7 29.2 %all-to-all-start.2 = ((bf16[8,64,1024]{2,1,0:T(8,128)(2,1)}), bf16[8,64,1024]{2,1,0:T(8,128)(2,1)S(1)}, u32[]{:S(2)}, u32[]{:S(2)}) async-start(bf16[8,64,1024]{2,1,0:T(8,128)(2,1)} %bitcast.5), calls=%async_computation.2 | async-start | bytes 2097152 | tf_op jit(solution)/shard_map/all_to_all | solution.py:240

commit v3 on v2

v3 whole, which is shorter than its diff:
```python
import functools

import jax
import jax.numpy as jnp
from jax import lax
from jax.experimental import pallas as pl
from jax.experimental.pallas import tpu as pltpu
from jax.sharding import PartitionSpec as P

HEADS = 4
F32 = jnp.float32
BF16 = jnp.bfloat16


def mm(left, right, left_dim=1, right_dim=0):
    return lax.dot_general(
        left, right, (((left_dim,), (right_dim,)), ((), ())), preferred_element_type=F32
    )


def index_spec():
    return pl.BlockSpec(memory_space=pltpu.SMEM)


def params():
    return pltpu.CompilerParams(vmem_limit_bytes=56 * 2**20)


def filter_kernel(place_ref, sig_ref, rim_ref, taps_ref, *refs):
    out_refs, kept = refs[:-1], refs[-1]
    batch, rows, slab = sig_ref.shape
    width = rim_ref.shape[2]
    blocks = slab // width
    pieces = len(out_refs) // batch
    span = slab // pieces
    signal = jnp.swapaxes(sig_ref[...].astype(F32), 0, 1)
    rim = jnp.swapaxes(rim_ref[...].astype(F32), 0, 1)
    results = []
    for row in range(rows):
        own = [signal[row, :, j * width : (j + 1) * width] for j in range(blocks)]
        current = jnp.concatenate(own, axis=0)
        before = jnp.concatenate([rim[row]] + own[:-1], axis=0)
        window = jnp.concatenate([before, current], axis=1).astype(BF16)
        spread = jnp.broadcast_to(taps_ref[row : row + 1, :], (width, 2 * width))
        rolled = pltpu.roll(spread, 0, 1, stride=1, stride_axis=0)
        table = jnp.concatenate([rolled[:, width:], rolled[:, :width]], axis=0).astype(BF16)
        product = mm(window, table)
        results.append(
            jnp.concatenate(
                [product[j * batch : (j + 1) * batch] for j in range(blocks)], axis=1
            )
        )
    filtered = jnp.swapaxes(jnp.stack(results, axis=0), 0, 1).astype(BF16)
    for index in range(batch):
        for piece in range(pieces):
            kept[index * pieces + piece] = filtered[index, :, piece * span : (piece + 1) * span]
    me = place_ref[1]
    for k, out_ref in enumerate(out_refs):
        out_ref[...] = kept[me ^ k]


def filter_all(place, signal, rim, taps, count):
    batch, contacts, slab = signal.shape
    width = rim.shape[2]
    rows = 16
    span = slab * batch // count
    return pl.pallas_call(
        filter_kernel,
        grid=(contacts // rows,),
        in_specs=[
            index_spec(),
            pl.BlockSpec((batch, rows, slab), lambda i: (0, i, 0)),
            pl.BlockSpec((batch, rows, width), lambda i: (0, i, 0)),
            pl.BlockSpec((rows, 2 * width), lambda i: (i, 0)),
        ],
        out_specs=[pl.BlockSpec((rows, span), lambda i: (i, 0))] * count,
        out_shape=[jax.ShapeDtypeStruct((contacts, span), BF16)] * count,
        scratch_shapes=[pltpu.VMEM((count, rows, span), BF16)],
        compiler_params=params(),
        cost_estimate=pl.CostEstimate(
            flops=4 * batch * contacts * slab * width,
            bytes_accessed=4 * batch * contacts * slab,
            transcendentals=0,
        ),
        name="filter",
    )(place, signal, rim, taps)


def split_kernel(place_ref, in_ref, *refs):
    out_refs, kept = refs[:-1], refs[-1]
    batch, _, slab = in_ref.shape
    pieces = len(out_refs) // batch
    span = slab // pieces
    me = place_ref[1]
    if pieces == 1:
        for k, out_ref in enumerate(out_refs):
            out_ref[...] = in_ref[me ^ k]
    else:
        for index in range(batch):
            for piece in range(pieces):
                kept[index * pieces + piece] = in_ref[index, :, piece * span : (piece + 1) * span]
        for k, out_ref in enumerate(out_refs):
            out_ref[...] = kept[me ^ k]


def split(place, value, count):
    batch, contacts, slab = value.shape
    span = slab * batch // count
    shape = (contacts, span)
    return pl.pallas_call(
        split_kernel,
        in_specs=[index_spec(), pl.BlockSpec(value.shape, lambda: (0, 0, 0))],
        out_specs=[pl.BlockSpec(shape, lambda: (0, 0))] * count,
        out_shape=[jax.ShapeDtypeStruct(shape, BF16)] * count,
        scratch_shapes=[pltpu.VMEM((count,) + shape, BF16)],
        compiler_params=params(),
        name="split",
    )(place, value)


def join_kernel(place_ref, *refs):
    in_refs, out_ref, kept = refs[:-2], refs[-2], refs[-1]
    batch, _, slab = out_ref.shape
    pieces = len(in_refs) // batch
    span = slab // pieces
    me = place_ref[1]
    if pieces == 1:
        for k, in_ref in enumerate(in_refs):
            out_ref[me ^ k] = in_ref[...]
    else:
        for k, in_ref in enumerate(in_refs):
            kept[me ^ k] = in_ref[...]
        for index in range(batch):
            for piece in range(pieces):
                out_ref[index, :, piece * span : (piece + 1) * span] = kept[index * pieces + piece]


def join(place, parts, batch):
    contacts, span = parts[0].shape
    shape = (batch, contacts, span * len(parts) // batch)
    return pl.pallas_call(
        join_kernel,
        in_specs=[index_spec()] + [pl.BlockSpec((contacts, span), lambda: (0, 0))] * len(parts),
        out_specs=pl.BlockSpec(shape, lambda: (0, 0, 0)),
        out_shape=jax.ShapeDtypeStruct(shape, BF16),
        scratch_shapes=[pltpu.VMEM((len(parts), contacts, span), BF16)],
        compiler_params=params(),
        name="join",
    )(place, *parts)


def head_masks(width):
    lane_head = lax.broadcasted_iota(jnp.int32, (1, width), 1) // (width // HEADS)
    return [(lane_head == h).astype(F32) for h in range(HEADS)]


def forward_kernel(blocks, place_ref, small_ref, wqkv_ref, wo_ref, *refs):
    feat_refs, refs = refs[:blocks], refs[blocks:]
    out_refs, refs = refs[:blocks], refs[blocks:]
    (
        prob_ref, value_ref, kblk_ref, query_t_ref, normed_ref, normed_t_ref, mixed_ref,
        mixed_t_ref, counts, columns, live_row, v_blocks,
    ) = refs
    rows, width = feat_refs[0].shape
    contacts = rows * blocks
    scale = (width // HEADS) ** (-0.5)
    slots = small_ref.shape[0] - 3

    @pl.when(pl.program_id(0) == 0)
    def _():
        me = place_ref[1]
        small = small_ref[...]
        filler = jnp.zeros((128 - small.shape[0], contacts), F32)
        columns[...] = jnp.concatenate([small, filler], axis=0).T
        turned = jnp.concatenate(
            [columns[pl.ds(pl.multiple_of((me ^ k) * rows, rows), rows), :] for k in range(blocks)],
            axis=0,
        )
        alive = turned.T[0:1]
        live_row[...] = alive
        ids = lax.broadcasted_iota(jnp.int32, (contacts, contacts), 1)
        total = jnp.zeros((contacts, contacts), F32)
        for slot in range(slots):
            here = turned[:, slot + 2 : slot + 3].astype(jnp.int32) ^ (me * rows)
            total = total + jnp.where(here == ids, alive, 0.0)
        counts[...] = total.astype(BF16)
        columns[:, 0:1] = turned[:, 0:1]
        columns[:, 1:2] = turned[:, 1:2]
        columns[:, 2:3] = jnp.sum(total, axis=1, keepdims=True)

    live = columns[:, 0:1]
    coef = columns[:, 1:2]
    field = jnp.concatenate([ref[...] for ref in feat_refs], axis=0)
    middle = field.astype(F32)
    beside = mm(counts[...], field)
    ready = live * (middle + coef * (beside - columns[:, 2:3] * middle))
    ready = ready.astype(BF16).astype(F32)
    mean_square = jnp.mean(ready * ready, axis=1, keepdims=True)
    normed = (ready * lax.rsqrt(mean_square + 1e-05)).astype(BF16)
    query = (mm(normed, wqkv_ref[:, :width]) * scale).astype(BF16)
    keys = mm(normed, wqkv_ref[:, width : 2 * width]).astype(BF16)
    value = mm(normed, wqkv_ref[:, 2 * width :]).astype(BF16)
    masks = [m.astype(BF16) for m in head_masks(width)]
    bias = jnp.where(live_row[...] > 0, 0.0, -1e30)
    for h in range(HEADS):
        kblk_ref[h * contacts : (h + 1) * contacts, :] = keys * masks[h]
        v_blocks[h * contacts : (h + 1) * contacts, :] = value * masks[h]
    for h in range(HEADS):
        scores = mm(query * masks[h], keys, 1, 1) + bias
        top = jnp.max(scores, axis=1, keepdims=True)
        raised = jnp.exp(scores - top)
        share = 1.0 / jnp.sum(raised, axis=1, keepdims=True)
        prob_ref[:, h * contacts : (h + 1) * contacts] = (raised * share).astype(BF16)
    mixed = mm(prob_ref[...], v_blocks[...]).astype(BF16)
    attended = mm(mixed, wo_ref[...]).astype(BF16)
    for k, out_ref in enumerate(out_refs):
        out_ref[...] = attended[k * rows : (k + 1) * rows]
    value_ref[...] = value
    query_t_ref[...] = query.T
    normed_ref[...] = normed
    normed_t_ref[...] = normed.T
    mixed_ref[...] = mixed
    mixed_t_ref[...] = mixed.T


def backward_kernel(blocks, place_ref, wo_ref, *refs):
    up_refs, refs = refs[:blocks], refs[blocks:]
    (
        prob_ref, value_ref, kblk_ref, query_t_ref, normed_ref, normed_t_ref, mixed_ref,
        mixed_t_ref,
    ) = refs[:8]
    out_refs, total, gs_all, chunks = refs[8:-3], refs[-3], refs[-2], refs[-1]
    contacts, width = normed_ref.shape
    head = width // HEADS
    scale = head ** (-0.5)
    step = pl.program_id(0)

    @pl.when(step == 0)
    def _():
        total[...] = jnp.zeros_like(total)

    upstream = jnp.concatenate([ref[...] for ref in up_refs], axis=0)
    normed = normed_ref[...]
    value = value_ref[...]
    back = mm(upstream, wo_ref[...], 1, 1).astype(BF16)
    back_t = back.T
    inner = back.astype(F32) * mixed_ref[...].astype(F32)
    masks = head_masks(width)
    grad_value_t = []
    grad_key_t = []
    for h in range(HEADS):
        grad_prob = mm(back * masks[h].astype(BF16), value, 1, 1)
        row_inner = jnp.sum(inner * masks[h], axis=1, keepdims=True)
        prob = prob_ref[:, h * contacts : (h + 1) * contacts]
        grad_score = (prob.astype(F32) * (grad_prob - row_inner)).astype(BF16)
        gs_all[:, h * contacts : (h + 1) * contacts] = grad_score
        grad_value_t.append(mm(back_t[h * head : (h + 1) * head], prob))
        grad_key_t.append(mm(query_t_ref[h * head : (h + 1) * head, :], grad_score))
    grad_query = (mm(gs_all[...], kblk_ref[...]) * scale).astype(BF16)
    total[0] += mm(normed_t_ref[...], grad_query)
    total[1] += mm(jnp.concatenate(grad_key_t, axis=0).astype(BF16), normed)
    total[2] += mm(jnp.concatenate(grad_value_t, axis=0).astype(BF16), normed)
    total[3] += mm(mixed_t_ref[...], upstream)

    @pl.when(step == pl.num_programs(0) - 1)
    def _():
        count, rows = chunks.shape[:2]
        parts = [total[0], total[1].T, total[2].T, total[3]]
        for c in range(count):
            first = (c * rows) % width
            chunks[c] = parts[c * rows // width][first : first + rows].astype(BF16)
        me = place_ref[0]
        for k, out_ref in enumerate(out_refs):
            out_ref[...] = chunks[me ^ k]


def whole(shape):
    return pl.BlockSpec(shape, lambda i: (0,) * len(shape))


def forward(place, features, small, w_qkv, w_out):
    blocks = len(features)
    rows, span = features[0].shape
    contacts = rows * blocks
    width = w_out.shape[0]
    groups = span // width
    shapes = [(rows, width)] * blocks + [
        (contacts, HEADS * contacts), (contacts, width),
        (HEADS * contacts, width), (width, contacts), (contacts, width), (width, contacts),
        (contacts, width), (width, contacts),
    ]
    specs = [pl.BlockSpec(shape, lambda i: (0, i)) for shape in shapes]
    results = pl.pallas_call(
        functools.partial(forward_kernel, blocks),
        grid=(groups,),
        in_specs=[index_spec(), whole(small.shape), whole(w_qkv.shape), whole(w_out.shape)]
        + specs[:blocks],
        out_specs=specs,
        out_shape=[
            jax.ShapeDtypeStruct((shape[0], groups * shape[1]), BF16) for shape in shapes
        ],
        scratch_shapes=[
            pltpu.VMEM((contacts, contacts), BF16),
            pltpu.VMEM((contacts, 128), F32),
            pltpu.VMEM((1, contacts), F32),
            pltpu.VMEM((HEADS * contacts, width), BF16),
        ],
        compiler_params=params(),
        cost_estimate=pl.CostEstimate(
            flops=groups * 5 * 10**9,
            bytes_accessed=20 * contacts * span,
            transcendentals=groups * HEADS * contacts * contacts,
        ),
        name="forward",
    )(place, small, w_qkv, w_out, *features)
    return results[:blocks], results[blocks:]


def backward(place, upstream, kept, w_out, tm_count):
    blocks = len(upstream)
    rows, span = upstream[0].shape
    contacts = rows * blocks
    width = w_out.shape[0]
    groups = span // width
    inputs = list(upstream) + list(kept)
    chunk = (4 * width // tm_count, width)
    return pl.pallas_call(
        functools.partial(backward_kernel, blocks),
        grid=(groups,),
        in_specs=[index_spec(), whole(w_out.shape)]
        + [
            pl.BlockSpec((item.shape[0], item.shape[1] // groups), lambda i: (0, i))
            for item in inputs
        ],
        out_specs=[whole(chunk)] * tm_count,
        out_shape=[jax.ShapeDtypeStruct(chunk, BF16)] * tm_count,
        scratch_shapes=[
            pltpu.VMEM((4, width, width), F32),
            pltpu.VMEM((contacts, HEADS * contacts), BF16),
            pltpu.VMEM((tm_count,) + chunk, BF16),
        ],
        compiler_params=params(),
        cost_estimate=pl.CostEstimate(
            flops=groups * 5 * 10**9, bytes_accessed=20 * contacts * span, transcendentals=0
        ),
        name="backward",
    )(place, w_out, *inputs)


def add_split(place, parts, count):
    rows, width = parts[0].shape
    piece = rows // count
    ways = len(parts)

    def body(place_ref, *refs):
        total = refs[0][...].astype(F32)
        for ref in refs[1:ways]:
            total = total + ref[...].astype(F32)
        kept = refs[-1]
        for j in range(count):
            kept[j] = total[j * piece : (j + 1) * piece]
        for k, out_ref in enumerate(refs[ways:-1]):
            out_ref[...] = kept[place_ref[1] ^ k].astype(BF16)

    return pl.pallas_call(
        body,
        in_specs=[index_spec()] + [pl.BlockSpec((rows, width), lambda: (0, 0))] * ways,
        out_specs=[pl.BlockSpec((piece, width), lambda: (0, 0))] * count,
        out_shape=[jax.ShapeDtypeStruct((piece, width), BF16)] * count,
        scratch_shapes=[pltpu.VMEM((count, piece, width), F32)],
        compiler_params=params(),
        name="add_split",
    )(place, *parts)


def place_all(place, parts, count):
    rows, width = parts[0].shape
    piece = rows // count
    ways = len(parts)

    def body(place_ref, *refs):
        out_ref = refs[-1]
        for k in range(ways):
            block = refs[k][...].astype(F32)
            for j in range(count):
                out_ref[place_ref[0] ^ k, place_ref[1] ^ j] = block[j * piece : (j + 1) * piece]

    shape = (ways, count, piece, width)
    return pl.pallas_call(
        body,
        in_specs=[index_spec()] + [pl.BlockSpec((rows, width), lambda: (0, 0))] * ways,
        out_specs=pl.BlockSpec(shape, lambda: (0, 0, 0, 0)),
        out_shape=jax.ShapeDtypeStruct(shape, F32),
        compiler_params=params(),
        name="place_all",
    )(place, *parts)


def swap(value, axis, k):
    return lax.ppermute(value, axis, [(i, i ^ k) for i in range(lax.axis_size(axis))])


def swap_all(parts, axis):
    return [parts[0]] + [swap(parts[k], axis, k) for k in range(1, len(parts))]


def local(
    signal, fir_taps, neighbours, live_mask, lap_coef, w_query, w_key, w_value, w_out, cotangent
):
    batch, contacts_here, slab = signal.shape
    rim_width = fir_taps.shape[1] - 1
    width = w_query.shape[0]
    tm_count = lax.axis_size("tm")
    count = lax.axis_size("contact")
    place = jnp.stack([lax.axis_index("tm"), lax.axis_index("contact")]).astype(jnp.int32)

    rim = lax.ppermute(
        signal[:, :, slab - rim_width :], "tm", [(i, i + 1) for i in range(tm_count - 1)]
    )
    early = count // 2
    cotangents = split(place, cotangent, count)
    upstream = swap_all(cotangents[:early], "contact")
    taps = jnp.pad(fir_taps.astype(F32), ((0, 0), (0, 2 * rim_width - fir_taps.shape[1])))
    filtered = filter_all(place, signal, rim, taps, count)
    features = swap_all(filtered, "contact")
    features, late = lax.optimization_barrier((features, cotangents[early:]))
    upstream = upstream + [swap(late[k - early], "contact", k) for k in range(early, count)]
    small = jnp.concatenate(
        [live_mask.astype(F32)[None], lap_coef[None], neighbours.T.astype(F32),
         jnp.zeros((1, neighbours.shape[0]), F32)],
        axis=0,
    )
    attended, kept = forward(
        place, features, small, jnp.concatenate([w_query, w_key, w_value], axis=1), w_out
    )
    returned = swap_all(attended, "contact")
    grads = backward(place, upstream, kept, w_out, tm_count)
    grads = swap_all(grads, "tm")
    pieces = swap_all(add_split(place, grads, count), "contact")
    grad_scale = (batch * (slab // width) * tm_count * neighbours.shape[0]) ** (-0.5)
    mine = sum(piece.astype(F32) for piece in pieces) * grad_scale
    mine = mine.astype(BF16)
    chunk = jnp.concatenate(swap_all([mine] * count, "contact"), axis=0)
    summed = place_all(place, swap_all([chunk] * tm_count, "tm"), count)
    return (join(place, returned, batch), summed.reshape(4, width, width))


def solution(mesh):
    in_specs = (
        P(None, "contact", "tm"),
        P("contact", None),
        P(),
        P(),
        P(),
        P(),
        P(),
        P(),
        P(),
        P(None, "contact", "tm"),
    )
    out_specs = (P(None, "contact", "tm"), P())
    return jax.shard_map(local, mesh=mesh, in_specs=in_specs, out_specs=out_specs, check_vma=False)
```

time: 169 us -> 171 us (1.012)
  starting transfers between devices: 16.9 us -> 67.7 us
  blocking collectives: 43 us -> 0 us
  waiting for transfers between devices: 52.3 us -> 39.3 us
  Pallas kernels: 38.1 us -> 50.2 us
  local copies, waits for them, and re-layouts: 11.7 us -> 5.14 us
  other arithmetic: 5.16 us -> 7.29 us
    ppermute x0 -> x41, starting transfers between devices: none -> 65.3 us  [swap(): lax.ppermute(value, axis, [(i, i ^ k) for i in range(lax.axis_size(axis))])]
    all_to_all x3 -> x0, waiting for transfers between devices: 52.1 us -> none  [the longest x2 27.6 us: to_attend(): lax.all_to_all(by_group(whole), 'contact', split_axis=0, concat_axis=1, t...]
    all_to_all x4 -> x0, blocking collectives: 43 us -> none  [exchange(): return lax.all_to_all(value, axis, split_axis=0, concat_axis=0, tiled=True)]
    ppermute x0 -> x41, waiting for transfers between devices: none -> 39.3 us  [swap(): lax.ppermute(value, axis, [(i, i ^ k) for i in range(lax.axis_size(axis))])]
    all_to_all x3 -> x0, starting transfers between devices: 14.5 us -> none  [the longest x2 10.9 us: to_attend(): lax.all_to_all(by_group(whole), 'contact', split_axis=0, concat_axis=1, t...]
    pallas_call x3 -> x7, Pallas kernels: 38.1 us -> 50.2 us  [the longest x1 19.1 us: forward(): pl.pallas_call(functools.partial(forward_kernel, blocks), grid=(groups,),...]
    unnamed x27 -> x78, local copies, waits for them, and re-layouts: 10.7 us -> 4.14 us
  transfers between devices with their start and end apart: 4 -> 42, of which waited for: 4 -> 14; matrix products, arithmetic and copies ran while one was open for 3% -> 4% of each run, Pallas kernels for 11% -> 17%
where the time goes in v3:
time: 171 us
  starting transfers between devices  67.7 us (40%)
  Pallas kernels  50.2 us (29%)
  waiting for transfers between devices  39.3 us (23%)
  other arithmetic  7.29 us (4%)
  local copies, waits for them, and re-layouts  5.14 us (3%)
    ppermute x41, starting transfers between devices, swap(): lax.ppermute(value, axis, [(i, i ^ k) for i in range(lax.axis_size(axis))])  65.3 us
    ppermute x41, waiting for transfers between devices, swap(): lax.ppermute(value, axis, [(i, i ^ k) for i in range(lax.axis_size(axis))])  39.3 us
    pallas_call x1, Pallas kernels, forward(): pl.pallas_call(functools.partial(forward_kernel, blocks), grid=(groups,),...  19.1 us
    pallas_call x1, Pallas kernels, backward(): pl.pallas_call(functools.partial(backward_kernel, blocks), grid=(groups,)...  17.8 us
    pallas_call x1, Pallas kernels, filter_all(): pl.pallas_call(filter_kernel, grid=(contacts // rows,), in_specs=[index_s...  4.66 us
    unnamed x78, local copies, waits for them, and re-layouts  4.14 us
  transfers between devices with their start and end apart: 42, of which 14 were waited for; matrix products, arithmetic and copies ran while one was open for 4% of the time, Pallas kernels for 17%

profile of v3, /device:TPU:0, one launch (start us, length us, event | category | flops | bytes accessed | tf_op | source)
XLA Modules:
  0.0 170.6 jit_solution(2513029963080855985)
XLA Ops:
  1.5 2.4 %collective-permute-start = (bf16[8,64,128]{2,1,0:T(8,128)(2,1)S(1)}, bf16[8,64,128]{2,1,0:T(8,128)(2,1)S(1)}, u32[]{:S(2)}, u32[]{:S(2)}) collective-permute-start(bf16[8,64,128]{2,1,0:T(8,128)(2,1)S(1)} %slice.3), channel_id=1, source_target_pairs={{0,8},{8,16},{16,24},{1,9},{9,17},{17,25},{2,10},{10,18},{18,26},{... | collective-permute-start | bytes 393224 | tf_op jit(solution)/shard_map/ppermute | solution.py:417
  6.8 2.3 %collective-permute-start.15 = (bf16[64,1024]{1,0:T(8,128)(2,1)}, bf16[64,1024]{1,0:T(8,128)(2,1)S(1)}, u32[]{:S(2)}, u32[]{:S(2)}) collective-permute-start(bf16[64,1024]{1,0:T(8,128)(2,1)} %get-tuple-element.87), channel_id=1, source_target_pairs={{0,1},{1,0},{2,3},{3,2},{4,5},{5,4},{6,7},{7,6},{8,9},{9,8},{10,11... | collective-permute-start | bytes 393224 | tf_op jit(solution)/shard_map/ppermute | solution.py:400
  12.0 4.7 %filter.1 = (bf16[64,1024]{1,0:T(8,128)(2,1)}, bf16[64,1024]{1,0:T(8,128)(2,1)}, bf16[64,1024]{1,0:T(8,128)(2,1)}, bf16[64,1024]{1,0:T(8,128)(2,1)}, bf16[64,102...) custom-call(s32[2]{0:T(128)} %pad_add_fusion.place_ref, ...), custom_call_target="tpu_custom_call" | custom-call | flops 268435456 | bytes 2097152 | tf_op jit(solution)/shard_map/filter/pallas_call | solution.py:67
  20.2 2.6 %collective-permute-start.4 = (bf16[64,1024]{1,0:T(8,128)(2,1)}, bf16[64,1024]{1,0:T(8,128)(2,1)S(1)}, u32[]{:S(2)}, u32[]{:S(2)}) collective-permute-start(bf16[64,1024]{1,0:T(8,128)(2,1)} %get-tuple-element.62), channel_id=1, source_target_pairs={{0,4},{1,5},{2,6},{3,7},{4,0},{5,1},{6,2},{7,3},{8,12},{9,13},{10,... | collective-permute-start | bytes 393224 | tf_op jit(solution)/shard_map/ppermute | solution.py:400
  27.1 3.0 %collective-permute-done.3.refs_3_ = bf16[64,1024]{1,0:T(8,128)(2,1)S(1)} collective-permute-done((bf16[64,1024]{1,0:T(8,128)(2,1)}, bf16[64,1024]{1,0:T(8,128)(2,1)S(1)}, u32[]{:S(2)}, u32[]{:S(2)}) %collective-permute-start.3) | collective-permute-done | bytes 131104 | tf_op jit(solution)/shard_map/ppermute | solution.py:400
  30.1 3.8 %collective-permute-start.6 = (bf16[64,1024]{1,0:T(8,128)(2,1)}, bf16[64,1024]{1,0:T(8,128)(2,1)S(1)}, u32[]{:S(2)}, u32[]{:S(2)}) collective-permute-start(bf16[64,1024]{1,0:T(8,128)(2,1)} %get-tuple-element.64), channel_id=1, source_target_pairs={{0,6},{1,7},{2,4},{3,5},{4,2},{5,3},{6,0},{7,1},{8,14},{9,15},{10,... | collective-permute-start | bytes 393224 | tf_op jit(solution)/shard_map/ppermute | solution.py:400
  38.8 3.6 %collective-permute-done.7.refs_7_ = bf16[64,1024]{1,0:T(8,128)(2,1)S(1)} collective-permute-done((bf16[64,1024]{1,0:T(8,128)(2,1)}, bf16[64,1024]{1,0:T(8,128)(2,1)S(1)}, u32[]{:S(2)}, u32[]{:S(2)}) %collective-permute-start.7) | collective-permute-done | bytes 131104 | tf_op jit(solution)/shard_map/ppermute | solution.py:400
  42.4 8.3 %collective-permute-start.18 = (bf16[64,1024]{1,0:T(8,128)(2,1)}, bf16[64,1024]{1,0:T(8,128)(2,1)S(1)}, u32[]{:S(2)}, u32[]{:S(2)}) collective-permute-start(bf16[64,1024]{1,0:T(8,128)(2,1)} %get-tuple-element.90), channel_id=1, source_target_pairs={{0,4},{1,5},{2,6},{3,7},{4,0},{5,1},{6,2},{7,3},{8,12},{9,13},{10,... | collective-permute-start | bytes 393224 | tf_op jit(solution)/shard_map/ppermute | solution.py:400
  50.8 3.0 %collective-permute-start.20 = (bf16[64,1024]{1,0:T(8,128)(2,1)}, bf16[64,1024]{1,0:T(8,128)(2,1)S(1)}, u32[]{:S(2)}, u32[]{:S(2)}) collective-permute-start(bf16[64,1024]{1,0:T(8,128)(2,1)} %get-tuple-element.92), channel_id=1, source_target_pairs={{0,6},{1,7},{2,4},{3,5},{4,2},{5,3},{6,0},{7,1},{8,14},{9,15},{10,... | collective-permute-start | bytes 393224 | tf_op jit(solution)/shard_map/ppermute | solution.py:400
  55.5 19.1 %forward.1 = (bf16[64,1024]{1,0:T(8,128)(2,1)}, bf16[64,1024]{1,0:T(8,128)(2,1)}, bf16[64,1024]{1,0:T(8,128)(2,1)}, bf16[64,1024]{1,0:T(8,128)(2,1)}, bf16[64,10...) custom-call(s32[2]{0:T(128)} %pad_add_fusion.place_ref, ...), custom_call_target="tpu_custom_call" | custom-call | flops 20000000000 | bytes 10485760 | tf_op jit(solution)/shard_map/forward/pallas_call | solution.py:293
  75.5 17.8 %backward.1 = (bf16[256,256]{1,0:T(8,128)(2,1)}, bf16[256,256]{1,0:T(8,128)(2,1)}, bf16[256,256]{1,0:T(8,128)(2,1)}, bf16[256,256]{1,0:T(8,128)(2,1)}) custom-call(s32[2]{0:T(128)} %pad_add_fusion.place_ref, bf16[256,256]{1,0:T(8,128)(2,1)} %wo_ref.3, bf16[64,1024]{1,0:T(8,128)(2,1)} %get-tuple-element.86.refs_0_, bf16[64,1024]{1,0:T(8,128)(2,1)} %copy-done.22, ...), custom_call_target="tpu_custom_call" | custom-call | flops 20000000000 | bytes 10485760 | tf_op jit(solution)/shard_map/backward/pallas_call | solution.py:327
  95.3 4.7 %collective-permute-done.23.refs_2_ = bf16[256,256]{1,0:T(8,128)(2,1)S(1)} collective-permute-done((bf16[256,256]{1,0:T(8,128)(2,1)}, bf16[256,256]{1,0:T(8,128)(2,1)S(1)}, u32[]{:S(2)}, u32[]{:S(2)}) %collective-permute-start.23) | collective-permute-done | bytes 131104 | tf_op jit(solution)/shard_map/ppermute | solution.py:400
  111.0 2.9 %collective-permute-start.30 = (bf16[32,256]{1,0:T(8,128)(2,1)}, bf16[32,256]{1,0:T(8,128)(2,1)S(1)}, u32[]{:S(2)}, u32[]{:S(2)}) collective-permute-start(bf16[32,256]{1,0:T(8,128)(2,1)} %get-tuple-element.112), channel_id=1, source_target_pairs={{0,6},{1,7},{2,4},{3,5},{4,2},{5,3},{6,0},{7,1},{8,14},{9,15},{10,... | collective-permute-start | bytes 49160 | tf_op jit(solution)/shard_map/ppermute | solution.py:400
  116.7 3.8 %collective-permute-done.31 = bf16[32,256]{1,0:T(8,128)(2,1)S(1)} collective-permute-done((bf16[32,256]{1,0:T(8,128)(2,1)}, bf16[32,256]{1,0:T(8,128)(2,1)S(1)}, u32[]{:S(2)}, u32[]{:S(2)}) %collective-permute-start.31) | collective-permute-done | bytes 16416 | tf_op jit(solution)/shard_map/ppermute | solution.py:400
  123.3 2.9 %collective-permute-start.10 = (bf16[64,1024]{1,0:T(8,128)(2,1)S(1)}, bf16[64,1024]{1,0:T(8,128)(2,1)S(1)}, u32[]{:S(2)}, u32[]{:S(2)}) collective-permute-start(bf16[64,1024]{1,0:T(8,128)(2,1)S(1)} %copy-done.19), channel_id=1, source_target_pairs={{0,3},{1,2},{2,1},{3,0},{4,7},{5,6},{6,5},{7,4},{8,11},{9,10},{10,... | collective-permute-start | bytes 393224 | tf_op jit(solution)/shard_map/ppermute | solution.py:400
  127.2 3.7 %collective-permute-done.33 = bf16[32,256]{1,0:T(8,128)(2,1)S(1)} collective-permute-done((bf16[32,256]{1,0:T(8,128)(2,1)S(1)}, bf16[32,256]{1,0:T(8,128)(2,1)S(1)}, u32[]{:S(2)}, u32[]{:S(2)}) %collective-permute-start.33) | collective-permute-done | bytes 16416 | tf_op jit(solution)/shard_map/ppermute | solution.py:400
  131.9 3.7 %collective-permute-done.34 = bf16[32,256]{1,0:T(8,128)(2,1)S(1)} collective-permute-done((bf16[32,256]{1,0:T(8,128)(2,1)S(1)}, bf16[32,256]{1,0:T(8,128)(2,1)S(1)}, u32[]{:S(2)}, u32[]{:S(2)}) %collective-permute-start.34) | collective-permute-done | bytes 16416 | tf_op jit(solution)/shard_map/ppermute | solution.py:400
  137.2 3.1 %collective-permute-done.35 = bf16[32,256]{1,0:T(8,128)(2,1)S(1)} collective-permute-done((bf16[32,256]{1,0:T(8,128)(2,1)S(1)}, bf16[32,256]{1,0:T(8,128)(2,1)S(1)}, u32[]{:S(2)}, u32[]{:S(2)}) %collective-permute-start.35) | collective-permute-done | bytes 16416 | tf_op jit(solution)/shard_map/ppermute | solution.py:400
  140.3 2.4 %collective-permute-start.36 = (bf16[32,256]{1,0:T(8,128)(2,1)S(1)}, bf16[32,256]{1,0:T(8,128)(2,1)S(1)}, u32[]{:S(2)}, u32[]{:S(2)}) collective-permute-start(bf16[32,256]{1,0:T(8,128)(2,1)S(1)} %get-tuple-element.115), channel_id=1, source_target_pairs={{0,5},{1,4},{2,7},{3,6},{4,1},{5,0},{6,3},{7,2},{8,13},{9,12},{10,... | collective-permute-start | bytes 49160 | tf_op jit(solution)/shard_map/ppermute | solution.py:400
  142.7 3.3 %collective-permute-done.36 = bf16[32,256]{1,0:T(8,128)(2,1)S(1)} collective-permute-done((bf16[32,256]{1,0:T(8,128)(2,1)S(1)}, bf16[32,256]{1,0:T(8,128)(2,1)S(1)}, u32[]{:S(2)}, u32[]{:S(2)}) %collective-permute-start.36) | collective-permute-done | bytes 16416 | tf_op jit(solution)/shard_map/ppermute | solution.py:400
  145.9 4.5 %collective-permute-start.37 = (bf16[32,256]{1,0:T(8,128)(2,1)S(1)}, bf16[32,256]{1,0:T(8,128)(2,1)S(1)}, u32[]{:S(2)}, u32[]{:S(2)}) collective-permute-start(bf16[32,256]{1,0:T(8,128)(2,1)S(1)} %get-tuple-element.115), channel_id=1, source_target_pairs={{0,6},{1,7},{2,4},{3,5},{4,2},{5,3},{6,0},{7,1},{8,14},{9,15},{10,... | collective-permute-start | bytes 49160 | tf_op jit(solution)/shard_map/ppermute | solution.py:400
  152.2 3.3 %collective-permute-start.12 = (bf16[64,1024]{1,0:T(8,128)(2,1)S(1)}, bf16[64,1024]{1,0:T(8,128)(2,1)S(1)}, u32[]{:S(2)}, u32[]{:S(2)}) collective-permute-start(bf16[64,1024]{1,0:T(8,128)(2,1)S(1)} %copy-done.17), channel_id=1, source_target_pairs={{0,5},{1,4},{2,7},{3,6},{4,1},{5,0},{6,3},{7,2},{8,13},{9,12},{10,... | collective-permute-start | bytes 393224 | tf_op jit(solution)/shard_map/ppermute | solution.py:400
  159.6 4.4 %collective-permute-done.12.refs_5_ = bf16[64,1024]{1,0:T(8,128)(2,1)S(1)} collective-permute-done((bf16[64,1024]{1,0:T(8,128)(2,1)S(1)}, bf16[64,1024]{1,0:T(8,128)(2,1)S(1)}, u32[]{:S(2)}, u32[]{:S(2)}) %collective-permute-start.12) | collective-permute-done | bytes 131104 | tf_op jit(solution)/shard_map/ppermute | solution.py:400
  164.8 2.3 %join.1 = bf16[8,64,1024]{2,1,0:T(8,128)(2,1)} custom-call(s32[2]{0:T(128)} %pad_add_fusion.place_ref, bf16[64,1024]{1,0:T(8,128)(2,1)} %get-tuple-element.78.refs_0_, bf16[64,1024]{1,0:T(8,128)(2,1)} %copy-done.1, bf16[64,1024]{1,0:T(8,128)(2,1)} %copy-done.2, bf16[64,1024]{1,0:T(8,128)(2,1)} %copy-done.3, bf16[64,1024]{1,0:T(8,128)(2,1)} %copy-done.4, ...), custom_call_target="tpu_custom_call" | custom-call | tf_op jit(solution)/shard_map/join/pallas_call | solution.py:141
  (155 shorter events, 54.1 us)
Async XLA Ops:
  1.5 9.8 %collective-permute-start = (bf16[8,64,128]{2,1,0:T(8,128)(2,1)S(1)}, bf16[8,64,128]{2,1,0:T(8,128)(2,1)S(1)}, u32[]{:S(2)}, u32[]{:S(2)}) collective-permute-start(bf16[8,64,128]{2,1,0:T(8,128)(2,1)S(1)} %slice.3), channel_id=1, source_target_pairs={{0,8},{8,16},{16,24},{1,9},{9,17},{17,25},{2,10},{10,18},{18,26},{... | collective-permute-start | bytes 393224 | tf_op jit(solution)/shard_map/ppermute | solution.py:417
  6.8 43.9 %collective-permute-start.15 = (bf16[64,1024]{1,0:T(8,128)(2,1)}, bf16[64,1024]{1,0:T(8,128)(2,1)S(1)}, u32[]{:S(2)}, u32[]{:S(2)}) collective-permute-start(bf16[64,1024]{1,0:T(8,128)(2,1)} %get-tuple-element.87), channel_id=1, source_target_pairs={{0,1},{1,0},{2,3},{3,2},{4,5},{5,4},{6,7},{7,6},{8,9},{9,8},{10,11... | collective-permute-start | bytes 393224 | tf_op jit(solution)/shard_map/ppermute | solution.py:400
  18.8 11.3 %collective-permute-start.3 = (bf16[64,1024]{1,0:T(8,128)(2,1)}, bf16[64,1024]{1,0:T(8,128)(2,1)S(1)}, u32[]{:S(2)}, u32[]{:S(2)}) collective-permute-start(bf16[64,1024]{1,0:T(8,128)(2,1)} %get-tuple-element.61), channel_id=1, source_target_pairs={{0,3},{1,2},{2,1},{3,0},{4,7},{5,6},{6,5},{7,4},{8,11},{9,10},{10,... | collective-permute-start | bytes 393224 | tf_op jit(solution)/shard_map/ppermute | solution.py:400
  20.2 13.8 %collective-permute-start.4 = (bf16[64,1024]{1,0:T(8,128)(2,1)}, bf16[64,1024]{1,0:T(8,128)(2,1)S(1)}, u32[]{:S(2)}, u32[]{:S(2)}) collective-permute-start(bf16[64,1024]{1,0:T(8,128)(2,1)} %get-tuple-element.62), channel_id=1, source_target_pairs={{0,4},{1,5},{2,6},{3,7},{4,0},{5,1},{6,2},{7,3},{8,12},{9,13},{10,... | collective-permute-start | bytes 393224 | tf_op jit(solution)/shard_map/ppermute | solution.py:400
  23.5 30.2 %collective-permute-start.16 = (bf16[64,1024]{1,0:T(8,128)(2,1)}, bf16[64,1024]{1,0:T(8,128)(2,1)S(1)}, u32[]{:S(2)}, u32[]{:S(2)}) collective-permute-start(bf16[64,1024]{1,0:T(8,128)(2,1)} %get-tuple-element.88), channel_id=1, source_target_pairs={{0,2},{1,3},{2,0},{3,1},{4,6},{5,7},{6,4},{7,5},{8,10},{9,11},{10,... | collective-permute-start | bytes 393224 | tf_op jit(solution)/shard_map/ppermute | solution.py:400
  25.1 12.1 %collective-permute-start.5 = (bf16[64,1024]{1,0:T(8,128)(2,1)}, bf16[64,1024]{1,0:T(8,128)(2,1)S(1)}, u32[]{:S(2)}, u32[]{:S(2)}) collective-permute-start(bf16[64,1024]{1,0:T(8,128)(2,1)} %get-tuple-element.63), channel_id=1, source_target_pairs={{0,5},{1,4},{2,7},{3,6},{4,1},{5,0},{6,3},{7,2},{8,13},{9,12},{10,... | collective-permute-start | bytes 393224 | tf_op jit(solution)/shard_map/ppermute | solution.py:400
  30.1 8.7 %collective-permute-start.6 = (bf16[64,1024]{1,0:T(8,128)(2,1)}, bf16[64,1024]{1,0:T(8,128)(2,1)S(1)}, u32[]{:S(2)}, u32[]{:S(2)}) collective-permute-start(bf16[64,1024]{1,0:T(8,128)(2,1)} %get-tuple-element.64), channel_id=1, source_target_pairs={{0,6},{1,7},{2,4},{3,5},{4,2},{5,3},{6,0},{7,1},{8,14},{9,15},{10,... | collective-permute-start | bytes 393224 | tf_op jit(solution)/shard_map/ppermute | solution.py:400
  34.0 8.5 %collective-permute-start.7 = (bf16[64,1024]{1,0:T(8,128)(2,1)}, bf16[64,1024]{1,0:T(8,128)(2,1)S(1)}, u32[]{:S(2)}, u32[]{:S(2)}) collective-permute-start(bf16[64,1024]{1,0:T(8,128)(2,1)} %get-tuple-element.65), channel_id=1, source_target_pairs={{0,7},{1,6},{2,5},{3,4},{4,3},{5,2},{6,1},{7,0},{8,15},{9,14},{10,... | collective-permute-start | bytes 393224 | tf_op jit(solution)/shard_map/ppermute | solution.py:400
  37.2 37.5 %collective-permute-start.17 = (bf16[64,1024]{1,0:T(8,128)(2,1)}, bf16[64,1024]{1,0:T(8,128)(2,1)S(1)}, u32[]{:S(2)}, u32[]{:S(2)}) collective-permute-start(bf16[64,1024]{1,0:T(8,128)(2,1)} %get-tuple-element.89), channel_id=1, source_target_pairs={{0,3},{1,2},{2,1},{3,0},{4,7},{5,6},{6,5},{7,4},{8,11},{9,10},{10,... | collective-permute-start | bytes 393224 | tf_op jit(solution)/shard_map/ppermute | solution.py:400
  42.4 32.2 %collective-permute-start.18 = (bf16[64,1024]{1,0:T(8,128)(2,1)}, bf16[64,1024]{1,0:T(8,128)(2,1)S(1)}, u32[]{:S(2)}, u32[]{:S(2)}) collective-permute-start(bf16[64,1024]{1,0:T(8,128)(2,1)} %get-tuple-element.90), channel_id=1, source_target_pairs={{0,4},{1,5},{2,6},{3,7},{4,0},{5,1},{6,2},{7,3},{8,12},{9,13},{10,... | collective-permute-start | bytes 393224 | tf_op jit(solution)/shard_map/ppermute | solution.py:400
  50.7 23.9 %collective-permute-start.19 = (bf16[64,1024]{1,0:T(8,128)(2,1)}, bf16[64,1024]{1,0:T(8,128)(2,1)S(1)}, u32[]{:S(2)}, u32[]{:S(2)}) collective-permute-start(bf16[64,1024]{1,0:T(8,128)(2,1)} %get-tuple-element.91), channel_id=1, source_target_pairs={{0,5},{1,4},{2,7},{3,6},{4,1},{5,0},{6,3},{7,2},{8,13},{9,12},{10,... | collective-permute-start | bytes 393224 | tf_op jit(solution)/shard_map/ppermute | solution.py:400
  50.8 23.9 %collective-permute-start.20 = (bf16[64,1024]{1,0:T(8,128)(2,1)}, bf16[64,1024]{1,0:T(8,128)(2,1)S(1)}, u32[]{:S(2)}, u32[]{:S(2)}) collective-permute-start(bf16[64,1024]{1,0:T(8,128)(2,1)} %get-tuple-element.92), channel_id=1, source_target_pairs={{0,6},{1,7},{2,4},{3,5},{4,2},{5,3},{6,0},{7,1},{8,14},{9,15},{10,... | collective-permute-start | bytes 393224 | tf_op jit(solution)/shard_map/ppermute | solution.py:400
  53.7 21.0 %collective-permute-start.21 = (bf16[64,1024]{1,0:T(8,128)(2,1)}, bf16[64,1024]{1,0:T(8,128)(2,1)S(1)}, u32[]{:S(2)}, u32[]{:S(2)}) collective-permute-start(bf16[64,1024]{1,0:T(8,128)(2,1)} %get-tuple-element.93), channel_id=1, source_target_pairs={{0,7},{1,6},{2,5},{3,4},{4,3},{5,2},{6,1},{7,0},{8,15},{9,14},{10,... | collective-permute-start | bytes 393224 | tf_op jit(solution)/shard_map/ppermute | solution.py:400
  93.5 8.4 %collective-permute-start.24 = (bf16[256,256]{1,0:T(8,128)(2,1)}, bf16[256,256]{1,0:T(8,128)(2,1)S(1)}, u32[]{:S(2)}, u32[]{:S(2)}) collective-permute-start(bf16[256,256]{1,0:T(8,128)(2,1)} %get-tuple-element.105), channel_id=1, source_target_pairs={{0,24},{8,16},{16,8},{24,0},{1,25},{9,17},{17,9},{25,1},{2,26},{10... | collective-permute-start | bytes 393224 | tf_op jit(solution)/shard_map/ppermute | solution.py:400
  105.1 8.7 %collective-permute-start.26 = (bf16[32,256]{1,0:T(8,128)(2,1)}, bf16[32,256]{1,0:T(8,128)(2,1)S(1)}, u32[]{:S(2)}, u32[]{:S(2)}) collective-permute-start(bf16[32,256]{1,0:T(8,128)(2,1)} %get-tuple-element.108), channel_id=1, source_target_pairs={{0,2},{1,3},{2,0},{3,1},{4,6},{5,7},{6,4},{7,5},{8,10},{9,11},{10,... | collective-permute-start | bytes 49160 | tf_op jit(solution)/shard_map/ppermute | solution.py:400
  106.2 9.4 %collective-permute-start.27 = (bf16[32,256]{1,0:T(8,128)(2,1)}, bf16[32,256]{1,0:T(8,128)(2,1)S(1)}, u32[]{:S(2)}, u32[]{:S(2)}) collective-permute-start(bf16[32,256]{1,0:T(8,128)(2,1)} %get-tuple-element.109), channel_id=1, source_target_pairs={{0,3},{1,2},{2,1},{3,0},{4,7},{5,6},{6,5},{7,4},{8,11},{9,10},{10,... | collective-permute-start | bytes 49160 | tf_op jit(solution)/shard_map/ppermute | solution.py:400
  122.7 32.8 %collective-permute-start.8 = (bf16[64,1024]{1,0:T(8,128)(2,1)S(1)}, bf16[64,1024]{1,0:T(8,128)(2,1)S(1)}, u32[]{:S(2)}, u32[]{:S(2)}) collective-permute-start(bf16[64,1024]{1,0:T(8,128)(2,1)S(1)} %copy-done.21), channel_id=1, source_target_pairs={{0,1},{1,0},{2,3},{3,2},{4,5},{5,4},{6,7},{7,6},{8,9},{9,8},{10,11... | collective-permute-start | bytes 393224 | tf_op jit(solution)/shard_map/ppermute | solution.py:400
  123.3 32.8 %collective-permute-start.9 = (bf16[64,1024]{1,0:T(8,128)(2,1)S(1)}, bf16[64,1024]{1,0:T(8,128)(2,1)S(1)}, u32[]{:S(2)}, u32[]{:S(2)}) collective-permute-start(bf16[64,1024]{1,0:T(8,128)(2,1)S(1)} %copy-done.20), channel_id=1, source_target_pairs={{0,2},{1,3},{2,0},{3,1},{4,6},{5,7},{6,4},{7,5},{8,10},{9,11},{10,... | collective-permute-start | bytes 393224 | tf_op jit(solution)/shard_map/ppermute | solution.py:400
  123.3 35.0 %collective-permute-start.10 = (bf16[64,1024]{1,0:T(8,128)(2,1)S(1)}, bf16[64,1024]{1,0:T(8,128)(2,1)S(1)}, u32[]{:S(2)}, u32[]{:S(2)}) collective-permute-start(bf16[64,1024]{1,0:T(8,128)(2,1)S(1)} %copy-done.19), channel_id=1, source_target_pairs={{0,3},{1,2},{2,1},{3,0},{4,7},{5,6},{6,5},{7,4},{8,11},{9,10},{10,... | collective-permute-start | bytes 393224 | tf_op jit(solution)/shard_map/ppermute | solution.py:400
  126.2 24.2 %collective-permute-start.38 = (bf16[32,256]{1,0:T(8,128)(2,1)S(1)}, bf16[32,256]{1,0:T(8,128)(2,1)S(1)}, u32[]{:S(2)}, u32[]{:S(2)}) collective-permute-start(bf16[32,256]{1,0:T(8,128)(2,1)S(1)} %get-tuple-element.115), channel_id=1, source_target_pairs={{0,7},{1,6},{2,5},{3,4},{4,3},{5,2},{6,1},{7,0},{8,15},{9,14},{10,... | collective-permute-start | bytes 49160 | tf_op jit(solution)/shard_map/ppermute | solution.py:400
  150.4 8.8 %collective-permute-start.11 = (bf16[64,1024]{1,0:T(8,128)(2,1)S(1)}, bf16[64,1024]{1,0:T(8,128)(2,1)S(1)}, u32[]{:S(2)}, u32[]{:S(2)}) collective-permute-start(bf16[64,1024]{1,0:T(8,128)(2,1)S(1)} %copy-done.18), channel_id=1, source_target_pairs={{0,4},{1,5},{2,6},{3,7},{4,0},{5,1},{6,2},{7,3},{8,12},{9,13},{10,... | collective-permute-start | bytes 393224 | tf_op jit(solution)/shard_map/ppermute | solution.py:400
  152.2 11.9 %collective-permute-start.12 = (bf16[64,1024]{1,0:T(8,128)(2,1)S(1)}, bf16[64,1024]{1,0:T(8,128)(2,1)S(1)}, u32[]{:S(2)}, u32[]{:S(2)}) collective-permute-start(bf16[64,1024]{1,0:T(8,128)(2,1)S(1)} %copy-done.17), channel_id=1, source_target_pairs={{0,5},{1,4},{2,7},{3,6},{4,1},{5,0},{6,3},{7,2},{8,13},{9,12},{10,... | collective-permute-start | bytes 393224 | tf_op jit(solution)/shard_map/ppermute | solution.py:400
  155.5 8.5 %collective-permute-start.13 = (bf16[64,1024]{1,0:T(8,128)(2,1)S(1)}, bf16[64,1024]{1,0:T(8,128)(2,1)S(1)}, u32[]{:S(2)}, u32[]{:S(2)}) collective-permute-start(bf16[64,1024]{1,0:T(8,128)(2,1)S(1)} %copy-done.16), channel_id=1, source_target_pairs={{0,6},{1,7},{2,4},{3,5},{4,2},{5,3},{6,0},{7,1},{8,14},{9,15},{10,... | collective-permute-start | bytes 393224 | tf_op jit(solution)/shard_map/ppermute | solution.py:400
  158.4 8.8 %collective-permute-start.41 = (bf16[256,256]{1,0:T(8,128)(2,1)S(1)}, bf16[256,256]{1,0:T(8,128)(2,1)S(1)}, u32[]{:S(2)}, u32[]{:S(2)}) collective-permute-start(bf16[256,256]{1,0:T(8,128)(2,1)S(1)} %constant_dynamic-update-slice_fusion.refs_0_), channel_id=1, source_target_pairs={{0,24},{8,16},{16,8},{24,0},{1,25},{9,17},{17,9},{25,1},{2,26},{10... | collective-permute-start | bytes 393224 | tf_op jit(solution)/shard_map/ppermute | solution.py:400
  (54 other events, 820.1 us)

commit v4 on v3

v4 whole, which is shorter than its diff:
```python
import functools

import jax
import jax.numpy as jnp
from jax import lax
from jax.experimental import pallas as pl
from jax.experimental.pallas import tpu as pltpu
from jax.sharding import PartitionSpec as P

HEADS = 4
F32 = jnp.float32
BF16 = jnp.bfloat16


def mm(left, right, left_dim=1, right_dim=0):
    return lax.dot_general(
        left, right, (((left_dim,), (right_dim,)), ((), ())), preferred_element_type=F32
    )


def index_spec():
    return pl.BlockSpec(memory_space=pltpu.SMEM)


def params():
    return pltpu.CompilerParams(vmem_limit_bytes=56 * 2**20)


def filter_kernel(place_ref, sig_ref, rim_ref, taps_ref, *refs):
    out_refs, kept = refs[:-1], refs[-1]
    batch, rows, slab = sig_ref.shape
    width = rim_ref.shape[2]
    blocks = slab // width
    pieces = len(out_refs) // batch
    span = slab // pieces
    signal = jnp.swapaxes(sig_ref[...].astype(F32), 0, 1)
    rim = jnp.swapaxes(rim_ref[...].astype(F32), 0, 1)
    taps = taps_ref[...].astype(F32)
    first = lax.broadcasted_iota(jnp.int32, (rows, width), 1) == 0
    taps = jnp.concatenate(
        [taps[:, :width], jnp.where(first, taps[:, width : width + 1], 0.0)], axis=1
    )
    results = []
    for row in range(rows):
        own = [signal[row, :, j * width : (j + 1) * width] for j in range(blocks)]
        current = jnp.concatenate(own, axis=0)
        before = jnp.concatenate([rim[row]] + own[:-1], axis=0)
        window = jnp.concatenate([before, current], axis=1).astype(BF16)
        spread = jnp.broadcast_to(taps[row : row + 1, :], (width, 2 * width))
        rolled = pltpu.roll(spread, 0, 1, stride=1, stride_axis=0)
        table = jnp.concatenate([rolled[:, width:], rolled[:, :width]], axis=0).astype(BF16)
        product = mm(window, table)
        results.append(
            jnp.concatenate(
                [product[j * batch : (j + 1) * batch] for j in range(blocks)], axis=1
            )
        )
    filtered = jnp.swapaxes(jnp.stack(results, axis=0), 0, 1).astype(BF16)
    for index in range(batch):
        for piece in range(pieces):
            kept[index * pieces + piece] = filtered[index, :, piece * span : (piece + 1) * span]
    me = place_ref[1]
    for k, out_ref in enumerate(out_refs):
        out_ref[...] = kept[me ^ k]


def filter_all(place, signal, rim, taps, count):
    batch, contacts, slab = signal.shape
    width = rim.shape[2]
    rows = 16
    span = slab * batch // count
    return pl.pallas_call(
        filter_kernel,
        grid=(contacts // rows,),
        in_specs=[
            index_spec(),
            pl.BlockSpec((batch, rows, slab), lambda i: (0, i, 0)),
            pl.BlockSpec((batch, rows, width), lambda i: (0, i, 0)),
            pl.BlockSpec((rows, taps.shape[1]), lambda i: (i, 0)),
        ],
        out_specs=[pl.BlockSpec((rows, span), lambda i: (i, 0))] * count,
        out_shape=[jax.ShapeDtypeStruct((contacts, span), BF16)] * count,
        scratch_shapes=[pltpu.VMEM((count, rows, span), BF16)],
        compiler_params=params(),
        cost_estimate=pl.CostEstimate(
            flops=4 * batch * contacts * slab * width,
            bytes_accessed=4 * batch * contacts * slab,
            transcendentals=0,
        ),
        name="filter",
    )(place, signal, rim, taps)


def head_masks(width):
    lane_head = lax.broadcasted_iota(jnp.int32, (1, width), 1) // (width // HEADS)
    return [(lane_head == h).astype(F32) for h in range(HEADS)]


def forward_kernel(
    blocks, place_ref, nbr_ref, live_ref, coef_ref, wq_ref, wk_ref, wv_ref, wo_ref, *refs
):
    feat_refs = refs[:blocks]
    (
        out_ref, prob_ref, value_ref, keys_ref, query_t_ref, normed_ref, normed_t_ref, mixed_ref,
        mixed_t_ref, counts, columns, packed, live_row,
    ) = refs[blocks:]
    rows, width = feat_refs[0].shape
    contacts = rows * blocks
    scale = (width // HEADS) ** (-0.5)
    slots = nbr_ref.shape[0]
    me = place_ref[1]

    @pl.when(pl.program_id(0) == 0)
    def _():
        packed[...] = jnp.zeros_like(packed)
        packed[0:1, :] = live_ref[...].astype(F32)
        packed[1:2, :] = coef_ref[...]
        for slot in range(slots):
            packed[2 + slot : 3 + slot, :] = nbr_ref[slot : slot + 1, :].astype(F32)
        columns[...] = packed[...].T
        turned = jnp.concatenate(
            [columns[pl.ds(pl.multiple_of((me ^ k) * rows, rows), rows), :] for k in range(blocks)],
            axis=0,
        )
        alive = turned.T[0:1]
        live_row[...] = alive
        ids = lax.broadcasted_iota(jnp.int32, (contacts, contacts), 1)
        total = jnp.zeros((contacts, contacts), F32)
        for slot in range(slots):
            here = turned[:, slot + 2 : slot + 3].astype(jnp.int32) ^ (me * rows)
            total = total + jnp.where(here == ids, alive, 0.0)
        counts[...] = total.astype(BF16)
        columns[:, 0:1] = turned[:, 0:1]
        columns[:, 1:2] = turned[:, 1:2]
        columns[:, 2:3] = jnp.sum(total, axis=1, keepdims=True)

    live = columns[:, 0:1]
    coef = columns[:, 1:2]
    field = jnp.concatenate([ref[...] for ref in feat_refs], axis=0)
    middle = field.astype(F32)
    beside = mm(counts[...], field)
    ready = live * (middle + coef * (beside - columns[:, 2:3] * middle))
    ready = ready.astype(BF16).astype(F32)
    mean_square = jnp.mean(ready * ready, axis=1, keepdims=True)
    normed = (ready * lax.rsqrt(mean_square + 1e-05)).astype(BF16)
    query = (mm(normed, wq_ref[...]) * scale).astype(BF16)
    keys = mm(normed, wk_ref[...]).astype(BF16)
    value = mm(normed, wv_ref[...]).astype(BF16)
    value_ref[...] = value
    keys_ref[...] = keys
    query_t_ref[...] = query.T
    normed_ref[...] = normed
    normed_t_ref[...] = normed.T
    masks = [m.astype(BF16) for m in head_masks(width)]
    bias = jnp.where(live_row[...] > 0, 0.0, -1e30)
    scores = mm(query * masks[0], keys, 1, 1)
    mixed = None
    for h in range(HEADS):
        following = mm(query * masks[h + 1], keys, 1, 1) if h + 1 < HEADS else None
        scores = scores + bias
        top = jnp.max(scores, axis=1, keepdims=True)
        raised = jnp.exp(scores - top)
        share = 1.0 / jnp.sum(raised, axis=1, keepdims=True)
        prob = (raised * share).astype(BF16)
        prob_ref[:, h * contacts : (h + 1) * contacts] = prob
        part = mm(prob, value * masks[h])
        mixed = part if mixed is None else mixed + part
        scores = following
    mixed = mixed.astype(BF16)
    attended = mm(mixed, wo_ref[...]).astype(BF16)
    for k in range(blocks):
        out_ref[me ^ k] = attended[k * rows : (k + 1) * rows]
    mixed_ref[...] = mixed
    mixed_t_ref[...] = mixed.T


def backward_kernel(
    blocks, place_ref, wo_ref, up_ref, prob_ref, value_ref, keys_ref, query_t_ref, normed_ref,
    normed_t_ref, mixed_ref, mixed_t_ref, *refs,
):
    out_refs, total, chunks = refs[:-2], refs[-2], refs[-1]
    contacts, width = normed_ref.shape
    head = width // HEADS
    scale = head ** (-0.5)
    step = pl.program_id(0)

    @pl.when(step == 0)
    def _():
        total[...] = jnp.zeros_like(total)

    me = place_ref[1]
    upstream = jnp.concatenate([up_ref[me ^ k] for k in range(blocks)], axis=0)
    normed = normed_ref[...]
    value = value_ref[...]
    keys = keys_ref[...]
    back = mm(upstream, wo_ref[...], 1, 1).astype(BF16)
    back_t = back.T
    inner = back.astype(F32) * mixed_ref[...].astype(F32)
    masks = head_masks(width)
    grad_value_t = []
    grad_key_t = []
    grad_query = None
    low = [m.astype(BF16) for m in masks]
    grad_prob = mm(back * low[0], value, 1, 1)
    for h in range(HEADS):
        following = mm(back * low[h + 1], value, 1, 1) if h + 1 < HEADS else None
        row_inner = jnp.sum(inner * masks[h], axis=1, keepdims=True)
        prob = prob_ref[:, h * contacts : (h + 1) * contacts]
        grad_value_t.append(mm(back_t[h * head : (h + 1) * head], prob))
        grad_score = (prob.astype(F32) * (grad_prob - row_inner)).astype(BF16)
        grad_key_t.append(mm(query_t_ref[h * head : (h + 1) * head, :], grad_score))
        part = mm(grad_score, keys * low[h])
        grad_query = part if grad_query is None else grad_query + part
        grad_prob = following
    grad_query = (grad_query * scale).astype(BF16)
    total[0] += mm(normed_t_ref[...], grad_query)
    total[1] += mm(jnp.concatenate(grad_key_t, axis=0).astype(BF16), normed)
    total[2] += mm(jnp.concatenate(grad_value_t, axis=0).astype(BF16), normed)
    total[3] += mm(mixed_t_ref[...], upstream)

    @pl.when(step == pl.num_programs(0) - 1)
    def _():
        count, rows = chunks.shape[:2]
        parts = [total[0], total[1].T, total[2].T, total[3]]
        for c in range(count):
            first = (c * rows) % width
            chunks[c] = parts[c * rows // width][first : first + rows].astype(BF16)
        for k, out_ref in enumerate(out_refs):
            out_ref[...] = chunks[place_ref[0] ^ k]


def whole(shape):
    return pl.BlockSpec(shape, lambda i: (0,) * len(shape))


def forward(place, features, neighbours, live, coef, weights):
    blocks = len(features)
    rows, span = features[0].shape
    contacts = rows * blocks
    width = weights[0].shape[0]
    groups = span // width
    shapes = [
        (contacts, HEADS * contacts), (contacts, width),
        (contacts, width), (width, contacts), (contacts, width), (width, contacts),
        (contacts, width), (width, contacts),
    ]
    small = [neighbours, live, coef] + list(weights)
    return pl.pallas_call(
        functools.partial(forward_kernel, blocks),
        grid=(groups,),
        in_specs=[index_spec()]
        + [whole(item.shape) for item in small]
        + [pl.BlockSpec((rows, width), lambda i: (0, i))] * blocks,
        out_specs=[pl.BlockSpec((blocks, rows, width), lambda i: (0, 0, i))]
        + [pl.BlockSpec(shape, lambda i: (0, i)) for shape in shapes],
        out_shape=[jax.ShapeDtypeStruct((blocks, rows, span), BF16)]
        + [jax.ShapeDtypeStruct((shape[0], groups * shape[1]), BF16) for shape in shapes],
        scratch_shapes=[
            pltpu.VMEM((contacts, contacts), BF16),
            pltpu.VMEM((contacts, 128), F32),
            pltpu.VMEM((128, contacts), F32),
            pltpu.VMEM((1, contacts), F32),
        ],
        compiler_params=params(),
        cost_estimate=pl.CostEstimate(
            flops=groups * 5 * 10**9,
            bytes_accessed=20 * contacts * span,
            transcendentals=groups * HEADS * contacts * contacts,
        ),
        name="forward",
    )(place, *small, *features)


def backward(place, upstream, kept, w_out, tm_count):
    blocks, rows, span = upstream.shape
    contacts = rows * blocks
    width = w_out.shape[0]
    groups = span // width
    chunk = (4 * width // tm_count, width)
    return pl.pallas_call(
        functools.partial(backward_kernel, blocks),
        grid=(groups,),
        in_specs=[
            index_spec(), whole(w_out.shape),
            pl.BlockSpec((blocks, rows, width), lambda i: (0, 0, i)),
        ]
        + [
            pl.BlockSpec((item.shape[0], item.shape[1] // groups), lambda i: (0, i))
            for item in kept
        ],
        out_specs=[whole(chunk)] * tm_count,
        out_shape=[jax.ShapeDtypeStruct(chunk, BF16)] * tm_count,
        scratch_shapes=[
            pltpu.VMEM((4, width, width), F32),
            pltpu.VMEM((tm_count,) + chunk, BF16),
        ],
        compiler_params=params(),
        cost_estimate=pl.CostEstimate(
            flops=groups * 5 * 10**9, bytes_accessed=20 * contacts * span, transcendentals=0
        ),
        name="backward",
    )(place, w_out, upstream, *kept)


def place_all(place, parts):
    rows, width = parts[0].shape
    ways = len(parts)

    def body(place_ref, *refs):
        for k in range(ways):
            refs[-1][place_ref[0] ^ k] = refs[k][...].astype(F32)

    shape = (ways, rows, width)
    return pl.pallas_call(
        body,
        in_specs=[index_spec()] + [pl.BlockSpec((rows, width), lambda: (0, 0))] * ways,
        out_specs=pl.BlockSpec(shape, lambda: (0, 0, 0)),
        out_shape=jax.ShapeDtypeStruct(shape, F32),
        compiler_params=params(),
        name="place_all",
    )(place, *parts)


def swap(value, axis, k):
    return lax.ppermute(value, axis, [(i, i ^ k) for i in range(lax.axis_size(axis))])


def swap_all(parts, axis):
    return [parts[0]] + [swap(parts[k], axis, k) for k in range(1, len(parts))]


def exchange(value, axis):
    return lax.all_to_all(value, axis, split_axis=0, concat_axis=0, tiled=True)


def local(
    signal, fir_taps, neighbours, live_mask, lap_coef, w_query, w_key, w_value, w_out, cotangent
):
    batch, contacts_here, slab = signal.shape
    rim_width = fir_taps.shape[1] - 1
    width = w_query.shape[0]
    tm_count = lax.axis_size("tm")
    count = lax.axis_size("contact")
    pieces = count // batch
    span = slab // pieces
    place = jnp.stack([lax.axis_index("tm"), lax.axis_index("contact")]).astype(jnp.int32)

    if pieces > 1:
        cotangent = cotangent.reshape(batch, contacts_here, pieces, span)
        cotangent = cotangent.transpose(0, 2, 1, 3).reshape(count, contacts_here, span)
    upstream = exchange(cotangent, "contact")
    rim = lax.ppermute(
        signal[:, :, slab - rim_width :], "tm", [(i, i + 1) for i in range(tm_count - 1)]
    )
    filtered = filter_all(place, signal, rim, fir_taps, count)
    features = swap_all(filtered, "contact")
    attended, *kept = forward(
        place, features, neighbours.T, live_mask[None], lap_coef[None],
        [w_query, w_key, w_value, w_out],
    )
    returned = exchange(attended, "contact")
    grads = backward(place, upstream, kept, w_out, tm_count)
    grads = swap_all(grads, "tm")
    part = sum(piece.astype(F32) for piece in grads).astype(BF16)
    part, returned = lax.optimization_barrier((part, returned))
    part = exchange(part, "contact").reshape(count, -1, width)
    grad_scale = (batch * (slab // width) * tm_count * neighbours.shape[0]) ** (-0.5)
    mine = (jnp.sum(part.astype(F32), axis=0) * grad_scale).astype(BF16)
    chunk = exchange(jnp.concatenate([mine] * count, axis=0), "contact")
    summed = place_all(place, swap_all([chunk] * tm_count, "tm"))
    if pieces > 1:
        returned = returned.reshape(batch, pieces, contacts_here, span)
        returned = returned.transpose(0, 2, 1, 3).reshape(batch, contacts_here, slab)
    return (returned, summed.reshape(4, width, width))


def solution(mesh):
    in_specs = (
        P(None, "contact", "tm"),
        P("contact", None),
        P(),
        P(),
        P(),
        P(),
        P(),
        P(),
        P(),
        P(None, "contact", "tm"),
    )
    out_specs = (P(None, "contact", "tm"), P())
    return jax.shard_map(local, mesh=mesh, in_specs=in_specs, out_specs=out_specs, check_vma=False)
```

time: 171 us -> 138 us (0.81)
  starting transfers between devices: 67.7 us -> 37.4 us
  blocking collectives: 0 us -> 20.5 us
  Pallas kernels: 50.2 us -> 40.9 us
  waiting for transfers between devices: 39.3 us -> 31.9 us
  other arithmetic: 7.29 us -> 1.67 us
    ppermute x41 -> x13, starting transfers between devices: 65.3 us -> 16.8 us  [swap(): lax.ppermute(value, axis, [(i, i ^ k) for i in range(lax.axis_size(axis))])]
    all_to_all x0 -> x2, blocking collectives: none -> 20.5 us  [exchange(): return lax.all_to_all(value, axis, split_axis=0, concat_axis=0, tiled=True)]
    all_to_all x0 -> x2, starting transfers between devices: none -> 18.2 us  [exchange(): return lax.all_to_all(value, axis, split_axis=0, concat_axis=0, tiled=True)]
    ppermute x41 -> x13, waiting for transfers between devices: 39.3 us -> 23.9 us  [swap(): lax.ppermute(value, axis, [(i, i ^ k) for i in range(lax.axis_size(axis))])]
    all_to_all x0 -> x2, waiting for transfers between devices: none -> 7.71 us  [exchange(): return lax.all_to_all(value, axis, split_axis=0, concat_axis=0, tiled=True)]
    pallas_call x3 -> x0, Pallas kernels: 6.49 us -> none  [the longest x1 2.33 us: join(): pl.pallas_call(join_kernel, in_specs=[index_spec()] + [pl.BlockSpec((cont...]
    concatenate x2 -> x0, other arithmetic: 3.19 us -> none  [the longest x1 1.82 us: local(): jnp.concatenate([w_query, w_key, w_value], axis=1)]
    pallas_call x1, Pallas kernels: 17.8 us -> 15.1 us  [backward(): pl.pallas_call(functools.partial(backward_kernel, blocks), grid=(groups,)...]
  transfers between devices with their start and end apart: 42 -> 16, of which waited for: 14 -> 8; matrix products, arithmetic and copies ran while one was open for 4% -> 1% of each run, Pallas kernels for 17% -> 25%
where the time goes in v4:
time: 138 us; the launch traced here: 137 us
  Pallas kernels  40.9 us (30%)
  starting transfers between devices  37.4 us (27%)
  waiting for transfers between devices  31.9 us (23%)
  blocking collectives  20.5 us (15%)
  local copies, waits for them, and re-layouts  3.94 us (3%)
  other arithmetic  1.67 us (1%)
    ppermute x13, waiting for transfers between devices, swap(): lax.ppermute(value, axis, [(i, i ^ k) for i in range(lax.axis_size(axis))])  23.9 us
    all_to_all x2, blocking collectives, exchange(): return lax.all_to_all(value, axis, split_axis=0, concat_axis=0, tiled=True)  20.5 us
    pallas_call x1, Pallas kernels, forward(): pl.pallas_call(functools.partial(forward_kernel, blocks), grid=(groups,),...  18.8 us
    all_to_all x2, starting transfers between devices, exchange(): return lax.all_to_all(value, axis, split_axis=0, concat_axis=0, tiled=True)  18.2 us
    ppermute x13, starting transfers between devices, swap(): lax.ppermute(value, axis, [(i, i ^ k) for i in range(lax.axis_size(axis))])  16.8 us
    pallas_call x1, Pallas kernels, backward(): pl.pallas_call(functools.partial(backward_kernel, blocks), grid=(groups,)...  15.1 us
    all_to_all x2, waiting for transfers between devices, exchange(): return lax.all_to_all(value, axis, split_axis=0, concat_axis=0, tiled=True)  7.71 us
    pallas_call x1, Pallas kernels, filter_all(): pl.pallas_call(filter_kernel, grid=(contacts // rows,), in_specs=[index_s...  4.86 us
  transfers between devices with their start and end apart: 16, of which 8 were waited for; matrix products, arithmetic and copies ran while one was open for 1% of the time, Pallas kernels for 25%

profile of v4, /device:TPU:0, one launch (start us, length us, event | category | flops | bytes accessed | tf_op | source)
XLA Modules:
  0.0 137.1 jit_solution(8768060132249266669)
XLA Ops:
  1.5 2.4 %collective-permute-start = (bf16[8,64,128]{2,1,0:T(8,128)(2,1)S(1)}, bf16[8,64,128]{2,1,0:T(8,128)(2,1)S(1)}, u32[]{:S(2)}, u32[]{:S(2)}) collective-permute-start(bf16[8,64,128]{2,1,0:T(8,128)(2,1)S(1)} %slice.3), channel_id=1, source_target_pairs={{0,8},{8,16},{16,24},{1,9},{9,17},{17,25},{2,10},{10,18},{18,26},{... | collective-permute-start | bytes 393224 | tf_op jit(solution)/shard_map/ppermute | solution.py:352
  5.5 4.9 %filter.1 = (bf16[64,1024]{1,0:T(8,128)(2,1)}, bf16[64,1024]{1,0:T(8,128)(2,1)}, bf16[64,1024]{1,0:T(8,128)(2,1)}, bf16[64,1024]{1,0:T(8,128)(2,1)}, bf16[64,102...) custom-call(s32[2]{0:T(128)} %pad_add_fusion.place_ref, ...), custom_call_target="tpu_custom_call" | custom-call | flops 268435456 | bytes 2097152 | tf_op jit(solution)/shard_map/filter/pallas_call | solution.py:72
  10.4 2.4 %collective-permute-start.1 = (bf16[64,1024]{1,0:T(8,128)(2,1)}, bf16[64,1024]{1,0:T(8,128)(2,1)S(1)}, u32[]{:S(2)}, u32[]{:S(2)}) collective-permute-start(bf16[64,1024]{1,0:T(8,128)(2,1)} %get-tuple-element.26), channel_id=1, source_target_pairs={{0,1},{1,0},{2,3},{3,2},{4,5},{5,4},{6,7},{7,6},{8,9},{9,8},{10,11... | collective-permute-start | bytes 393224 | tf_op jit(solution)/shard_map/ppermute | solution.py:325
  12.8 1.6 %collective-permute-start.2 = (bf16[64,1024]{1,0:T(8,128)(2,1)}, bf16[64,1024]{1,0:T(8,128)(2,1)S(1)}, u32[]{:S(2)}, u32[]{:S(2)}) collective-permute-start(bf16[64,1024]{1,0:T(8,128)(2,1)} %get-tuple-element.27), channel_id=1, source_target_pairs={{0,2},{1,3},{2,0},{3,1},{4,6},{5,7},{6,4},{7,5},{8,10},{9,11},{10,... | collective-permute-start | bytes 393224 | tf_op jit(solution)/shard_map/ppermute | solution.py:325
  14.4 3.0 %collective-permute-start.4 = (bf16[64,1024]{1,0:T(8,128)(2,1)}, bf16[64,1024]{1,0:T(8,128)(2,1)S(1)}, u32[]{:S(2)}, u32[]{:S(2)}) collective-permute-start(bf16[64,1024]{1,0:T(8,128)(2,1)} %get-tuple-element.29), channel_id=1, source_target_pairs={{0,4},{1,5},{2,6},{3,7},{4,0},{5,1},{6,2},{7,3},{8,12},{9,13},{10,... | collective-permute-start | bytes 393224 | tf_op jit(solution)/shard_map/ppermute | solution.py:325
  17.4 1.3 collective-permute-start.5
  18.7 3.6 %collective-permute-start.6 = (bf16[64,1024]{1,0:T(8,128)(2,1)}, bf16[64,1024]{1,0:T(8,128)(2,1)S(1)}, u32[]{:S(2)}, u32[]{:S(2)}) collective-permute-start(bf16[64,1024]{1,0:T(8,128)(2,1)} %get-tuple-element.31), channel_id=1, source_target_pairs={{0,6},{1,7},{2,4},{3,5},{4,2},{5,3},{6,0},{7,1},{8,14},{9,15},{10,... | collective-permute-start | bytes 393224 | tf_op jit(solution)/shard_map/ppermute | solution.py:325
  22.3 6.0 %all-to-all-start = ((bf16[8,64,1024]{2,1,0:T(8,128)(2,1)}), bf16[8,64,1024]{2,1,0:T(8,128)(2,1)S(1)}, u32[]{:S(2)}, u32[]{:S(2)}) async-start(bf16[8,64,1024]{2,1,0:T(8,128)(2,1)} %param.19), calls=%async_computation | async-start | bytes 2097152 | tf_op jit(solution)/shard_map/all_to_all | solution.py:333
  28.3 11.6 %collective-permute-done.5.refs_5_ = bf16[64,1024]{1,0:T(8,128)(2,1)S(1)} collective-permute-done((bf16[64,1024]{1,0:T(8,128)(2,1)}, bf16[64,1024]{1,0:T(8,128)(2,1)S(1)}, u32[]{:S(2)}, u32[]{:S(2)}) %collective-permute-start.5) | collective-permute-done | bytes 131104 | tf_op jit(solution)/shard_map/ppermute | solution.py:325
  40.7 18.8 %forward.1 = (bf16[8,64,1024]{2,1,0:T(8,128)(2,1)}, bf16[512,8192]{1,0:T(8,128)(2,1)}, bf16[512,1024]{1,0:T(8,128)(2,1)}, bf16[512,1024]{1,0:T(8,128)(2,1)}, bf1...) custom-call(s32[2]{0:T(128)} %pad_add_fusion.place_ref, ...), custom_call_target="tpu_custom_call" | custom-call | flops 20000000000 | bytes 10485760 | tf_op jit(solution)/shard_map/forward/pallas_call | solution.py:248
  59.5 5.4 %all-to-all-done.up_ref = bf16[8,64,1024]{2,1,0:T(8,128)(2,1)S(1)} async-done(((bf16[8,64,1024]{2,1,0:T(8,128)(2,1)}), bf16[8,64,1024]{2,1,0:T(8,128)(2,1)S(1)}, u32[]{:S(2)}, u32[]{:S(2)}) %all-to-all-start) | async-done | bytes 1048608 | tf_op jit(solution)/shard_map/all_to_all | solution.py:333
  64.8 12.3 %all-to-all-start.1 = ((bf16[8,64,1024]{2,1,0:T(8,128)(2,1)}), bf16[8,64,1024]{2,1,0:T(8,128)(2,1)S(1)}, u32[]{:S(2)}, u32[]{:S(2)}) async-start(bf16[8,64,1024]{2,1,0:T(8,128)(2,1)} %get-tuple-element.45), calls=%async_computation.1 | async-start | bytes 2097152 | tf_op jit(solution)/shard_map/all_to_all | solution.py:333
  77.1 15.1 %backward.1 = (bf16[256,256]{1,0:T(8,128)(2,1)}, bf16[256,256]{1,0:T(8,128)(2,1)}, bf16[256,256]{1,0:T(8,128)(2,1)}, bf16[256,256]{1,0:T(8,128)(2,1)}) custom-call(s32[2]{0:T(128)} %pad_add_fusion.place_ref, bf16[256,256]{1,0:T(8,128)(2,1)} %wo_ref.3, bf16[8,64,1024]{2,1,0:T(8,128)(2,1)} %copy-done, bf16[512,8192]{1,0:T(8,128)(2,1)} %get-tuple-element.33.prob_ref, ...), custom_call_target="tpu_custom_call" | custom-call | flops 20000000000 | bytes 10485760 | tf_op jit(solution)/shard_map/backward/pallas_call | solution.py:280
  92.2 2.9 %collective-permute-start.8 = (bf16[256,256]{1,0:T(8,128)(2,1)}, bf16[256,256]{1,0:T(8,128)(2,1)S(1)}, u32[]{:S(2)}, u32[]{:S(2)}) collective-permute-start(bf16[256,256]{1,0:T(8,128)(2,1)} %get-tuple-element.42), channel_id=1, source_target_pairs={{0,8},{8,0},{16,24},{24,16},{1,9},{9,1},{17,25},{25,17},{2,10},{10... | collective-permute-start | bytes 393224 | tf_op jit(solution)/shard_map/ppermute | solution.py:325
  95.2 1.6 %collective-permute-done.10 = bf16[256,256]{1,0:T(8,128)(2,1)S(1)} collective-permute-done((bf16[256,256]{1,0:T(8,128)(2,1)}, bf16[256,256]{1,0:T(8,128)(2,1)S(1)}, u32[]{:S(2)}, u32[]{:S(2)}) %collective-permute-start.10) | collective-permute-done | bytes 131104 | tf_op jit(solution)/shard_map/ppermute | solution.py:325
  96.8 4.2 %collective-permute-done.9 = bf16[256,256]{1,0:T(8,128)(2,1)S(1)} collective-permute-done((bf16[256,256]{1,0:T(8,128)(2,1)}, bf16[256,256]{1,0:T(8,128)(2,1)S(1)}, u32[]{:S(2)}, u32[]{:S(2)}) %collective-permute-start.9) | collective-permute-done | bytes 131104 | tf_op jit(solution)/shard_map/ppermute | solution.py:325
  101.1 1.0 add_convert_fusion
  102.0 2.3 %all-to-all-done.1 = bf16[8,64,1024]{2,1,0:T(8,128)(2,1)S(1)} async-done(((bf16[8,64,1024]{2,1,0:T(8,128)(2,1)}), bf16[8,64,1024]{2,1,0:T(8,128)(2,1)S(1)}, u32[]{:S(2)}, u32[]{:S(2)}) %all-to-all-start.1) | async-done | bytes 1048608 | tf_op jit(solution)/shard_map/all_to_all | solution.py:333
  104.4 10.8 %all_to_all.30 = bf16[8,32,256]{2,1,0:T(8,128)(2,1)S(1)} all-to-all(bf16[8,32,256]{2,1,0:T(8,128)(2,1)S(1)} %bitcast.12), channel_id=1, replica_groups=mesh['tm'=4,'contact'=8] {'contact'}, dimensions={0} | all-to-all | bytes 262144 | tf_op jit(solution)/shard_map/all_to_all | solution.py:333
  115.3 9.7 %all_to_all.31 = bf16[8,32,256]{2,1,0:T(8,128)(2,1)S(1)} all-to-all(bf16[8,32,256]{2,1,0:T(8,128)(2,1)S(1)} %bitcast.13), channel_id=1, replica_groups=mesh['tm'=4,'contact'=8] {'contact'}, dimensions={0} | all-to-all | bytes 262144 | tf_op jit(solution)/shard_map/all_to_all | solution.py:333
  125.0 1.2 collective-permute-start.12
  126.9 4.4 %collective-permute-done.12.refs_2_ = bf16[256,256]{1,0:T(8,128)(2,1)S(1)} collective-permute-done((bf16[256,256]{1,0:T(8,128)(2,1)S(1)}, bf16[256,256]{1,0:T(8,128)(2,1)S(1)}, u32[]{:S(2)}, u32[]{:S(2)}) %collective-permute-start.12) | collective-permute-done | bytes 131104 | tf_op jit(solution)/shard_map/ppermute | solution.py:325
  131.3 2.0 %collective-permute-done.13.refs_3_ = bf16[256,256]{1,0:T(8,128)(2,1)S(1)} collective-permute-done((bf16[256,256]{1,0:T(8,128)(2,1)S(1)}, bf16[256,256]{1,0:T(8,128)(2,1)S(1)}, u32[]{:S(2)}, u32[]{:S(2)}) %collective-permute-start.13) | collective-permute-done | bytes 131104 | tf_op jit(solution)/shard_map/ppermute | solution.py:325
  134.0 2.1 %place_all.1 = f32[4,256,256]{2,1,0:T(8,128)} custom-call(s32[2]{0:T(128)} %pad_add_fusion.place_ref, bf16[256,256]{1,0:T(8,128)(2,1)} %bitcast.11, bf16[256,256]{1,0:T(8,128)(2,1)} %copy-done.3, bf16[256,256]{1,0:T(8,128)(2,1)} %copy-done.4, bf16[256,256]{1,0:T(8,128)(2,1)} %copy-done.5), custom_call_target="tpu_custom_call" | custom-call | tf_op jit(solution)/shard_map/place_all/pallas_call | solution.py:314
  (53 shorter events, 5.8 us)
Async XLA Ops:
  1.5 3.3 %collective-permute-start = (bf16[8,64,128]{2,1,0:T(8,128)(2,1)S(1)}, bf16[8,64,128]{2,1,0:T(8,128)(2,1)S(1)}, u32[]{:S(2)}, u32[]{:S(2)}) collective-permute-start(bf16[8,64,128]{2,1,0:T(8,128)(2,1)S(1)} %slice.3), channel_id=1, source_target_pairs={{0,8},{8,16},{16,24},{1,9},{9,17},{17,25},{2,10},{10,18},{18,26},{... | collective-permute-start | bytes 393224 | tf_op jit(solution)/shard_map/ppermute | solution.py:352
  10.4 8.3 %collective-permute-start.1 = (bf16[64,1024]{1,0:T(8,128)(2,1)}, bf16[64,1024]{1,0:T(8,128)(2,1)S(1)}, u32[]{:S(2)}, u32[]{:S(2)}) collective-permute-start(bf16[64,1024]{1,0:T(8,128)(2,1)} %get-tuple-element.26), channel_id=1, source_target_pairs={{0,1},{1,0},{2,3},{3,2},{4,5},{5,4},{6,7},{7,6},{8,9},{9,8},{10,11... | collective-permute-start | bytes 393224 | tf_op jit(solution)/shard_map/ppermute | solution.py:325
  12.8 9.5 %collective-permute-start.2 = (bf16[64,1024]{1,0:T(8,128)(2,1)}, bf16[64,1024]{1,0:T(8,128)(2,1)S(1)}, u32[]{:S(2)}, u32[]{:S(2)}) collective-permute-start(bf16[64,1024]{1,0:T(8,128)(2,1)} %get-tuple-element.27), channel_id=1, source_target_pairs={{0,2},{1,3},{2,0},{3,1},{4,6},{5,7},{6,4},{7,5},{8,10},{9,11},{10,... | collective-permute-start | bytes 393224 | tf_op jit(solution)/shard_map/ppermute | solution.py:325
  14.4 13.9 %collective-permute-start.3 = (bf16[64,1024]{1,0:T(8,128)(2,1)}, bf16[64,1024]{1,0:T(8,128)(2,1)S(1)}, u32[]{:S(2)}, u32[]{:S(2)}) collective-permute-start(bf16[64,1024]{1,0:T(8,128)(2,1)} %get-tuple-element.28), channel_id=1, source_target_pairs={{0,3},{1,2},{2,1},{3,0},{4,7},{5,6},{6,5},{7,4},{8,11},{9,10},{10,... | collective-permute-start | bytes 393224 | tf_op jit(solution)/shard_map/ppermute | solution.py:325
  14.4 13.9 %collective-permute-start.4 = (bf16[64,1024]{1,0:T(8,128)(2,1)}, bf16[64,1024]{1,0:T(8,128)(2,1)S(1)}, u32[]{:S(2)}, u32[]{:S(2)}) collective-permute-start(bf16[64,1024]{1,0:T(8,128)(2,1)} %get-tuple-element.29), channel_id=1, source_target_pairs={{0,4},{1,5},{2,6},{3,7},{4,0},{5,1},{6,2},{7,3},{8,12},{9,13},{10,... | collective-permute-start | bytes 393224 | tf_op jit(solution)/shard_map/ppermute | solution.py:325
  17.4 22.5 %collective-permute-start.5 = (bf16[64,1024]{1,0:T(8,128)(2,1)}, bf16[64,1024]{1,0:T(8,128)(2,1)S(1)}, u32[]{:S(2)}, u32[]{:S(2)}) collective-permute-start(bf16[64,1024]{1,0:T(8,128)(2,1)} %get-tuple-element.30), channel_id=1, source_target_pairs={{0,5},{1,4},{2,7},{3,6},{4,1},{5,0},{6,3},{7,2},{8,13},{9,12},{10,... | collective-permute-start | bytes 393224 | tf_op jit(solution)/shard_map/ppermute | solution.py:325
  18.7 21.3 %copy-start.6 = (bf16[64,1024]{1,0:T(8,128)(2,1)}, bf16[64,1024]{1,0:T(8,128)(2,1)S(1)}, u32[]{:S(2)}) copy-start(bf16[64,1024]{1,0:T(8,128)(2,1)S(1)} %collective-permute-done.1.refs_1_) | copy-start | bytes 393220
  18.7 21.2 %collective-permute-start.6 = (bf16[64,1024]{1,0:T(8,128)(2,1)}, bf16[64,1024]{1,0:T(8,128)(2,1)S(1)}, u32[]{:S(2)}, u32[]{:S(2)}) collective-permute-start(bf16[64,1024]{1,0:T(8,128)(2,1)} %get-tuple-element.31), channel_id=1, source_target_pairs={{0,6},{1,7},{2,4},{3,5},{4,2},{5,3},{6,0},{7,1},{8,14},{9,15},{10,... | collective-permute-start | bytes 393224 | tf_op jit(solution)/shard_map/ppermute | solution.py:325
  22.3 17.7 %copy-start.7 = (bf16[64,1024]{1,0:T(8,128)(2,1)}, bf16[64,1024]{1,0:T(8,128)(2,1)S(1)}, u32[]{:S(2)}) copy-start(bf16[64,1024]{1,0:T(8,128)(2,1)S(1)} %collective-permute-done.2.refs_2_) | copy-start | bytes 393220
  22.3 17.6 %collective-permute-start.7 = (bf16[64,1024]{1,0:T(8,128)(2,1)}, bf16[64,1024]{1,0:T(8,128)(2,1)S(1)}, u32[]{:S(2)}, u32[]{:S(2)}) collective-permute-start(bf16[64,1024]{1,0:T(8,128)(2,1)} %get-tuple-element.32), channel_id=1, source_target_pairs={{0,7},{1,6},{2,5},{3,4},{4,3},{5,2},{6,1},{7,0},{8,15},{9,14},{10,... | collective-permute-start | bytes 393224 | tf_op jit(solution)/shard_map/ppermute | solution.py:325
  22.3 42.5 %all-to-all-start = ((bf16[8,64,1024]{2,1,0:T(8,128)(2,1)}), bf16[8,64,1024]{2,1,0:T(8,128)(2,1)S(1)}, u32[]{:S(2)}, u32[]{:S(2)}) async-start(bf16[8,64,1024]{2,1,0:T(8,128)(2,1)} %param.19), calls=%async_computation | async-start | bytes 2097152 | tf_op jit(solution)/shard_map/all_to_all | solution.py:333
  28.3 11.7 %copy-start.8 = (bf16[64,1024]{1,0:T(8,128)(2,1)}, bf16[64,1024]{1,0:T(8,128)(2,1)S(1)}, u32[]{:S(2)}) copy-start(bf16[64,1024]{1,0:T(8,128)(2,1)S(1)} %collective-permute-done.3.refs_3_) | copy-start | bytes 393220
  28.3 11.7 %copy-start.9 = (bf16[64,1024]{1,0:T(8,128)(2,1)}, bf16[64,1024]{1,0:T(8,128)(2,1)S(1)}, u32[]{:S(2)}) copy-start(bf16[64,1024]{1,0:T(8,128)(2,1)S(1)} %collective-permute-done.4.refs_4_) | copy-start | bytes 393220
  64.8 12.3 %copy-start = (bf16[8,64,1024]{2,1,0:T(8,128)(2,1)}, bf16[8,64,1024]{2,1,0:T(8,128)(2,1)S(1)}, u32[]{:S(2)}) copy-start(bf16[8,64,1024]{2,1,0:T(8,128)(2,1)S(1)} %all-to-all-done.up_ref) | copy-start | bytes 3145732
  64.8 39.5 %all-to-all-start.1 = ((bf16[8,64,1024]{2,1,0:T(8,128)(2,1)}), bf16[8,64,1024]{2,1,0:T(8,128)(2,1)S(1)}, u32[]{:S(2)}, u32[]{:S(2)}) async-start(bf16[8,64,1024]{2,1,0:T(8,128)(2,1)} %get-tuple-element.45), calls=%async_computation.1 | async-start | bytes 2097152 | tf_op jit(solution)/shard_map/all_to_all | solution.py:333
  92.2 4.6 %collective-permute-start.10 = (bf16[256,256]{1,0:T(8,128)(2,1)}, bf16[256,256]{1,0:T(8,128)(2,1)S(1)}, u32[]{:S(2)}, u32[]{:S(2)}) collective-permute-start(bf16[256,256]{1,0:T(8,128)(2,1)} %get-tuple-element.44), channel_id=1, source_target_pairs={{0,24},{8,16},{16,8},{24,0},{1,25},{9,17},{17,9},{25,1},{2,26},{10... | collective-permute-start | bytes 393224 | tf_op jit(solution)/shard_map/ppermute | solution.py:325
  92.2 4.6 %collective-permute-start.8 = (bf16[256,256]{1,0:T(8,128)(2,1)}, bf16[256,256]{1,0:T(8,128)(2,1)S(1)}, u32[]{:S(2)}, u32[]{:S(2)}) collective-permute-start(bf16[256,256]{1,0:T(8,128)(2,1)} %get-tuple-element.42), channel_id=1, source_target_pairs={{0,8},{8,0},{16,24},{24,16},{1,9},{9,1},{17,25},{25,17},{2,10},{10... | collective-permute-start | bytes 393224 | tf_op jit(solution)/shard_map/ppermute | solution.py:325
  95.2 5.9 %collective-permute-start.9 = (bf16[256,256]{1,0:T(8,128)(2,1)}, bf16[256,256]{1,0:T(8,128)(2,1)S(1)}, u32[]{:S(2)}, u32[]{:S(2)}) collective-permute-start(bf16[256,256]{1,0:T(8,128)(2,1)} %get-tuple-element.43), channel_id=1, source_target_pairs={{0,16},{8,24},{16,0},{24,8},{1,17},{9,25},{17,1},{25,9},{2,18},{10... | collective-permute-start | bytes 393224 | tf_op jit(solution)/shard_map/ppermute | solution.py:325
  125.0 8.3 %copy-start.1 = (bf16[8,32,256]{2,1,0:T(8,128)(2,1)}, bf16[8,32,256]{2,1,0:T(8,128)(2,1)S(1)}, u32[]{:S(2)}) copy-start(bf16[8,32,256]{2,1,0:T(8,128)(2,1)S(1)} %all_to_all.31) | copy-start | bytes 393220
  125.0 1.9 %collective-permute-start.11 = (bf16[256,256]{1,0:T(8,128)(2,1)S(1)}, bf16[256,256]{1,0:T(8,128)(2,1)S(1)}, u32[]{:S(2)}, u32[]{:S(2)}) collective-permute-start(bf16[256,256]{1,0:T(8,128)(2,1)S(1)} %bitcast.8), channel_id=1, source_target_pairs={{0,8},{8,0},{16,24},{24,16},{1,9},{9,1},{17,25},{25,17},{2,10},{10... | collective-permute-start | bytes 393224 | tf_op jit(solution)/shard_map/ppermute | solution.py:325
  125.0 6.3 %collective-permute-start.12 = (bf16[256,256]{1,0:T(8,128)(2,1)S(1)}, bf16[256,256]{1,0:T(8,128)(2,1)S(1)}, u32[]{:S(2)}, u32[]{:S(2)}) collective-permute-start(bf16[256,256]{1,0:T(8,128)(2,1)S(1)} %bitcast.9), channel_id=1, source_target_pairs={{0,16},{8,24},{16,0},{24,8},{1,17},{9,25},{17,1},{25,9},{2,18},{10... | collective-permute-start | bytes 393224 | tf_op jit(solution)/shard_map/ppermute | solution.py:325
  126.2 7.2 %collective-permute-start.13 = (bf16[256,256]{1,0:T(8,128)(2,1)S(1)}, bf16[256,256]{1,0:T(8,128)(2,1)S(1)}, u32[]{:S(2)}, u32[]{:S(2)}) collective-permute-start(bf16[256,256]{1,0:T(8,128)(2,1)S(1)} %bitcast.10), channel_id=1, source_target_pairs={{0,24},{8,16},{16,8},{24,0},{1,25},{9,17},{17,9},{25,1},{2,26},{10... | collective-permute-start | bytes 393224 | tf_op jit(solution)/shard_map/ppermute | solution.py:325
  126.9 6.5 %copy-start.3 = (bf16[256,256]{1,0:T(8,128)(2,1)}, bf16[256,256]{1,0:T(8,128)(2,1)S(1)}, u32[]{:S(2)}) copy-start(bf16[256,256]{1,0:T(8,128)(2,1)S(1)} %collective-permute-done.11.refs_1_) | copy-start | bytes 393220
  131.3 2.0 %copy-start.4 = (bf16[256,256]{1,0:T(8,128)(2,1)}, bf16[256,256]{1,0:T(8,128)(2,1)S(1)}, u32[]{:S(2)}) copy-start(bf16[256,256]{1,0:T(8,128)(2,1)S(1)} %collective-permute-done.12.refs_2_) | copy-start | bytes 393220
  (5 other events, 3.4 us)

commit v5 on v4

--- a/solution.py
+++ b/solution.py
@@ -175,7 +175,7 @@
 
 
 def backward_kernel(
-    blocks, place_ref, wo_ref, up_ref, prob_ref, value_ref, keys_ref, query_t_ref, normed_ref,
+    blocks, place_ref, wo_ref, up_ref, late_ref, prob_ref, value_ref, keys_ref, query_t_ref, normed_ref,
     normed_t_ref, mixed_ref, mixed_t_ref, *refs,
 ):
     out_refs, total, chunks = refs[:-2], refs[-2], refs[-1]
@@ -189,7 +189,9 @@
         total[...] = jnp.zeros_like(total)
 
     me = place_ref[1]
-    upstream = jnp.concatenate([up_ref[me ^ k] for k in range(blocks)], axis=0)
+    upstream = jnp.concatenate(
+        [ref[me ^ k] for k in range(blocks) for ref in (up_ref, late_ref)], axis=0
+    )
     normed = normed_ref[...]
     value = value_ref[...]
     keys = keys_ref[...]
@@ -271,9 +273,9 @@
     )(place, *small, *features)
 
 
-def backward(place, upstream, kept, w_out, tm_count):
+def backward(place, upstream, late, kept, w_out, tm_count):
     blocks, rows, span = upstream.shape
-    contacts = rows * blocks
+    contacts = 2 * rows * blocks
     width = w_out.shape[0]
     groups = span // width
     chunk = (4 * width // tm_count, width)
@@ -282,6 +284,7 @@
         grid=(groups,),
         in_specs=[
             index_spec(), whole(w_out.shape),
+            pl.BlockSpec((blocks, rows, width), lambda i: (0, 0, i)),
             pl.BlockSpec((blocks, rows, width), lambda i: (0, 0, i)),
         ]
         + [
@@ -299,7 +302,7 @@
             flops=groups * 5 * 10**9, bytes_accessed=20 * contacts * span, transcendentals=0
         ),
         name="backward",
-    )(place, w_out, upstream, *kept)
+    )(place, w_out, upstream, late, *kept)
 
 
 def place_all(place, parts):
@@ -348,21 +351,26 @@
     if pieces > 1:
         cotangent = cotangent.reshape(batch, contacts_here, pieces, span)
         cotangent = cotangent.transpose(0, 2, 1, 3).reshape(count, contacts_here, span)
-    upstream = exchange(cotangent, "contact")
+    half = contacts_here // 2
+    upstream = exchange(cotangent[:, :half], "contact")
     rim = lax.ppermute(
         signal[:, :, slab - rim_width :], "tm", [(i, i + 1) for i in range(tm_count - 1)]
     )
     filtered = filter_all(place, signal, rim, fir_taps, count)
     features = swap_all(filtered, "contact")
+    features, upstream, late = lax.optimization_barrier(
+        (features, upstream, cotangent[:, half:])
+    )
+    late = exchange(late, "contact")
     attended, *kept = forward(
         place, features, neighbours.T, live_mask[None], lap_coef[None],
         [w_query, w_key, w_value, w_out],
     )
     returned = exchange(attended, "contact")
-    grads = backward(place, upstream, kept, w_out, tm_count)
+    grads = backward(place, upstream, late, kept, w_out, tm_count)
     grads = swap_all(grads, "tm")
     part = sum(piece.astype(F32) for piece in grads).astype(BF16)
-    part, returned = lax.optimization_barrier((part, returned))
+    part, _ = lax.optimization_barrier((part, returned))
     part = exchange(part, "contact").reshape(count, -1, width)
     grad_scale = (batch * (slab // width) * tm_count * neighbours.shape[0]) ** (-0.5)
     mine = (jnp.sum(part.astype(F32), axis=0) * grad_scale).astype(BF16)

time: 138 us -> 140 us (1.014)
  local copies, waits for them, and re-layouts: 3.94 us -> 6.15 us
  waiting for transfers between devices: 31.9 us -> 29.8 us
    all_to_all x2 -> x3, waiting for transfers between devices: 7.71 us -> 1.86 us  [exchange(): return lax.all_to_all(value, axis, split_axis=0, concat_axis=0, tiled=True)]
    all_to_all x2 -> x3, starting transfers between devices: 18.2 us -> 22.2 us  [exchange(): return lax.all_to_all(value, axis, split_axis=0, concat_axis=0, tiled=True)]
    ppermute x13, waiting for transfers between devices: 23.9 us -> 27.5 us  [swap(): lax.ppermute(value, axis, [(i, i ^ k) for i in range(lax.axis_size(axis))])]
    slice x0 -> x1, local copies, waits for them, and re-layouts: none -> 2.27 us  [local(): cotangent[:, half:]]
    ppermute x13, starting transfers between devices: 16.8 us -> 15 us  [swap(): lax.ppermute(value, axis, [(i, i ^ k) for i in range(lax.axis_size(axis))])]
    unnamed x33 -> x35, local copies, waits for them, and re-layouts: 3.02 us -> 2.97 us
  transfers between devices with their start and end apart: 16 -> 17, of which waited for: 8 -> 8; matrix products, arithmetic and copies ran while one was open for 1% -> 2% of each run, Pallas kernels for 25% -> 28%
where the time goes in v5:
time: 140 us; the launch traced here: 139 us
  Pallas kernels  40.4 us (29%)
  starting transfers between devices  38.7 us (28%)
  waiting for transfers between devices  29.8 us (21%)
  blocking collectives  21.5 us (15%)
  local copies, waits for them, and re-layouts  6.15 us (4%)
  other arithmetic  1.56 us (1%)
    ppermute x13, waiting for transfers between devices, swap(): lax.ppermute(value, axis, [(i, i ^ k) for i in range(lax.axis_size(axis))])  27.5 us
    all_to_all x3, starting transfers between devices, exchange(): return lax.all_to_all(value, axis, split_axis=0, concat_axis=0, tiled=True)  22.2 us
    all_to_all x2, blocking collectives, exchange(): return lax.all_to_all(value, axis, split_axis=0, concat_axis=0, tiled=True)  21.5 us
    pallas_call x1, Pallas kernels, forward(): pl.pallas_call(functools.partial(forward_kernel, blocks), grid=(groups,),...  18.8 us
    ppermute x13, starting transfers between devices, swap(): lax.ppermute(value, axis, [(i, i ^ k) for i in range(lax.axis_size(axis))])  15 us
    pallas_call x1, Pallas kernels, backward(): pl.pallas_call(functools.partial(backward_kernel, blocks), grid=(groups,)...  14.5 us
    pallas_call x1, Pallas kernels, filter_all(): pl.pallas_call(filter_kernel, grid=(contacts // rows,), in_specs=[index_s...  4.89 us
    unnamed x35, local copies, waits for them, and re-layouts  2.97 us
  transfers between devices with their start and end apart: 17, of which 8 were waited for; matrix products, arithmetic and copies ran while one was open for 2% of the time, Pallas kernels for 28%

profile of v5, /device:TPU:0, one launch (start us, length us, event | category | flops | bytes accessed | tf_op | source)
XLA Modules:
  0.0 139.0 jit_solution(14273365712918172598)
XLA Ops:
  0.6 2.3 %fusion = (bf16[8,32,1024]{2,1,0:T(8,128)(2,1)}, bf16[8,32,1024]{2,1,0:T(8,128)(2,1)}) fusion(bf16[8,64,1024]{2,1,0:T(8,128)(2,1)} %param.19), kind=kLoop, calls=%fused_computation.12 | loop fusion | bytes 2097152 | tf_op jit(solution)/shard_map/slice | solution.py:362
  2.9 7.3 %all-to-all-start = ((bf16[8,32,1024]{2,1,0:T(8,128)(2,1)}), bf16[8,32,1024]{2,1,0:T(8,128)(2,1)S(1)}, u32[]{:S(2)}, u32[]{:S(2)}) async-start(bf16[8,32,1024]{2,1,0:T(8,128)(2,1)} %get-tuple-element.69), calls=%async_computation | async-start | bytes 1048576 | tf_op jit(solution)/shard_map/all_to_all | solution.py:336
  11.1 1.5 %collective-permute-start = (bf16[8,64,128]{2,1,0:T(8,128)(2,1)S(1)}, bf16[8,64,128]{2,1,0:T(8,128)(2,1)S(1)}, u32[]{:S(2)}, u32[]{:S(2)}) collective-permute-start(bf16[8,64,128]{2,1,0:T(8,128)(2,1)S(1)} %slice.9), channel_id=1, source_target_pairs={{0,8},{8,16},{16,24},{1,9},{9,17},{17,25},{2,10},{10,18},{18,26},{... | collective-permute-start | bytes 393224 | tf_op jit(solution)/shard_map/ppermute | solution.py:356
  14.2 4.9 %filter.1 = (bf16[64,1024]{1,0:T(8,128)(2,1)}, bf16[64,1024]{1,0:T(8,128)(2,1)}, bf16[64,1024]{1,0:T(8,128)(2,1)}, bf16[64,1024]{1,0:T(8,128)(2,1)}, bf16[64,102...) custom-call(s32[2]{0:T(128)} %pad_add_fusion.place_ref, ...), custom_call_target="tpu_custom_call" | custom-call | flops 268435456 | bytes 2097152 | tf_op jit(solution)/shard_map/filter/pallas_call | solution.py:72
  19.1 1.9 %collective-permute-start.1 = (bf16[64,1024]{1,0:T(8,128)(2,1)}, bf16[64,1024]{1,0:T(8,128)(2,1)S(1)}, u32[]{:S(2)}, u32[]{:S(2)}) collective-permute-start(bf16[64,1024]{1,0:T(8,128)(2,1)} %get-tuple-element.35), channel_id=1, source_target_pairs={{0,1},{1,0},{2,3},{3,2},{4,5},{5,4},{6,7},{7,6},{8,9},{9,8},{10,11... | collective-permute-start | bytes 393224 | tf_op jit(solution)/shard_map/ppermute | solution.py:328
  21.0 1.5 %collective-permute-start.2 = (bf16[64,1024]{1,0:T(8,128)(2,1)}, bf16[64,1024]{1,0:T(8,128)(2,1)S(1)}, u32[]{:S(2)}, u32[]{:S(2)}) collective-permute-start(bf16[64,1024]{1,0:T(8,128)(2,1)} %get-tuple-element.36), channel_id=1, source_target_pairs={{0,2},{1,3},{2,0},{3,1},{4,6},{5,7},{6,4},{7,5},{8,10},{9,11},{10,... | collective-permute-start | bytes 393224 | tf_op jit(solution)/shard_map/ppermute | solution.py:328
  22.6 2.8 %collective-permute-start.4 = (bf16[64,1024]{1,0:T(8,128)(2,1)}, bf16[64,1024]{1,0:T(8,128)(2,1)S(1)}, u32[]{:S(2)}, u32[]{:S(2)}) collective-permute-start(bf16[64,1024]{1,0:T(8,128)(2,1)} %get-tuple-element.38), channel_id=1, source_target_pairs={{0,4},{1,5},{2,6},{3,7},{4,0},{5,1},{6,2},{7,3},{8,12},{9,13},{10,... | collective-permute-start | bytes 393224 | tf_op jit(solution)/shard_map/ppermute | solution.py:328
  25.4 1.5 %collective-permute-start.5 = (bf16[64,1024]{1,0:T(8,128)(2,1)}, bf16[64,1024]{1,0:T(8,128)(2,1)S(1)}, u32[]{:S(2)}, u32[]{:S(2)}) collective-permute-start(bf16[64,1024]{1,0:T(8,128)(2,1)} %get-tuple-element.39), channel_id=1, source_target_pairs={{0,5},{1,4},{2,7},{3,6},{4,1},{5,0},{6,3},{7,2},{8,13},{9,12},{10,... | collective-permute-start | bytes 393224 | tf_op jit(solution)/shard_map/ppermute | solution.py:328
  26.8 3.3 %collective-permute-start.6 = (bf16[64,1024]{1,0:T(8,128)(2,1)}, bf16[64,1024]{1,0:T(8,128)(2,1)S(1)}, u32[]{:S(2)}, u32[]{:S(2)}) collective-permute-start(bf16[64,1024]{1,0:T(8,128)(2,1)} %get-tuple-element.40), channel_id=1, source_target_pairs={{0,6},{1,7},{2,4},{3,5},{4,2},{5,3},{6,0},{7,1},{8,14},{9,15},{10,... | collective-permute-start | bytes 393224 | tf_op jit(solution)/shard_map/ppermute | solution.py:328
  30.3 3.8 %collective-permute-done.3.refs_3_ = bf16[64,1024]{1,0:T(8,128)(2,1)S(1)} collective-permute-done((bf16[64,1024]{1,0:T(8,128)(2,1)}, bf16[64,1024]{1,0:T(8,128)(2,1)S(1)}, u32[]{:S(2)}, u32[]{:S(2)}) %collective-permute-start.3) | collective-permute-done | bytes 131104 | tf_op jit(solution)/shard_map/ppermute | solution.py:328
  34.1 10.9 %collective-permute-done.5.refs_5_ = bf16[64,1024]{1,0:T(8,128)(2,1)S(1)} collective-permute-done((bf16[64,1024]{1,0:T(8,128)(2,1)}, bf16[64,1024]{1,0:T(8,128)(2,1)S(1)}, u32[]{:S(2)}, u32[]{:S(2)}) %collective-permute-start.5) | collective-permute-done | bytes 131104 | tf_op jit(solution)/shard_map/ppermute | solution.py:328
  45.0 8.9 %all-to-all-start.2 = ((bf16[8,32,1024]{2,1,0:T(8,128)(2,1)}), bf16[8,32,1024]{2,1,0:T(8,128)(2,1)S(1)}, u32[]{:S(2)}, u32[]{:S(2)}) async-start(bf16[8,32,1024]{2,1,0:T(8,128)(2,1)} %get-tuple-element.52), calls=%async_computation.2 | async-start | bytes 1048576 | tf_op jit(solution)/shard_map/all_to_all | solution.py:336
  54.0 18.8 %forward.1 = (bf16[8,64,1024]{2,1,0:T(8,128)(2,1)}, bf16[512,8192]{1,0:T(8,128)(2,1)}, bf16[512,1024]{1,0:T(8,128)(2,1)}, bf16[512,1024]{1,0:T(8,128)(2,1)}, bf1...) custom-call(s32[2]{0:T(128)} %pad_add_fusion.place_ref, ...), custom_call_target="tpu_custom_call" | custom-call | flops 20000000000 | bytes 10485760 | tf_op jit(solution)/shard_map/forward/pallas_call | solution.py:250
  72.9 6.0 %all-to-all-start.1 = ((bf16[8,64,1024]{2,1,0:T(8,128)(2,1)}), bf16[8,64,1024]{2,1,0:T(8,128)(2,1)S(1)}, u32[]{:S(2)}, u32[]{:S(2)}) async-start(bf16[8,64,1024]{2,1,0:T(8,128)(2,1)} %get-tuple-element.50), calls=%async_computation.1 | async-start | bytes 2097152 | tf_op jit(solution)/shard_map/all_to_all | solution.py:336
  78.9 14.5 %backward.1 = (bf16[256,256]{1,0:T(8,128)(2,1)}, bf16[256,256]{1,0:T(8,128)(2,1)}, bf16[256,256]{1,0:T(8,128)(2,1)}, bf16[256,256]{1,0:T(8,128)(2,1)}) custom-call(s32[2]{0:T(128)} %pad_add_fusion.place_ref, bf16[256,256]{1,0:T(8,128)(2,1)} %wo_ref.3, bf16[8,32,1024]{2,1,0:T(8,128)(2,1)} %copy-done.1, bf16[8,32,1024]{2,1,0:T(8,128)(2,1)} %copy-done.2, ...), custom_call_target="tpu_custom_call" | custom-call | flops 20000000000 | bytes 10485760 | tf_op jit(solution)/shard_map/backward/pallas_call | solution.py:282
  93.5 1.5 %collective-permute-start.9 = (bf16[256,256]{1,0:T(8,128)(2,1)}, bf16[256,256]{1,0:T(8,128)(2,1)S(1)}, u32[]{:S(2)}, u32[]{:S(2)}) collective-permute-start(bf16[256,256]{1,0:T(8,128)(2,1)} %get-tuple-element.63), channel_id=1, source_target_pairs={{0,16},{8,24},{16,0},{24,8},{1,17},{9,25},{17,1},{25,9},{2,18},{10... | collective-permute-start | bytes 393224 | tf_op jit(solution)/shard_map/ppermute | solution.py:328
  95.4 4.7 %collective-permute-done.9 = bf16[256,256]{1,0:T(8,128)(2,1)S(1)} collective-permute-done((bf16[256,256]{1,0:T(8,128)(2,1)}, bf16[256,256]{1,0:T(8,128)(2,1)S(1)}, u32[]{:S(2)}, u32[]{:S(2)}) %collective-permute-start.9) | collective-permute-done | bytes 131104 | tf_op jit(solution)/shard_map/ppermute | solution.py:328
  100.1 1.9 %collective-permute-done.10 = bf16[256,256]{1,0:T(8,128)(2,1)S(1)} collective-permute-done((bf16[256,256]{1,0:T(8,128)(2,1)}, bf16[256,256]{1,0:T(8,128)(2,1)S(1)}, u32[]{:S(2)}, u32[]{:S(2)}) %collective-permute-start.10) | collective-permute-done | bytes 131104 | tf_op jit(solution)/shard_map/ppermute | solution.py:328
  103.0 1.9 %all-to-all-done.1 = bf16[8,64,1024]{2,1,0:T(8,128)(2,1)S(1)} async-done(((bf16[8,64,1024]{2,1,0:T(8,128)(2,1)}), bf16[8,64,1024]{2,1,0:T(8,128)(2,1)S(1)}, u32[]{:S(2)}, u32[]{:S(2)}) %all-to-all-start.1) | async-done | bytes 1048608 | tf_op jit(solution)/shard_map/all_to_all | solution.py:336
  104.8 11.7 %all_to_all.35 = bf16[8,32,256]{2,1,0:T(8,128)(2,1)S(1)} all-to-all(bf16[8,32,256]{2,1,0:T(8,128)(2,1)S(1)} %bitcast.12), channel_id=1, replica_groups=mesh['tm'=4,'contact'=8] {'contact'}, dimensions={0} | all-to-all | bytes 262144 | tf_op jit(solution)/shard_map/all_to_all | solution.py:336
  116.6 9.9 %all_to_all.36 = bf16[8,32,256]{2,1,0:T(8,128)(2,1)S(1)} all-to-all(bf16[8,32,256]{2,1,0:T(8,128)(2,1)S(1)} %bitcast.13), channel_id=1, replica_groups=mesh['tm'=4,'contact'=8] {'contact'}, dimensions={0} | all-to-all | bytes 262144 | tf_op jit(solution)/shard_map/all_to_all | solution.py:336
  128.3 3.9 %collective-permute-done.13.refs_3_ = bf16[256,256]{1,0:T(8,128)(2,1)S(1)} collective-permute-done((bf16[256,256]{1,0:T(8,128)(2,1)S(1)}, bf16[256,256]{1,0:T(8,128)(2,1)S(1)}, u32[]{:S(2)}, u32[]{:S(2)}) %collective-permute-start.13) | collective-permute-done | bytes 131104 | tf_op jit(solution)/shard_map/ppermute | solution.py:328
  132.3 2.3 %collective-permute-done.12.refs_2_ = bf16[256,256]{1,0:T(8,128)(2,1)S(1)} collective-permute-done((bf16[256,256]{1,0:T(8,128)(2,1)S(1)}, bf16[256,256]{1,0:T(8,128)(2,1)S(1)}, u32[]{:S(2)}, u32[]{:S(2)}) %collective-permute-start.12) | collective-permute-done | bytes 131104 | tf_op jit(solution)/shard_map/ppermute | solution.py:328
  135.9 2.1 %place_all.1 = f32[4,256,256]{2,1,0:T(8,128)} custom-call(s32[2]{0:T(128)} %pad_add_fusion.place_ref, bf16[256,256]{1,0:T(8,128)(2,1)} %bitcast.11, bf16[256,256]{1,0:T(8,128)(2,1)} %copy-done.6, bf16[256,256]{1,0:T(8,128)(2,1)} %copy-done.5, bf16[256,256]{1,0:T(8,128)(2,1)} %copy-done.4), custom_call_target="tpu_custom_call" | custom-call | tf_op jit(solution)/shard_map/place_all/pallas_call | solution.py:317
  (58 shorter events, 8.5 us)
Async XLA Ops:
  2.9 42.1 %all-to-all-start = ((bf16[8,32,1024]{2,1,0:T(8,128)(2,1)}), bf16[8,32,1024]{2,1,0:T(8,128)(2,1)S(1)}, u32[]{:S(2)}, u32[]{:S(2)}) async-start(bf16[8,32,1024]{2,1,0:T(8,128)(2,1)} %get-tuple-element.69), calls=%async_computation | async-start | bytes 1048576 | tf_op jit(solution)/shard_map/all_to_all | solution.py:336
  11.1 2.4 %collective-permute-start = (bf16[8,64,128]{2,1,0:T(8,128)(2,1)S(1)}, bf16[8,64,128]{2,1,0:T(8,128)(2,1)S(1)}, u32[]{:S(2)}, u32[]{:S(2)}) collective-permute-start(bf16[8,64,128]{2,1,0:T(8,128)(2,1)S(1)} %slice.9), channel_id=1, source_target_pairs={{0,8},{8,16},{16,24},{1,9},{9,17},{17,25},{2,10},{10,18},{18,26},{... | collective-permute-start | bytes 393224 | tf_op jit(solution)/shard_map/ppermute | solution.py:356
  19.1 7.8 %collective-permute-start.1 = (bf16[64,1024]{1,0:T(8,128)(2,1)}, bf16[64,1024]{1,0:T(8,128)(2,1)S(1)}, u32[]{:S(2)}, u32[]{:S(2)}) collective-permute-start(bf16[64,1024]{1,0:T(8,128)(2,1)} %get-tuple-element.35), channel_id=1, source_target_pairs={{0,1},{1,0},{2,3},{3,2},{4,5},{5,4},{6,7},{7,6},{8,9},{9,8},{10,11... | collective-permute-start | bytes 393224 | tf_op jit(solution)/shard_map/ppermute | solution.py:328
  21.0 9.1 %collective-permute-start.2 = (bf16[64,1024]{1,0:T(8,128)(2,1)}, bf16[64,1024]{1,0:T(8,128)(2,1)S(1)}, u32[]{:S(2)}, u32[]{:S(2)}) collective-permute-start(bf16[64,1024]{1,0:T(8,128)(2,1)} %get-tuple-element.36), channel_id=1, source_target_pairs={{0,2},{1,3},{2,0},{3,1},{4,6},{5,7},{6,4},{7,5},{8,10},{9,11},{10,... | collective-permute-start | bytes 393224 | tf_op jit(solution)/shard_map/ppermute | solution.py:328
  22.4 11.6 %collective-permute-start.3 = (bf16[64,1024]{1,0:T(8,128)(2,1)}, bf16[64,1024]{1,0:T(8,128)(2,1)S(1)}, u32[]{:S(2)}, u32[]{:S(2)}) collective-permute-start(bf16[64,1024]{1,0:T(8,128)(2,1)} %get-tuple-element.37), channel_id=1, source_target_pairs={{0,3},{1,2},{2,1},{3,0},{4,7},{5,6},{6,5},{7,4},{8,11},{9,10},{10,... | collective-permute-start | bytes 393224 | tf_op jit(solution)/shard_map/ppermute | solution.py:328
  22.6 11.4 %collective-permute-start.4 = (bf16[64,1024]{1,0:T(8,128)(2,1)}, bf16[64,1024]{1,0:T(8,128)(2,1)S(1)}, u32[]{:S(2)}, u32[]{:S(2)}) collective-permute-start(bf16[64,1024]{1,0:T(8,128)(2,1)} %get-tuple-element.38), channel_id=1, source_target_pairs={{0,4},{1,5},{2,6},{3,7},{4,0},{5,1},{6,2},{7,3},{8,12},{9,13},{10,... | collective-permute-start | bytes 393224 | tf_op jit(solution)/shard_map/ppermute | solution.py:328
  25.4 19.6 %collective-permute-start.5 = (bf16[64,1024]{1,0:T(8,128)(2,1)}, bf16[64,1024]{1,0:T(8,128)(2,1)S(1)}, u32[]{:S(2)}, u32[]{:S(2)}) collective-permute-start(bf16[64,1024]{1,0:T(8,128)(2,1)} %get-tuple-element.39), channel_id=1, source_target_pairs={{0,5},{1,4},{2,7},{3,6},{4,1},{5,0},{6,3},{7,2},{8,13},{9,12},{10,... | collective-permute-start | bytes 393224 | tf_op jit(solution)/shard_map/ppermute | solution.py:328
  26.8 27.1 %copy-start.7 = (bf16[64,1024]{1,0:T(8,128)(2,1)}, bf16[64,1024]{1,0:T(8,128)(2,1)S(1)}, u32[]{:S(2)}) copy-start(bf16[64,1024]{1,0:T(8,128)(2,1)S(1)} %collective-permute-done.1.refs_1_) | copy-start | bytes 393220
  26.8 18.2 %collective-permute-start.6 = (bf16[64,1024]{1,0:T(8,128)(2,1)}, bf16[64,1024]{1,0:T(8,128)(2,1)S(1)}, u32[]{:S(2)}, u32[]{:S(2)}) collective-permute-start(bf16[64,1024]{1,0:T(8,128)(2,1)} %get-tuple-element.40), channel_id=1, source_target_pairs={{0,6},{1,7},{2,4},{3,5},{4,2},{5,3},{6,0},{7,1},{8,14},{9,15},{10,... | collective-permute-start | bytes 393224 | tf_op jit(solution)/shard_map/ppermute | solution.py:328
  30.1 23.9 %copy-start.8 = (bf16[64,1024]{1,0:T(8,128)(2,1)}, bf16[64,1024]{1,0:T(8,128)(2,1)S(1)}, u32[]{:S(2)}) copy-start(bf16[64,1024]{1,0:T(8,128)(2,1)S(1)} %collective-permute-done.2.refs_2_) | copy-start | bytes 393220
  30.1 14.9 %collective-permute-start.7 = (bf16[64,1024]{1,0:T(8,128)(2,1)}, bf16[64,1024]{1,0:T(8,128)(2,1)S(1)}, u32[]{:S(2)}, u32[]{:S(2)}) collective-permute-start(bf16[64,1024]{1,0:T(8,128)(2,1)} %get-tuple-element.41), channel_id=1, source_target_pairs={{0,7},{1,6},{2,5},{3,4},{4,3},{5,2},{6,1},{7,0},{8,15},{9,14},{10,... | collective-permute-start | bytes 393224 | tf_op jit(solution)/shard_map/ppermute | solution.py:328
  34.1 19.9 %copy-start.9 = (bf16[64,1024]{1,0:T(8,128)(2,1)}, bf16[64,1024]{1,0:T(8,128)(2,1)S(1)}, u32[]{:S(2)}) copy-start(bf16[64,1024]{1,0:T(8,128)(2,1)S(1)} %collective-permute-done.3.refs_3_) | copy-start | bytes 393220
  34.1 19.9 %copy-start.10 = (bf16[64,1024]{1,0:T(8,128)(2,1)}, bf16[64,1024]{1,0:T(8,128)(2,1)S(1)}, u32[]{:S(2)}) copy-start(bf16[64,1024]{1,0:T(8,128)(2,1)S(1)} %collective-permute-done.4.refs_4_) | copy-start | bytes 393220
  45.0 9.0 %copy-start.12 = (bf16[64,1024]{1,0:T(8,128)(2,1)}, bf16[64,1024]{1,0:T(8,128)(2,1)S(1)}, u32[]{:S(2)}) copy-start(bf16[64,1024]{1,0:T(8,128)(2,1)S(1)} %collective-permute-done.6.refs_6_) | copy-start | bytes 393220
  45.0 9.0 %copy-start.13 = (bf16[64,1024]{1,0:T(8,128)(2,1)}, bf16[64,1024]{1,0:T(8,128)(2,1)S(1)}, u32[]{:S(2)}) copy-start(bf16[64,1024]{1,0:T(8,128)(2,1)S(1)} %collective-permute-done.7.refs_7_) | copy-start | bytes 393220
  45.0 27.8 %copy-start.1 = (bf16[8,32,1024]{2,1,0:T(8,128)(2,1)}, bf16[8,32,1024]{2,1,0:T(8,128)(2,1)S(1)}, u32[]{:S(2)}) copy-start(bf16[8,32,1024]{2,1,0:T(8,128)(2,1)S(1)} %all-to-all-done.up_ref) | copy-start | bytes 1572868
  45.0 27.8 %all-to-all-start.2 = ((bf16[8,32,1024]{2,1,0:T(8,128)(2,1)}), bf16[8,32,1024]{2,1,0:T(8,128)(2,1)S(1)}, u32[]{:S(2)}, u32[]{:S(2)}) async-start(bf16[8,32,1024]{2,1,0:T(8,128)(2,1)} %get-tuple-element.52), calls=%async_computation.2 | async-start | bytes 1048576 | tf_op jit(solution)/shard_map/all_to_all | solution.py:336
  72.9 32.0 %all-to-all-start.1 = ((bf16[8,64,1024]{2,1,0:T(8,128)(2,1)}), bf16[8,64,1024]{2,1,0:T(8,128)(2,1)S(1)}, u32[]{:S(2)}, u32[]{:S(2)}) async-start(bf16[8,64,1024]{2,1,0:T(8,128)(2,1)} %get-tuple-element.50), calls=%async_computation.1 | async-start | bytes 2097152 | tf_op jit(solution)/shard_map/all_to_all | solution.py:336
  93.5 1.9 %collective-permute-start.8 = (bf16[256,256]{1,0:T(8,128)(2,1)}, bf16[256,256]{1,0:T(8,128)(2,1)S(1)}, u32[]{:S(2)}, u32[]{:S(2)}) collective-permute-start(bf16[256,256]{1,0:T(8,128)(2,1)} %get-tuple-element.62), channel_id=1, source_target_pairs={{0,8},{8,0},{16,24},{24,16},{1,9},{9,1},{17,25},{25,17},{2,10},{10... | collective-permute-start | bytes 393224 | tf_op jit(solution)/shard_map/ppermute | solution.py:328
  93.5 6.6 %collective-permute-start.9 = (bf16[256,256]{1,0:T(8,128)(2,1)}, bf16[256,256]{1,0:T(8,128)(2,1)S(1)}, u32[]{:S(2)}, u32[]{:S(2)}) collective-permute-start(bf16[256,256]{1,0:T(8,128)(2,1)} %get-tuple-element.63), channel_id=1, source_target_pairs={{0,16},{8,24},{16,0},{24,8},{1,17},{9,25},{17,1},{25,9},{2,18},{10... | collective-permute-start | bytes 393224 | tf_op jit(solution)/shard_map/ppermute | solution.py:328
  95.1 6.9 %collective-permute-start.10 = (bf16[256,256]{1,0:T(8,128)(2,1)}, bf16[256,256]{1,0:T(8,128)(2,1)S(1)}, u32[]{:S(2)}, u32[]{:S(2)}) collective-permute-start(bf16[256,256]{1,0:T(8,128)(2,1)} %get-tuple-element.64), channel_id=1, source_target_pairs={{0,24},{8,16},{16,8},{24,0},{1,25},{9,17},{17,9},{25,1},{2,26},{10... | collective-permute-start | bytes 393224 | tf_op jit(solution)/shard_map/ppermute | solution.py:328
  126.5 5.8 %collective-permute-start.13 = (bf16[256,256]{1,0:T(8,128)(2,1)S(1)}, bf16[256,256]{1,0:T(8,128)(2,1)S(1)}, u32[]{:S(2)}, u32[]{:S(2)}) collective-permute-start(bf16[256,256]{1,0:T(8,128)(2,1)S(1)} %bitcast.8), channel_id=1, source_target_pairs={{0,24},{8,16},{16,8},{24,0},{1,25},{9,17},{17,9},{25,1},{2,26},{10... | collective-permute-start | bytes 393224 | tf_op jit(solution)/shard_map/ppermute | solution.py:328
  126.5 8.1 %collective-permute-start.12 = (bf16[256,256]{1,0:T(8,128)(2,1)S(1)}, bf16[256,256]{1,0:T(8,128)(2,1)S(1)}, u32[]{:S(2)}, u32[]{:S(2)}) collective-permute-start(bf16[256,256]{1,0:T(8,128)(2,1)S(1)} %bitcast.9), channel_id=1, source_target_pairs={{0,16},{8,24},{16,0},{24,8},{1,17},{9,25},{17,1},{25,9},{2,18},{10... | collective-permute-start | bytes 393224 | tf_op jit(solution)/shard_map/ppermute | solution.py:328
  127.7 6.9 %collective-permute-start.11 = (bf16[256,256]{1,0:T(8,128)(2,1)S(1)}, bf16[256,256]{1,0:T(8,128)(2,1)S(1)}, u32[]{:S(2)}, u32[]{:S(2)}) collective-permute-start(bf16[256,256]{1,0:T(8,128)(2,1)S(1)} %bitcast.10), channel_id=1, source_target_pairs={{0,8},{8,0},{16,24},{24,16},{1,9},{9,1},{17,25},{25,17},{2,10},{10... | collective-permute-start | bytes 393224 | tf_op jit(solution)/shard_map/ppermute | solution.py:328
  (7 other events, 27.3 us)

commit v6 on v4

--- a/solution.py
+++ b/solution.py
@@ -348,12 +348,13 @@
     if pieces > 1:
         cotangent = cotangent.reshape(batch, contacts_here, pieces, span)
         cotangent = cotangent.transpose(0, 2, 1, 3).reshape(count, contacts_here, span)
-    upstream = exchange(cotangent, "contact")
     rim = lax.ppermute(
         signal[:, :, slab - rim_width :], "tm", [(i, i + 1) for i in range(tm_count - 1)]
     )
     filtered = filter_all(place, signal, rim, fir_taps, count)
     features = swap_all(filtered, "contact")
+    features, cotangent = lax.optimization_barrier((features, cotangent))
+    upstream = exchange(cotangent, "contact")
     attended, *kept = forward(
         place, features, neighbours.T, live_mask[None], lap_coef[None],
         [w_query, w_key, w_value, w_out],
@@ -362,7 +363,7 @@
     grads = backward(place, upstream, kept, w_out, tm_count)
     grads = swap_all(grads, "tm")
     part = sum(piece.astype(F32) for piece in grads).astype(BF16)
-    part, returned = lax.optimization_barrier((part, returned))
+    part, _ = lax.optimization_barrier((part, returned))
     part = exchange(part, "contact").reshape(count, -1, width)
     grad_scale = (batch * (slab // width) * tm_count * neighbours.shape[0]) ** (-0.5)
     mine = (jnp.sum(part.astype(F32), axis=0) * grad_scale).astype(BF16)

time: 138 us -> 136 us (0.986)
  starting transfers between devices: 37.4 us -> 31.2 us
  waiting for transfers between devices: 31.9 us -> 36.5 us
    all_to_all x2, starting transfers between devices: 18.2 us -> 13 us  [exchange(): return lax.all_to_all(value, axis, split_axis=0, concat_axis=0, tiled=True)]
    ppermute x13, waiting for transfers between devices: 23.9 us -> 27.7 us  [swap(): lax.ppermute(value, axis, [(i, i ^ k) for i in range(lax.axis_size(axis))])]
  transfers between devices with their start and end apart: 16 -> 16, of which waited for: 8 -> 9; matrix products, arithmetic and copies ran while one was open for 1% -> 1% of each run, Pallas kernels for 25% -> 25%
where the time goes in v6:
time: 136 us
  Pallas kernels  40.9 us (30%)
  waiting for transfers between devices  36.5 us (27%)
  starting transfers between devices  31.2 us (23%)
  blocking collectives  21.5 us (16%)
  local copies, waits for them, and re-layouts  3.27 us (2%)
  other arithmetic  1.67 us (1%)
    ppermute x13, waiting for transfers between devices, swap(): lax.ppermute(value, axis, [(i, i ^ k) for i in range(lax.axis_size(axis))])  27.7 us
    all_to_all x2, blocking collectives, exchange(): return lax.all_to_all(value, axis, split_axis=0, concat_axis=0, tiled=True)  21.5 us
    pallas_call x1, Pallas kernels, forward(): pl.pallas_call(functools.partial(forward_kernel, blocks), grid=(groups,),...  18.8 us
    ppermute x13, starting transfers between devices, swap(): lax.ppermute(value, axis, [(i, i ^ k) for i in range(lax.axis_size(axis))])  15.9 us
    pallas_call x1, Pallas kernels, backward(): pl.pallas_call(functools.partial(backward_kernel, blocks), grid=(groups,)...  15.1 us
    all_to_all x2, starting transfers between devices, exchange(): return lax.all_to_all(value, axis, split_axis=0, concat_axis=0, tiled=True)  13 us
    all_to_all x2, waiting for transfers between devices, exchange(): return lax.all_to_all(value, axis, split_axis=0, concat_axis=0, tiled=True)  8.51 us
    pallas_call x1, Pallas kernels, filter_all(): pl.pallas_call(filter_kernel, grid=(contacts // rows,), in_specs=[index_s...  4.86 us
  transfers between devices with their start and end apart: 16, of which 9 were waited for; matrix products, arithmetic and copies ran while one was open for 1% of the time, Pallas kernels for 25%

profile of v6, /device:TPU:0, one launch (start us, length us, event | category | flops | bytes accessed | tf_op | source)
XLA Modules:
  0.0 136.0 jit_solution(16052782993496235907)
XLA Ops:
  1.5 2.4 %collective-permute-start = (bf16[8,64,128]{2,1,0:T(8,128)(2,1)S(1)}, bf16[8,64,128]{2,1,0:T(8,128)(2,1)S(1)}, u32[]{:S(2)}, u32[]{:S(2)}) collective-permute-start(bf16[8,64,128]{2,1,0:T(8,128)(2,1)S(1)} %slice.3), channel_id=1, source_target_pairs={{0,8},{8,16},{16,24},{1,9},{9,17},{17,25},{2,10},{10,18},{18,26},{... | collective-permute-start | bytes 393224 | tf_op jit(solution)/shard_map/ppermute | solution.py:351
  5.5 4.9 %filter.1 = (bf16[64,1024]{1,0:T(8,128)(2,1)}, bf16[64,1024]{1,0:T(8,128)(2,1)}, bf16[64,1024]{1,0:T(8,128)(2,1)}, bf16[64,1024]{1,0:T(8,128)(2,1)}, bf16[64,102...) custom-call(s32[2]{0:T(128)} %pad_add_fusion.place_ref, ...), custom_call_target="tpu_custom_call" | custom-call | flops 268435456 | bytes 2097152 | tf_op jit(solution)/shard_map/filter/pallas_call | solution.py:72
  10.4 2.4 %collective-permute-start.1 = (bf16[64,1024]{1,0:T(8,128)(2,1)}, bf16[64,1024]{1,0:T(8,128)(2,1)S(1)}, u32[]{:S(2)}, u32[]{:S(2)}) collective-permute-start(bf16[64,1024]{1,0:T(8,128)(2,1)} %get-tuple-element.34), channel_id=1, source_target_pairs={{0,1},{1,0},{2,3},{3,2},{4,5},{5,4},{6,7},{7,6},{8,9},{9,8},{10,11... | collective-permute-start | bytes 393224 | tf_op jit(solution)/shard_map/ppermute | solution.py:325
  12.8 1.6 %collective-permute-start.2 = (bf16[64,1024]{1,0:T(8,128)(2,1)}, bf16[64,1024]{1,0:T(8,128)(2,1)S(1)}, u32[]{:S(2)}, u32[]{:S(2)}) collective-permute-start(bf16[64,1024]{1,0:T(8,128)(2,1)} %get-tuple-element.35), channel_id=1, source_target_pairs={{0,2},{1,3},{2,0},{3,1},{4,6},{5,7},{6,4},{7,5},{8,10},{9,11},{10,... | collective-permute-start | bytes 393224 | tf_op jit(solution)/shard_map/ppermute | solution.py:325
  14.4 3.0 %collective-permute-start.4 = (bf16[64,1024]{1,0:T(8,128)(2,1)}, bf16[64,1024]{1,0:T(8,128)(2,1)S(1)}, u32[]{:S(2)}, u32[]{:S(2)}) collective-permute-start(bf16[64,1024]{1,0:T(8,128)(2,1)} %get-tuple-element.37), channel_id=1, source_target_pairs={{0,4},{1,5},{2,6},{3,7},{4,0},{5,1},{6,2},{7,3},{8,12},{9,13},{10,... | collective-permute-start | bytes 393224 | tf_op jit(solution)/shard_map/ppermute | solution.py:325
  17.4 1.3 collective-permute-start.5
  18.7 3.6 %collective-permute-start.6 = (bf16[64,1024]{1,0:T(8,128)(2,1)}, bf16[64,1024]{1,0:T(8,128)(2,1)S(1)}, u32[]{:S(2)}, u32[]{:S(2)}) collective-permute-start(bf16[64,1024]{1,0:T(8,128)(2,1)} %get-tuple-element.39), channel_id=1, source_target_pairs={{0,6},{1,7},{2,4},{3,5},{4,2},{5,3},{6,0},{7,1},{8,14},{9,15},{10,... | collective-permute-start | bytes 393224 | tf_op jit(solution)/shard_map/ppermute | solution.py:325
  22.3 2.9 %collective-permute-done.3.refs_3_ = bf16[64,1024]{1,0:T(8,128)(2,1)S(1)} collective-permute-done((bf16[64,1024]{1,0:T(8,128)(2,1)}, bf16[64,1024]{1,0:T(8,128)(2,1)S(1)}, u32[]{:S(2)}, u32[]{:S(2)}) %collective-permute-start.3) | collective-permute-done | bytes 131104 | tf_op jit(solution)/shard_map/ppermute | solution.py:325
  25.3 11.8 %collective-permute-done.5.refs_5_ = bf16[64,1024]{1,0:T(8,128)(2,1)S(1)} collective-permute-done((bf16[64,1024]{1,0:T(8,128)(2,1)}, bf16[64,1024]{1,0:T(8,128)(2,1)S(1)}, u32[]{:S(2)}, u32[]{:S(2)}) %collective-permute-start.5) | collective-permute-done | bytes 131104 | tf_op jit(solution)/shard_map/ppermute | solution.py:325
  37.1 9.3 %all-to-all-start.1 = ((bf16[8,64,1024]{2,1,0:T(8,128)(2,1)}), bf16[8,64,1024]{2,1,0:T(8,128)(2,1)S(1)}, u32[]{:S(2)}, u32[]{:S(2)}) async-start(bf16[8,64,1024]{2,1,0:T(8,128)(2,1)} %param.19), calls=%async_computation.1 | async-start | bytes 2097152 | tf_op jit(solution)/shard_map/all_to_all | solution.py:333
  46.5 18.8 %forward.1 = (bf16[8,64,1024]{2,1,0:T(8,128)(2,1)}, bf16[512,8192]{1,0:T(8,128)(2,1)}, bf16[512,1024]{1,0:T(8,128)(2,1)}, bf16[512,1024]{1,0:T(8,128)(2,1)}, bf1...) custom-call(s32[2]{0:T(128)} %pad_add_fusion.place_ref, ...), custom_call_target="tpu_custom_call" | custom-call | flops 20000000000 | bytes 10485760 | tf_op jit(solution)/shard_map/forward/pallas_call | solution.py:248
  65.3 7.3 %all-to-all-done.1.up_ref = bf16[8,64,1024]{2,1,0:T(8,128)(2,1)S(1)} async-done(((bf16[8,64,1024]{2,1,0:T(8,128)(2,1)}), bf16[8,64,1024]{2,1,0:T(8,128)(2,1)S(1)}, u32[]{:S(2)}, u32[]{:S(2)}) %all-to-all-start.1) | async-done | bytes 1048608 | tf_op jit(solution)/shard_map/all_to_all | solution.py:333
  72.6 3.6 %all-to-all-start = ((bf16[8,64,1024]{2,1,0:T(8,128)(2,1)}), bf16[8,64,1024]{2,1,0:T(8,128)(2,1)S(1)}, u32[]{:S(2)}, u32[]{:S(2)}) async-start(bf16[8,64,1024]{2,1,0:T(8,128)(2,1)} %get-tuple-element.49), calls=%async_computation | async-start | bytes 2097152 | tf_op jit(solution)/shard_map/all_to_all | solution.py:333
  76.2 15.1 %backward.1 = (bf16[256,256]{1,0:T(8,128)(2,1)}, bf16[256,256]{1,0:T(8,128)(2,1)}, bf16[256,256]{1,0:T(8,128)(2,1)}, bf16[256,256]{1,0:T(8,128)(2,1)}) custom-call(s32[2]{0:T(128)} %pad_add_fusion.place_ref, bf16[256,256]{1,0:T(8,128)(2,1)} %wo_ref.3, bf16[8,64,1024]{2,1,0:T(8,128)(2,1)} %copy-done, bf16[512,8192]{1,0:T(8,128)(2,1)} %get-tuple-element.51.prob_ref, ...), custom_call_target="tpu_custom_call" | custom-call | flops 20000000000 | bytes 10485760 | tf_op jit(solution)/shard_map/backward/pallas_call | solution.py:280
  91.5 2.1 %collective-permute-start.9 = (bf16[256,256]{1,0:T(8,128)(2,1)}, bf16[256,256]{1,0:T(8,128)(2,1)S(1)}, u32[]{:S(2)}, u32[]{:S(2)}) collective-permute-start(bf16[256,256]{1,0:T(8,128)(2,1)} %get-tuple-element.61), channel_id=1, source_target_pairs={{0,16},{8,24},{16,0},{24,8},{1,17},{9,25},{17,1},{25,9},{2,18},{10... | collective-permute-start | bytes 393224 | tf_op jit(solution)/shard_map/ppermute | solution.py:325
  93.5 3.9 %collective-permute-done.10 = bf16[256,256]{1,0:T(8,128)(2,1)S(1)} collective-permute-done((bf16[256,256]{1,0:T(8,128)(2,1)}, bf16[256,256]{1,0:T(8,128)(2,1)S(1)}, u32[]{:S(2)}, u32[]{:S(2)}) %collective-permute-start.10) | collective-permute-done | bytes 131104 | tf_op jit(solution)/shard_map/ppermute | solution.py:325
  97.4 2.6 %collective-permute-done.9 = bf16[256,256]{1,0:T(8,128)(2,1)S(1)} collective-permute-done((bf16[256,256]{1,0:T(8,128)(2,1)}, bf16[256,256]{1,0:T(8,128)(2,1)S(1)}, u32[]{:S(2)}, u32[]{:S(2)}) %collective-permute-start.9) | collective-permute-done | bytes 131104 | tf_op jit(solution)/shard_map/ppermute | solution.py:325
  101.0 1.2 all-to-all-done
  102.2 11.7 %all_to_all.30 = bf16[8,32,256]{2,1,0:T(8,128)(2,1)S(1)} all-to-all(bf16[8,32,256]{2,1,0:T(8,128)(2,1)S(1)} %bitcast.12), channel_id=1, replica_groups=mesh['tm'=4,'contact'=8] {'contact'}, dimensions={0} | all-to-all | bytes 262144 | tf_op jit(solution)/shard_map/all_to_all | solution.py:333
  114.0 9.9 %all_to_all.31 = bf16[8,32,256]{2,1,0:T(8,128)(2,1)S(1)} all-to-all(bf16[8,32,256]{2,1,0:T(8,128)(2,1)S(1)} %bitcast.13), channel_id=1, replica_groups=mesh['tm'=4,'contact'=8] {'contact'}, dimensions={0} | all-to-all | bytes 262144 | tf_op jit(solution)/shard_map/all_to_all | solution.py:333
  123.9 1.9 %collective-permute-start.13 = (bf16[256,256]{1,0:T(8,128)(2,1)S(1)}, bf16[256,256]{1,0:T(8,128)(2,1)S(1)}, u32[]{:S(2)}, u32[]{:S(2)}) collective-permute-start(bf16[256,256]{1,0:T(8,128)(2,1)S(1)} %bitcast.10), channel_id=1, source_target_pairs={{0,24},{8,16},{16,8},{24,0},{1,25},{9,17},{17,9},{25,1},{2,26},{10... | collective-permute-start | bytes 393224 | tf_op jit(solution)/shard_map/ppermute | solution.py:325
  125.7 4.4 %collective-permute-done.12.refs_2_ = bf16[256,256]{1,0:T(8,128)(2,1)S(1)} collective-permute-done((bf16[256,256]{1,0:T(8,128)(2,1)S(1)}, bf16[256,256]{1,0:T(8,128)(2,1)S(1)}, u32[]{:S(2)}, u32[]{:S(2)}) %collective-permute-start.12) | collective-permute-done | bytes 131104 | tf_op jit(solution)/shard_map/ppermute | solution.py:325
  130.1 2.0 %collective-permute-done.13.refs_3_ = bf16[256,256]{1,0:T(8,128)(2,1)S(1)} collective-permute-done((bf16[256,256]{1,0:T(8,128)(2,1)S(1)}, bf16[256,256]{1,0:T(8,128)(2,1)S(1)}, u32[]{:S(2)}, u32[]{:S(2)}) %collective-permute-start.13) | collective-permute-done | bytes 131104 | tf_op jit(solution)/shard_map/ppermute | solution.py:325
  132.9 2.1 %place_all.1 = f32[4,256,256]{2,1,0:T(8,128)} custom-call(s32[2]{0:T(128)} %pad_add_fusion.place_ref, bf16[256,256]{1,0:T(8,128)(2,1)} %bitcast.11, bf16[256,256]{1,0:T(8,128)(2,1)} %copy-done.3, bf16[256,256]{1,0:T(8,128)(2,1)} %copy-done.4, bf16[256,256]{1,0:T(8,128)(2,1)} %copy-done.5), custom_call_target="tpu_custom_call" | custom-call | tf_op jit(solution)/shard_map/place_all/pallas_call | solution.py:314
  (53 shorter events, 5.4 us)
Async XLA Ops:
  1.5 3.3 %collective-permute-start = (bf16[8,64,128]{2,1,0:T(8,128)(2,1)S(1)}, bf16[8,64,128]{2,1,0:T(8,128)(2,1)S(1)}, u32[]{:S(2)}, u32[]{:S(2)}) collective-permute-start(bf16[8,64,128]{2,1,0:T(8,128)(2,1)S(1)} %slice.3), channel_id=1, source_target_pairs={{0,8},{8,16},{16,24},{1,9},{9,17},{17,25},{2,10},{10,18},{18,26},{... | collective-permute-start | bytes 393224 | tf_op jit(solution)/shard_map/ppermute | solution.py:351
  10.4 8.3 %collective-permute-start.1 = (bf16[64,1024]{1,0:T(8,128)(2,1)}, bf16[64,1024]{1,0:T(8,128)(2,1)S(1)}, u32[]{:S(2)}, u32[]{:S(2)}) collective-permute-start(bf16[64,1024]{1,0:T(8,128)(2,1)} %get-tuple-element.34), channel_id=1, source_target_pairs={{0,1},{1,0},{2,3},{3,2},{4,5},{5,4},{6,7},{7,6},{8,9},{9,8},{10,11... | collective-permute-start | bytes 393224 | tf_op jit(solution)/shard_map/ppermute | solution.py:325
  12.8 9.5 %collective-permute-start.2 = (bf16[64,1024]{1,0:T(8,128)(2,1)}, bf16[64,1024]{1,0:T(8,128)(2,1)S(1)}, u32[]{:S(2)}, u32[]{:S(2)}) collective-permute-start(bf16[64,1024]{1,0:T(8,128)(2,1)} %get-tuple-element.35), channel_id=1, source_target_pairs={{0,2},{1,3},{2,0},{3,1},{4,6},{5,7},{6,4},{7,5},{8,10},{9,11},{10,... | collective-permute-start | bytes 393224 | tf_op jit(solution)/shard_map/ppermute | solution.py:325
  14.4 10.9 %collective-permute-start.3 = (bf16[64,1024]{1,0:T(8,128)(2,1)}, bf16[64,1024]{1,0:T(8,128)(2,1)S(1)}, u32[]{:S(2)}, u32[]{:S(2)}) collective-permute-start(bf16[64,1024]{1,0:T(8,128)(2,1)} %get-tuple-element.36), channel_id=1, source_target_pairs={{0,3},{1,2},{2,1},{3,0},{4,7},{5,6},{6,5},{7,4},{8,11},{9,10},{10,... | collective-permute-start | bytes 393224 | tf_op jit(solution)/shard_map/ppermute | solution.py:325
  14.4 10.9 %collective-permute-start.4 = (bf16[64,1024]{1,0:T(8,128)(2,1)}, bf16[64,1024]{1,0:T(8,128)(2,1)S(1)}, u32[]{:S(2)}, u32[]{:S(2)}) collective-permute-start(bf16[64,1024]{1,0:T(8,128)(2,1)} %get-tuple-element.37), channel_id=1, source_target_pairs={{0,4},{1,5},{2,6},{3,7},{4,0},{5,1},{6,2},{7,3},{8,12},{9,13},{10,... | collective-permute-start | bytes 393224 | tf_op jit(solution)/shard_map/ppermute | solution.py:325
  17.4 19.7 %collective-permute-start.5 = (bf16[64,1024]{1,0:T(8,128)(2,1)}, bf16[64,1024]{1,0:T(8,128)(2,1)S(1)}, u32[]{:S(2)}, u32[]{:S(2)}) collective-permute-start(bf16[64,1024]{1,0:T(8,128)(2,1)} %get-tuple-element.38), channel_id=1, source_target_pairs={{0,5},{1,4},{2,7},{3,6},{4,1},{5,0},{6,3},{7,2},{8,13},{9,12},{10,... | collective-permute-start | bytes 393224 | tf_op jit(solution)/shard_map/ppermute | solution.py:325
  18.7 27.7 %copy-start.6 = (bf16[64,1024]{1,0:T(8,128)(2,1)}, bf16[64,1024]{1,0:T(8,128)(2,1)S(1)}, u32[]{:S(2)}) copy-start(bf16[64,1024]{1,0:T(8,128)(2,1)S(1)} %collective-permute-done.1.refs_1_) | copy-start | bytes 393220
  18.7 18.4 %collective-permute-start.6 = (bf16[64,1024]{1,0:T(8,128)(2,1)}, bf16[64,1024]{1,0:T(8,128)(2,1)S(1)}, u32[]{:S(2)}, u32[]{:S(2)}) collective-permute-start(bf16[64,1024]{1,0:T(8,128)(2,1)} %get-tuple-element.39), channel_id=1, source_target_pairs={{0,6},{1,7},{2,4},{3,5},{4,2},{5,3},{6,0},{7,1},{8,14},{9,15},{10,... | collective-permute-start | bytes 393224 | tf_op jit(solution)/shard_map/ppermute | solution.py:325
  22.3 24.1 %copy-start.7 = (bf16[64,1024]{1,0:T(8,128)(2,1)}, bf16[64,1024]{1,0:T(8,128)(2,1)S(1)}, u32[]{:S(2)}) copy-start(bf16[64,1024]{1,0:T(8,128)(2,1)S(1)} %collective-permute-done.2.refs_2_) | copy-start | bytes 393220
  22.3 14.8 %collective-permute-start.7 = (bf16[64,1024]{1,0:T(8,128)(2,1)}, bf16[64,1024]{1,0:T(8,128)(2,1)S(1)}, u32[]{:S(2)}, u32[]{:S(2)}) collective-permute-start(bf16[64,1024]{1,0:T(8,128)(2,1)} %get-tuple-element.40), channel_id=1, source_target_pairs={{0,7},{1,6},{2,5},{3,4},{4,3},{5,2},{6,1},{7,0},{8,15},{9,14},{10,... | collective-permute-start | bytes 393224 | tf_op jit(solution)/shard_map/ppermute | solution.py:325
  25.2 21.2 %copy-start.8 = (bf16[64,1024]{1,0:T(8,128)(2,1)}, bf16[64,1024]{1,0:T(8,128)(2,1)S(1)}, u32[]{:S(2)}) copy-start(bf16[64,1024]{1,0:T(8,128)(2,1)S(1)} %collective-permute-done.3.refs_3_) | copy-start | bytes 393220
  25.3 21.2 %copy-start.9 = (bf16[64,1024]{1,0:T(8,128)(2,1)}, bf16[64,1024]{1,0:T(8,128)(2,1)S(1)}, u32[]{:S(2)}) copy-start(bf16[64,1024]{1,0:T(8,128)(2,1)S(1)} %collective-permute-done.4.refs_4_) | copy-start | bytes 393220
  37.1 9.4 %copy-start.10 = (bf16[64,1024]{1,0:T(8,128)(2,1)}, bf16[64,1024]{1,0:T(8,128)(2,1)S(1)}, u32[]{:S(2)}) copy-start(bf16[64,1024]{1,0:T(8,128)(2,1)S(1)} %collective-permute-done.5.refs_5_) | copy-start | bytes 393220
  37.1 9.4 %copy-start.11 = (bf16[64,1024]{1,0:T(8,128)(2,1)}, bf16[64,1024]{1,0:T(8,128)(2,1)S(1)}, u32[]{:S(2)}) copy-start(bf16[64,1024]{1,0:T(8,128)(2,1)S(1)} %collective-permute-done.6.refs_6_) | copy-start | bytes 393220
  37.1 9.4 %copy-start.12 = (bf16[64,1024]{1,0:T(8,128)(2,1)}, bf16[64,1024]{1,0:T(8,128)(2,1)S(1)}, u32[]{:S(2)}) copy-start(bf16[64,1024]{1,0:T(8,128)(2,1)S(1)} %collective-permute-done.7.refs_7_) | copy-start | bytes 393220
  37.1 35.5 %all-to-all-start.1 = ((bf16[8,64,1024]{2,1,0:T(8,128)(2,1)}), bf16[8,64,1024]{2,1,0:T(8,128)(2,1)S(1)}, u32[]{:S(2)}, u32[]{:S(2)}) async-start(bf16[8,64,1024]{2,1,0:T(8,128)(2,1)} %param.19), calls=%async_computation.1 | async-start | bytes 2097152 | tf_op jit(solution)/shard_map/all_to_all | solution.py:333
  72.6 29.6 %all-to-all-start = ((bf16[8,64,1024]{2,1,0:T(8,128)(2,1)}), bf16[8,64,1024]{2,1,0:T(8,128)(2,1)S(1)}, u32[]{:S(2)}, u32[]{:S(2)}) async-start(bf16[8,64,1024]{2,1,0:T(8,128)(2,1)} %get-tuple-element.49), calls=%async_computation | async-start | bytes 2097152 | tf_op jit(solution)/shard_map/all_to_all | solution.py:333
  91.3 6.0 %collective-permute-start.10 = (bf16[256,256]{1,0:T(8,128)(2,1)}, bf16[256,256]{1,0:T(8,128)(2,1)S(1)}, u32[]{:S(2)}, u32[]{:S(2)}) collective-permute-start(bf16[256,256]{1,0:T(8,128)(2,1)} %get-tuple-element.62), channel_id=1, source_target_pairs={{0,24},{8,16},{16,8},{24,0},{1,25},{9,17},{17,9},{25,1},{2,26},{10... | collective-permute-start | bytes 393224 | tf_op jit(solution)/shard_map/ppermute | solution.py:325
  91.4 6.0 %collective-permute-start.8 = (bf16[256,256]{1,0:T(8,128)(2,1)}, bf16[256,256]{1,0:T(8,128)(2,1)S(1)}, u32[]{:S(2)}, u32[]{:S(2)}) collective-permute-start(bf16[256,256]{1,0:T(8,128)(2,1)} %get-tuple-element.60), channel_id=1, source_target_pairs={{0,8},{8,0},{16,24},{24,16},{1,9},{9,1},{17,25},{25,17},{2,10},{10... | collective-permute-start | bytes 393224 | tf_op jit(solution)/shard_map/ppermute | solution.py:325
  91.5 8.6 %collective-permute-start.9 = (bf16[256,256]{1,0:T(8,128)(2,1)}, bf16[256,256]{1,0:T(8,128)(2,1)S(1)}, u32[]{:S(2)}, u32[]{:S(2)}) collective-permute-start(bf16[256,256]{1,0:T(8,128)(2,1)} %get-tuple-element.61), channel_id=1, source_target_pairs={{0,16},{8,24},{16,0},{24,8},{1,17},{9,25},{17,1},{25,9},{2,18},{10... | collective-permute-start | bytes 393224 | tf_op jit(solution)/shard_map/ppermute | solution.py:325
  123.8 8.3 %copy-start.1 = (bf16[8,32,256]{2,1,0:T(8,128)(2,1)}, bf16[8,32,256]{2,1,0:T(8,128)(2,1)S(1)}, u32[]{:S(2)}) copy-start(bf16[8,32,256]{2,1,0:T(8,128)(2,1)S(1)} %all_to_all.31) | copy-start | bytes 393220
  123.8 1.9 %collective-permute-start.11 = (bf16[256,256]{1,0:T(8,128)(2,1)S(1)}, bf16[256,256]{1,0:T(8,128)(2,1)S(1)}, u32[]{:S(2)}, u32[]{:S(2)}) collective-permute-start(bf16[256,256]{1,0:T(8,128)(2,1)S(1)} %bitcast.8), channel_id=1, source_target_pairs={{0,8},{8,0},{16,24},{24,16},{1,9},{9,1},{17,25},{25,17},{2,10},{10... | collective-permute-start | bytes 393224 | tf_op jit(solution)/shard_map/ppermute | solution.py:325
  123.8 6.3 %collective-permute-start.12 = (bf16[256,256]{1,0:T(8,128)(2,1)S(1)}, bf16[256,256]{1,0:T(8,128)(2,1)S(1)}, u32[]{:S(2)}, u32[]{:S(2)}) collective-permute-start(bf16[256,256]{1,0:T(8,128)(2,1)S(1)} %bitcast.9), channel_id=1, source_target_pairs={{0,16},{8,24},{16,0},{24,8},{1,17},{9,25},{17,1},{25,9},{2,18},{10... | collective-permute-start | bytes 393224 | tf_op jit(solution)/shard_map/ppermute | solution.py:325
  123.9 8.3 %collective-permute-start.13 = (bf16[256,256]{1,0:T(8,128)(2,1)S(1)}, bf16[256,256]{1,0:T(8,128)(2,1)S(1)}, u32[]{:S(2)}, u32[]{:S(2)}) collective-permute-start(bf16[256,256]{1,0:T(8,128)(2,1)S(1)} %bitcast.10), channel_id=1, source_target_pairs={{0,24},{8,16},{16,8},{24,0},{1,25},{9,17},{17,9},{25,1},{2,26},{10... | collective-permute-start | bytes 393224 | tf_op jit(solution)/shard_map/ppermute | solution.py:325
  (5 other events, 13.5 us)

commit v7 on v6

--- a/solution.py
+++ b/solution.py
@@ -326,7 +326,8 @@
 
 
 def swap_all(parts, axis):
-    return [parts[0]] + [swap(parts[k], axis, k) for k in range(1, len(parts))]
+    moved = [swap(parts[k], axis, k) for k in range(len(parts) - 1, 0, -1)]
+    return [parts[0]] + moved[::-1]
 
 
 def exchange(value, axis):
@@ -353,7 +354,8 @@
     )
     filtered = filter_all(place, signal, rim, fir_taps, count)
     features = swap_all(filtered, "contact")
-    features, cotangent = lax.optimization_barrier((features, cotangent))
+    arrived = count - max(2, count // 4)
+    features[arrived:], cotangent = lax.optimization_barrier((features[arrived:], cotangent))
     upstream = exchange(cotangent, "contact")
     attended, *kept = forward(
         place, features, neighbours.T, live_mask[None], lap_coef[None],

time: 136 us -> 132 us (0.971)
  waiting for transfers between devices: 36.5 us -> 21.5 us
  starting transfers between devices: 31.2 us -> 40.3 us
  blocking collectives: 21.5 us -> 22.9 us
    ppermute x13, starting transfers between devices: 15.9 us -> 28.1 us  [swap(): lax.ppermute(value, axis, [(i, i ^ k) for i in range(lax.axis_size(axis))])]
    ppermute x13, waiting for transfers between devices: 27.7 us -> 19.1 us  [swap(): lax.ppermute(value, axis, [(i, i ^ k) for i in range(lax.axis_size(axis))])]
    all_to_all x2, waiting for transfers between devices: 8.51 us -> 2.06 us  [exchange(): return lax.all_to_all(value, axis, split_axis=0, concat_axis=0, tiled=True)]
    all_to_all x2, starting transfers between devices: 13 us -> 9.76 us  [exchange(): return lax.all_to_all(value, axis, split_axis=0, concat_axis=0, tiled=True)]
  transfers between devices with their start and end apart: 16 -> 16, of which waited for: 9 -> 8; matrix products, arithmetic and copies ran while one was open for 1% -> 1% of each run, Pallas kernels for 25% -> 26%
where the time goes in v7:
time: 132 us
  Pallas kernels  40.9 us (31%)
  starting transfers between devices  40.3 us (31%)
  blocking collectives  22.9 us (17%)
  waiting for transfers between devices  21.5 us (16%)
  local copies, waits for them, and re-layouts  3.86 us (3%)
  other arithmetic  1.67 us (1%)
    ppermute x13, starting transfers between devices, swap(): lax.ppermute(value, axis, [(i, i ^ k) for i in range(lax.axis_size(axis))])  28.1 us
    all_to_all x2, blocking collectives, exchange(): return lax.all_to_all(value, axis, split_axis=0, concat_axis=0, tiled=True)  22.9 us
    ppermute x13, waiting for transfers between devices, swap(): lax.ppermute(value, axis, [(i, i ^ k) for i in range(lax.axis_size(axis))])  19.1 us
    pallas_call x1, Pallas kernels, forward(): pl.pallas_call(functools.partial(forward_kernel, blocks), grid=(groups,),...  18.8 us
    pallas_call x1, Pallas kernels, backward(): pl.pallas_call(functools.partial(backward_kernel, blocks), grid=(groups,)...  15.1 us
    all_to_all x2, starting transfers between devices, exchange(): return lax.all_to_all(value, axis, split_axis=0, concat_axis=0, tiled=True)  9.76 us
    pallas_call x1, Pallas kernels, filter_all(): pl.pallas_call(filter_kernel, grid=(contacts // rows,), in_specs=[index_s...  4.87 us
    unnamed x33, local copies, waits for them, and re-layouts  2.94 us
  transfers between devices with their start and end apart: 16, of which 8 were waited for; matrix products, arithmetic and copies ran while one was open for 1% of the time, Pallas kernels for 26%

profile of v7, /device:TPU:0, one launch (start us, length us, event | category | flops | bytes accessed | tf_op | source)
XLA Modules:
  0.0 131.9 jit_solution(3230860801254793746)
XLA Ops:
  1.5 2.4 %collective-permute-start = (bf16[8,64,128]{2,1,0:T(8,128)(2,1)S(1)}, bf16[8,64,128]{2,1,0:T(8,128)(2,1)S(1)}, u32[]{:S(2)}, u32[]{:S(2)}) collective-permute-start(bf16[8,64,128]{2,1,0:T(8,128)(2,1)S(1)} %slice.3), channel_id=1, source_target_pairs={{0,8},{8,16},{16,24},{1,9},{9,17},{17,25},{2,10},{10,18},{18,26},{... | collective-permute-start | bytes 393224 | tf_op jit(solution)/shard_map/ppermute | solution.py:352
  5.5 4.9 %filter.1 = (bf16[64,1024]{1,0:T(8,128)(2,1)}, bf16[64,1024]{1,0:T(8,128)(2,1)}, bf16[64,1024]{1,0:T(8,128)(2,1)}, bf16[64,1024]{1,0:T(8,128)(2,1)}, bf16[64,102...) custom-call(s32[2]{0:T(128)} %pad_add_fusion.place_ref, ...), custom_call_target="tpu_custom_call" | custom-call | flops 268435456 | bytes 2097152 | tf_op jit(solution)/shard_map/filter/pallas_call | solution.py:72
  10.4 4.5 %collective-permute-start.6 = (bf16[64,1024]{1,0:T(8,128)(2,1)}, bf16[64,1024]{1,0:T(8,128)(2,1)S(1)}, u32[]{:S(2)}, u32[]{:S(2)}) collective-permute-start(bf16[64,1024]{1,0:T(8,128)(2,1)} %get-tuple-element.33), channel_id=1, source_target_pairs={{0,6},{1,7},{2,4},{3,5},{4,2},{5,3},{6,0},{7,1},{8,14},{9,15},{10,... | collective-permute-start | bytes 393224 | tf_op jit(solution)/shard_map/ppermute | solution.py:325
  14.9 1.2 collective-permute-start.7
  16.4 3.1 %collective-permute-start.3 = (bf16[64,1024]{1,0:T(8,128)(2,1)}, bf16[64,1024]{1,0:T(8,128)(2,1)S(1)}, u32[]{:S(2)}, u32[]{:S(2)}) collective-permute-start(bf16[64,1024]{1,0:T(8,128)(2,1)} %get-tuple-element.30), channel_id=1, source_target_pairs={{0,3},{1,2},{2,1},{3,0},{4,7},{5,6},{6,5},{7,4},{8,11},{9,10},{10,... | collective-permute-start | bytes 393224 | tf_op jit(solution)/shard_map/ppermute | solution.py:325
  19.6 2.1 %collective-permute-start.4 = (bf16[64,1024]{1,0:T(8,128)(2,1)}, bf16[64,1024]{1,0:T(8,128)(2,1)S(1)}, u32[]{:S(2)}, u32[]{:S(2)}) collective-permute-start(bf16[64,1024]{1,0:T(8,128)(2,1)} %get-tuple-element.31), channel_id=1, source_target_pairs={{0,4},{1,5},{2,6},{3,7},{4,0},{5,1},{6,2},{7,3},{8,12},{9,13},{10,... | collective-permute-start | bytes 393224 | tf_op jit(solution)/shard_map/ppermute | solution.py:325
  21.7 1.2 collective-permute-done.7.refs_7_
  22.9 5.0 %collective-permute-start.5 = (bf16[64,1024]{1,0:T(8,128)(2,1)}, bf16[64,1024]{1,0:T(8,128)(2,1)S(1)}, u32[]{:S(2)}, u32[]{:S(2)}) collective-permute-start(bf16[64,1024]{1,0:T(8,128)(2,1)} %get-tuple-element.32), channel_id=1, source_target_pairs={{0,5},{1,4},{2,7},{3,6},{4,1},{5,0},{6,3},{7,2},{8,13},{9,12},{10,... | collective-permute-start | bytes 393224 | tf_op jit(solution)/shard_map/ppermute | solution.py:325
  28.0 4.9 %all-to-all-start.1 = ((bf16[8,64,1024]{2,1,0:T(8,128)(2,1)}), bf16[8,64,1024]{2,1,0:T(8,128)(2,1)S(1)}, u32[]{:S(2)}, u32[]{:S(2)}) async-start(bf16[8,64,1024]{2,1,0:T(8,128)(2,1)} %param.19), calls=%async_computation.1 | async-start | bytes 2097152 | tf_op jit(solution)/shard_map/all_to_all | solution.py:334
  33.0 5.6 %collective-permute-done.5.refs_5_ = bf16[64,1024]{1,0:T(8,128)(2,1)S(1)} collective-permute-done((bf16[64,1024]{1,0:T(8,128)(2,1)}, bf16[64,1024]{1,0:T(8,128)(2,1)S(1)}, u32[]{:S(2)}, u32[]{:S(2)}) %collective-permute-start.5) | collective-permute-done | bytes 131104 | tf_op jit(solution)/shard_map/ppermute | solution.py:325
  39.2 18.8 %forward.1 = (bf16[8,64,1024]{2,1,0:T(8,128)(2,1)}, bf16[512,8192]{1,0:T(8,128)(2,1)}, bf16[512,1024]{1,0:T(8,128)(2,1)}, bf16[512,1024]{1,0:T(8,128)(2,1)}, bf1...) custom-call(s32[2]{0:T(128)} %pad_add_fusion.place_ref, ...), custom_call_target="tpu_custom_call" | custom-call | flops 20000000000 | bytes 10485760 | tf_op jit(solution)/shard_map/forward/pallas_call | solution.py:248
  58.0 2.1 %all-to-all-done.1.up_ref = bf16[8,64,1024]{2,1,0:T(8,128)(2,1)S(1)} async-done(((bf16[8,64,1024]{2,1,0:T(8,128)(2,1)}), bf16[8,64,1024]{2,1,0:T(8,128)(2,1)S(1)}, u32[]{:S(2)}, u32[]{:S(2)}) %all-to-all-start.1) | async-done | bytes 1048608 | tf_op jit(solution)/shard_map/all_to_all | solution.py:334
  60.1 4.9 %all-to-all-start = ((bf16[8,64,1024]{2,1,0:T(8,128)(2,1)}), bf16[8,64,1024]{2,1,0:T(8,128)(2,1)S(1)}, u32[]{:S(2)}, u32[]{:S(2)}) async-start(bf16[8,64,1024]{2,1,0:T(8,128)(2,1)} %get-tuple-element.37), calls=%async_computation | async-start | bytes 2097152 | tf_op jit(solution)/shard_map/all_to_all | solution.py:334
  64.9 15.1 %backward.1 = (bf16[256,256]{1,0:T(8,128)(2,1)}, bf16[256,256]{1,0:T(8,128)(2,1)}, bf16[256,256]{1,0:T(8,128)(2,1)}, bf16[256,256]{1,0:T(8,128)(2,1)}) custom-call(s32[2]{0:T(128)} %pad_add_fusion.place_ref, bf16[256,256]{1,0:T(8,128)(2,1)} %wo_ref.3, bf16[8,64,1024]{2,1,0:T(8,128)(2,1)} %copy-done, bf16[512,8192]{1,0:T(8,128)(2,1)} %get-tuple-element.39.prob_ref, ...), custom_call_target="tpu_custom_call" | custom-call | flops 20000000000 | bytes 10485760 | tf_op jit(solution)/shard_map/backward/pallas_call | solution.py:280
  80.1 9.8 %collective-permute-start.8 = (bf16[256,256]{1,0:T(8,128)(2,1)}, bf16[256,256]{1,0:T(8,128)(2,1)S(1)}, u32[]{:S(2)}, u32[]{:S(2)}) collective-permute-start(bf16[256,256]{1,0:T(8,128)(2,1)} %get-tuple-element.48), channel_id=1, source_target_pairs={{0,8},{8,0},{16,24},{24,16},{1,9},{9,1},{17,25},{25,17},{2,10},{10... | collective-permute-start | bytes 393224 | tf_op jit(solution)/shard_map/ppermute | solution.py:325
  90.0 1.2 collective-permute-done.8
  91.1 4.7 %collective-permute-done.9 = bf16[256,256]{1,0:T(8,128)(2,1)S(1)} collective-permute-done((bf16[256,256]{1,0:T(8,128)(2,1)}, bf16[256,256]{1,0:T(8,128)(2,1)S(1)}, u32[]{:S(2)}, u32[]{:S(2)}) %collective-permute-start.9) | collective-permute-done | bytes 131104 | tf_op jit(solution)/shard_map/ppermute | solution.py:325
  95.8 1.0 add_convert_fusion
  96.8 13.1 %all_to_all.30 = bf16[8,32,256]{2,1,0:T(8,128)(2,1)S(1)} all-to-all(bf16[8,32,256]{2,1,0:T(8,128)(2,1)S(1)} %bitcast.12), channel_id=1, replica_groups=mesh['tm'=4,'contact'=8] {'contact'}, dimensions={0} | all-to-all | bytes 262144 | tf_op jit(solution)/shard_map/all_to_all | solution.py:334
  110.0 9.7 %all_to_all.31 = bf16[8,32,256]{2,1,0:T(8,128)(2,1)S(1)} all-to-all(bf16[8,32,256]{2,1,0:T(8,128)(2,1)S(1)} %bitcast.13), channel_id=1, replica_groups=mesh['tm'=4,'contact'=8] {'contact'}, dimensions={0} | all-to-all | bytes 262144 | tf_op jit(solution)/shard_map/all_to_all | solution.py:334
  119.8 1.2 collective-permute-start.12
  121.6 4.4 %collective-permute-done.12.refs_2_ = bf16[256,256]{1,0:T(8,128)(2,1)S(1)} collective-permute-done((bf16[256,256]{1,0:T(8,128)(2,1)S(1)}, bf16[256,256]{1,0:T(8,128)(2,1)S(1)}, u32[]{:S(2)}, u32[]{:S(2)}) %collective-permute-start.12) | collective-permute-done | bytes 131104 | tf_op jit(solution)/shard_map/ppermute | solution.py:325
  126.1 2.0 %collective-permute-done.13.refs_3_ = bf16[256,256]{1,0:T(8,128)(2,1)S(1)} collective-permute-done((bf16[256,256]{1,0:T(8,128)(2,1)S(1)}, bf16[256,256]{1,0:T(8,128)(2,1)S(1)}, u32[]{:S(2)}, u32[]{:S(2)}) %collective-permute-start.13) | collective-permute-done | bytes 131104 | tf_op jit(solution)/shard_map/ppermute | solution.py:325
  128.8 2.1 %place_all.1 = f32[4,256,256]{2,1,0:T(8,128)} custom-call(s32[2]{0:T(128)} %pad_add_fusion.place_ref, bf16[256,256]{1,0:T(8,128)(2,1)} %bitcast.11, bf16[256,256]{1,0:T(8,128)(2,1)} %copy-done.3, bf16[256,256]{1,0:T(8,128)(2,1)} %copy-done.4, bf16[256,256]{1,0:T(8,128)(2,1)} %copy-done.5), custom_call_target="tpu_custom_call" | custom-call | tf_op jit(solution)/shard_map/place_all/pallas_call | solution.py:314
  (53 shorter events, 6.0 us)
Async XLA Ops:
  1.5 3.3 %collective-permute-start = (bf16[8,64,128]{2,1,0:T(8,128)(2,1)S(1)}, bf16[8,64,128]{2,1,0:T(8,128)(2,1)S(1)}, u32[]{:S(2)}, u32[]{:S(2)}) collective-permute-start(bf16[8,64,128]{2,1,0:T(8,128)(2,1)S(1)} %slice.3), channel_id=1, source_target_pairs={{0,8},{8,16},{16,24},{1,9},{9,17},{17,25},{2,10},{10,18},{18,26},{... | collective-permute-start | bytes 393224 | tf_op jit(solution)/shard_map/ppermute | solution.py:352
  10.4 9.2 %collective-permute-start.6 = (bf16[64,1024]{1,0:T(8,128)(2,1)}, bf16[64,1024]{1,0:T(8,128)(2,1)S(1)}, u32[]{:S(2)}, u32[]{:S(2)}) collective-permute-start(bf16[64,1024]{1,0:T(8,128)(2,1)} %get-tuple-element.33), channel_id=1, source_target_pairs={{0,6},{1,7},{2,4},{3,5},{4,2},{5,3},{6,0},{7,1},{8,14},{9,15},{10,... | collective-permute-start | bytes 393224 | tf_op jit(solution)/shard_map/ppermute | solution.py:325
  14.9 8.0 %collective-permute-start.7 = (bf16[64,1024]{1,0:T(8,128)(2,1)}, bf16[64,1024]{1,0:T(8,128)(2,1)S(1)}, u32[]{:S(2)}, u32[]{:S(2)}) collective-permute-start(bf16[64,1024]{1,0:T(8,128)(2,1)} %get-tuple-element.34), channel_id=1, source_target_pairs={{0,7},{1,6},{2,5},{3,4},{4,3},{5,2},{6,1},{7,0},{8,15},{9,14},{10,... | collective-permute-start | bytes 393224 | tf_op jit(solution)/shard_map/ppermute | solution.py:325
  16.1 16.8 %collective-permute-start.1 = (bf16[64,1024]{1,0:T(8,128)(2,1)}, bf16[64,1024]{1,0:T(8,128)(2,1)S(1)}, u32[]{:S(2)}, u32[]{:S(2)}) collective-permute-start(bf16[64,1024]{1,0:T(8,128)(2,1)} %get-tuple-element.28), channel_id=1, source_target_pairs={{0,1},{1,0},{2,3},{3,2},{4,5},{5,4},{6,7},{7,6},{8,9},{9,8},{10,11... | collective-permute-start | bytes 393224 | tf_op jit(solution)/shard_map/ppermute | solution.py:325
  16.4 16.5 %collective-permute-start.2 = (bf16[64,1024]{1,0:T(8,128)(2,1)}, bf16[64,1024]{1,0:T(8,128)(2,1)S(1)}, u32[]{:S(2)}, u32[]{:S(2)}) collective-permute-start(bf16[64,1024]{1,0:T(8,128)(2,1)} %get-tuple-element.29), channel_id=1, source_target_pairs={{0,2},{1,3},{2,0},{3,1},{4,6},{5,7},{6,4},{7,5},{8,10},{9,11},{10,... | collective-permute-start | bytes 393224 | tf_op jit(solution)/shard_map/ppermute | solution.py:325
  16.4 16.5 %collective-permute-start.3 = (bf16[64,1024]{1,0:T(8,128)(2,1)}, bf16[64,1024]{1,0:T(8,128)(2,1)S(1)}, u32[]{:S(2)}, u32[]{:S(2)}) collective-permute-start(bf16[64,1024]{1,0:T(8,128)(2,1)} %get-tuple-element.30), channel_id=1, source_target_pairs={{0,3},{1,2},{2,1},{3,0},{4,7},{5,6},{6,5},{7,4},{8,11},{9,10},{10,... | collective-permute-start | bytes 393224 | tf_op jit(solution)/shard_map/ppermute | solution.py:325
  19.6 19.0 %copy-start.6 = (bf16[64,1024]{1,0:T(8,128)(2,1)}, bf16[64,1024]{1,0:T(8,128)(2,1)S(1)}, u32[]{:S(2)}) copy-start(bf16[64,1024]{1,0:T(8,128)(2,1)S(1)} %collective-permute-done.6.refs_6_) | copy-start | bytes 393220
  19.6 13.4 %collective-permute-start.4 = (bf16[64,1024]{1,0:T(8,128)(2,1)}, bf16[64,1024]{1,0:T(8,128)(2,1)S(1)}, u32[]{:S(2)}, u32[]{:S(2)}) collective-permute-start(bf16[64,1024]{1,0:T(8,128)(2,1)} %get-tuple-element.31), channel_id=1, source_target_pairs={{0,4},{1,5},{2,6},{3,7},{4,0},{5,1},{6,2},{7,3},{8,12},{9,13},{10,... | collective-permute-start | bytes 393224 | tf_op jit(solution)/shard_map/ppermute | solution.py:325
  22.9 15.7 %copy-start.7 = (bf16[64,1024]{1,0:T(8,128)(2,1)}, bf16[64,1024]{1,0:T(8,128)(2,1)S(1)}, u32[]{:S(2)}) copy-start(bf16[64,1024]{1,0:T(8,128)(2,1)S(1)} %collective-permute-done.7.refs_7_) | copy-start | bytes 393220
  22.9 15.6 %collective-permute-start.5 = (bf16[64,1024]{1,0:T(8,128)(2,1)}, bf16[64,1024]{1,0:T(8,128)(2,1)S(1)}, u32[]{:S(2)}, u32[]{:S(2)}) collective-permute-start(bf16[64,1024]{1,0:T(8,128)(2,1)} %get-tuple-element.32), channel_id=1, source_target_pairs={{0,5},{1,4},{2,7},{3,6},{4,1},{5,0},{6,3},{7,2},{8,13},{9,12},{10,... | collective-permute-start | bytes 393224 | tf_op jit(solution)/shard_map/ppermute | solution.py:325
  28.0 32.1 %all-to-all-start.1 = ((bf16[8,64,1024]{2,1,0:T(8,128)(2,1)}), bf16[8,64,1024]{2,1,0:T(8,128)(2,1)S(1)}, u32[]{:S(2)}, u32[]{:S(2)}) async-start(bf16[8,64,1024]{2,1,0:T(8,128)(2,1)} %param.19), calls=%async_computation.1 | async-start | bytes 2097152 | tf_op jit(solution)/shard_map/all_to_all | solution.py:334
  32.9 5.7 %copy-start.8 = (bf16[64,1024]{1,0:T(8,128)(2,1)}, bf16[64,1024]{1,0:T(8,128)(2,1)S(1)}, u32[]{:S(2)}) copy-start(bf16[64,1024]{1,0:T(8,128)(2,1)S(1)} %collective-permute-done.1.refs_1_) | copy-start | bytes 393220
  32.9 5.7 %copy-start.9 = (bf16[64,1024]{1,0:T(8,128)(2,1)}, bf16[64,1024]{1,0:T(8,128)(2,1)S(1)}, u32[]{:S(2)}) copy-start(bf16[64,1024]{1,0:T(8,128)(2,1)S(1)} %collective-permute-done.2.refs_2_) | copy-start | bytes 393220
  32.9 5.7 %copy-start.10 = (bf16[64,1024]{1,0:T(8,128)(2,1)}, bf16[64,1024]{1,0:T(8,128)(2,1)S(1)}, u32[]{:S(2)}) copy-start(bf16[64,1024]{1,0:T(8,128)(2,1)S(1)} %collective-permute-done.3.refs_3_) | copy-start | bytes 393220
  32.9 5.7 %copy-start.11 = (bf16[64,1024]{1,0:T(8,128)(2,1)}, bf16[64,1024]{1,0:T(8,128)(2,1)S(1)}, u32[]{:S(2)}) copy-start(bf16[64,1024]{1,0:T(8,128)(2,1)S(1)} %collective-permute-done.4.refs_4_) | copy-start | bytes 393220
  60.1 36.7 %all-to-all-start = ((bf16[8,64,1024]{2,1,0:T(8,128)(2,1)}), bf16[8,64,1024]{2,1,0:T(8,128)(2,1)S(1)}, u32[]{:S(2)}, u32[]{:S(2)}) async-start(bf16[8,64,1024]{2,1,0:T(8,128)(2,1)} %get-tuple-element.37), calls=%async_computation | async-start | bytes 2097152 | tf_op jit(solution)/shard_map/all_to_all | solution.py:334
  80.0 9.9 %collective-permute-start.10 = (bf16[256,256]{1,0:T(8,128)(2,1)}, bf16[256,256]{1,0:T(8,128)(2,1)S(1)}, u32[]{:S(2)}, u32[]{:S(2)}) collective-permute-start(bf16[256,256]{1,0:T(8,128)(2,1)} %get-tuple-element.50), channel_id=1, source_target_pairs={{0,24},{8,16},{16,8},{24,0},{1,25},{9,17},{17,9},{25,1},{2,26},{10... | collective-permute-start | bytes 393224 | tf_op jit(solution)/shard_map/ppermute | solution.py:325
  80.1 11.0 %collective-permute-start.8 = (bf16[256,256]{1,0:T(8,128)(2,1)}, bf16[256,256]{1,0:T(8,128)(2,1)S(1)}, u32[]{:S(2)}, u32[]{:S(2)}) collective-permute-start(bf16[256,256]{1,0:T(8,128)(2,1)} %get-tuple-element.48), channel_id=1, source_target_pairs={{0,8},{8,0},{16,24},{24,16},{1,9},{9,1},{17,25},{25,17},{2,10},{10... | collective-permute-start | bytes 393224 | tf_op jit(solution)/shard_map/ppermute | solution.py:325
  89.9 5.9 %collective-permute-start.9 = (bf16[256,256]{1,0:T(8,128)(2,1)}, bf16[256,256]{1,0:T(8,128)(2,1)S(1)}, u32[]{:S(2)}, u32[]{:S(2)}) collective-permute-start(bf16[256,256]{1,0:T(8,128)(2,1)} %get-tuple-element.49), channel_id=1, source_target_pairs={{0,16},{8,24},{16,0},{24,8},{1,17},{9,25},{17,1},{25,9},{2,18},{10... | collective-permute-start | bytes 393224 | tf_op jit(solution)/shard_map/ppermute | solution.py:325
  119.8 8.3 %copy-start.1 = (bf16[8,32,256]{2,1,0:T(8,128)(2,1)}, bf16[8,32,256]{2,1,0:T(8,128)(2,1)S(1)}, u32[]{:S(2)}) copy-start(bf16[8,32,256]{2,1,0:T(8,128)(2,1)S(1)} %all_to_all.31) | copy-start | bytes 393220
  119.8 1.9 %collective-permute-start.11 = (bf16[256,256]{1,0:T(8,128)(2,1)S(1)}, bf16[256,256]{1,0:T(8,128)(2,1)S(1)}, u32[]{:S(2)}, u32[]{:S(2)}) collective-permute-start(bf16[256,256]{1,0:T(8,128)(2,1)S(1)} %bitcast.8), channel_id=1, source_target_pairs={{0,8},{8,0},{16,24},{24,16},{1,9},{9,1},{17,25},{25,17},{2,10},{10... | collective-permute-start | bytes 393224 | tf_op jit(solution)/shard_map/ppermute | solution.py:325
  119.8 6.3 %collective-permute-start.12 = (bf16[256,256]{1,0:T(8,128)(2,1)S(1)}, bf16[256,256]{1,0:T(8,128)(2,1)S(1)}, u32[]{:S(2)}, u32[]{:S(2)}) collective-permute-start(bf16[256,256]{1,0:T(8,128)(2,1)S(1)} %bitcast.9), channel_id=1, source_target_pairs={{0,16},{8,24},{16,0},{24,8},{1,17},{9,25},{17,1},{25,9},{2,18},{10... | collective-permute-start | bytes 393224 | tf_op jit(solution)/shard_map/ppermute | solution.py:325
  121.0 7.1 %collective-permute-start.13 = (bf16[256,256]{1,0:T(8,128)(2,1)S(1)}, bf16[256,256]{1,0:T(8,128)(2,1)S(1)}, u32[]{:S(2)}, u32[]{:S(2)}) collective-permute-start(bf16[256,256]{1,0:T(8,128)(2,1)S(1)} %bitcast.10), channel_id=1, source_target_pairs={{0,24},{8,16},{16,8},{24,0},{1,25},{9,17},{17,9},{25,1},{2,26},{10... | collective-permute-start | bytes 393224 | tf_op jit(solution)/shard_map/ppermute | solution.py:325
  121.6 6.5 %copy-start.3 = (bf16[256,256]{1,0:T(8,128)(2,1)}, bf16[256,256]{1,0:T(8,128)(2,1)S(1)}, u32[]{:S(2)}) copy-start(bf16[256,256]{1,0:T(8,128)(2,1)S(1)} %collective-permute-done.11.refs_1_) | copy-start | bytes 393220
  (5 other events, 8.9 us)

commit v8 on v7

--- a/solution.py
+++ b/solution.py
@@ -102,7 +102,7 @@
     feat_refs = refs[:blocks]
     (
         out_ref, prob_ref, value_ref, keys_ref, query_t_ref, normed_ref, normed_t_ref, mixed_ref,
-        mixed_t_ref, counts, columns, packed, live_row,
+        mixed_t_ref, inverse_ref, counts, columns, packed, live_row,
     ) = refs[blocks:]
     rows, width = feat_refs[0].shape
     contacts = rows * blocks
@@ -153,20 +153,30 @@
     normed_t_ref[...] = normed.T
     masks = [m.astype(BF16) for m in head_masks(width)]
     bias = jnp.where(live_row[...] > 0, 0.0, -1e30)
+    block = min(64, contacts)
+    lane_head = lax.broadcasted_iota(jnp.int32, (block, width), 1) // (width // HEADS)
+    shares = [[] for _ in range(contacts // block)]
     scores = mm(query * masks[0], keys, 1, 1)
     mixed = None
     for h in range(HEADS):
         following = mm(query * masks[h + 1], keys, 1, 1) if h + 1 < HEADS else None
-        scores = scores + bias
-        top = jnp.max(scores, axis=1, keepdims=True)
-        raised = jnp.exp(scores - top)
-        share = 1.0 / jnp.sum(raised, axis=1, keepdims=True)
-        prob = (raised * share).astype(BF16)
-        prob_ref[:, h * contacts : (h + 1) * contacts] = prob
-        part = mm(prob, value * masks[h])
+        columns_h = slice(h * contacts, (h + 1) * contacts)
+        for r, share in enumerate(shares):
+            here = slice(r * block, (r + 1) * block)
+            part = scores[here] + bias
+            raised = jnp.exp(part - jnp.max(part, axis=1, keepdims=True))
+            prob_ref[here, columns_h] = raised.astype(BF16)
+            share.append(1.0 / jnp.sum(raised, axis=1, keepdims=True))
+        part = mm(prob_ref[:, columns_h], value * masks[h])
         mixed = part if mixed is None else mixed + part
         scores = following
-    mixed = mixed.astype(BF16)
+    for r, share in enumerate(shares):
+        here = slice(r * block, (r + 1) * block)
+        inverse = jnp.broadcast_to(share[0], (block, width))
+        for h in range(1, HEADS):
+            inverse = jnp.where(lane_head >= h, share[h], inverse)
+        inverse_ref[here, :] = inverse
+    mixed = (mixed * inverse_ref[...]).astype(BF16)
     attended = mm(mixed, wo_ref[...]).astype(BF16)
     for k in range(blocks):
         out_ref[me ^ k] = attended[k * rows : (k + 1) * rows]
@@ -176,9 +186,9 @@
 
 def backward_kernel(
     blocks, place_ref, wo_ref, up_ref, prob_ref, value_ref, keys_ref, query_t_ref, normed_ref,
-    normed_t_ref, mixed_ref, mixed_t_ref, *refs,
+    normed_t_ref, mixed_ref, mixed_t_ref, inverse_ref, *refs,
 ):
-    out_refs, total, chunks = refs[:-2], refs[-2], refs[-1]
+    out_refs, total, chunks, changes = refs[:-3], refs[-3], refs[-2], refs[-1]
     contacts, width = normed_ref.shape
     head = width // HEADS
     scale = head ** (-0.5)
@@ -194,6 +204,7 @@
     value = value_ref[...]
     keys = keys_ref[...]
     back = mm(upstream, wo_ref[...], 1, 1).astype(BF16)
+    back = (back.astype(F32) * inverse_ref[...]).astype(BF16)
     back_t = back.T
     inner = back.astype(F32) * mixed_ref[...].astype(F32)
     masks = head_masks(width)
@@ -201,13 +212,18 @@
     grad_key_t = []
     grad_query = None
     low = [m.astype(BF16) for m in masks]
+    block = min(64, contacts)
     grad_prob = mm(back * low[0], value, 1, 1)
     for h in range(HEADS):
         following = mm(back * low[h + 1], value, 1, 1) if h + 1 < HEADS else None
-        row_inner = jnp.sum(inner * masks[h], axis=1, keepdims=True)
-        prob = prob_ref[:, h * contacts : (h + 1) * contacts]
-        grad_value_t.append(mm(back_t[h * head : (h + 1) * head], prob))
-        grad_score = (prob.astype(F32) * (grad_prob - row_inner)).astype(BF16)
+        columns_h = slice(h * contacts, (h + 1) * contacts)
+        grad_value_t.append(mm(back_t[h * head : (h + 1) * head], prob_ref[:, columns_h]))
+        for r in range(contacts // block):
+            here = slice(r * block, (r + 1) * block)
+            row_inner = jnp.sum(inner[here] * masks[h], axis=1, keepdims=True)
+            shift = (grad_prob[here] - row_inner).astype(BF16)
+            changes[here, columns_h] = prob_ref[here, columns_h] * shift
+        grad_score = changes[:, columns_h]
         grad_key_t.append(mm(query_t_ref[h * head : (h + 1) * head, :], grad_score))
         part = mm(grad_score, keys * low[h])
         grad_query = part if grad_query is None else grad_query + part
@@ -242,7 +258,7 @@
     shapes = [
         (contacts, HEADS * contacts), (contacts, width),
         (contacts, width), (width, contacts), (contacts, width), (width, contacts),
-        (contacts, width), (width, contacts),
+        (contacts, width), (width, contacts), (contacts, width),
     ]
     small = [neighbours, live, coef] + list(weights)
     return pl.pallas_call(
@@ -254,7 +270,10 @@
         out_specs=[pl.BlockSpec((blocks, rows, width), lambda i: (0, 0, i))]
         + [pl.BlockSpec(shape, lambda i: (0, i)) for shape in shapes],
         out_shape=[jax.ShapeDtypeStruct((blocks, rows, span), BF16)]
-        + [jax.ShapeDtypeStruct((shape[0], groups * shape[1]), BF16) for shape in shapes],
+        + [
+            jax.ShapeDtypeStruct((shape[0], groups * shape[1]), kind)
+            for shape, kind in zip(shapes, [BF16] * (len(shapes) - 1) + [F32])
+        ],
         scratch_shapes=[
             pltpu.VMEM((contacts, contacts), BF16),
             pltpu.VMEM((contacts, 128), F32),
@@ -293,6 +312,7 @@
         scratch_shapes=[
             pltpu.VMEM((4, width, width), F32),
             pltpu.VMEM((tm_count,) + chunk, BF16),
+            pltpu.VMEM((contacts, HEADS * contacts), BF16),
         ],
         compiler_params=params(),
         cost_estimate=pl.CostEstimate(
@@ -353,7 +373,10 @@
         signal[:, :, slab - rim_width :], "tm", [(i, i + 1) for i in range(tm_count - 1)]
     )
     filtered = filter_all(place, signal, rim, fir_taps, count)
-    features = swap_all(filtered, "contact")
+    far = {k: swap(filtered[k], "contact", k) for k in range(count - 1, count // 2 - 1, -1)}
+    far[count - 1], near = lax.optimization_barrier((far[count - 1], filtered[1 : count // 2]))
+    features = [filtered[0]] + [swap(near[k - 1], "contact", k) for k in range(1, count // 2)]
+    features += [far[k] for k in range(count // 2, count)]
     arrived = count - max(2, count // 4)
     features[arrived:], cotangent = lax.optimization_barrier((features[arrived:], cotangent))
     upstream = exchange(cotangent, "contact")

time: 132 us -> 135 us (1.023)
  starting transfers between devices: 40.3 us -> 42.2 us
    ppermute x13, starting transfers between devices: 28.1 us -> 32.6 us  [swap(): lax.ppermute(value, axis, [(i, i ^ k) for i in range(lax.axis_size(axis))])]
    all_to_all x2, starting transfers between devices: 9.76 us -> 7.24 us  [exchange(): return lax.all_to_all(value, axis, split_axis=0, concat_axis=0, tiled=True)]
    ppermute x13, waiting for transfers between devices: 19.1 us -> 21.3 us  [swap(): lax.ppermute(value, axis, [(i, i ^ k) for i in range(lax.axis_size(axis))])]
    all_to_all x2, waiting for transfers between devices: 2.06 us -> 0.01 us  [exchange(): return lax.all_to_all(value, axis, split_axis=0, concat_axis=0, tiled=True)]
  transfers between devices with their start and end apart: 16 -> 16, of which waited for: 8 -> 9; matrix products, arithmetic and copies ran while one was open for 1% -> 1% of each run, Pallas kernels for 26% -> 25%
where the time goes in v8:
time: 135 us; the launch traced here: 134 us
  starting transfers between devices  42.2 us (31%)
  Pallas kernels  41.3 us (31%)
  blocking collectives  22.9 us (17%)
  waiting for transfers between devices  21.7 us (16%)
  local copies, waits for them, and re-layouts  3.88 us (3%)
  other arithmetic  1.6 us (1%)
    ppermute x13, starting transfers between devices, swap(): lax.ppermute(value, axis, [(i, i ^ k) for i in range(lax.axis_size(axis))])  32.6 us
    all_to_all x2, blocking collectives, exchange(): return lax.all_to_all(value, axis, split_axis=0, concat_axis=0, tiled=True)  22.9 us
    ppermute x13, waiting for transfers between devices, swap(): lax.ppermute(value, axis, [(i, i ^ k) for i in range(lax.axis_size(axis))])  21.3 us
    pallas_call x1, Pallas kernels, forward(): pl.pallas_call(functools.partial(forward_kernel, blocks), grid=(groups,),...  18.9 us
    pallas_call x1, Pallas kernels, backward(): pl.pallas_call(functools.partial(backward_kernel, blocks), grid=(groups,)...  15.3 us
    all_to_all x2, starting transfers between devices, exchange(): return lax.all_to_all(value, axis, split_axis=0, concat_axis=0, tiled=True)  7.24 us
    pallas_call x1, Pallas kernels, filter_all(): pl.pallas_call(filter_kernel, grid=(contacts // rows,), in_specs=[index_s...  4.86 us
    unnamed x33, local copies, waits for them, and re-layouts  2.96 us
  transfers between devices with their start and end apart: 16, of which 9 were waited for; matrix products, arithmetic and copies ran while one was open for 1% of the time, Pallas kernels for 25%

profile of v8, /device:TPU:0, one launch (start us, length us, event | category | flops | bytes accessed | tf_op | source)
XLA Modules:
  0.0 134.4 jit_solution(6078298828409985177)
XLA Ops:
  1.5 2.4 %collective-permute-start = (bf16[8,64,128]{2,1,0:T(8,128)(2,1)S(1)}, bf16[8,64,128]{2,1,0:T(8,128)(2,1)S(1)}, u32[]{:S(2)}, u32[]{:S(2)}) collective-permute-start(bf16[8,64,128]{2,1,0:T(8,128)(2,1)S(1)} %slice.3), channel_id=1, source_target_pairs={{0,8},{8,16},{16,24},{1,9},{9,17},{17,25},{2,10},{10,18},{18,26},{... | collective-permute-start | bytes 393224 | tf_op jit(solution)/shard_map/ppermute | solution.py:372
  5.5 4.9 %filter.1 = (bf16[64,1024]{1,0:T(8,128)(2,1)}, bf16[64,1024]{1,0:T(8,128)(2,1)}, bf16[64,1024]{1,0:T(8,128)(2,1)}, bf16[64,1024]{1,0:T(8,128)(2,1)}, bf16[64,102...) custom-call(s32[2]{0:T(128)} %pad_add_fusion.place_ref, ...), custom_call_target="tpu_custom_call" | custom-call | flops 268435456 | bytes 2097152 | tf_op jit(solution)/shard_map/filter/pallas_call | solution.py:72
  10.4 5.5 %collective-permute-start.1 = (bf16[64,1024]{1,0:T(8,128)(2,1)}, bf16[64,1024]{1,0:T(8,128)(2,1)S(1)}, u32[]{:S(2)}, u32[]{:S(2)}) collective-permute-start(bf16[64,1024]{1,0:T(8,128)(2,1)} %get-tuple-element.33), channel_id=1, source_target_pairs={{0,7},{1,6},{2,5},{3,4},{4,3},{5,2},{6,1},{7,0},{8,15},{9,14},{10,... | collective-permute-start | bytes 393224 | tf_op jit(solution)/shard_map/ppermute | solution.py:345
  16.9 2.0 %collective-permute-start.6 = (bf16[64,1024]{1,0:T(8,128)(2,1)}, bf16[64,1024]{1,0:T(8,128)(2,1)S(1)}, u32[]{:S(2)}, u32[]{:S(2)}) collective-permute-start(bf16[64,1024]{1,0:T(8,128)(2,1)} %get-tuple-element.41), channel_id=1, source_target_pairs={{0,5},{1,4},{2,7},{3,6},{4,1},{5,0},{6,3},{7,2},{8,13},{9,12},{10,... | collective-permute-start | bytes 393224 | tf_op jit(solution)/shard_map/ppermute | solution.py:345
  19.1 1.7 %collective-permute-start.2 = (bf16[64,1024]{1,0:T(8,128)(2,1)}, bf16[64,1024]{1,0:T(8,128)(2,1)S(1)}, u32[]{:S(2)}, u32[]{:S(2)}) collective-permute-start(bf16[64,1024]{1,0:T(8,128)(2,1)} %get-tuple-element.37), channel_id=1, source_target_pairs={{0,1},{1,0},{2,3},{3,2},{4,5},{5,4},{6,7},{7,6},{8,9},{9,8},{10,11... | collective-permute-start | bytes 393224 | tf_op jit(solution)/shard_map/ppermute | solution.py:345
  20.8 11.4 %collective-permute-start.3 = (bf16[64,1024]{1,0:T(8,128)(2,1)}, bf16[64,1024]{1,0:T(8,128)(2,1)S(1)}, u32[]{:S(2)}, u32[]{:S(2)}) collective-permute-start(bf16[64,1024]{1,0:T(8,128)(2,1)} %get-tuple-element.38), channel_id=1, source_target_pairs={{0,2},{1,3},{2,0},{3,1},{4,6},{5,7},{6,4},{7,5},{8,10},{9,11},{10,... | collective-permute-start | bytes 393224 | tf_op jit(solution)/shard_map/ppermute | solution.py:345
  32.2 1.4 %collective-permute-start.4 = (bf16[64,1024]{1,0:T(8,128)(2,1)}, bf16[64,1024]{1,0:T(8,128)(2,1)S(1)}, u32[]{:S(2)}, u32[]{:S(2)}) collective-permute-start(bf16[64,1024]{1,0:T(8,128)(2,1)} %get-tuple-element.39), channel_id=1, source_target_pairs={{0,3},{1,2},{2,1},{3,0},{4,7},{5,6},{6,5},{7,4},{8,11},{9,10},{10,... | collective-permute-start | bytes 393224 | tf_op jit(solution)/shard_map/ppermute | solution.py:345
  33.6 3.7 %all-to-all-start.1 = ((bf16[8,64,1024]{2,1,0:T(8,128)(2,1)}), bf16[8,64,1024]{2,1,0:T(8,128)(2,1)S(1)}, u32[]{:S(2)}, u32[]{:S(2)}) async-start(bf16[8,64,1024]{2,1,0:T(8,128)(2,1)} %param.19), calls=%async_computation.1 | async-start | bytes 2097152 | tf_op jit(solution)/shard_map/all_to_all | solution.py:354
  37.3 1.5 %collective-permute-done.6.refs_5_ = bf16[64,1024]{1,0:T(8,128)(2,1)S(1)} collective-permute-done((bf16[64,1024]{1,0:T(8,128)(2,1)}, bf16[64,1024]{1,0:T(8,128)(2,1)S(1)}, u32[]{:S(2)}, u32[]{:S(2)}) %collective-permute-start.6) | collective-permute-done | bytes 131104 | tf_op jit(solution)/shard_map/ppermute | solution.py:345
  38.8 2.8 %collective-permute-done.3.refs_2_ = bf16[64,1024]{1,0:T(8,128)(2,1)S(1)} collective-permute-done((bf16[64,1024]{1,0:T(8,128)(2,1)}, bf16[64,1024]{1,0:T(8,128)(2,1)S(1)}, u32[]{:S(2)}, u32[]{:S(2)}) %collective-permute-start.3) | collective-permute-done | bytes 131104 | tf_op jit(solution)/shard_map/ppermute | solution.py:345
  41.5 4.6 %collective-permute-done.4.refs_3_ = bf16[64,1024]{1,0:T(8,128)(2,1)S(1)} collective-permute-done((bf16[64,1024]{1,0:T(8,128)(2,1)}, bf16[64,1024]{1,0:T(8,128)(2,1)S(1)}, u32[]{:S(2)}, u32[]{:S(2)}) %collective-permute-start.4) | collective-permute-done | bytes 131104 | tf_op jit(solution)/shard_map/ppermute | solution.py:345
  46.8 18.9 %forward.1 = (bf16[8,64,1024]{2,1,0:T(8,128)(2,1)}, bf16[512,8192]{1,0:T(8,128)(2,1)}, bf16[512,1024]{1,0:T(8,128)(2,1)}, bf16[512,1024]{1,0:T(8,128)(2,1)}, bf1...) custom-call(s32[2]{0:T(128)} %pad_add_fusion.place_ref, ...), custom_call_target="tpu_custom_call" | custom-call | flops 20000000000 | bytes 10485760 | tf_op jit(solution)/shard_map/forward/pallas_call | solution.py:264
  65.7 3.6 %all-to-all-start = ((bf16[8,64,1024]{2,1,0:T(8,128)(2,1)}), bf16[8,64,1024]{2,1,0:T(8,128)(2,1)S(1)}, u32[]{:S(2)}, u32[]{:S(2)}) async-start(bf16[8,64,1024]{2,1,0:T(8,128)(2,1)} %get-tuple-element.46), calls=%async_computation | async-start | bytes 2097152 | tf_op jit(solution)/shard_map/all_to_all | solution.py:354
  69.3 15.3 %backward.1 = (bf16[256,256]{1,0:T(8,128)(2,1)}, bf16[256,256]{1,0:T(8,128)(2,1)}, bf16[256,256]{1,0:T(8,128)(2,1)}, bf16[256,256]{1,0:T(8,128)(2,1)}) custom-call(s32[2]{0:T(128)} %pad_add_fusion.place_ref, bf16[256,256]{1,0:T(8,128)(2,1)} %wo_ref.3, bf16[8,64,1024]{2,1,0:T(8,128)(2,1)} %copy-done, bf16[512,8192]{1,0:T(8,128)(2,1)} %get-tuple-element.48.prob_ref, ...), custom_call_target="tpu_custom_call" | custom-call | flops 20000000000 | bytes 10485760 | tf_op jit(solution)/shard_map/backward/pallas_call | solution.py:299
  84.7 7.7 %collective-permute-start.8 = (bf16[256,256]{1,0:T(8,128)(2,1)}, bf16[256,256]{1,0:T(8,128)(2,1)S(1)}, u32[]{:S(2)}, u32[]{:S(2)}) collective-permute-start(bf16[256,256]{1,0:T(8,128)(2,1)} %get-tuple-element.58), channel_id=1, source_target_pairs={{0,8},{8,0},{16,24},{24,16},{1,9},{9,1},{17,25},{25,17},{2,10},{10... | collective-permute-start | bytes 393224 | tf_op jit(solution)/shard_map/ppermute | solution.py:345
  92.5 1.2 collective-permute-done.8
  93.6 4.7 %collective-permute-done.9 = bf16[256,256]{1,0:T(8,128)(2,1)S(1)} collective-permute-done((bf16[256,256]{1,0:T(8,128)(2,1)}, bf16[256,256]{1,0:T(8,128)(2,1)S(1)}, u32[]{:S(2)}, u32[]{:S(2)}) %collective-permute-start.9) | collective-permute-done | bytes 131104 | tf_op jit(solution)/shard_map/ppermute | solution.py:345
  98.3 1.0 add_convert_fusion
  99.3 13.1 %all_to_all.30 = bf16[8,32,256]{2,1,0:T(8,128)(2,1)S(1)} all-to-all(bf16[8,32,256]{2,1,0:T(8,128)(2,1)S(1)} %bitcast.12), channel_id=1, replica_groups=mesh['tm'=4,'contact'=8] {'contact'}, dimensions={0} | all-to-all | bytes 262144 | tf_op jit(solution)/shard_map/all_to_all | solution.py:354
  112.5 9.7 %all_to_all.31 = bf16[8,32,256]{2,1,0:T(8,128)(2,1)S(1)} all-to-all(bf16[8,32,256]{2,1,0:T(8,128)(2,1)S(1)} %bitcast.13), channel_id=1, replica_groups=mesh['tm'=4,'contact'=8] {'contact'}, dimensions={0} | all-to-all | bytes 262144 | tf_op jit(solution)/shard_map/all_to_all | solution.py:354
  122.3 1.2 collective-permute-start.12
  124.1 4.4 %collective-permute-done.12.refs_2_ = bf16[256,256]{1,0:T(8,128)(2,1)S(1)} collective-permute-done((bf16[256,256]{1,0:T(8,128)(2,1)S(1)}, bf16[256,256]{1,0:T(8,128)(2,1)S(1)}, u32[]{:S(2)}, u32[]{:S(2)}) %collective-permute-start.12) | collective-permute-done | bytes 131104 | tf_op jit(solution)/shard_map/ppermute | solution.py:345
  128.5 2.0 %collective-permute-done.13.refs_3_ = bf16[256,256]{1,0:T(8,128)(2,1)S(1)} collective-permute-done((bf16[256,256]{1,0:T(8,128)(2,1)S(1)}, bf16[256,256]{1,0:T(8,128)(2,1)S(1)}, u32[]{:S(2)}, u32[]{:S(2)}) %collective-permute-start.13) | collective-permute-done | bytes 131104 | tf_op jit(solution)/shard_map/ppermute | solution.py:345
  131.3 2.1 %place_all.1 = f32[4,256,256]{2,1,0:T(8,128)} custom-call(s32[2]{0:T(128)} %pad_add_fusion.place_ref, bf16[256,256]{1,0:T(8,128)(2,1)} %bitcast.11, bf16[256,256]{1,0:T(8,128)(2,1)} %copy-done.3, bf16[256,256]{1,0:T(8,128)(2,1)} %copy-done.4, bf16[256,256]{1,0:T(8,128)(2,1)} %copy-done.5), custom_call_target="tpu_custom_call" | custom-call | tf_op jit(solution)/shard_map/place_all/pallas_call | solution.py:334
  (53 shorter events, 6.9 us)
Async XLA Ops:
  1.5 3.3 %collective-permute-start = (bf16[8,64,128]{2,1,0:T(8,128)(2,1)S(1)}, bf16[8,64,128]{2,1,0:T(8,128)(2,1)S(1)}, u32[]{:S(2)}, u32[]{:S(2)}) collective-permute-start(bf16[8,64,128]{2,1,0:T(8,128)(2,1)S(1)} %slice.3), channel_id=1, source_target_pairs={{0,8},{8,16},{16,24},{1,9},{9,17},{17,25},{2,10},{10,18},{18,26},{... | collective-permute-start | bytes 393224 | tf_op jit(solution)/shard_map/ppermute | solution.py:372
  10.4 8.7 %collective-permute-start.1 = (bf16[64,1024]{1,0:T(8,128)(2,1)}, bf16[64,1024]{1,0:T(8,128)(2,1)S(1)}, u32[]{:S(2)}, u32[]{:S(2)}) collective-permute-start(bf16[64,1024]{1,0:T(8,128)(2,1)} %get-tuple-element.33), channel_id=1, source_target_pairs={{0,7},{1,6},{2,5},{3,4},{4,3},{5,2},{6,1},{7,0},{8,15},{9,14},{10,... | collective-permute-start | bytes 393224 | tf_op jit(solution)/shard_map/ppermute | solution.py:345
  15.9 16.3 %collective-permute-start.7 = (bf16[64,1024]{1,0:T(8,128)(2,1)}, bf16[64,1024]{1,0:T(8,128)(2,1)S(1)}, u32[]{:S(2)}, u32[]{:S(2)}) collective-permute-start(bf16[64,1024]{1,0:T(8,128)(2,1)} %get-tuple-element.42), channel_id=1, source_target_pairs={{0,6},{1,7},{2,4},{3,5},{4,2},{5,3},{6,0},{7,1},{8,14},{9,15},{10,... | collective-permute-start | bytes 393224 | tf_op jit(solution)/shard_map/ppermute | solution.py:345
  16.1 21.2 %collective-permute-start.5 = (bf16[64,1024]{1,0:T(8,128)(2,1)}, bf16[64,1024]{1,0:T(8,128)(2,1)S(1)}, u32[]{:S(2)}, u32[]{:S(2)}) collective-permute-start(bf16[64,1024]{1,0:T(8,128)(2,1)} %get-tuple-element.40), channel_id=1, source_target_pairs={{0,4},{1,5},{2,6},{3,7},{4,0},{5,1},{6,2},{7,3},{8,12},{9,13},{10,... | collective-permute-start | bytes 393224 | tf_op jit(solution)/shard_map/ppermute | solution.py:345
  16.9 21.9 %collective-permute-start.6 = (bf16[64,1024]{1,0:T(8,128)(2,1)}, bf16[64,1024]{1,0:T(8,128)(2,1)S(1)}, u32[]{:S(2)}, u32[]{:S(2)}) collective-permute-start(bf16[64,1024]{1,0:T(8,128)(2,1)} %get-tuple-element.41), channel_id=1, source_target_pairs={{0,5},{1,4},{2,7},{3,6},{4,1},{5,0},{6,3},{7,2},{8,13},{9,12},{10,... | collective-permute-start | bytes 393224 | tf_op jit(solution)/shard_map/ppermute | solution.py:345
  19.1 27.0 %copy-start.6 = (bf16[64,1024]{1,0:T(8,128)(2,1)}, bf16[64,1024]{1,0:T(8,128)(2,1)S(1)}, u32[]{:S(2)}) copy-start(bf16[64,1024]{1,0:T(8,128)(2,1)S(1)} %collective-permute-done.1.refs_7_) | copy-start | bytes 393220
  19.1 19.6 %collective-permute-start.2 = (bf16[64,1024]{1,0:T(8,128)(2,1)}, bf16[64,1024]{1,0:T(8,128)(2,1)S(1)}, u32[]{:S(2)}, u32[]{:S(2)}) collective-permute-start(bf16[64,1024]{1,0:T(8,128)(2,1)} %get-tuple-element.37), channel_id=1, source_target_pairs={{0,1},{1,0},{2,3},{3,2},{4,5},{5,4},{6,7},{7,6},{8,9},{9,8},{10,11... | collective-permute-start | bytes 393224 | tf_op jit(solution)/shard_map/ppermute | solution.py:345
  20.8 20.7 %collective-permute-start.3 = (bf16[64,1024]{1,0:T(8,128)(2,1)}, bf16[64,1024]{1,0:T(8,128)(2,1)S(1)}, u32[]{:S(2)}, u32[]{:S(2)}) collective-permute-start(bf16[64,1024]{1,0:T(8,128)(2,1)} %get-tuple-element.38), channel_id=1, source_target_pairs={{0,2},{1,3},{2,0},{3,1},{4,6},{5,7},{6,4},{7,5},{8,10},{9,11},{10,... | collective-permute-start | bytes 393224 | tf_op jit(solution)/shard_map/ppermute | solution.py:345
  32.2 14.0 %copy-start.7 = (bf16[64,1024]{1,0:T(8,128)(2,1)}, bf16[64,1024]{1,0:T(8,128)(2,1)S(1)}, u32[]{:S(2)}) copy-start(bf16[64,1024]{1,0:T(8,128)(2,1)S(1)} %collective-permute-done.7.refs_6_) | copy-start | bytes 393220
  32.2 13.9 %collective-permute-start.4 = (bf16[64,1024]{1,0:T(8,128)(2,1)}, bf16[64,1024]{1,0:T(8,128)(2,1)S(1)}, u32[]{:S(2)}, u32[]{:S(2)}) collective-permute-start(bf16[64,1024]{1,0:T(8,128)(2,1)} %get-tuple-element.39), channel_id=1, source_target_pairs={{0,3},{1,2},{2,1},{3,0},{4,7},{5,6},{6,5},{7,4},{8,11},{9,10},{10,... | collective-permute-start | bytes 393224 | tf_op jit(solution)/shard_map/ppermute | solution.py:345
  33.6 32.1 %all-to-all-start.1 = ((bf16[8,64,1024]{2,1,0:T(8,128)(2,1)}), bf16[8,64,1024]{2,1,0:T(8,128)(2,1)S(1)}, u32[]{:S(2)}, u32[]{:S(2)}) async-start(bf16[8,64,1024]{2,1,0:T(8,128)(2,1)} %param.19), calls=%async_computation.1 | async-start | bytes 2097152 | tf_op jit(solution)/shard_map/all_to_all | solution.py:354
  37.3 8.8 %copy-start.8 = (bf16[64,1024]{1,0:T(8,128)(2,1)}, bf16[64,1024]{1,0:T(8,128)(2,1)S(1)}, u32[]{:S(2)}) copy-start(bf16[64,1024]{1,0:T(8,128)(2,1)S(1)} %collective-permute-done.5.refs_4_) | copy-start | bytes 393220
  38.8 7.4 %copy-start.9 = (bf16[64,1024]{1,0:T(8,128)(2,1)}, bf16[64,1024]{1,0:T(8,128)(2,1)S(1)}, u32[]{:S(2)}) copy-start(bf16[64,1024]{1,0:T(8,128)(2,1)S(1)} %collective-permute-done.6.refs_5_) | copy-start | bytes 393220
  38.8 7.4 %copy-start.10 = (bf16[64,1024]{1,0:T(8,128)(2,1)}, bf16[64,1024]{1,0:T(8,128)(2,1)S(1)}, u32[]{:S(2)}) copy-start(bf16[64,1024]{1,0:T(8,128)(2,1)S(1)} %collective-permute-done.2.refs_1_) | copy-start | bytes 393220
  41.5 4.6 %copy-start.11 = (bf16[64,1024]{1,0:T(8,128)(2,1)}, bf16[64,1024]{1,0:T(8,128)(2,1)S(1)}, u32[]{:S(2)}) copy-start(bf16[64,1024]{1,0:T(8,128)(2,1)S(1)} %collective-permute-done.3.refs_2_) | copy-start | bytes 393220
  65.7 33.5 %all-to-all-start = ((bf16[8,64,1024]{2,1,0:T(8,128)(2,1)}), bf16[8,64,1024]{2,1,0:T(8,128)(2,1)S(1)}, u32[]{:S(2)}, u32[]{:S(2)}) async-start(bf16[8,64,1024]{2,1,0:T(8,128)(2,1)} %get-tuple-element.46), calls=%async_computation | async-start | bytes 2097152 | tf_op jit(solution)/shard_map/all_to_all | solution.py:354
  84.7 7.8 %collective-permute-start.10 = (bf16[256,256]{1,0:T(8,128)(2,1)}, bf16[256,256]{1,0:T(8,128)(2,1)S(1)}, u32[]{:S(2)}, u32[]{:S(2)}) collective-permute-start(bf16[256,256]{1,0:T(8,128)(2,1)} %get-tuple-element.60), channel_id=1, source_target_pairs={{0,24},{8,16},{16,8},{24,0},{1,25},{9,17},{17,9},{25,1},{2,26},{10... | collective-permute-start | bytes 393224 | tf_op jit(solution)/shard_map/ppermute | solution.py:345
  84.7 8.9 %collective-permute-start.8 = (bf16[256,256]{1,0:T(8,128)(2,1)}, bf16[256,256]{1,0:T(8,128)(2,1)S(1)}, u32[]{:S(2)}, u32[]{:S(2)}) collective-permute-start(bf16[256,256]{1,0:T(8,128)(2,1)} %get-tuple-element.58), channel_id=1, source_target_pairs={{0,8},{8,0},{16,24},{24,16},{1,9},{9,1},{17,25},{25,17},{2,10},{10... | collective-permute-start | bytes 393224 | tf_op jit(solution)/shard_map/ppermute | solution.py:345
  92.4 5.9 %collective-permute-start.9 = (bf16[256,256]{1,0:T(8,128)(2,1)}, bf16[256,256]{1,0:T(8,128)(2,1)S(1)}, u32[]{:S(2)}, u32[]{:S(2)}) collective-permute-start(bf16[256,256]{1,0:T(8,128)(2,1)} %get-tuple-element.59), channel_id=1, source_target_pairs={{0,16},{8,24},{16,0},{24,8},{1,17},{9,25},{17,1},{25,9},{2,18},{10... | collective-permute-start | bytes 393224 | tf_op jit(solution)/shard_map/ppermute | solution.py:345
  122.2 8.3 %copy-start.1 = (bf16[8,32,256]{2,1,0:T(8,128)(2,1)}, bf16[8,32,256]{2,1,0:T(8,128)(2,1)S(1)}, u32[]{:S(2)}) copy-start(bf16[8,32,256]{2,1,0:T(8,128)(2,1)S(1)} %all_to_all.31) | copy-start | bytes 393220
  122.2 1.9 %collective-permute-start.11 = (bf16[256,256]{1,0:T(8,128)(2,1)S(1)}, bf16[256,256]{1,0:T(8,128)(2,1)S(1)}, u32[]{:S(2)}, u32[]{:S(2)}) collective-permute-start(bf16[256,256]{1,0:T(8,128)(2,1)S(1)} %bitcast.8), channel_id=1, source_target_pairs={{0,8},{8,0},{16,24},{24,16},{1,9},{9,1},{17,25},{25,17},{2,10},{10... | collective-permute-start | bytes 393224 | tf_op jit(solution)/shard_map/ppermute | solution.py:345
  122.3 6.3 %collective-permute-start.12 = (bf16[256,256]{1,0:T(8,128)(2,1)S(1)}, bf16[256,256]{1,0:T(8,128)(2,1)S(1)}, u32[]{:S(2)}, u32[]{:S(2)}) collective-permute-start(bf16[256,256]{1,0:T(8,128)(2,1)S(1)} %bitcast.9), channel_id=1, source_target_pairs={{0,16},{8,24},{16,0},{24,8},{1,17},{9,25},{17,1},{25,9},{2,18},{10... | collective-permute-start | bytes 393224 | tf_op jit(solution)/shard_map/ppermute | solution.py:345
  123.4 7.1 %collective-permute-start.13 = (bf16[256,256]{1,0:T(8,128)(2,1)S(1)}, bf16[256,256]{1,0:T(8,128)(2,1)S(1)}, u32[]{:S(2)}, u32[]{:S(2)}) collective-permute-start(bf16[256,256]{1,0:T(8,128)(2,1)S(1)} %bitcast.10), channel_id=1, source_target_pairs={{0,24},{8,16},{16,8},{24,0},{1,25},{9,17},{17,9},{25,1},{2,26},{10... | collective-permute-start | bytes 393224 | tf_op jit(solution)/shard_map/ppermute | solution.py:345
  124.1 6.5 %copy-start.3 = (bf16[256,256]{1,0:T(8,128)(2,1)}, bf16[256,256]{1,0:T(8,128)(2,1)S(1)}, u32[]{:S(2)}) copy-start(bf16[256,256]{1,0:T(8,128)(2,1)S(1)} %collective-permute-done.11.refs_1_) | copy-start | bytes 393220
  (5 other events, 7.6 us)

commit v9 on v8

--- a/solution.py
+++ b/solution.py
@@ -91,6 +91,11 @@
     )(place, signal, rim, taps)
 
 
+def pair_masks(pair):
+    lane = lax.broadcasted_iota(jnp.int32, (1, pair), 1)
+    return [(lane < pair // 2).astype(F32).astype(BF16), (lane >= pair // 2).astype(F32).astype(BF16)]
+
+
 def head_masks(width):
     lane_head = lax.broadcasted_iota(jnp.int32, (1, width), 1) // (width // HEADS)
     return [(lane_head == h).astype(F32) for h in range(HEADS)]
@@ -101,8 +106,8 @@
 ):
     feat_refs = refs[:blocks]
     (
-        out_ref, prob_ref, value_ref, keys_ref, query_t_ref, normed_ref, normed_t_ref, mixed_ref,
-        mixed_t_ref, inverse_ref, counts, columns, packed, live_row,
+        out_ref, prob_ref, value_t_ref, keys_ref, query_t_ref, normed_ref, normed_t_ref, mixed_ref,
+        mixed_t_ref, inverse_ref, counts, columns, packed, live_row, turned_w,
     ) = refs[blocks:]
     rows, width = feat_refs[0].shape
     contacts = rows * blocks
@@ -133,6 +138,9 @@
         columns[:, 0:1] = turned[:, 0:1]
         columns[:, 1:2] = turned[:, 1:2]
         columns[:, 2:3] = jnp.sum(total, axis=1, keepdims=True)
+        turned_w[0] = wq_ref[...].T
+        turned_w[1] = wk_ref[...].T
+        turned_w[2] = wv_ref[...].T
 
     live = columns[:, 0:1]
     coef = columns[:, 1:2]
@@ -146,20 +154,28 @@
     query = (mm(normed, wq_ref[...]) * scale).astype(BF16)
     keys = mm(normed, wk_ref[...]).astype(BF16)
     value = mm(normed, wv_ref[...]).astype(BF16)
-    value_ref[...] = value
+    normed_t = normed.T
+    keys_t = mm(turned_w[1], normed_t).astype(BF16)
+    value_t_ref[...] = mm(turned_w[2], normed_t).astype(BF16)
     keys_ref[...] = keys
-    query_t_ref[...] = query.T
+    query_t_ref[...] = (mm(turned_w[0], normed_t) * scale).astype(BF16)
     normed_ref[...] = normed
-    normed_t_ref[...] = normed.T
-    masks = [m.astype(BF16) for m in head_masks(width)]
+    normed_t_ref[...] = normed_t
+    pair = 2 * width // HEADS
+    masks = pair_masks(pair)
+
+    def score(h):
+        lanes = slice(h // 2 * pair, (h // 2 + 1) * pair)
+        return mm(query[:, lanes] * masks[h % 2], keys_t[lanes, :])
+
     bias = jnp.where(live_row[...] > 0, 0.0, -1e30)
     block = min(64, contacts)
     lane_head = lax.broadcasted_iota(jnp.int32, (block, width), 1) // (width // HEADS)
     shares = [[] for _ in range(contacts // block)]
-    scores = mm(query * masks[0], keys, 1, 1)
-    mixed = None
+    scores = score(0)
+    mixed = [None] * (HEADS // 2)
     for h in range(HEADS):
-        following = mm(query * masks[h + 1], keys, 1, 1) if h + 1 < HEADS else None
+        following = score(h + 1) if h + 1 < HEADS else None
         columns_h = slice(h * contacts, (h + 1) * contacts)
         for r, share in enumerate(shares):
             here = slice(r * block, (r + 1) * block)
@@ -167,8 +183,9 @@
             raised = jnp.exp(part - jnp.max(part, axis=1, keepdims=True))
             prob_ref[here, columns_h] = raised.astype(BF16)
             share.append(1.0 / jnp.sum(raised, axis=1, keepdims=True))
-        part = mm(prob_ref[:, columns_h], value * masks[h])
-        mixed = part if mixed is None else mixed + part
+        lanes = slice(h // 2 * pair, (h // 2 + 1) * pair)
+        part = mm(prob_ref[:, columns_h], value[:, lanes] * masks[h % 2])
+        mixed[h // 2] = part if h % 2 == 0 else mixed[h // 2] + part
         scores = following
     for r, share in enumerate(shares):
         here = slice(r * block, (r + 1) * block)
@@ -176,7 +193,7 @@
         for h in range(1, HEADS):
             inverse = jnp.where(lane_head >= h, share[h], inverse)
         inverse_ref[here, :] = inverse
-    mixed = (mixed * inverse_ref[...]).astype(BF16)
+    mixed = (jnp.concatenate(mixed, axis=1) * inverse_ref[...]).astype(BF16)
     attended = mm(mixed, wo_ref[...]).astype(BF16)
     for k in range(blocks):
         out_ref[me ^ k] = attended[k * rows : (k + 1) * rows]
@@ -185,10 +202,10 @@
 
 
 def backward_kernel(
-    blocks, place_ref, wo_ref, up_ref, prob_ref, value_ref, keys_ref, query_t_ref, normed_ref,
+    blocks, place_ref, wo_ref, up_ref, prob_ref, value_t_ref, keys_ref, query_t_ref, normed_ref,
     normed_t_ref, mixed_ref, mixed_t_ref, inverse_ref, *refs,
 ):
-    out_refs, total, chunks, changes = refs[:-3], refs[-3], refs[-2], refs[-1]
+    out_refs, (total, chunks, changes, turned_w) = refs[:-4], refs[-4:]
     contacts, width = normed_ref.shape
     head = width // HEADS
     scale = head ** (-0.5)
@@ -197,25 +214,31 @@
     @pl.when(step == 0)
     def _():
         total[...] = jnp.zeros_like(total)
+        turned_w[...] = wo_ref[...].T
 
     me = place_ref[1]
     upstream = jnp.concatenate([up_ref[me ^ k] for k in range(blocks)], axis=0)
     normed = normed_ref[...]
-    value = value_ref[...]
     keys = keys_ref[...]
-    back = mm(upstream, wo_ref[...], 1, 1).astype(BF16)
+    back = mm(upstream, turned_w[...]).astype(BF16)
     back = (back.astype(F32) * inverse_ref[...]).astype(BF16)
     back_t = back.T
     inner = back.astype(F32) * mixed_ref[...].astype(F32)
     masks = head_masks(width)
     grad_value_t = []
     grad_key_t = []
-    grad_query = None
-    low = [m.astype(BF16) for m in masks]
+    pair = 2 * head
+    grad_query = [None] * (HEADS // 2)
+    low = pair_masks(pair)
+
+    def change(h):
+        lanes = slice(h // 2 * pair, (h // 2 + 1) * pair)
+        return mm(back[:, lanes] * low[h % 2], value_t_ref[lanes, :])
+
     block = min(64, contacts)
-    grad_prob = mm(back * low[0], value, 1, 1)
+    grad_prob = change(0)
     for h in range(HEADS):
-        following = mm(back * low[h + 1], value, 1, 1) if h + 1 < HEADS else None
+        following = change(h + 1) if h + 1 < HEADS else None
         columns_h = slice(h * contacts, (h + 1) * contacts)
         grad_value_t.append(mm(back_t[h * head : (h + 1) * head], prob_ref[:, columns_h]))
         for r in range(contacts // block):
@@ -225,10 +248,11 @@
             changes[here, columns_h] = prob_ref[here, columns_h] * shift
         grad_score = changes[:, columns_h]
         grad_key_t.append(mm(query_t_ref[h * head : (h + 1) * head, :], grad_score))
-        part = mm(grad_score, keys * low[h])
-        grad_query = part if grad_query is None else grad_query + part
+        lanes = slice(h // 2 * pair, (h // 2 + 1) * pair)
+        part = mm(grad_score, keys[:, lanes] * low[h % 2])
+        grad_query[h // 2] = part if h % 2 == 0 else grad_query[h // 2] + part
         grad_prob = following
-    grad_query = (grad_query * scale).astype(BF16)
+    grad_query = (jnp.concatenate(grad_query, axis=1) * scale).astype(BF16)
     total[0] += mm(normed_t_ref[...], grad_query)
     total[1] += mm(jnp.concatenate(grad_key_t, axis=0).astype(BF16), normed)
     total[2] += mm(jnp.concatenate(grad_value_t, axis=0).astype(BF16), normed)
@@ -256,7 +280,7 @@
     width = weights[0].shape[0]
     groups = span // width
     shapes = [
-        (contacts, HEADS * contacts), (contacts, width),
+        (contacts, HEADS * contacts), (width, contacts),
         (contacts, width), (width, contacts), (contacts, width), (width, contacts),
         (contacts, width), (width, contacts), (contacts, width),
     ]
@@ -279,6 +303,7 @@
             pltpu.VMEM((contacts, 128), F32),
             pltpu.VMEM((128, contacts), F32),
             pltpu.VMEM((1, contacts), F32),
+            pltpu.VMEM((3, width, width), BF16),
         ],
         compiler_params=params(),
         cost_estimate=pl.CostEstimate(
@@ -313,6 +338,7 @@
             pltpu.VMEM((4, width, width), F32),
             pltpu.VMEM((tm_count,) + chunk, BF16),
             pltpu.VMEM((contacts, HEADS * contacts), BF16),
+            pltpu.VMEM((width, width), BF16),
         ],
         compiler_params=params(),
         cost_estimate=pl.CostEstimate(
@@ -373,10 +399,7 @@
         signal[:, :, slab - rim_width :], "tm", [(i, i + 1) for i in range(tm_count - 1)]
     )
     filtered = filter_all(place, signal, rim, fir_taps, count)
-    far = {k: swap(filtered[k], "contact", k) for k in range(count - 1, count // 2 - 1, -1)}
-    far[count - 1], near = lax.optimization_barrier((far[count - 1], filtered[1 : count // 2]))
-    features = [filtered[0]] + [swap(near[k - 1], "contact", k) for k in range(1, count // 2)]
-    features += [far[k] for k in range(count // 2, count)]
+    features = swap_all(filtered, "contact")
     arrived = count - max(2, count // 4)
     features[arrived:], cotangent = lax.optimization_barrier((features[arrived:], cotangent))
     upstream = exchange(cotangent, "contact")

time: 135 us -> 133 us (0.985)
  starting transfers between devices: 42.2 us -> 40.2 us
    ppermute x13, starting transfers between devices: 32.6 us -> 28.2 us  [swap(): lax.ppermute(value, axis, [(i, i ^ k) for i in range(lax.axis_size(axis))])]
    all_to_all x2, starting transfers between devices: 7.24 us -> 9.65 us  [exchange(): return lax.all_to_all(value, axis, split_axis=0, concat_axis=0, tiled=True)]
    ppermute x13, waiting for transfers between devices: 21.3 us -> 19.1 us  [swap(): lax.ppermute(value, axis, [(i, i ^ k) for i in range(lax.axis_size(axis))])]
    all_to_all x2, waiting for transfers between devices: 0.01 us -> 2.17 us  [exchange(): return lax.all_to_all(value, axis, split_axis=0, concat_axis=0, tiled=True)]
  transfers between devices with their start and end apart: 16 -> 16, of which waited for: 9 -> 8; matrix products, arithmetic and copies ran while one was open for 1% -> 1% of each run, Pallas kernels for 25% -> 26%
where the time goes in v9:
time: 133 us
  Pallas kernels  42 us (32%)
  starting transfers between devices  40.2 us (30%)
  blocking collectives  22.8 us (17%)
  waiting for transfers between devices  21.7 us (16%)
  local copies, waits for them, and re-layouts  3.88 us (3%)
  other arithmetic  1.6 us (1%)
    ppermute x13, starting transfers between devices, swap(): lax.ppermute(value, axis, [(i, i ^ k) for i in range(lax.axis_size(axis))])  28.2 us
    all_to_all x2, blocking collectives, exchange(): return lax.all_to_all(value, axis, split_axis=0, concat_axis=0, tiled=True)  22.8 us
    ppermute x13, waiting for transfers between devices, swap(): lax.ppermute(value, axis, [(i, i ^ k) for i in range(lax.axis_size(axis))])  19.1 us
    pallas_call x1, Pallas kernels, forward(): pl.pallas_call(functools.partial(forward_kernel, blocks), grid=(groups,),...  18.7 us
    pallas_call x1, Pallas kernels, backward(): pl.pallas_call(functools.partial(backward_kernel, blocks), grid=(groups,)...  16.3 us
    all_to_all x2, starting transfers between devices, exchange(): return lax.all_to_all(value, axis, split_axis=0, concat_axis=0, tiled=True)  9.65 us
    pallas_call x1, Pallas kernels, filter_all(): pl.pallas_call(filter_kernel, grid=(contacts // rows,), in_specs=[index_s...  4.87 us
    unnamed x33, local copies, waits for them, and re-layouts  2.96 us
  transfers between devices with their start and end apart: 16, of which 8 were waited for; matrix products, arithmetic and copies ran while one was open for 1% of the time, Pallas kernels for 26%

profile of v9, /device:TPU:0, one launch (start us, length us, event | category | flops | bytes accessed | tf_op | source)
XLA Modules:
  0.0 133.0 jit_solution(17071825650128174169)
XLA Ops:
  1.5 2.4 %collective-permute-start = (bf16[8,64,128]{2,1,0:T(8,128)(2,1)S(1)}, bf16[8,64,128]{2,1,0:T(8,128)(2,1)S(1)}, u32[]{:S(2)}, u32[]{:S(2)}) collective-permute-start(bf16[8,64,128]{2,1,0:T(8,128)(2,1)S(1)} %slice.3), channel_id=1, source_target_pairs={{0,8},{8,16},{16,24},{1,9},{9,17},{17,25},{2,10},{10,18},{18,26},{... | collective-permute-start | bytes 393224 | tf_op jit(solution)/shard_map/ppermute | solution.py:398
  5.5 4.9 %filter.1 = (bf16[64,1024]{1,0:T(8,128)(2,1)}, bf16[64,1024]{1,0:T(8,128)(2,1)}, bf16[64,1024]{1,0:T(8,128)(2,1)}, bf16[64,1024]{1,0:T(8,128)(2,1)}, bf16[64,102...) custom-call(s32[2]{0:T(128)} %pad_add_fusion.place_ref, ...), custom_call_target="tpu_custom_call" | custom-call | flops 268435456 | bytes 2097152 | tf_op jit(solution)/shard_map/filter/pallas_call | solution.py:72
  10.4 4.5 %collective-permute-start.6 = (bf16[64,1024]{1,0:T(8,128)(2,1)}, bf16[64,1024]{1,0:T(8,128)(2,1)S(1)}, u32[]{:S(2)}, u32[]{:S(2)}) collective-permute-start(bf16[64,1024]{1,0:T(8,128)(2,1)} %get-tuple-element.34), channel_id=1, source_target_pairs={{0,6},{1,7},{2,4},{3,5},{4,2},{5,3},{6,0},{7,1},{8,14},{9,15},{10,... | collective-permute-start | bytes 393224 | tf_op jit(solution)/shard_map/ppermute | solution.py:371
  14.9 1.2 collective-permute-start.7
  16.4 3.1 %collective-permute-start.3 = (bf16[64,1024]{1,0:T(8,128)(2,1)}, bf16[64,1024]{1,0:T(8,128)(2,1)S(1)}, u32[]{:S(2)}, u32[]{:S(2)}) collective-permute-start(bf16[64,1024]{1,0:T(8,128)(2,1)} %get-tuple-element.31), channel_id=1, source_target_pairs={{0,3},{1,2},{2,1},{3,0},{4,7},{5,6},{6,5},{7,4},{8,11},{9,10},{10,... | collective-permute-start | bytes 393224 | tf_op jit(solution)/shard_map/ppermute | solution.py:371
  19.6 2.1 %collective-permute-start.4 = (bf16[64,1024]{1,0:T(8,128)(2,1)}, bf16[64,1024]{1,0:T(8,128)(2,1)S(1)}, u32[]{:S(2)}, u32[]{:S(2)}) collective-permute-start(bf16[64,1024]{1,0:T(8,128)(2,1)} %get-tuple-element.32), channel_id=1, source_target_pairs={{0,4},{1,5},{2,6},{3,7},{4,0},{5,1},{6,2},{7,3},{8,12},{9,13},{10,... | collective-permute-start | bytes 393224 | tf_op jit(solution)/shard_map/ppermute | solution.py:371
  21.7 1.2 collective-permute-done.7.refs_7_
  22.9 5.0 %collective-permute-start.5 = (bf16[64,1024]{1,0:T(8,128)(2,1)}, bf16[64,1024]{1,0:T(8,128)(2,1)S(1)}, u32[]{:S(2)}, u32[]{:S(2)}) collective-permute-start(bf16[64,1024]{1,0:T(8,128)(2,1)} %get-tuple-element.33), channel_id=1, source_target_pairs={{0,5},{1,4},{2,7},{3,6},{4,1},{5,0},{6,3},{7,2},{8,13},{9,12},{10,... | collective-permute-start | bytes 393224 | tf_op jit(solution)/shard_map/ppermute | solution.py:371
  28.0 4.9 %all-to-all-start.1 = ((bf16[8,64,1024]{2,1,0:T(8,128)(2,1)}), bf16[8,64,1024]{2,1,0:T(8,128)(2,1)S(1)}, u32[]{:S(2)}, u32[]{:S(2)}) async-start(bf16[8,64,1024]{2,1,0:T(8,128)(2,1)} %param.19), calls=%async_computation.1 | async-start | bytes 2097152 | tf_op jit(solution)/shard_map/all_to_all | solution.py:380
  33.0 5.6 %collective-permute-done.5.refs_5_ = bf16[64,1024]{1,0:T(8,128)(2,1)S(1)} collective-permute-done((bf16[64,1024]{1,0:T(8,128)(2,1)}, bf16[64,1024]{1,0:T(8,128)(2,1)S(1)}, u32[]{:S(2)}, u32[]{:S(2)}) %collective-permute-start.5) | collective-permute-done | bytes 131104 | tf_op jit(solution)/shard_map/ppermute | solution.py:371
  39.2 18.7 %forward.1 = (bf16[8,64,1024]{2,1,0:T(8,128)(2,1)}, bf16[512,8192]{1,0:T(8,128)(2,1)}, bf16[256,2048]{1,0:T(8,128)(2,1)}, bf16[512,1024]{1,0:T(8,128)(2,1)}, bf1...) custom-call(s32[2]{0:T(128)} %pad_add_fusion.place_ref, ...), custom_call_target="tpu_custom_call" | custom-call | flops 20000000000 | bytes 10485760 | tf_op jit(solution)/shard_map/forward/pallas_call | solution.py:288
  57.9 2.2 %all-to-all-done.1.up_ref = bf16[8,64,1024]{2,1,0:T(8,128)(2,1)S(1)} async-done(((bf16[8,64,1024]{2,1,0:T(8,128)(2,1)}), bf16[8,64,1024]{2,1,0:T(8,128)(2,1)S(1)}, u32[]{:S(2)}, u32[]{:S(2)}) %all-to-all-start.1) | async-done | bytes 1048608 | tf_op jit(solution)/shard_map/all_to_all | solution.py:380
  60.1 4.7 %all-to-all-start = ((bf16[8,64,1024]{2,1,0:T(8,128)(2,1)}), bf16[8,64,1024]{2,1,0:T(8,128)(2,1)S(1)}, u32[]{:S(2)}, u32[]{:S(2)}) async-start(bf16[8,64,1024]{2,1,0:T(8,128)(2,1)} %get-tuple-element.38), calls=%async_computation | async-start | bytes 2097152 | tf_op jit(solution)/shard_map/all_to_all | solution.py:380
  64.8 16.3 %backward.1 = (bf16[256,256]{1,0:T(8,128)(2,1)}, bf16[256,256]{1,0:T(8,128)(2,1)}, bf16[256,256]{1,0:T(8,128)(2,1)}, bf16[256,256]{1,0:T(8,128)(2,1)}) custom-call(s32[2]{0:T(128)} %pad_add_fusion.place_ref, bf16[256,256]{1,0:T(8,128)(2,1)} %wo_ref.3, bf16[8,64,1024]{2,1,0:T(8,128)(2,1)} %copy-done, bf16[512,8192]{1,0:T(8,128)(2,1)} %get-tuple-element.40.prob_ref, ...), custom_call_target="tpu_custom_call" | custom-call | flops 20000000000 | bytes 10485760 | tf_op jit(solution)/shard_map/backward/pallas_call | solution.py:324
  81.2 9.9 %collective-permute-start.8 = (bf16[256,256]{1,0:T(8,128)(2,1)}, bf16[256,256]{1,0:T(8,128)(2,1)S(1)}, u32[]{:S(2)}, u32[]{:S(2)}) collective-permute-start(bf16[256,256]{1,0:T(8,128)(2,1)} %get-tuple-element.50), channel_id=1, source_target_pairs={{0,8},{8,0},{16,24},{24,16},{1,9},{9,1},{17,25},{25,17},{2,10},{10... | collective-permute-start | bytes 393224 | tf_op jit(solution)/shard_map/ppermute | solution.py:371
  91.1 1.2 collective-permute-done.8
  92.3 4.7 %collective-permute-done.9 = bf16[256,256]{1,0:T(8,128)(2,1)S(1)} collective-permute-done((bf16[256,256]{1,0:T(8,128)(2,1)}, bf16[256,256]{1,0:T(8,128)(2,1)S(1)}, u32[]{:S(2)}, u32[]{:S(2)}) %collective-permute-start.9) | collective-permute-done | bytes 131104 | tf_op jit(solution)/shard_map/ppermute | solution.py:371
  96.9 1.0 add_convert_fusion
  97.9 13.1 %all_to_all.30 = bf16[8,32,256]{2,1,0:T(8,128)(2,1)S(1)} all-to-all(bf16[8,32,256]{2,1,0:T(8,128)(2,1)S(1)} %bitcast.12), channel_id=1, replica_groups=mesh['tm'=4,'contact'=8] {'contact'}, dimensions={0} | all-to-all | bytes 262144 | tf_op jit(solution)/shard_map/all_to_all | solution.py:380
  111.2 9.7 %all_to_all.31 = bf16[8,32,256]{2,1,0:T(8,128)(2,1)S(1)} all-to-all(bf16[8,32,256]{2,1,0:T(8,128)(2,1)S(1)} %bitcast.13), channel_id=1, replica_groups=mesh['tm'=4,'contact'=8] {'contact'}, dimensions={0} | all-to-all | bytes 262144 | tf_op jit(solution)/shard_map/all_to_all | solution.py:380
  120.9 1.2 collective-permute-start.12
  122.8 4.4 %collective-permute-done.12.refs_2_ = bf16[256,256]{1,0:T(8,128)(2,1)S(1)} collective-permute-done((bf16[256,256]{1,0:T(8,128)(2,1)S(1)}, bf16[256,256]{1,0:T(8,128)(2,1)S(1)}, u32[]{:S(2)}, u32[]{:S(2)}) %collective-permute-start.12) | collective-permute-done | bytes 131104 | tf_op jit(solution)/shard_map/ppermute | solution.py:371
  127.2 2.0 %collective-permute-done.13.refs_3_ = bf16[256,256]{1,0:T(8,128)(2,1)S(1)} collective-permute-done((bf16[256,256]{1,0:T(8,128)(2,1)S(1)}, bf16[256,256]{1,0:T(8,128)(2,1)S(1)}, u32[]{:S(2)}, u32[]{:S(2)}) %collective-permute-start.13) | collective-permute-done | bytes 131104 | tf_op jit(solution)/shard_map/ppermute | solution.py:371
  129.9 2.1 %place_all.1 = f32[4,256,256]{2,1,0:T(8,128)} custom-call(s32[2]{0:T(128)} %pad_add_fusion.place_ref, bf16[256,256]{1,0:T(8,128)(2,1)} %bitcast.11, bf16[256,256]{1,0:T(8,128)(2,1)} %copy-done.3, bf16[256,256]{1,0:T(8,128)(2,1)} %copy-done.4, bf16[256,256]{1,0:T(8,128)(2,1)} %copy-done.5), custom_call_target="tpu_custom_call" | custom-call | tf_op jit(solution)/shard_map/place_all/pallas_call | solution.py:360
  (53 shorter events, 6.0 us)
Async XLA Ops:
  1.5 3.3 %collective-permute-start = (bf16[8,64,128]{2,1,0:T(8,128)(2,1)S(1)}, bf16[8,64,128]{2,1,0:T(8,128)(2,1)S(1)}, u32[]{:S(2)}, u32[]{:S(2)}) collective-permute-start(bf16[8,64,128]{2,1,0:T(8,128)(2,1)S(1)} %slice.3), channel_id=1, source_target_pairs={{0,8},{8,16},{16,24},{1,9},{9,17},{17,25},{2,10},{10,18},{18,26},{... | collective-permute-start | bytes 393224 | tf_op jit(solution)/shard_map/ppermute | solution.py:398
  10.4 9.2 %collective-permute-start.6 = (bf16[64,1024]{1,0:T(8,128)(2,1)}, bf16[64,1024]{1,0:T(8,128)(2,1)S(1)}, u32[]{:S(2)}, u32[]{:S(2)}) collective-permute-start(bf16[64,1024]{1,0:T(8,128)(2,1)} %get-tuple-element.34), channel_id=1, source_target_pairs={{0,6},{1,7},{2,4},{3,5},{4,2},{5,3},{6,0},{7,1},{8,14},{9,15},{10,... | collective-permute-start | bytes 393224 | tf_op jit(solution)/shard_map/ppermute | solution.py:371
  14.9 8.0 %collective-permute-start.7 = (bf16[64,1024]{1,0:T(8,128)(2,1)}, bf16[64,1024]{1,0:T(8,128)(2,1)S(1)}, u32[]{:S(2)}, u32[]{:S(2)}) collective-permute-start(bf16[64,1024]{1,0:T(8,128)(2,1)} %get-tuple-element.35), channel_id=1, source_target_pairs={{0,7},{1,6},{2,5},{3,4},{4,3},{5,2},{6,1},{7,0},{8,15},{9,14},{10,... | collective-permute-start | bytes 393224 | tf_op jit(solution)/shard_map/ppermute | solution.py:371
  16.1 16.8 %collective-permute-start.1 = (bf16[64,1024]{1,0:T(8,128)(2,1)}, bf16[64,1024]{1,0:T(8,128)(2,1)S(1)}, u32[]{:S(2)}, u32[]{:S(2)}) collective-permute-start(bf16[64,1024]{1,0:T(8,128)(2,1)} %get-tuple-element.29), channel_id=1, source_target_pairs={{0,1},{1,0},{2,3},{3,2},{4,5},{5,4},{6,7},{7,6},{8,9},{9,8},{10,11... | collective-permute-start | bytes 393224 | tf_op jit(solution)/shard_map/ppermute | solution.py:371
  16.4 16.5 %collective-permute-start.2 = (bf16[64,1024]{1,0:T(8,128)(2,1)}, bf16[64,1024]{1,0:T(8,128)(2,1)S(1)}, u32[]{:S(2)}, u32[]{:S(2)}) collective-permute-start(bf16[64,1024]{1,0:T(8,128)(2,1)} %get-tuple-element.30), channel_id=1, source_target_pairs={{0,2},{1,3},{2,0},{3,1},{4,6},{5,7},{6,4},{7,5},{8,10},{9,11},{10,... | collective-permute-start | bytes 393224 | tf_op jit(solution)/shard_map/ppermute | solution.py:371
  16.4 16.5 %collective-permute-start.3 = (bf16[64,1024]{1,0:T(8,128)(2,1)}, bf16[64,1024]{1,0:T(8,128)(2,1)S(1)}, u32[]{:S(2)}, u32[]{:S(2)}) collective-permute-start(bf16[64,1024]{1,0:T(8,128)(2,1)} %get-tuple-element.31), channel_id=1, source_target_pairs={{0,3},{1,2},{2,1},{3,0},{4,7},{5,6},{6,5},{7,4},{8,11},{9,10},{10,... | collective-permute-start | bytes 393224 | tf_op jit(solution)/shard_map/ppermute | solution.py:371
  19.6 19.0 %copy-start.6 = (bf16[64,1024]{1,0:T(8,128)(2,1)}, bf16[64,1024]{1,0:T(8,128)(2,1)S(1)}, u32[]{:S(2)}) copy-start(bf16[64,1024]{1,0:T(8,128)(2,1)S(1)} %collective-permute-done.6.refs_6_) | copy-start | bytes 393220
  19.6 13.4 %collective-permute-start.4 = (bf16[64,1024]{1,0:T(8,128)(2,1)}, bf16[64,1024]{1,0:T(8,128)(2,1)S(1)}, u32[]{:S(2)}, u32[]{:S(2)}) collective-permute-start(bf16[64,1024]{1,0:T(8,128)(2,1)} %get-tuple-element.32), channel_id=1, source_target_pairs={{0,4},{1,5},{2,6},{3,7},{4,0},{5,1},{6,2},{7,3},{8,12},{9,13},{10,... | collective-permute-start | bytes 393224 | tf_op jit(solution)/shard_map/ppermute | solution.py:371
  22.9 15.7 %copy-start.7 = (bf16[64,1024]{1,0:T(8,128)(2,1)}, bf16[64,1024]{1,0:T(8,128)(2,1)S(1)}, u32[]{:S(2)}) copy-start(bf16[64,1024]{1,0:T(8,128)(2,1)S(1)} %collective-permute-done.7.refs_7_) | copy-start | bytes 393220
  22.9 15.6 %collective-permute-start.5 = (bf16[64,1024]{1,0:T(8,128)(2,1)}, bf16[64,1024]{1,0:T(8,128)(2,1)S(1)}, u32[]{:S(2)}, u32[]{:S(2)}) collective-permute-start(bf16[64,1024]{1,0:T(8,128)(2,1)} %get-tuple-element.33), channel_id=1, source_target_pairs={{0,5},{1,4},{2,7},{3,6},{4,1},{5,0},{6,3},{7,2},{8,13},{9,12},{10,... | collective-permute-start | bytes 393224 | tf_op jit(solution)/shard_map/ppermute | solution.py:371
  28.0 32.1 %all-to-all-start.1 = ((bf16[8,64,1024]{2,1,0:T(8,128)(2,1)}), bf16[8,64,1024]{2,1,0:T(8,128)(2,1)S(1)}, u32[]{:S(2)}, u32[]{:S(2)}) async-start(bf16[8,64,1024]{2,1,0:T(8,128)(2,1)} %param.19), calls=%async_computation.1 | async-start | bytes 2097152 | tf_op jit(solution)/shard_map/all_to_all | solution.py:380
  32.9 5.7 %copy-start.8 = (bf16[64,1024]{1,0:T(8,128)(2,1)}, bf16[64,1024]{1,0:T(8,128)(2,1)S(1)}, u32[]{:S(2)}) copy-start(bf16[64,1024]{1,0:T(8,128)(2,1)S(1)} %collective-permute-done.1.refs_1_) | copy-start | bytes 393220
  32.9 5.7 %copy-start.9 = (bf16[64,1024]{1,0:T(8,128)(2,1)}, bf16[64,1024]{1,0:T(8,128)(2,1)S(1)}, u32[]{:S(2)}) copy-start(bf16[64,1024]{1,0:T(8,128)(2,1)S(1)} %collective-permute-done.2.refs_2_) | copy-start | bytes 393220
  32.9 5.7 %copy-start.10 = (bf16[64,1024]{1,0:T(8,128)(2,1)}, bf16[64,1024]{1,0:T(8,128)(2,1)S(1)}, u32[]{:S(2)}) copy-start(bf16[64,1024]{1,0:T(8,128)(2,1)S(1)} %collective-permute-done.3.refs_3_) | copy-start | bytes 393220
  32.9 5.7 %copy-start.11 = (bf16[64,1024]{1,0:T(8,128)(2,1)}, bf16[64,1024]{1,0:T(8,128)(2,1)S(1)}, u32[]{:S(2)}) copy-start(bf16[64,1024]{1,0:T(8,128)(2,1)S(1)} %collective-permute-done.4.refs_4_) | copy-start | bytes 393220
  60.1 37.8 %all-to-all-start = ((bf16[8,64,1024]{2,1,0:T(8,128)(2,1)}), bf16[8,64,1024]{2,1,0:T(8,128)(2,1)S(1)}, u32[]{:S(2)}, u32[]{:S(2)}) async-start(bf16[8,64,1024]{2,1,0:T(8,128)(2,1)} %get-tuple-element.38), calls=%async_computation | async-start | bytes 2097152 | tf_op jit(solution)/shard_map/all_to_all | solution.py:380
  81.2 10.0 %collective-permute-start.10 = (bf16[256,256]{1,0:T(8,128)(2,1)}, bf16[256,256]{1,0:T(8,128)(2,1)S(1)}, u32[]{:S(2)}, u32[]{:S(2)}) collective-permute-start(bf16[256,256]{1,0:T(8,128)(2,1)} %get-tuple-element.52), channel_id=1, source_target_pairs={{0,24},{8,16},{16,8},{24,0},{1,25},{9,17},{17,9},{25,1},{2,26},{10... | collective-permute-start | bytes 393224 | tf_op jit(solution)/shard_map/ppermute | solution.py:371
  81.2 11.1 %collective-permute-start.8 = (bf16[256,256]{1,0:T(8,128)(2,1)}, bf16[256,256]{1,0:T(8,128)(2,1)S(1)}, u32[]{:S(2)}, u32[]{:S(2)}) collective-permute-start(bf16[256,256]{1,0:T(8,128)(2,1)} %get-tuple-element.50), channel_id=1, source_target_pairs={{0,8},{8,0},{16,24},{24,16},{1,9},{9,1},{17,25},{25,17},{2,10},{10... | collective-permute-start | bytes 393224 | tf_op jit(solution)/shard_map/ppermute | solution.py:371
  91.1 5.9 %collective-permute-start.9 = (bf16[256,256]{1,0:T(8,128)(2,1)}, bf16[256,256]{1,0:T(8,128)(2,1)S(1)}, u32[]{:S(2)}, u32[]{:S(2)}) collective-permute-start(bf16[256,256]{1,0:T(8,128)(2,1)} %get-tuple-element.51), channel_id=1, source_target_pairs={{0,16},{8,24},{16,0},{24,8},{1,17},{9,25},{17,1},{25,9},{2,18},{10... | collective-permute-start | bytes 393224 | tf_op jit(solution)/shard_map/ppermute | solution.py:371
  120.9 8.3 %copy-start.1 = (bf16[8,32,256]{2,1,0:T(8,128)(2,1)}, bf16[8,32,256]{2,1,0:T(8,128)(2,1)S(1)}, u32[]{:S(2)}) copy-start(bf16[8,32,256]{2,1,0:T(8,128)(2,1)S(1)} %all_to_all.31) | copy-start | bytes 393220
  120.9 1.9 %collective-permute-start.11 = (bf16[256,256]{1,0:T(8,128)(2,1)S(1)}, bf16[256,256]{1,0:T(8,128)(2,1)S(1)}, u32[]{:S(2)}, u32[]{:S(2)}) collective-permute-start(bf16[256,256]{1,0:T(8,128)(2,1)S(1)} %bitcast.8), channel_id=1, source_target_pairs={{0,8},{8,0},{16,24},{24,16},{1,9},{9,1},{17,25},{25,17},{2,10},{10... | collective-permute-start | bytes 393224 | tf_op jit(solution)/shard_map/ppermute | solution.py:371
  120.9 6.3 %collective-permute-start.12 = (bf16[256,256]{1,0:T(8,128)(2,1)S(1)}, bf16[256,256]{1,0:T(8,128)(2,1)S(1)}, u32[]{:S(2)}, u32[]{:S(2)}) collective-permute-start(bf16[256,256]{1,0:T(8,128)(2,1)S(1)} %bitcast.9), channel_id=1, source_target_pairs={{0,16},{8,24},{16,0},{24,8},{1,17},{9,25},{17,1},{25,9},{2,18},{10... | collective-permute-start | bytes 393224 | tf_op jit(solution)/shard_map/ppermute | solution.py:371
  122.1 7.1 %collective-permute-start.13 = (bf16[256,256]{1,0:T(8,128)(2,1)S(1)}, bf16[256,256]{1,0:T(8,128)(2,1)S(1)}, u32[]{:S(2)}, u32[]{:S(2)}) collective-permute-start(bf16[256,256]{1,0:T(8,128)(2,1)S(1)} %bitcast.10), channel_id=1, source_target_pairs={{0,24},{8,16},{16,8},{24,0},{1,25},{9,17},{17,9},{25,1},{2,26},{10... | collective-permute-start | bytes 393224 | tf_op jit(solution)/shard_map/ppermute | solution.py:371
  122.8 6.5 %copy-start.3 = (bf16[256,256]{1,0:T(8,128)(2,1)}, bf16[256,256]{1,0:T(8,128)(2,1)S(1)}, u32[]{:S(2)}) copy-start(bf16[256,256]{1,0:T(8,128)(2,1)S(1)} %collective-permute-done.11.refs_1_) | copy-start | bytes 393220
  (5 other events, 8.8 us)

commit v10 on v8

--- a/solution.py
+++ b/solution.py
@@ -23,7 +23,7 @@
 
 
 def params():
-    return pltpu.CompilerParams(vmem_limit_bytes=56 * 2**20)
+    return pltpu.CompilerParams(vmem_limit_bytes=63 * 2**20)
 
 
 def filter_kernel(place_ref, sig_ref, rim_ref, taps_ref, *refs):
@@ -91,6 +91,11 @@
     )(place, signal, rim, taps)
 
 
+def pair_masks(pair):
+    lane = lax.broadcasted_iota(jnp.int32, (1, pair), 1)
+    return [(lane < pair // 2).astype(F32).astype(BF16), (lane >= pair // 2).astype(F32).astype(BF16)]
+
+
 def head_masks(width):
     lane_head = lax.broadcasted_iota(jnp.int32, (1, width), 1) // (width // HEADS)
     return [(lane_head == h).astype(F32) for h in range(HEADS)]
@@ -102,7 +107,7 @@
     feat_refs = refs[:blocks]
     (
         out_ref, prob_ref, value_ref, keys_ref, query_t_ref, normed_ref, normed_t_ref, mixed_ref,
-        mixed_t_ref, inverse_ref, counts, columns, packed, live_row,
+        mixed_t_ref, inverse_ref, counts, columns, packed, live_row, turned_w,
     ) = refs[blocks:]
     rows, width = feat_refs[0].shape
     contacts = rows * blocks
@@ -133,6 +138,8 @@
         columns[:, 0:1] = turned[:, 0:1]
         columns[:, 1:2] = turned[:, 1:2]
         columns[:, 2:3] = jnp.sum(total, axis=1, keepdims=True)
+        turned_w[0] = wq_ref[...].T
+        turned_w[1] = wk_ref[...].T
 
     live = columns[:, 0:1]
     coef = columns[:, 1:2]
@@ -146,37 +153,44 @@
     query = (mm(normed, wq_ref[...]) * scale).astype(BF16)
     keys = mm(normed, wk_ref[...]).astype(BF16)
     value = mm(normed, wv_ref[...]).astype(BF16)
+    normed_t = normed.T
+    keys_t = mm(turned_w[1], normed_t).astype(BF16)
     value_ref[...] = value
     keys_ref[...] = keys
-    query_t_ref[...] = query.T
+    query_t_ref[...] = (mm(turned_w[0], normed_t) * scale).astype(BF16)
     normed_ref[...] = normed
-    normed_t_ref[...] = normed.T
-    masks = [m.astype(BF16) for m in head_masks(width)]
+    normed_t_ref[...] = normed_t
+    pair = 2 * width // HEADS
+    masks = pair_masks(pair)
+
+    def score(h):
+        lanes = slice(h // 2 * pair, (h // 2 + 1) * pair)
+        return mm(query[:, lanes] * masks[h % 2], keys_t[lanes, :])
+
     bias = jnp.where(live_row[...] > 0, 0.0, -1e30)
     block = min(64, contacts)
-    lane_head = lax.broadcasted_iota(jnp.int32, (block, width), 1) // (width // HEADS)
-    shares = [[] for _ in range(contacts // block)]
-    scores = mm(query * masks[0], keys, 1, 1)
-    mixed = None
+    scores = score(0)
+    products = []
     for h in range(HEADS):
-        following = mm(query * masks[h + 1], keys, 1, 1) if h + 1 < HEADS else None
+        following = score(h + 1) if h + 1 < HEADS else None
         columns_h = slice(h * contacts, (h + 1) * contacts)
-        for r, share in enumerate(shares):
+        for r in range(contacts // block):
             here = slice(r * block, (r + 1) * block)
             part = scores[here] + bias
             raised = jnp.exp(part - jnp.max(part, axis=1, keepdims=True))
             prob_ref[here, columns_h] = raised.astype(BF16)
-            share.append(1.0 / jnp.sum(raised, axis=1, keepdims=True))
-        part = mm(prob_ref[:, columns_h], value * masks[h])
-        mixed = part if mixed is None else mixed + part
+        lanes = slice(h // 2 * pair, (h // 2 + 1) * pair)
+        with_ones = value[:, lanes] * masks[h % 2] + masks[1 - h % 2]
+        products.append(mm(prob_ref[:, columns_h], with_ones))
         scores = following
-    for r, share in enumerate(shares):
-        here = slice(r * block, (r + 1) * block)
-        inverse = jnp.broadcast_to(share[0], (block, width))
-        for h in range(1, HEADS):
-            inverse = jnp.where(lane_head >= h, share[h], inverse)
-        inverse_ref[here, :] = inverse
-    mixed = (mixed * inverse_ref[...]).astype(BF16)
+    low_lanes = lax.broadcasted_iota(jnp.int32, (contacts, pair), 1) < pair // 2
+    mixed = []
+    for p in range(HEADS // 2):
+        even, odd = products[2 * p], products[2 * p + 1]
+        inverse = 1.0 / pltpu.roll(jnp.where(low_lanes, odd, even), pair // 2, 1)
+        inverse_ref[:, p * pair : (p + 1) * pair] = inverse
+        mixed.append((jnp.where(low_lanes, even, odd) * inverse).astype(BF16))
+    mixed = jnp.concatenate(mixed, axis=1)
     attended = mm(mixed, wo_ref[...]).astype(BF16)
     for k in range(blocks):
         out_ref[me ^ k] = attended[k * rows : (k + 1) * rows]
@@ -279,6 +293,7 @@
             pltpu.VMEM((contacts, 128), F32),
             pltpu.VMEM((128, contacts), F32),
             pltpu.VMEM((1, contacts), F32),
+            pltpu.VMEM((2, width, width), BF16),
         ],
         compiler_params=params(),
         cost_estimate=pl.CostEstimate(
@@ -373,10 +388,7 @@
         signal[:, :, slab - rim_width :], "tm", [(i, i + 1) for i in range(tm_count - 1)]
     )
     filtered = filter_all(place, signal, rim, fir_taps, count)
-    far = {k: swap(filtered[k], "contact", k) for k in range(count - 1, count // 2 - 1, -1)}
-    far[count - 1], near = lax.optimization_barrier((far[count - 1], filtered[1 : count // 2]))
-    features = [filtered[0]] + [swap(near[k - 1], "contact", k) for k in range(1, count // 2)]
-    features += [far[k] for k in range(count // 2, count)]
+    features = swap_all(filtered, "contact")
     arrived = count - max(2, count // 4)
     features[arrived:], cotangent = lax.optimization_barrier((features[arrived:], cotangent))
     upstream = exchange(cotangent, "contact")

time: 135 us -> 133 us (0.985)
  starting transfers between devices: 42.2 us -> 39.7 us
    ppermute x13, starting transfers between devices: 32.6 us -> 28.1 us  [swap(): lax.ppermute(value, axis, [(i, i ^ k) for i in range(lax.axis_size(axis))])]
    ppermute x13, waiting for transfers between devices: 21.3 us -> 19.1 us  [swap(): lax.ppermute(value, axis, [(i, i ^ k) for i in range(lax.axis_size(axis))])]
    all_to_all x2, starting transfers between devices: 7.24 us -> 9.32 us  [exchange(): return lax.all_to_all(value, axis, split_axis=0, concat_axis=0, tiled=True)]
    all_to_all x2, waiting for transfers between devices: 0.01 us -> 2.08 us  [exchange(): return lax.all_to_all(value, axis, split_axis=0, concat_axis=0, tiled=True)]
    unnamed x33 -> x31, local copies, waits for them, and re-layouts: 2.96 us -> 4.22 us
  transfers between devices with their start and end apart: 16 -> 16, of which waited for: 9 -> 8; matrix products, arithmetic and copies ran while one was open for 1% -> 1% of each run, Pallas kernels for 25% -> 25%
where the time goes in v10:
time: 133 us; the launch traced here: 132 us
  Pallas kernels  40.7 us (31%)
  starting transfers between devices  39.7 us (30%)
  blocking collectives  22.9 us (17%)
  waiting for transfers between devices  21.6 us (16%)
  local copies, waits for them, and re-layouts  5.14 us (4%)
  other arithmetic  1.6 us (1%)
    ppermute x13, starting transfers between devices, swap(): lax.ppermute(value, axis, [(i, i ^ k) for i in range(lax.axis_size(axis))])  28.1 us
    all_to_all x2, blocking collectives, exchange(): return lax.all_to_all(value, axis, split_axis=0, concat_axis=0, tiled=True)  22.9 us
    ppermute x13, waiting for transfers between devices, swap(): lax.ppermute(value, axis, [(i, i ^ k) for i in range(lax.axis_size(axis))])  19.1 us
    pallas_call x1, Pallas kernels, forward(): pl.pallas_call(functools.partial(forward_kernel, blocks), grid=(groups,),...  18.3 us
    pallas_call x1, Pallas kernels, backward(): pl.pallas_call(functools.partial(backward_kernel, blocks), grid=(groups,)...  15.3 us
    all_to_all x2, starting transfers between devices, exchange(): return lax.all_to_all(value, axis, split_axis=0, concat_axis=0, tiled=True)  9.32 us
    pallas_call x1, Pallas kernels, filter_all(): pl.pallas_call(filter_kernel, grid=(contacts // rows,), in_specs=[index_s...  4.86 us
    unnamed x31, local copies, waits for them, and re-layouts  4.22 us
  transfers between devices with their start and end apart: 16, of which 8 were waited for; matrix products, arithmetic and copies ran while one was open for 1% of the time, Pallas kernels for 25%

profile of v10, /device:TPU:0, one launch (start us, length us, event | category | flops | bytes accessed | tf_op | source)
XLA Modules:
  0.0 132.5 jit_solution(11492531707960607871)
XLA Ops:
  1.5 2.4 %collective-permute-start = (bf16[8,64,128]{2,1,0:T(8,128)(2,1)S(1)}, bf16[8,64,128]{2,1,0:T(8,128)(2,1)S(1)}, u32[]{:S(2)}, u32[]{:S(2)}) collective-permute-start(bf16[8,64,128]{2,1,0:T(8,128)(2,1)S(1)} %slice.3), channel_id=1, source_target_pairs={{0,8},{8,16},{16,24},{1,9},{9,17},{17,25},{2,10},{10,18},{18,26},{... | collective-permute-start | bytes 393224 | tf_op jit(solution)/shard_map/ppermute | solution.py:387
  5.5 4.9 %filter.1 = (bf16[64,1024]{1,0:T(8,128)(2,1)}, bf16[64,1024]{1,0:T(8,128)(2,1)}, bf16[64,1024]{1,0:T(8,128)(2,1)}, bf16[64,1024]{1,0:T(8,128)(2,1)}, bf16[64,102...) custom-call(s32[2]{0:T(128)} %pad_add_fusion.place_ref, ...), custom_call_target="tpu_custom_call" | custom-call | flops 268435456 | bytes 2097152 | tf_op jit(solution)/shard_map/filter/pallas_call | solution.py:72
  10.4 4.5 %collective-permute-start.6 = (bf16[64,1024]{1,0:T(8,128)(2,1)}, bf16[64,1024]{1,0:T(8,128)(2,1)S(1)}, u32[]{:S(2)}, u32[]{:S(2)}) collective-permute-start(bf16[64,1024]{1,0:T(8,128)(2,1)} %get-tuple-element.34), channel_id=1, source_target_pairs={{0,6},{1,7},{2,4},{3,5},{4,2},{5,3},{6,0},{7,1},{8,14},{9,15},{10,... | collective-permute-start | bytes 393224 | tf_op jit(solution)/shard_map/ppermute | solution.py:360
  14.9 1.2 collective-permute-start.7
  16.4 3.1 %collective-permute-start.3 = (bf16[64,1024]{1,0:T(8,128)(2,1)}, bf16[64,1024]{1,0:T(8,128)(2,1)S(1)}, u32[]{:S(2)}, u32[]{:S(2)}) collective-permute-start(bf16[64,1024]{1,0:T(8,128)(2,1)} %get-tuple-element.31), channel_id=1, source_target_pairs={{0,3},{1,2},{2,1},{3,0},{4,7},{5,6},{6,5},{7,4},{8,11},{9,10},{10,... | collective-permute-start | bytes 393224 | tf_op jit(solution)/shard_map/ppermute | solution.py:360
  19.6 2.1 %collective-permute-start.4 = (bf16[64,1024]{1,0:T(8,128)(2,1)}, bf16[64,1024]{1,0:T(8,128)(2,1)S(1)}, u32[]{:S(2)}, u32[]{:S(2)}) collective-permute-start(bf16[64,1024]{1,0:T(8,128)(2,1)} %get-tuple-element.32), channel_id=1, source_target_pairs={{0,4},{1,5},{2,6},{3,7},{4,0},{5,1},{6,2},{7,3},{8,12},{9,13},{10,... | collective-permute-start | bytes 393224 | tf_op jit(solution)/shard_map/ppermute | solution.py:360
  21.7 1.2 collective-permute-done.7.refs_7_
  22.9 5.0 %collective-permute-start.5 = (bf16[64,1024]{1,0:T(8,128)(2,1)}, bf16[64,1024]{1,0:T(8,128)(2,1)S(1)}, u32[]{:S(2)}, u32[]{:S(2)}) collective-permute-start(bf16[64,1024]{1,0:T(8,128)(2,1)} %get-tuple-element.33), channel_id=1, source_target_pairs={{0,5},{1,4},{2,7},{3,6},{4,1},{5,0},{6,3},{7,2},{8,13},{9,12},{10,... | collective-permute-start | bytes 393224 | tf_op jit(solution)/shard_map/ppermute | solution.py:360
  28.0 4.9 %all-to-all-start.1 = ((bf16[8,64,1024]{2,1,0:T(8,128)(2,1)}), bf16[8,64,1024]{2,1,0:T(8,128)(2,1)}, u32[]{:S(2)}, u32[]{:S(2)}) async-start(bf16[8,64,1024]{2,1,0:T(8,128)(2,1)} %param.19), calls=%async_computation.1 | async-start | bytes 2097152 | tf_op jit(solution)/shard_map/all_to_all | solution.py:369
  33.0 5.6 %collective-permute-done.5.refs_5_ = bf16[64,1024]{1,0:T(8,128)(2,1)S(1)} collective-permute-done((bf16[64,1024]{1,0:T(8,128)(2,1)}, bf16[64,1024]{1,0:T(8,128)(2,1)S(1)}, u32[]{:S(2)}, u32[]{:S(2)}) %collective-permute-start.5) | collective-permute-done | bytes 131104 | tf_op jit(solution)/shard_map/ppermute | solution.py:360
  39.2 18.3 %forward.1 = (bf16[8,64,1024]{2,1,0:T(8,128)(2,1)}, bf16[512,8192]{1,0:T(8,128)(2,1)}, bf16[512,1024]{1,0:T(8,128)(2,1)}, bf16[512,1024]{1,0:T(8,128)(2,1)}, bf1...) custom-call(s32[2]{0:T(128)} %pad_add_fusion.place_ref, ...), custom_call_target="tpu_custom_call" | custom-call | flops 20000000000 | bytes 10485760 | tf_op jit(solution)/shard_map/forward/pallas_call | solution.py:278
  57.6 2.1 %all-to-all-done.1.up_ref = bf16[8,64,1024]{2,1,0:T(8,128)(2,1)} async-done(((bf16[8,64,1024]{2,1,0:T(8,128)(2,1)}), bf16[8,64,1024]{2,1,0:T(8,128)(2,1)}, u32[]{:S(2)}, u32[]{:S(2)}) %all-to-all-start.1) | async-done | bytes 1048608 | tf_op jit(solution)/shard_map/all_to_all | solution.py:369
  59.7 4.4 %all-to-all-start = ((bf16[8,64,1024]{2,1,0:T(8,128)(2,1)}), bf16[8,64,1024]{2,1,0:T(8,128)(2,1)}, u32[]{:S(2)}, u32[]{:S(2)}) async-start(bf16[8,64,1024]{2,1,0:T(8,128)(2,1)} %get-tuple-element.38), calls=%async_computation | async-start | bytes 2097152 | tf_op jit(solution)/shard_map/all_to_all | solution.py:369
  64.1 15.3 %backward.1 = (bf16[256,256]{1,0:T(8,128)(2,1)}, bf16[256,256]{1,0:T(8,128)(2,1)}, bf16[256,256]{1,0:T(8,128)(2,1)}, bf16[256,256]{1,0:T(8,128)(2,1)}) custom-call(s32[2]{0:T(128)} %pad_add_fusion.place_ref, bf16[256,256]{1,0:T(8,128)(2,1)} %wo_ref.3, bf16[8,64,1024]{2,1,0:T(8,128)(2,1)} %all-to-all-done.1.up_ref, ...), custom_call_target="tpu_custom_call" | custom-call | flops 20000000000 | bytes 10485760 | tf_op jit(solution)/shard_map/backward/pallas_call | solution.py:314
  79.9 9.3 %collective-permute-start.8 = (bf16[256,256]{1,0:T(8,128)(2,1)}, bf16[256,256]{1,0:T(8,128)(2,1)S(1)}, u32[]{:S(2)}, u32[]{:S(2)}) collective-permute-start(bf16[256,256]{1,0:T(8,128)(2,1)} %get-tuple-element.50), channel_id=1, source_target_pairs={{0,8},{8,0},{16,24},{24,16},{1,9},{9,1},{17,25},{25,17},{2,10},{10... | collective-permute-start | bytes 393224 | tf_op jit(solution)/shard_map/ppermute | solution.py:360
  89.3 1.2 collective-permute-done.8
  90.4 4.7 %collective-permute-done.9 = bf16[256,256]{1,0:T(8,128)(2,1)S(1)} collective-permute-done((bf16[256,256]{1,0:T(8,128)(2,1)}, bf16[256,256]{1,0:T(8,128)(2,1)S(1)}, u32[]{:S(2)}, u32[]{:S(2)}) %collective-permute-start.9) | collective-permute-done | bytes 131104 | tf_op jit(solution)/shard_map/ppermute | solution.py:360
  96.1 13.1 %all_to_all.30 = bf16[8,32,256]{2,1,0:T(8,128)(2,1)S(1)} all-to-all(bf16[8,32,256]{2,1,0:T(8,128)(2,1)S(1)} %bitcast.12), channel_id=1, replica_groups=mesh['tm'=4,'contact'=8] {'contact'}, dimensions={0} | all-to-all | bytes 262144 | tf_op jit(solution)/shard_map/all_to_all | solution.py:369
  109.3 9.7 %all_to_all.31 = bf16[8,32,256]{2,1,0:T(8,128)(2,1)S(1)} all-to-all(bf16[8,32,256]{2,1,0:T(8,128)(2,1)S(1)} %bitcast.13), channel_id=1, replica_groups=mesh['tm'=4,'contact'=8] {'contact'}, dimensions={0} | all-to-all | bytes 262144 | tf_op jit(solution)/shard_map/all_to_all | solution.py:369
  119.1 1.2 collective-permute-start.12
  120.9 4.4 %collective-permute-done.12.refs_2_ = bf16[256,256]{1,0:T(8,128)(2,1)S(1)} collective-permute-done((bf16[256,256]{1,0:T(8,128)(2,1)S(1)}, bf16[256,256]{1,0:T(8,128)(2,1)S(1)}, u32[]{:S(2)}, u32[]{:S(2)}) %collective-permute-start.12) | collective-permute-done | bytes 131104 | tf_op jit(solution)/shard_map/ppermute | solution.py:360
  125.4 2.0 %collective-permute-done.13.refs_3_ = bf16[256,256]{1,0:T(8,128)(2,1)S(1)} collective-permute-done((bf16[256,256]{1,0:T(8,128)(2,1)S(1)}, bf16[256,256]{1,0:T(8,128)(2,1)S(1)}, u32[]{:S(2)}, u32[]{:S(2)}) %collective-permute-start.13) | collective-permute-done | bytes 131104 | tf_op jit(solution)/shard_map/ppermute | solution.py:360
  128.0 2.1 %place_all.1 = f32[4,256,256]{2,1,0:T(8,128)} custom-call(s32[2]{0:T(128)} %pad_add_fusion.place_ref, bf16[256,256]{1,0:T(8,128)(2,1)} %bitcast.11, bf16[256,256]{1,0:T(8,128)(2,1)} %copy-done.2, bf16[256,256]{1,0:T(8,128)(2,1)} %copy-done.3, bf16[256,256]{1,0:T(8,128)(2,1)} %copy-done.4), custom_call_target="tpu_custom_call" | custom-call | tf_op jit(solution)/shard_map/place_all/pallas_call | solution.py:349
  130.2 2.3 %copy.20 = bf16[8,64,1024]{2,1,0:T(8,128)(2,1)} copy(bf16[8,64,1024]{2,1,0:T(8,128)(2,1)} %all-to-all-done) | data formatting | bytes 2097152
  (51 shorter events, 6.4 us)
Async XLA Ops:
  1.5 3.3 %collective-permute-start = (bf16[8,64,128]{2,1,0:T(8,128)(2,1)S(1)}, bf16[8,64,128]{2,1,0:T(8,128)(2,1)S(1)}, u32[]{:S(2)}, u32[]{:S(2)}) collective-permute-start(bf16[8,64,128]{2,1,0:T(8,128)(2,1)S(1)} %slice.3), channel_id=1, source_target_pairs={{0,8},{8,16},{16,24},{1,9},{9,17},{17,25},{2,10},{10,18},{18,26},{... | collective-permute-start | bytes 393224 | tf_op jit(solution)/shard_map/ppermute | solution.py:387
  10.4 9.2 %collective-permute-start.6 = (bf16[64,1024]{1,0:T(8,128)(2,1)}, bf16[64,1024]{1,0:T(8,128)(2,1)S(1)}, u32[]{:S(2)}, u32[]{:S(2)}) collective-permute-start(bf16[64,1024]{1,0:T(8,128)(2,1)} %get-tuple-element.34), channel_id=1, source_target_pairs={{0,6},{1,7},{2,4},{3,5},{4,2},{5,3},{6,0},{7,1},{8,14},{9,15},{10,... | collective-permute-start | bytes 393224 | tf_op jit(solution)/shard_map/ppermute | solution.py:360
  14.9 8.0 %collective-permute-start.7 = (bf16[64,1024]{1,0:T(8,128)(2,1)}, bf16[64,1024]{1,0:T(8,128)(2,1)S(1)}, u32[]{:S(2)}, u32[]{:S(2)}) collective-permute-start(bf16[64,1024]{1,0:T(8,128)(2,1)} %get-tuple-element.35), channel_id=1, source_target_pairs={{0,7},{1,6},{2,5},{3,4},{4,3},{5,2},{6,1},{7,0},{8,15},{9,14},{10,... | collective-permute-start | bytes 393224 | tf_op jit(solution)/shard_map/ppermute | solution.py:360
  16.1 16.8 %collective-permute-start.1 = (bf16[64,1024]{1,0:T(8,128)(2,1)}, bf16[64,1024]{1,0:T(8,128)(2,1)S(1)}, u32[]{:S(2)}, u32[]{:S(2)}) collective-permute-start(bf16[64,1024]{1,0:T(8,128)(2,1)} %get-tuple-element.29), channel_id=1, source_target_pairs={{0,1},{1,0},{2,3},{3,2},{4,5},{5,4},{6,7},{7,6},{8,9},{9,8},{10,11... | collective-permute-start | bytes 393224 | tf_op jit(solution)/shard_map/ppermute | solution.py:360
  16.4 16.5 %collective-permute-start.2 = (bf16[64,1024]{1,0:T(8,128)(2,1)}, bf16[64,1024]{1,0:T(8,128)(2,1)S(1)}, u32[]{:S(2)}, u32[]{:S(2)}) collective-permute-start(bf16[64,1024]{1,0:T(8,128)(2,1)} %get-tuple-element.30), channel_id=1, source_target_pairs={{0,2},{1,3},{2,0},{3,1},{4,6},{5,7},{6,4},{7,5},{8,10},{9,11},{10,... | collective-permute-start | bytes 393224 | tf_op jit(solution)/shard_map/ppermute | solution.py:360
  16.4 16.5 %collective-permute-start.3 = (bf16[64,1024]{1,0:T(8,128)(2,1)}, bf16[64,1024]{1,0:T(8,128)(2,1)S(1)}, u32[]{:S(2)}, u32[]{:S(2)}) collective-permute-start(bf16[64,1024]{1,0:T(8,128)(2,1)} %get-tuple-element.31), channel_id=1, source_target_pairs={{0,3},{1,2},{2,1},{3,0},{4,7},{5,6},{6,5},{7,4},{8,11},{9,10},{10,... | collective-permute-start | bytes 393224 | tf_op jit(solution)/shard_map/ppermute | solution.py:360
  19.6 19.0 %copy-start.5 = (bf16[64,1024]{1,0:T(8,128)(2,1)}, bf16[64,1024]{1,0:T(8,128)(2,1)S(1)}, u32[]{:S(2)}) copy-start(bf16[64,1024]{1,0:T(8,128)(2,1)S(1)} %collective-permute-done.6.refs_6_) | copy-start | bytes 393220
  19.6 13.4 %collective-permute-start.4 = (bf16[64,1024]{1,0:T(8,128)(2,1)}, bf16[64,1024]{1,0:T(8,128)(2,1)S(1)}, u32[]{:S(2)}, u32[]{:S(2)}) collective-permute-start(bf16[64,1024]{1,0:T(8,128)(2,1)} %get-tuple-element.32), channel_id=1, source_target_pairs={{0,4},{1,5},{2,6},{3,7},{4,0},{5,1},{6,2},{7,3},{8,12},{9,13},{10,... | collective-permute-start | bytes 393224 | tf_op jit(solution)/shard_map/ppermute | solution.py:360
  22.9 15.7 %copy-start.6 = (bf16[64,1024]{1,0:T(8,128)(2,1)}, bf16[64,1024]{1,0:T(8,128)(2,1)S(1)}, u32[]{:S(2)}) copy-start(bf16[64,1024]{1,0:T(8,128)(2,1)S(1)} %collective-permute-done.7.refs_7_) | copy-start | bytes 393220
  22.9 15.6 %collective-permute-start.5 = (bf16[64,1024]{1,0:T(8,128)(2,1)}, bf16[64,1024]{1,0:T(8,128)(2,1)S(1)}, u32[]{:S(2)}, u32[]{:S(2)}) collective-permute-start(bf16[64,1024]{1,0:T(8,128)(2,1)} %get-tuple-element.33), channel_id=1, source_target_pairs={{0,5},{1,4},{2,7},{3,6},{4,1},{5,0},{6,3},{7,2},{8,13},{9,12},{10,... | collective-permute-start | bytes 393224 | tf_op jit(solution)/shard_map/ppermute | solution.py:360
  28.0 31.7 %all-to-all-start.1 = ((bf16[8,64,1024]{2,1,0:T(8,128)(2,1)}), bf16[8,64,1024]{2,1,0:T(8,128)(2,1)}, u32[]{:S(2)}, u32[]{:S(2)}) async-start(bf16[8,64,1024]{2,1,0:T(8,128)(2,1)} %param.19), calls=%async_computation.1 | async-start | bytes 2097152 | tf_op jit(solution)/shard_map/all_to_all | solution.py:369
  32.9 5.7 %copy-start.7 = (bf16[64,1024]{1,0:T(8,128)(2,1)}, bf16[64,1024]{1,0:T(8,128)(2,1)S(1)}, u32[]{:S(2)}) copy-start(bf16[64,1024]{1,0:T(8,128)(2,1)S(1)} %collective-permute-done.1.refs_1_) | copy-start | bytes 393220
  32.9 5.7 %copy-start.8 = (bf16[64,1024]{1,0:T(8,128)(2,1)}, bf16[64,1024]{1,0:T(8,128)(2,1)S(1)}, u32[]{:S(2)}) copy-start(bf16[64,1024]{1,0:T(8,128)(2,1)S(1)} %collective-permute-done.2.refs_2_) | copy-start | bytes 393220
  32.9 5.7 %copy-start.9 = (bf16[64,1024]{1,0:T(8,128)(2,1)}, bf16[64,1024]{1,0:T(8,128)(2,1)S(1)}, u32[]{:S(2)}) copy-start(bf16[64,1024]{1,0:T(8,128)(2,1)S(1)} %collective-permute-done.3.refs_3_) | copy-start | bytes 393220
  32.9 5.7 %copy-start.10 = (bf16[64,1024]{1,0:T(8,128)(2,1)}, bf16[64,1024]{1,0:T(8,128)(2,1)S(1)}, u32[]{:S(2)}) copy-start(bf16[64,1024]{1,0:T(8,128)(2,1)S(1)} %collective-permute-done.4.refs_4_) | copy-start | bytes 393220
  59.7 36.4 %all-to-all-start = ((bf16[8,64,1024]{2,1,0:T(8,128)(2,1)}), bf16[8,64,1024]{2,1,0:T(8,128)(2,1)}, u32[]{:S(2)}, u32[]{:S(2)}) async-start(bf16[8,64,1024]{2,1,0:T(8,128)(2,1)} %get-tuple-element.38), calls=%async_computation | async-start | bytes 2097152 | tf_op jit(solution)/shard_map/all_to_all | solution.py:369
  79.4 9.9 %collective-permute-start.10 = (bf16[256,256]{1,0:T(8,128)(2,1)}, bf16[256,256]{1,0:T(8,128)(2,1)S(1)}, u32[]{:S(2)}, u32[]{:S(2)}) collective-permute-start(bf16[256,256]{1,0:T(8,128)(2,1)} %get-tuple-element.52), channel_id=1, source_target_pairs={{0,24},{8,16},{16,8},{24,0},{1,25},{9,17},{17,9},{25,1},{2,26},{10... | collective-permute-start | bytes 393224 | tf_op jit(solution)/shard_map/ppermute | solution.py:360
  79.9 10.5 %collective-permute-start.8 = (bf16[256,256]{1,0:T(8,128)(2,1)}, bf16[256,256]{1,0:T(8,128)(2,1)S(1)}, u32[]{:S(2)}, u32[]{:S(2)}) collective-permute-start(bf16[256,256]{1,0:T(8,128)(2,1)} %get-tuple-element.50), channel_id=1, source_target_pairs={{0,8},{8,0},{16,24},{24,16},{1,9},{9,1},{17,25},{25,17},{2,10},{10... | collective-permute-start | bytes 393224 | tf_op jit(solution)/shard_map/ppermute | solution.py:360
  89.2 5.9 %collective-permute-start.9 = (bf16[256,256]{1,0:T(8,128)(2,1)}, bf16[256,256]{1,0:T(8,128)(2,1)S(1)}, u32[]{:S(2)}, u32[]{:S(2)}) collective-permute-start(bf16[256,256]{1,0:T(8,128)(2,1)} %get-tuple-element.51), channel_id=1, source_target_pairs={{0,16},{8,24},{16,0},{24,8},{1,17},{9,25},{17,1},{25,9},{2,18},{10... | collective-permute-start | bytes 393224 | tf_op jit(solution)/shard_map/ppermute | solution.py:360
  119.1 8.3 %copy-start = (bf16[8,32,256]{2,1,0:T(8,128)(2,1)}, bf16[8,32,256]{2,1,0:T(8,128)(2,1)S(1)}, u32[]{:S(2)}) copy-start(bf16[8,32,256]{2,1,0:T(8,128)(2,1)S(1)} %all_to_all.31) | copy-start | bytes 393220
  119.1 1.9 %collective-permute-start.11 = (bf16[256,256]{1,0:T(8,128)(2,1)S(1)}, bf16[256,256]{1,0:T(8,128)(2,1)S(1)}, u32[]{:S(2)}, u32[]{:S(2)}) collective-permute-start(bf16[256,256]{1,0:T(8,128)(2,1)S(1)} %bitcast.8), channel_id=1, source_target_pairs={{0,8},{8,0},{16,24},{24,16},{1,9},{9,1},{17,25},{25,17},{2,10},{10... | collective-permute-start | bytes 393224 | tf_op jit(solution)/shard_map/ppermute | solution.py:360
  119.1 6.3 %collective-permute-start.12 = (bf16[256,256]{1,0:T(8,128)(2,1)S(1)}, bf16[256,256]{1,0:T(8,128)(2,1)S(1)}, u32[]{:S(2)}, u32[]{:S(2)}) collective-permute-start(bf16[256,256]{1,0:T(8,128)(2,1)S(1)} %bitcast.9), channel_id=1, source_target_pairs={{0,16},{8,24},{16,0},{24,8},{1,17},{9,25},{17,1},{25,9},{2,18},{10... | collective-permute-start | bytes 393224 | tf_op jit(solution)/shard_map/ppermute | solution.py:360
  120.2 7.1 %collective-permute-start.13 = (bf16[256,256]{1,0:T(8,128)(2,1)S(1)}, bf16[256,256]{1,0:T(8,128)(2,1)S(1)}, u32[]{:S(2)}, u32[]{:S(2)}) collective-permute-start(bf16[256,256]{1,0:T(8,128)(2,1)S(1)} %bitcast.10), channel_id=1, source_target_pairs={{0,24},{8,16},{16,8},{24,0},{1,25},{9,17},{17,9},{25,1},{2,26},{10... | collective-permute-start | bytes 393224 | tf_op jit(solution)/shard_map/ppermute | solution.py:360
  120.9 6.5 %copy-start.2 = (bf16[256,256]{1,0:T(8,128)(2,1)}, bf16[256,256]{1,0:T(8,128)(2,1)S(1)}, u32[]{:S(2)}) copy-start(bf16[256,256]{1,0:T(8,128)(2,1)S(1)} %collective-permute-done.11.refs_1_) | copy-start | bytes 393220
  (4 other events, 4.0 us)

commit v11 on v10

--- a/solution.py
+++ b/solution.py
@@ -23,7 +23,7 @@
 
 
 def params():
-    return pltpu.CompilerParams(vmem_limit_bytes=63 * 2**20)
+    return pltpu.CompilerParams(vmem_limit_bytes=56 * 2**20)
 
 
 def filter_kernel(place_ref, sig_ref, rim_ref, taps_ref, *refs):
@@ -401,11 +401,13 @@
     grads = swap_all(grads, "tm")
     part = sum(piece.astype(F32) for piece in grads).astype(BF16)
     part, _ = lax.optimization_barrier((part, returned))
-    part = exchange(part, "contact").reshape(count, -1, width)
     grad_scale = (batch * (slab // width) * tm_count * neighbours.shape[0]) ** (-0.5)
-    mine = (jnp.sum(part.astype(F32), axis=0) * grad_scale).astype(BF16)
-    chunk = exchange(jnp.concatenate([mine] * count, axis=0), "contact")
-    summed = place_all(place, swap_all([chunk] * tm_count, "tm"))
+    step = 1
+    while step < count:
+        both = part.astype(F32) + swap(part, "contact", step).astype(F32)
+        step *= 2
+        part = lax.optimization_barrier((both * (1.0 if step < count else grad_scale)).astype(BF16))
+    summed = place_all(place, swap_all([part] * tm_count, "tm"))
     if pieces > 1:
         returned = returned.reshape(batch, pieces, contacts_here, span)
         returned = returned.transpose(0, 2, 1, 3).reshape(batch, contacts_here, slab)

time: 133 us -> 128 us (0.962)
  blocking collectives: 22.9 us -> 0 us
  waiting for transfers between devices: 21.6 us -> 32.5 us
  starting transfers between devices: 39.7 us -> 48.4 us
    all_to_all x2 -> x0, blocking collectives: 22.9 us -> none  [exchange(): return lax.all_to_all(value, axis, split_axis=0, concat_axis=0, tiled=True)]
    ppermute x13 -> x16, waiting for transfers between devices: 19.1 us -> 29.7 us  [swap(): lax.ppermute(value, axis, [(i, i ^ k) for i in range(lax.axis_size(axis))])]
    ppermute x13 -> x16, starting transfers between devices: 28.1 us -> 36.7 us  [swap(): lax.ppermute(value, axis, [(i, i ^ k) for i in range(lax.axis_size(axis))])]
    unnamed x31 -> x27, local copies, waits for them, and re-layouts: 4.22 us -> 2.91 us
  transfers between devices with their start and end apart: 16 -> 19, of which waited for: 8 -> 11; matrix products, arithmetic and copies ran while one was open for 1% -> 1% of each run, Pallas kernels for 25% -> 26%
where the time goes in v11:
time: 128 us
  starting transfers between devices  48.4 us (38%)
  Pallas kernels  40.7 us (32%)
  waiting for transfers between devices  32.5 us (25%)
  local copies, waits for them, and re-layouts  3.83 us (3%)
  other arithmetic  1.71 us (1%)
    ppermute x16, starting transfers between devices, swap(): lax.ppermute(value, axis, [(i, i ^ k) for i in range(lax.axis_size(axis))])  36.7 us
    ppermute x16, waiting for transfers between devices, swap(): lax.ppermute(value, axis, [(i, i ^ k) for i in range(lax.axis_size(axis))])  29.7 us
    pallas_call x1, Pallas kernels, forward(): pl.pallas_call(functools.partial(forward_kernel, blocks), grid=(groups,),...  18.3 us
    pallas_call x1, Pallas kernels, backward(): pl.pallas_call(functools.partial(backward_kernel, blocks), grid=(groups,)...  15.3 us
    all_to_all x2, starting transfers between devices, exchange(): return lax.all_to_all(value, axis, split_axis=0, concat_axis=0, tiled=True)  9.33 us
    pallas_call x1, Pallas kernels, filter_all(): pl.pallas_call(filter_kernel, grid=(contacts // rows,), in_specs=[index_s...  4.87 us
    unnamed x27, local copies, waits for them, and re-layouts  2.91 us
  transfers between devices with their start and end apart: 19, of which 11 were waited for; matrix products, arithmetic and copies ran while one was open for 1% of the time, Pallas kernels for 26%

profile of v11, /device:TPU:0, one launch (start us, length us, event | category | flops | bytes accessed | tf_op | source)
XLA Modules:
  0.0 127.9 jit_solution(7514030604701593077)
XLA Ops:
  1.5 2.4 %collective-permute-start = (bf16[8,64,128]{2,1,0:T(8,128)(2,1)S(1)}, bf16[8,64,128]{2,1,0:T(8,128)(2,1)S(1)}, u32[]{:S(2)}, u32[]{:S(2)}) collective-permute-start(bf16[8,64,128]{2,1,0:T(8,128)(2,1)S(1)} %slice.3), channel_id=1, source_target_pairs={{0,8},{8,16},{16,24},{1,9},{9,17},{17,25},{2,10},{10,18},{18,26},{... | collective-permute-start | bytes 393224 | tf_op jit(solution)/shard_map/ppermute | solution.py:387
  5.5 4.9 %filter.1 = (bf16[64,1024]{1,0:T(8,128)(2,1)}, bf16[64,1024]{1,0:T(8,128)(2,1)}, bf16[64,1024]{1,0:T(8,128)(2,1)}, bf16[64,1024]{1,0:T(8,128)(2,1)}, bf16[64,102...) custom-call(s32[2]{0:T(128)} %pad_add_fusion.place_ref, ...), custom_call_target="tpu_custom_call" | custom-call | flops 268435456 | bytes 2097152 | tf_op jit(solution)/shard_map/filter/pallas_call | solution.py:72
  10.4 4.5 %collective-permute-start.6 = (bf16[64,1024]{1,0:T(8,128)(2,1)}, bf16[64,1024]{1,0:T(8,128)(2,1)S(1)}, u32[]{:S(2)}, u32[]{:S(2)}) collective-permute-start(bf16[64,1024]{1,0:T(8,128)(2,1)} %get-tuple-element.34), channel_id=1, source_target_pairs={{0,6},{1,7},{2,4},{3,5},{4,2},{5,3},{6,0},{7,1},{8,14},{9,15},{10,... | collective-permute-start | bytes 393224 | tf_op jit(solution)/shard_map/ppermute | solution.py:360
  16.4 3.1 %collective-permute-start.3 = (bf16[64,1024]{1,0:T(8,128)(2,1)}, bf16[64,1024]{1,0:T(8,128)(2,1)S(1)}, u32[]{:S(2)}, u32[]{:S(2)}) collective-permute-start(bf16[64,1024]{1,0:T(8,128)(2,1)} %get-tuple-element.31), channel_id=1, source_target_pairs={{0,3},{1,2},{2,1},{3,0},{4,7},{5,6},{6,5},{7,4},{8,11},{9,10},{10,... | collective-permute-start | bytes 393224 | tf_op jit(solution)/shard_map/ppermute | solution.py:360
  19.6 2.1 %collective-permute-start.4 = (bf16[64,1024]{1,0:T(8,128)(2,1)}, bf16[64,1024]{1,0:T(8,128)(2,1)S(1)}, u32[]{:S(2)}, u32[]{:S(2)}) collective-permute-start(bf16[64,1024]{1,0:T(8,128)(2,1)} %get-tuple-element.32), channel_id=1, source_target_pairs={{0,4},{1,5},{2,6},{3,7},{4,0},{5,1},{6,2},{7,3},{8,12},{9,13},{10,... | collective-permute-start | bytes 393224 | tf_op jit(solution)/shard_map/ppermute | solution.py:360
  22.9 5.0 %collective-permute-start.5 = (bf16[64,1024]{1,0:T(8,128)(2,1)}, bf16[64,1024]{1,0:T(8,128)(2,1)S(1)}, u32[]{:S(2)}, u32[]{:S(2)}) collective-permute-start(bf16[64,1024]{1,0:T(8,128)(2,1)} %get-tuple-element.33), channel_id=1, source_target_pairs={{0,5},{1,4},{2,7},{3,6},{4,1},{5,0},{6,3},{7,2},{8,13},{9,12},{10,... | collective-permute-start | bytes 393224 | tf_op jit(solution)/shard_map/ppermute | solution.py:360
  28.0 4.9 %all-to-all-start.1 = ((bf16[8,64,1024]{2,1,0:T(8,128)(2,1)}), bf16[8,64,1024]{2,1,0:T(8,128)(2,1)S(1)}, u32[]{:S(2)}, u32[]{:S(2)}) async-start(bf16[8,64,1024]{2,1,0:T(8,128)(2,1)} %param.19), calls=%async_computation.1 | async-start | bytes 2097152 | tf_op jit(solution)/shard_map/all_to_all | solution.py:369
  33.0 5.6 %collective-permute-done.5.refs_5_ = bf16[64,1024]{1,0:T(8,128)(2,1)S(1)} collective-permute-done((bf16[64,1024]{1,0:T(8,128)(2,1)}, bf16[64,1024]{1,0:T(8,128)(2,1)S(1)}, u32[]{:S(2)}, u32[]{:S(2)}) %collective-permute-start.5) | collective-permute-done | bytes 131104 | tf_op jit(solution)/shard_map/ppermute | solution.py:360
  39.2 18.3 %forward.1 = (bf16[8,64,1024]{2,1,0:T(8,128)(2,1)}, bf16[512,8192]{1,0:T(8,128)(2,1)}, bf16[512,1024]{1,0:T(8,128)(2,1)}, bf16[512,1024]{1,0:T(8,128)(2,1)}, bf1...) custom-call(s32[2]{0:T(128)} %pad_add_fusion.place_ref, ...), custom_call_target="tpu_custom_call" | custom-call | flops 20000000000 | bytes 10485760 | tf_op jit(solution)/shard_map/forward/pallas_call | solution.py:278
  57.6 2.5 %all-to-all-done.1.up_ref = bf16[8,64,1024]{2,1,0:T(8,128)(2,1)S(1)} async-done(((bf16[8,64,1024]{2,1,0:T(8,128)(2,1)}), bf16[8,64,1024]{2,1,0:T(8,128)(2,1)S(1)}, u32[]{:S(2)}, u32[]{:S(2)}) %all-to-all-start.1) | async-done | bytes 1048608 | tf_op jit(solution)/shard_map/all_to_all | solution.py:369
  60.1 4.4 %all-to-all-start = ((bf16[8,64,1024]{2,1,0:T(8,128)(2,1)}), bf16[8,64,1024]{2,1,0:T(8,128)(2,1)S(1)}, u32[]{:S(2)}, u32[]{:S(2)}) async-start(bf16[8,64,1024]{2,1,0:T(8,128)(2,1)} %get-tuple-element.38), calls=%async_computation | async-start | bytes 2097152 | tf_op jit(solution)/shard_map/all_to_all | solution.py:369
  64.5 15.3 %backward.1 = (bf16[256,256]{1,0:T(8,128)(2,1)}, bf16[256,256]{1,0:T(8,128)(2,1)}, bf16[256,256]{1,0:T(8,128)(2,1)}, bf16[256,256]{1,0:T(8,128)(2,1)}) custom-call(s32[2]{0:T(128)} %pad_add_fusion.place_ref, bf16[256,256]{1,0:T(8,128)(2,1)} %wo_ref.3, bf16[8,64,1024]{2,1,0:T(8,128)(2,1)} %copy-done, bf16[512,8192]{1,0:T(8,128)(2,1)} %get-tuple-element.40.prob_ref, ...), custom_call_target="tpu_custom_call" | custom-call | flops 20000000000 | bytes 10485760 | tf_op jit(solution)/shard_map/backward/pallas_call | solution.py:314
  80.2 9.6 %collective-permute-start.8 = (bf16[256,256]{1,0:T(8,128)(2,1)}, bf16[256,256]{1,0:T(8,128)(2,1)S(1)}, u32[]{:S(2)}, u32[]{:S(2)}) collective-permute-start(bf16[256,256]{1,0:T(8,128)(2,1)} %get-tuple-element.50), channel_id=1, source_target_pairs={{0,8},{8,0},{16,24},{24,16},{1,9},{9,1},{17,25},{25,17},{2,10},{10... | collective-permute-start | bytes 393224 | tf_op jit(solution)/shard_map/ppermute | solution.py:360
  91.0 4.7 %collective-permute-done.9 = bf16[256,256]{1,0:T(8,128)(2,1)S(1)} collective-permute-done((bf16[256,256]{1,0:T(8,128)(2,1)}, bf16[256,256]{1,0:T(8,128)(2,1)S(1)}, u32[]{:S(2)}, u32[]{:S(2)}) %collective-permute-start.9) | collective-permute-done | bytes 131104 | tf_op jit(solution)/shard_map/ppermute | solution.py:360
  96.6 2.1 %collective-permute-start.11 = (bf16[256,256]{1,0:T(8,128)(2,1)S(1)}, bf16[256,256]{1,0:T(8,128)(2,1)S(1)}, u32[]{:S(2)}, u32[]{:S(2)}) collective-permute-start(bf16[256,256]{1,0:T(8,128)(2,1)S(1)} %add_convert_fusion.2), channel_id=1, source_target_pairs={{0,1},{1,0},{2,3},{3,2},{4,5},{5,4},{6,7},{7,6},{8,9},{9,8},{10,11... | collective-permute-start | bytes 393224 | tf_op jit(solution)/shard_map/ppermute | solution.py:360
  98.7 3.0 %collective-permute-done.11 = bf16[256,256]{1,0:T(8,128)(2,1)S(1)} collective-permute-done((bf16[256,256]{1,0:T(8,128)(2,1)S(1)}, bf16[256,256]{1,0:T(8,128)(2,1)S(1)}, u32[]{:S(2)}, u32[]{:S(2)}) %collective-permute-start.11) | collective-permute-done | bytes 131104 | tf_op jit(solution)/shard_map/ppermute | solution.py:360
  101.7 2.0 %collective-permute-start.12 = (bf16[256,256]{1,0:T(8,128)(2,1)S(1)}, bf16[256,256]{1,0:T(8,128)(2,1)S(1)}, u32[]{:S(2)}, u32[]{:S(2)}) collective-permute-start(bf16[256,256]{1,0:T(8,128)(2,1)S(1)} %add_convert_fusion.1), channel_id=1, source_target_pairs={{0,2},{1,3},{2,0},{3,1},{4,6},{5,7},{6,4},{7,5},{8,10},{9,11},{10,... | collective-permute-start | bytes 393224 | tf_op jit(solution)/shard_map/ppermute | solution.py:360
  103.7 3.0 %collective-permute-done.12 = bf16[256,256]{1,0:T(8,128)(2,1)S(1)} collective-permute-done((bf16[256,256]{1,0:T(8,128)(2,1)S(1)}, bf16[256,256]{1,0:T(8,128)(2,1)S(1)}, u32[]{:S(2)}, u32[]{:S(2)}) %collective-permute-start.12) | collective-permute-done | bytes 131104 | tf_op jit(solution)/shard_map/ppermute | solution.py:360
  106.8 3.1 %collective-permute-start.13 = (bf16[256,256]{1,0:T(8,128)(2,1)S(1)}, bf16[256,256]{1,0:T(8,128)(2,1)S(1)}, u32[]{:S(2)}, u32[]{:S(2)}) collective-permute-start(bf16[256,256]{1,0:T(8,128)(2,1)S(1)} %add_convert_fusion), channel_id=1, source_target_pairs={{0,4},{1,5},{2,6},{3,7},{4,0},{5,1},{6,2},{7,3},{8,12},{9,13},{10,... | collective-permute-start | bytes 393224 | tf_op jit(solution)/shard_map/ppermute | solution.py:360
  109.9 4.4 %collective-permute-done.13 = bf16[256,256]{1,0:T(8,128)(2,1)S(1)} collective-permute-done((bf16[256,256]{1,0:T(8,128)(2,1)S(1)}, bf16[256,256]{1,0:T(8,128)(2,1)S(1)}, u32[]{:S(2)}, u32[]{:S(2)}) %collective-permute-start.13) | collective-permute-done | bytes 131104 | tf_op jit(solution)/shard_map/ppermute | solution.py:360
  114.4 3.1 %collective-permute-start.15 = (bf16[256,256]{1,0:T(8,128)(2,1)S(1)}, bf16[256,256]{1,0:T(8,128)(2,1)S(1)}, u32[]{:S(2)}, u32[]{:S(2)}) collective-permute-start(bf16[256,256]{1,0:T(8,128)(2,1)S(1)} %multiply_convert_fusion.refs_0_), channel_id=1, source_target_pairs={{0,16},{8,24},{16,0},{24,8},{1,17},{9,25},{17,1},{25,9},{2,18},{10... | collective-permute-start | bytes 393224 | tf_op jit(solution)/shard_map/ppermute | solution.py:360
  117.6 4.3 %collective-permute-done.15.refs_2_ = bf16[256,256]{1,0:T(8,128)(2,1)S(1)} collective-permute-done((bf16[256,256]{1,0:T(8,128)(2,1)S(1)}, bf16[256,256]{1,0:T(8,128)(2,1)S(1)}, u32[]{:S(2)}, u32[]{:S(2)}) %collective-permute-start.15) | collective-permute-done | bytes 131104 | tf_op jit(solution)/shard_map/ppermute | solution.py:360
  121.9 2.3 %collective-permute-done.16.refs_3_ = bf16[256,256]{1,0:T(8,128)(2,1)S(1)} collective-permute-done((bf16[256,256]{1,0:T(8,128)(2,1)S(1)}, bf16[256,256]{1,0:T(8,128)(2,1)S(1)}, u32[]{:S(2)}, u32[]{:S(2)}) %collective-permute-start.16) | collective-permute-done | bytes 131104 | tf_op jit(solution)/shard_map/ppermute | solution.py:360
  124.8 2.1 %place_all.1 = f32[4,256,256]{2,1,0:T(8,128)} custom-call(s32[2]{0:T(128)} %pad_add_fusion.place_ref, bf16[256,256]{1,0:T(8,128)(2,1)} %copy-done.1, bf16[256,256]{1,0:T(8,128)(2,1)} %copy-done.3, bf16[256,256]{1,0:T(8,128)(2,1)} %copy-done.4, bf16[256,256]{1,0:T(8,128)(2,1)} %copy-done.5), custom_call_target="tpu_custom_call" | custom-call | tf_op jit(solution)/shard_map/place_all/pallas_call | solution.py:349
  (51 shorter events, 10.3 us)
Async XLA Ops:
  1.5 3.3 %collective-permute-start = (bf16[8,64,128]{2,1,0:T(8,128)(2,1)S(1)}, bf16[8,64,128]{2,1,0:T(8,128)(2,1)S(1)}, u32[]{:S(2)}, u32[]{:S(2)}) collective-permute-start(bf16[8,64,128]{2,1,0:T(8,128)(2,1)S(1)} %slice.3), channel_id=1, source_target_pairs={{0,8},{8,16},{16,24},{1,9},{9,17},{17,25},{2,10},{10,18},{18,26},{... | collective-permute-start | bytes 393224 | tf_op jit(solution)/shard_map/ppermute | solution.py:387
  10.4 9.2 %collective-permute-start.6 = (bf16[64,1024]{1,0:T(8,128)(2,1)}, bf16[64,1024]{1,0:T(8,128)(2,1)S(1)}, u32[]{:S(2)}, u32[]{:S(2)}) collective-permute-start(bf16[64,1024]{1,0:T(8,128)(2,1)} %get-tuple-element.34), channel_id=1, source_target_pairs={{0,6},{1,7},{2,4},{3,5},{4,2},{5,3},{6,0},{7,1},{8,14},{9,15},{10,... | collective-permute-start | bytes 393224 | tf_op jit(solution)/shard_map/ppermute | solution.py:360
  14.9 8.0 %collective-permute-start.7 = (bf16[64,1024]{1,0:T(8,128)(2,1)}, bf16[64,1024]{1,0:T(8,128)(2,1)S(1)}, u32[]{:S(2)}, u32[]{:S(2)}) collective-permute-start(bf16[64,1024]{1,0:T(8,128)(2,1)} %get-tuple-element.35), channel_id=1, source_target_pairs={{0,7},{1,6},{2,5},{3,4},{4,3},{5,2},{6,1},{7,0},{8,15},{9,14},{10,... | collective-permute-start | bytes 393224 | tf_op jit(solution)/shard_map/ppermute | solution.py:360
  16.1 16.8 %collective-permute-start.1 = (bf16[64,1024]{1,0:T(8,128)(2,1)}, bf16[64,1024]{1,0:T(8,128)(2,1)S(1)}, u32[]{:S(2)}, u32[]{:S(2)}) collective-permute-start(bf16[64,1024]{1,0:T(8,128)(2,1)} %get-tuple-element.29), channel_id=1, source_target_pairs={{0,1},{1,0},{2,3},{3,2},{4,5},{5,4},{6,7},{7,6},{8,9},{9,8},{10,11... | collective-permute-start | bytes 393224 | tf_op jit(solution)/shard_map/ppermute | solution.py:360
  16.4 16.5 %collective-permute-start.2 = (bf16[64,1024]{1,0:T(8,128)(2,1)}, bf16[64,1024]{1,0:T(8,128)(2,1)S(1)}, u32[]{:S(2)}, u32[]{:S(2)}) collective-permute-start(bf16[64,1024]{1,0:T(8,128)(2,1)} %get-tuple-element.30), channel_id=1, source_target_pairs={{0,2},{1,3},{2,0},{3,1},{4,6},{5,7},{6,4},{7,5},{8,10},{9,11},{10,... | collective-permute-start | bytes 393224 | tf_op jit(solution)/shard_map/ppermute | solution.py:360
  16.4 16.5 %collective-permute-start.3 = (bf16[64,1024]{1,0:T(8,128)(2,1)}, bf16[64,1024]{1,0:T(8,128)(2,1)S(1)}, u32[]{:S(2)}, u32[]{:S(2)}) collective-permute-start(bf16[64,1024]{1,0:T(8,128)(2,1)} %get-tuple-element.31), channel_id=1, source_target_pairs={{0,3},{1,2},{2,1},{3,0},{4,7},{5,6},{6,5},{7,4},{8,11},{9,10},{10,... | collective-permute-start | bytes 393224 | tf_op jit(solution)/shard_map/ppermute | solution.py:360
  19.6 19.0 %copy-start.6 = (bf16[64,1024]{1,0:T(8,128)(2,1)}, bf16[64,1024]{1,0:T(8,128)(2,1)S(1)}, u32[]{:S(2)}) copy-start(bf16[64,1024]{1,0:T(8,128)(2,1)S(1)} %collective-permute-done.6.refs_6_) | copy-start | bytes 393220
  19.6 13.4 %collective-permute-start.4 = (bf16[64,1024]{1,0:T(8,128)(2,1)}, bf16[64,1024]{1,0:T(8,128)(2,1)S(1)}, u32[]{:S(2)}, u32[]{:S(2)}) collective-permute-start(bf16[64,1024]{1,0:T(8,128)(2,1)} %get-tuple-element.32), channel_id=1, source_target_pairs={{0,4},{1,5},{2,6},{3,7},{4,0},{5,1},{6,2},{7,3},{8,12},{9,13},{10,... | collective-permute-start | bytes 393224 | tf_op jit(solution)/shard_map/ppermute | solution.py:360
  22.9 15.7 %copy-start.7 = (bf16[64,1024]{1,0:T(8,128)(2,1)}, bf16[64,1024]{1,0:T(8,128)(2,1)S(1)}, u32[]{:S(2)}) copy-start(bf16[64,1024]{1,0:T(8,128)(2,1)S(1)} %collective-permute-done.7.refs_7_) | copy-start | bytes 393220
  22.9 15.6 %collective-permute-start.5 = (bf16[64,1024]{1,0:T(8,128)(2,1)}, bf16[64,1024]{1,0:T(8,128)(2,1)S(1)}, u32[]{:S(2)}, u32[]{:S(2)}) collective-permute-start(bf16[64,1024]{1,0:T(8,128)(2,1)} %get-tuple-element.33), channel_id=1, source_target_pairs={{0,5},{1,4},{2,7},{3,6},{4,1},{5,0},{6,3},{7,2},{8,13},{9,12},{10,... | collective-permute-start | bytes 393224 | tf_op jit(solution)/shard_map/ppermute | solution.py:360
  28.0 32.1 %all-to-all-start.1 = ((bf16[8,64,1024]{2,1,0:T(8,128)(2,1)}), bf16[8,64,1024]{2,1,0:T(8,128)(2,1)S(1)}, u32[]{:S(2)}, u32[]{:S(2)}) async-start(bf16[8,64,1024]{2,1,0:T(8,128)(2,1)} %param.19), calls=%async_computation.1 | async-start | bytes 2097152 | tf_op jit(solution)/shard_map/all_to_all | solution.py:369
  32.9 5.7 %copy-start.8 = (bf16[64,1024]{1,0:T(8,128)(2,1)}, bf16[64,1024]{1,0:T(8,128)(2,1)S(1)}, u32[]{:S(2)}) copy-start(bf16[64,1024]{1,0:T(8,128)(2,1)S(1)} %collective-permute-done.1.refs_1_) | copy-start | bytes 393220
  60.1 36.5 %all-to-all-start = ((bf16[8,64,1024]{2,1,0:T(8,128)(2,1)}), bf16[8,64,1024]{2,1,0:T(8,128)(2,1)S(1)}, u32[]{:S(2)}, u32[]{:S(2)}) async-start(bf16[8,64,1024]{2,1,0:T(8,128)(2,1)} %get-tuple-element.38), calls=%async_computation | async-start | bytes 2097152 | tf_op jit(solution)/shard_map/all_to_all | solution.py:369
  79.8 10.0 %collective-permute-start.10 = (bf16[256,256]{1,0:T(8,128)(2,1)}, bf16[256,256]{1,0:T(8,128)(2,1)S(1)}, u32[]{:S(2)}, u32[]{:S(2)}) collective-permute-start(bf16[256,256]{1,0:T(8,128)(2,1)} %get-tuple-element.52), channel_id=1, source_target_pairs={{0,24},{8,16},{16,8},{24,0},{1,25},{9,17},{17,9},{25,1},{2,26},{10... | collective-permute-start | bytes 393224 | tf_op jit(solution)/shard_map/ppermute | solution.py:360
  80.2 10.8 %collective-permute-start.8 = (bf16[256,256]{1,0:T(8,128)(2,1)}, bf16[256,256]{1,0:T(8,128)(2,1)S(1)}, u32[]{:S(2)}, u32[]{:S(2)}) collective-permute-start(bf16[256,256]{1,0:T(8,128)(2,1)} %get-tuple-element.50), channel_id=1, source_target_pairs={{0,8},{8,0},{16,24},{24,16},{1,9},{9,1},{17,25},{25,17},{2,10},{10... | collective-permute-start | bytes 393224 | tf_op jit(solution)/shard_map/ppermute | solution.py:360
  89.8 5.9 %collective-permute-start.9 = (bf16[256,256]{1,0:T(8,128)(2,1)}, bf16[256,256]{1,0:T(8,128)(2,1)S(1)}, u32[]{:S(2)}, u32[]{:S(2)}) collective-permute-start(bf16[256,256]{1,0:T(8,128)(2,1)} %get-tuple-element.51), channel_id=1, source_target_pairs={{0,16},{8,24},{16,0},{24,8},{1,17},{9,25},{17,1},{25,9},{2,18},{10... | collective-permute-start | bytes 393224 | tf_op jit(solution)/shard_map/ppermute | solution.py:360
  96.6 5.1 %collective-permute-start.11 = (bf16[256,256]{1,0:T(8,128)(2,1)S(1)}, bf16[256,256]{1,0:T(8,128)(2,1)S(1)}, u32[]{:S(2)}, u32[]{:S(2)}) collective-permute-start(bf16[256,256]{1,0:T(8,128)(2,1)S(1)} %add_convert_fusion.2), channel_id=1, source_target_pairs={{0,1},{1,0},{2,3},{3,2},{4,5},{5,4},{6,7},{7,6},{8,9},{9,8},{10,11... | collective-permute-start | bytes 393224 | tf_op jit(solution)/shard_map/ppermute | solution.py:360
  101.7 5.0 %collective-permute-start.12 = (bf16[256,256]{1,0:T(8,128)(2,1)S(1)}, bf16[256,256]{1,0:T(8,128)(2,1)S(1)}, u32[]{:S(2)}, u32[]{:S(2)}) collective-permute-start(bf16[256,256]{1,0:T(8,128)(2,1)S(1)} %add_convert_fusion.1), channel_id=1, source_target_pairs={{0,2},{1,3},{2,0},{3,1},{4,6},{5,7},{6,4},{7,5},{8,10},{9,11},{10,... | collective-permute-start | bytes 393224 | tf_op jit(solution)/shard_map/ppermute | solution.py:360
  106.8 7.4 %collective-permute-start.13 = (bf16[256,256]{1,0:T(8,128)(2,1)S(1)}, bf16[256,256]{1,0:T(8,128)(2,1)S(1)}, u32[]{:S(2)}, u32[]{:S(2)}) collective-permute-start(bf16[256,256]{1,0:T(8,128)(2,1)S(1)} %add_convert_fusion), channel_id=1, source_target_pairs={{0,4},{1,5},{2,6},{3,7},{4,0},{5,1},{6,2},{7,3},{8,12},{9,13},{10,... | collective-permute-start | bytes 393224 | tf_op jit(solution)/shard_map/ppermute | solution.py:360
  114.3 9.9 %copy-start.1 = (bf16[256,256]{1,0:T(8,128)(2,1)}, bf16[256,256]{1,0:T(8,128)(2,1)S(1)}, u32[]{:S(2)}) copy-start(bf16[256,256]{1,0:T(8,128)(2,1)S(1)} %multiply_convert_fusion.refs_0_) | copy-start | bytes 393220
  114.3 3.3 %collective-permute-start.14 = (bf16[256,256]{1,0:T(8,128)(2,1)S(1)}, bf16[256,256]{1,0:T(8,128)(2,1)S(1)}, u32[]{:S(2)}, u32[]{:S(2)}) collective-permute-start(bf16[256,256]{1,0:T(8,128)(2,1)S(1)} %multiply_convert_fusion.refs_0_), channel_id=1, source_target_pairs={{0,8},{8,0},{16,24},{24,16},{1,9},{9,1},{17,25},{25,17},{2,10},{10... | collective-permute-start | bytes 393224 | tf_op jit(solution)/shard_map/ppermute | solution.py:360
  114.4 7.5 %collective-permute-start.15 = (bf16[256,256]{1,0:T(8,128)(2,1)S(1)}, bf16[256,256]{1,0:T(8,128)(2,1)S(1)}, u32[]{:S(2)}, u32[]{:S(2)}) collective-permute-start(bf16[256,256]{1,0:T(8,128)(2,1)S(1)} %multiply_convert_fusion.refs_0_), channel_id=1, source_target_pairs={{0,16},{8,24},{16,0},{24,8},{1,17},{9,25},{17,1},{25,9},{2,18},{10... | collective-permute-start | bytes 393224 | tf_op jit(solution)/shard_map/ppermute | solution.py:360
  117.5 6.6 %collective-permute-start.16 = (bf16[256,256]{1,0:T(8,128)(2,1)S(1)}, bf16[256,256]{1,0:T(8,128)(2,1)S(1)}, u32[]{:S(2)}, u32[]{:S(2)}) collective-permute-start(bf16[256,256]{1,0:T(8,128)(2,1)S(1)} %multiply_convert_fusion.refs_0_), channel_id=1, source_target_pairs={{0,24},{8,16},{16,8},{24,0},{1,25},{9,17},{17,9},{25,1},{2,26},{10... | collective-permute-start | bytes 393224 | tf_op jit(solution)/shard_map/ppermute | solution.py:360
  117.6 6.6 %copy-start.3 = (bf16[256,256]{1,0:T(8,128)(2,1)}, bf16[256,256]{1,0:T(8,128)(2,1)S(1)}, u32[]{:S(2)}) copy-start(bf16[256,256]{1,0:T(8,128)(2,1)S(1)} %collective-permute-done.14.refs_1_) | copy-start | bytes 393220
  (8 other events, 25.7 us)

commit v12 on v11

--- a/solution.py
+++ b/solution.py
@@ -396,17 +396,18 @@
         place, features, neighbours.T, live_mask[None], lap_coef[None],
         [w_query, w_key, w_value, w_out],
     )
+    grads = backward(place, upstream, kept, w_out, tm_count)
+    attended, grads = lax.optimization_barrier((attended, grads))
     returned = exchange(attended, "contact")
-    grads = backward(place, upstream, kept, w_out, tm_count)
     grads = swap_all(grads, "tm")
     part = sum(piece.astype(F32) for piece in grads).astype(BF16)
-    part, _ = lax.optimization_barrier((part, returned))
     grad_scale = (batch * (slab // width) * tm_count * neighbours.shape[0]) ** (-0.5)
     step = 1
     while step < count:
         both = part.astype(F32) + swap(part, "contact", step).astype(F32)
         step *= 2
         part = lax.optimization_barrier((both * (1.0 if step < count else grad_scale)).astype(BF16))
+    part, _ = lax.optimization_barrier((part, returned))
     summed = place_all(place, swap_all([part] * tm_count, "tm"))
     if pieces > 1:
         returned = returned.reshape(batch, pieces, contacts_here, span)

time: 128 us -> 132 us (1.031)
  waiting for transfers between devices: 32.5 us -> 40.4 us
  starting transfers between devices: 48.4 us -> 43.3 us
    ppermute x16, waiting for transfers between devices: 29.7 us -> 37.6 us  [swap(): lax.ppermute(value, axis, [(i, i ^ k) for i in range(lax.axis_size(axis))])]
    ppermute x16, starting transfers between devices: 36.7 us -> 31.6 us  [swap(): lax.ppermute(value, axis, [(i, i ^ k) for i in range(lax.axis_size(axis))])]
  transfers between devices with their start and end apart: 19 -> 19, of which waited for: 11 -> 10; matrix products, arithmetic and copies ran while one was open for 1% -> 1% of each run, Pallas kernels for 26% -> 14%
where the time goes in v12:
time: 132 us
  starting transfers between devices  43.3 us (33%)
  Pallas kernels  40.7 us (31%)
  waiting for transfers between devices  40.4 us (31%)
  local copies, waits for them, and re-layouts  4.8 us (4%)
  other arithmetic  1.71 us (1%)
    ppermute x16, waiting for transfers between devices, swap(): lax.ppermute(value, axis, [(i, i ^ k) for i in range(lax.axis_size(axis))])  37.6 us
    ppermute x16, starting transfers between devices, swap(): lax.ppermute(value, axis, [(i, i ^ k) for i in range(lax.axis_size(axis))])  31.6 us
    pallas_call x1, Pallas kernels, forward(): pl.pallas_call(functools.partial(forward_kernel, blocks), grid=(groups,),...  18.3 us
    pallas_call x1, Pallas kernels, backward(): pl.pallas_call(functools.partial(backward_kernel, blocks), grid=(groups,)...  15.3 us
    all_to_all x2, starting transfers between devices, exchange(): return lax.all_to_all(value, axis, split_axis=0, concat_axis=0, tiled=True)  9.32 us
    pallas_call x1, Pallas kernels, filter_all(): pl.pallas_call(filter_kernel, grid=(contacts // rows,), in_specs=[index_s...  4.87 us
    unnamed x27, local copies, waits for them, and re-layouts  3.88 us
  transfers between devices with their start and end apart: 19, of which 10 were waited for; matrix products, arithmetic and copies ran while one was open for 1% of the time, Pallas kernels for 14%

profile of v12, /device:TPU:0, one launch (start us, length us, event | category | flops | bytes accessed | tf_op | source)
XLA Modules:
  0.0 131.7 jit_solution(17407203692814616204)
XLA Ops:
  1.5 2.4 %collective-permute-start = (bf16[8,64,128]{2,1,0:T(8,128)(2,1)S(1)}, bf16[8,64,128]{2,1,0:T(8,128)(2,1)S(1)}, u32[]{:S(2)}, u32[]{:S(2)}) collective-permute-start(bf16[8,64,128]{2,1,0:T(8,128)(2,1)S(1)} %slice.3), channel_id=1, source_target_pairs={{0,8},{8,16},{16,24},{1,9},{9,17},{17,25},{2,10},{10,18},{18,26},{... | collective-permute-start | bytes 393224 | tf_op jit(solution)/shard_map/ppermute | solution.py:387
  5.5 4.9 %filter.1 = (bf16[64,1024]{1,0:T(8,128)(2,1)}, bf16[64,1024]{1,0:T(8,128)(2,1)}, bf16[64,1024]{1,0:T(8,128)(2,1)}, bf16[64,1024]{1,0:T(8,128)(2,1)}, bf16[64,102...) custom-call(s32[2]{0:T(128)} %pad_add_fusion.place_ref, ...), custom_call_target="tpu_custom_call" | custom-call | flops 268435456 | bytes 2097152 | tf_op jit(solution)/shard_map/filter/pallas_call | solution.py:72
  10.4 4.5 %collective-permute-start.6 = (bf16[64,1024]{1,0:T(8,128)(2,1)}, bf16[64,1024]{1,0:T(8,128)(2,1)S(1)}, u32[]{:S(2)}, u32[]{:S(2)}) collective-permute-start(bf16[64,1024]{1,0:T(8,128)(2,1)} %get-tuple-element.39), channel_id=1, source_target_pairs={{0,6},{1,7},{2,4},{3,5},{4,2},{5,3},{6,0},{7,1},{8,14},{9,15},{10,... | collective-permute-start | bytes 393224 | tf_op jit(solution)/shard_map/ppermute | solution.py:360
  14.9 1.2 collective-permute-start.7
  16.4 3.1 %collective-permute-start.3 = (bf16[64,1024]{1,0:T(8,128)(2,1)}, bf16[64,1024]{1,0:T(8,128)(2,1)S(1)}, u32[]{:S(2)}, u32[]{:S(2)}) collective-permute-start(bf16[64,1024]{1,0:T(8,128)(2,1)} %get-tuple-element.36), channel_id=1, source_target_pairs={{0,3},{1,2},{2,1},{3,0},{4,7},{5,6},{6,5},{7,4},{8,11},{9,10},{10,... | collective-permute-start | bytes 393224 | tf_op jit(solution)/shard_map/ppermute | solution.py:360
  19.6 2.1 %collective-permute-start.4 = (bf16[64,1024]{1,0:T(8,128)(2,1)}, bf16[64,1024]{1,0:T(8,128)(2,1)S(1)}, u32[]{:S(2)}, u32[]{:S(2)}) collective-permute-start(bf16[64,1024]{1,0:T(8,128)(2,1)} %get-tuple-element.37), channel_id=1, source_target_pairs={{0,4},{1,5},{2,6},{3,7},{4,0},{5,1},{6,2},{7,3},{8,12},{9,13},{10,... | collective-permute-start | bytes 393224 | tf_op jit(solution)/shard_map/ppermute | solution.py:360
  21.7 1.2 collective-permute-done.7.refs_7_
  22.9 5.0 %collective-permute-start.5 = (bf16[64,1024]{1,0:T(8,128)(2,1)}, bf16[64,1024]{1,0:T(8,128)(2,1)S(1)}, u32[]{:S(2)}, u32[]{:S(2)}) collective-permute-start(bf16[64,1024]{1,0:T(8,128)(2,1)} %get-tuple-element.38), channel_id=1, source_target_pairs={{0,5},{1,4},{2,7},{3,6},{4,1},{5,0},{6,3},{7,2},{8,13},{9,12},{10,... | collective-permute-start | bytes 393224 | tf_op jit(solution)/shard_map/ppermute | solution.py:360
  28.0 4.9 %all-to-all-start = ((bf16[8,64,1024]{2,1,0:T(8,128)(2,1)}), bf16[8,64,1024]{2,1,0:T(8,128)(2,1)S(1)}, u32[]{:S(2)}, u32[]{:S(2)}) async-start(bf16[8,64,1024]{2,1,0:T(8,128)(2,1)} %param.19), calls=%async_computation | async-start | bytes 2097152 | tf_op jit(solution)/shard_map/all_to_all | solution.py:369
  33.0 5.6 %collective-permute-done.5.refs_5_ = bf16[64,1024]{1,0:T(8,128)(2,1)S(1)} collective-permute-done((bf16[64,1024]{1,0:T(8,128)(2,1)}, bf16[64,1024]{1,0:T(8,128)(2,1)S(1)}, u32[]{:S(2)}, u32[]{:S(2)}) %collective-permute-start.5) | collective-permute-done | bytes 131104 | tf_op jit(solution)/shard_map/ppermute | solution.py:360
  39.2 18.3 %forward.1 = (bf16[8,64,1024]{2,1,0:T(8,128)(2,1)}, bf16[512,8192]{1,0:T(8,128)(2,1)}, bf16[512,1024]{1,0:T(8,128)(2,1)}, bf16[512,1024]{1,0:T(8,128)(2,1)}, bf1...) custom-call(s32[2]{0:T(128)} %pad_add_fusion.place_ref, ...), custom_call_target="tpu_custom_call" | custom-call | flops 20000000000 | bytes 10485760 | tf_op jit(solution)/shard_map/forward/pallas_call | solution.py:278
  57.6 2.5 %all-to-all-done.up_ref = bf16[8,64,1024]{2,1,0:T(8,128)(2,1)S(1)} async-done(((bf16[8,64,1024]{2,1,0:T(8,128)(2,1)}), bf16[8,64,1024]{2,1,0:T(8,128)(2,1)S(1)}, u32[]{:S(2)}, u32[]{:S(2)}) %all-to-all-start) | async-done | bytes 1048608 | tf_op jit(solution)/shard_map/all_to_all | solution.py:369
  61.1 15.3 %backward.1 = (bf16[256,256]{1,0:T(8,128)(2,1)}, bf16[256,256]{1,0:T(8,128)(2,1)}, bf16[256,256]{1,0:T(8,128)(2,1)}, bf16[256,256]{1,0:T(8,128)(2,1)}) custom-call(s32[2]{0:T(128)} %pad_add_fusion.place_ref, bf16[256,256]{1,0:T(8,128)(2,1)} %wo_ref.3, bf16[8,64,1024]{2,1,0:T(8,128)(2,1)} %copy-done, bf16[512,8192]{1,0:T(8,128)(2,1)} %get-tuple-element.45.prob_ref, ...), custom_call_target="tpu_custom_call" | custom-call | flops 20000000000 | bytes 10485760 | tf_op jit(solution)/shard_map/backward/pallas_call | solution.py:314
  76.4 4.4 %all-to-all-start.1 = ((bf16[8,64,1024]{2,1,0:T(8,128)(2,1)}), bf16[8,64,1024]{2,1,0:T(8,128)(2,1)S(1)}, u32[]{:S(2)}, u32[]{:S(2)}) async-start(bf16[8,64,1024]{2,1,0:T(8,128)(2,1)} %get-tuple-element.58), calls=%async_computation.1 | async-start | bytes 2097152 | tf_op jit(solution)/shard_map/all_to_all | solution.py:369
  81.1 9.5 %collective-permute-start.9 = (bf16[256,256]{1,0:T(8,128)(2,1)}, bf16[256,256]{1,0:T(8,128)(2,1)S(1)}, u32[]{:S(2)}, u32[]{:S(2)}) collective-permute-start(bf16[256,256]{1,0:T(8,128)(2,1)} %get-tuple-element.61), channel_id=1, source_target_pairs={{0,16},{8,24},{16,0},{24,8},{1,17},{9,25},{17,1},{25,9},{2,18},{10... | collective-permute-start | bytes 393224 | tf_op jit(solution)/shard_map/ppermute | solution.py:360
  90.6 5.8 %collective-permute-done.9 = bf16[256,256]{1,0:T(8,128)(2,1)S(1)} collective-permute-done((bf16[256,256]{1,0:T(8,128)(2,1)}, bf16[256,256]{1,0:T(8,128)(2,1)S(1)}, u32[]{:S(2)}, u32[]{:S(2)}) %collective-permute-start.9) | collective-permute-done | bytes 131104 | tf_op jit(solution)/shard_map/ppermute | solution.py:360
  97.5 2.1 %collective-permute-start.11 = (bf16[256,256]{1,0:T(8,128)(2,1)S(1)}, bf16[256,256]{1,0:T(8,128)(2,1)S(1)}, u32[]{:S(2)}, u32[]{:S(2)}) collective-permute-start(bf16[256,256]{1,0:T(8,128)(2,1)S(1)} %add_convert_fusion.2), channel_id=1, source_target_pairs={{0,1},{1,0},{2,3},{3,2},{4,5},{5,4},{6,7},{7,6},{8,9},{9,8},{10,11... | collective-permute-start | bytes 393224 | tf_op jit(solution)/shard_map/ppermute | solution.py:360
  99.5 5.0 %collective-permute-done.11 = bf16[256,256]{1,0:T(8,128)(2,1)S(1)} collective-permute-done((bf16[256,256]{1,0:T(8,128)(2,1)S(1)}, bf16[256,256]{1,0:T(8,128)(2,1)S(1)}, u32[]{:S(2)}, u32[]{:S(2)}) %collective-permute-start.11) | collective-permute-done | bytes 131104 | tf_op jit(solution)/shard_map/ppermute | solution.py:360
  105.0 6.3 %collective-permute-done.12 = bf16[256,256]{1,0:T(8,128)(2,1)S(1)} collective-permute-done((bf16[256,256]{1,0:T(8,128)(2,1)S(1)}, bf16[256,256]{1,0:T(8,128)(2,1)S(1)}, u32[]{:S(2)}, u32[]{:S(2)}) %collective-permute-start.12) | collective-permute-done | bytes 131104 | tf_op jit(solution)/shard_map/ppermute | solution.py:360
  112.3 7.1 %collective-permute-done.13 = bf16[256,256]{1,0:T(8,128)(2,1)S(1)} collective-permute-done((bf16[256,256]{1,0:T(8,128)(2,1)S(1)}, bf16[256,256]{1,0:T(8,128)(2,1)S(1)}, u32[]{:S(2)}, u32[]{:S(2)}) %collective-permute-start.13) | collective-permute-done | bytes 131104 | tf_op jit(solution)/shard_map/ppermute | solution.py:360
  119.6 1.1 collective-permute-start.15
  121.5 4.5 %collective-permute-done.15.refs_2_ = bf16[256,256]{1,0:T(8,128)(2,1)S(1)} collective-permute-done((bf16[256,256]{1,0:T(8,128)(2,1)S(1)}, bf16[256,256]{1,0:T(8,128)(2,1)S(1)}, u32[]{:S(2)}, u32[]{:S(2)}) %collective-permute-start.15) | collective-permute-done | bytes 131104 | tf_op jit(solution)/shard_map/ppermute | solution.py:360
  126.0 1.9 %collective-permute-done.16.refs_3_ = bf16[256,256]{1,0:T(8,128)(2,1)S(1)} collective-permute-done((bf16[256,256]{1,0:T(8,128)(2,1)S(1)}, bf16[256,256]{1,0:T(8,128)(2,1)S(1)}, u32[]{:S(2)}, u32[]{:S(2)}) %collective-permute-start.16) | collective-permute-done | bytes 131104 | tf_op jit(solution)/shard_map/ppermute | solution.py:360
  128.5 2.1 %place_all.1 = f32[4,256,256]{2,1,0:T(8,128)} custom-call(s32[2]{0:T(128)} %pad_add_fusion.place_ref, bf16[256,256]{1,0:T(8,128)(2,1)} %copy-done.1, bf16[256,256]{1,0:T(8,128)(2,1)} %copy-done.3, bf16[256,256]{1,0:T(8,128)(2,1)} %copy-done.4, bf16[256,256]{1,0:T(8,128)(2,1)} %copy-done.5), custom_call_target="tpu_custom_call" | custom-call | tf_op jit(solution)/shard_map/place_all/pallas_call | solution.py:349
  (51 shorter events, 9.8 us)
Async XLA Ops:
  1.5 3.3 %collective-permute-start = (bf16[8,64,128]{2,1,0:T(8,128)(2,1)S(1)}, bf16[8,64,128]{2,1,0:T(8,128)(2,1)S(1)}, u32[]{:S(2)}, u32[]{:S(2)}) collective-permute-start(bf16[8,64,128]{2,1,0:T(8,128)(2,1)S(1)} %slice.3), channel_id=1, source_target_pairs={{0,8},{8,16},{16,24},{1,9},{9,17},{17,25},{2,10},{10,18},{18,26},{... | collective-permute-start | bytes 393224 | tf_op jit(solution)/shard_map/ppermute | solution.py:387
  10.4 9.2 %collective-permute-start.6 = (bf16[64,1024]{1,0:T(8,128)(2,1)}, bf16[64,1024]{1,0:T(8,128)(2,1)S(1)}, u32[]{:S(2)}, u32[]{:S(2)}) collective-permute-start(bf16[64,1024]{1,0:T(8,128)(2,1)} %get-tuple-element.39), channel_id=1, source_target_pairs={{0,6},{1,7},{2,4},{3,5},{4,2},{5,3},{6,0},{7,1},{8,14},{9,15},{10,... | collective-permute-start | bytes 393224 | tf_op jit(solution)/shard_map/ppermute | solution.py:360
  14.9 8.0 %collective-permute-start.7 = (bf16[64,1024]{1,0:T(8,128)(2,1)}, bf16[64,1024]{1,0:T(8,128)(2,1)S(1)}, u32[]{:S(2)}, u32[]{:S(2)}) collective-permute-start(bf16[64,1024]{1,0:T(8,128)(2,1)} %get-tuple-element.40), channel_id=1, source_target_pairs={{0,7},{1,6},{2,5},{3,4},{4,3},{5,2},{6,1},{7,0},{8,15},{9,14},{10,... | collective-permute-start | bytes 393224 | tf_op jit(solution)/shard_map/ppermute | solution.py:360
  16.1 16.8 %collective-permute-start.1 = (bf16[64,1024]{1,0:T(8,128)(2,1)}, bf16[64,1024]{1,0:T(8,128)(2,1)S(1)}, u32[]{:S(2)}, u32[]{:S(2)}) collective-permute-start(bf16[64,1024]{1,0:T(8,128)(2,1)} %get-tuple-element.34), channel_id=1, source_target_pairs={{0,1},{1,0},{2,3},{3,2},{4,5},{5,4},{6,7},{7,6},{8,9},{9,8},{10,11... | collective-permute-start | bytes 393224 | tf_op jit(solution)/shard_map/ppermute | solution.py:360
  16.4 16.5 %collective-permute-start.2 = (bf16[64,1024]{1,0:T(8,128)(2,1)}, bf16[64,1024]{1,0:T(8,128)(2,1)S(1)}, u32[]{:S(2)}, u32[]{:S(2)}) collective-permute-start(bf16[64,1024]{1,0:T(8,128)(2,1)} %get-tuple-element.35), channel_id=1, source_target_pairs={{0,2},{1,3},{2,0},{3,1},{4,6},{5,7},{6,4},{7,5},{8,10},{9,11},{10,... | collective-permute-start | bytes 393224 | tf_op jit(solution)/shard_map/ppermute | solution.py:360
  16.4 16.5 %collective-permute-start.3 = (bf16[64,1024]{1,0:T(8,128)(2,1)}, bf16[64,1024]{1,0:T(8,128)(2,1)S(1)}, u32[]{:S(2)}, u32[]{:S(2)}) collective-permute-start(bf16[64,1024]{1,0:T(8,128)(2,1)} %get-tuple-element.36), channel_id=1, source_target_pairs={{0,3},{1,2},{2,1},{3,0},{4,7},{5,6},{6,5},{7,4},{8,11},{9,10},{10,... | collective-permute-start | bytes 393224 | tf_op jit(solution)/shard_map/ppermute | solution.py:360
  19.6 19.0 %copy-start.6 = (bf16[64,1024]{1,0:T(8,128)(2,1)}, bf16[64,1024]{1,0:T(8,128)(2,1)S(1)}, u32[]{:S(2)}) copy-start(bf16[64,1024]{1,0:T(8,128)(2,1)S(1)} %collective-permute-done.6.refs_6_) | copy-start | bytes 393220
  19.6 13.4 %collective-permute-start.4 = (bf16[64,1024]{1,0:T(8,128)(2,1)}, bf16[64,1024]{1,0:T(8,128)(2,1)S(1)}, u32[]{:S(2)}, u32[]{:S(2)}) collective-permute-start(bf16[64,1024]{1,0:T(8,128)(2,1)} %get-tuple-element.37), channel_id=1, source_target_pairs={{0,4},{1,5},{2,6},{3,7},{4,0},{5,1},{6,2},{7,3},{8,12},{9,13},{10,... | collective-permute-start | bytes 393224 | tf_op jit(solution)/shard_map/ppermute | solution.py:360
  22.9 15.7 %copy-start.7 = (bf16[64,1024]{1,0:T(8,128)(2,1)}, bf16[64,1024]{1,0:T(8,128)(2,1)S(1)}, u32[]{:S(2)}) copy-start(bf16[64,1024]{1,0:T(8,128)(2,1)S(1)} %collective-permute-done.7.refs_7_) | copy-start | bytes 393220
  22.9 15.6 %collective-permute-start.5 = (bf16[64,1024]{1,0:T(8,128)(2,1)}, bf16[64,1024]{1,0:T(8,128)(2,1)S(1)}, u32[]{:S(2)}, u32[]{:S(2)}) collective-permute-start(bf16[64,1024]{1,0:T(8,128)(2,1)} %get-tuple-element.38), channel_id=1, source_target_pairs={{0,5},{1,4},{2,7},{3,6},{4,1},{5,0},{6,3},{7,2},{8,13},{9,12},{10,... | collective-permute-start | bytes 393224 | tf_op jit(solution)/shard_map/ppermute | solution.py:360
  28.0 32.1 %all-to-all-start = ((bf16[8,64,1024]{2,1,0:T(8,128)(2,1)}), bf16[8,64,1024]{2,1,0:T(8,128)(2,1)S(1)}, u32[]{:S(2)}, u32[]{:S(2)}) async-start(bf16[8,64,1024]{2,1,0:T(8,128)(2,1)} %param.19), calls=%async_computation | async-start | bytes 2097152 | tf_op jit(solution)/shard_map/all_to_all | solution.py:369
  32.9 5.7 %copy-start.8 = (bf16[64,1024]{1,0:T(8,128)(2,1)}, bf16[64,1024]{1,0:T(8,128)(2,1)S(1)}, u32[]{:S(2)}) copy-start(bf16[64,1024]{1,0:T(8,128)(2,1)S(1)} %collective-permute-done.1.refs_1_) | copy-start | bytes 393220
  76.4 43.2 %all-to-all-start.1 = ((bf16[8,64,1024]{2,1,0:T(8,128)(2,1)}), bf16[8,64,1024]{2,1,0:T(8,128)(2,1)S(1)}, u32[]{:S(2)}, u32[]{:S(2)}) async-start(bf16[8,64,1024]{2,1,0:T(8,128)(2,1)} %get-tuple-element.58), calls=%async_computation.1 | async-start | bytes 2097152 | tf_op jit(solution)/shard_map/all_to_all | solution.py:369
  80.8 9.9 %collective-permute-start.10 = (bf16[256,256]{1,0:T(8,128)(2,1)}, bf16[256,256]{1,0:T(8,128)(2,1)S(1)}, u32[]{:S(2)}, u32[]{:S(2)}) collective-permute-start(bf16[256,256]{1,0:T(8,128)(2,1)} %get-tuple-element.62), channel_id=1, source_target_pairs={{0,24},{8,16},{16,8},{24,0},{1,25},{9,17},{17,9},{25,1},{2,26},{10... | collective-permute-start | bytes 393224 | tf_op jit(solution)/shard_map/ppermute | solution.py:360
  81.1 15.4 %collective-permute-start.9 = (bf16[256,256]{1,0:T(8,128)(2,1)}, bf16[256,256]{1,0:T(8,128)(2,1)S(1)}, u32[]{:S(2)}, u32[]{:S(2)}) collective-permute-start(bf16[256,256]{1,0:T(8,128)(2,1)} %get-tuple-element.61), channel_id=1, source_target_pairs={{0,16},{8,24},{16,0},{24,8},{1,17},{9,25},{17,1},{25,9},{2,18},{10... | collective-permute-start | bytes 393224 | tf_op jit(solution)/shard_map/ppermute | solution.py:360
  90.6 5.9 %collective-permute-start.8 = (bf16[256,256]{1,0:T(8,128)(2,1)}, bf16[256,256]{1,0:T(8,128)(2,1)S(1)}, u32[]{:S(2)}, u32[]{:S(2)}) collective-permute-start(bf16[256,256]{1,0:T(8,128)(2,1)} %get-tuple-element.60), channel_id=1, source_target_pairs={{0,8},{8,0},{16,24},{24,16},{1,9},{9,1},{17,25},{25,17},{2,10},{10... | collective-permute-start | bytes 393224 | tf_op jit(solution)/shard_map/ppermute | solution.py:360
  97.5 7.1 %collective-permute-start.11 = (bf16[256,256]{1,0:T(8,128)(2,1)S(1)}, bf16[256,256]{1,0:T(8,128)(2,1)S(1)}, u32[]{:S(2)}, u32[]{:S(2)}) collective-permute-start(bf16[256,256]{1,0:T(8,128)(2,1)S(1)} %add_convert_fusion.2), channel_id=1, source_target_pairs={{0,1},{1,0},{2,3},{3,2},{4,5},{5,4},{6,7},{7,6},{8,9},{9,8},{10,11... | collective-permute-start | bytes 393224 | tf_op jit(solution)/shard_map/ppermute | solution.py:360
  104.6 6.6 %collective-permute-start.12 = (bf16[256,256]{1,0:T(8,128)(2,1)S(1)}, bf16[256,256]{1,0:T(8,128)(2,1)S(1)}, u32[]{:S(2)}, u32[]{:S(2)}) collective-permute-start(bf16[256,256]{1,0:T(8,128)(2,1)S(1)} %add_convert_fusion.1), channel_id=1, source_target_pairs={{0,2},{1,3},{2,0},{3,1},{4,6},{5,7},{6,4},{7,5},{8,10},{9,11},{10,... | collective-permute-start | bytes 393224 | tf_op jit(solution)/shard_map/ppermute | solution.py:360
  111.3 8.2 %collective-permute-start.13 = (bf16[256,256]{1,0:T(8,128)(2,1)S(1)}, bf16[256,256]{1,0:T(8,128)(2,1)S(1)}, u32[]{:S(2)}, u32[]{:S(2)}) collective-permute-start(bf16[256,256]{1,0:T(8,128)(2,1)S(1)} %add_convert_fusion), channel_id=1, source_target_pairs={{0,4},{1,5},{2,6},{3,7},{4,0},{5,1},{6,2},{7,3},{8,12},{9,13},{10,... | collective-permute-start | bytes 393224 | tf_op jit(solution)/shard_map/ppermute | solution.py:360
  119.5 8.4 %copy-start.1 = (bf16[256,256]{1,0:T(8,128)(2,1)}, bf16[256,256]{1,0:T(8,128)(2,1)S(1)}, u32[]{:S(2)}) copy-start(bf16[256,256]{1,0:T(8,128)(2,1)S(1)} %multiply_convert_fusion.refs_0_) | copy-start | bytes 393220
  119.5 1.9 %collective-permute-start.14 = (bf16[256,256]{1,0:T(8,128)(2,1)S(1)}, bf16[256,256]{1,0:T(8,128)(2,1)S(1)}, u32[]{:S(2)}, u32[]{:S(2)}) collective-permute-start(bf16[256,256]{1,0:T(8,128)(2,1)S(1)} %multiply_convert_fusion.refs_0_), channel_id=1, source_target_pairs={{0,8},{8,0},{16,24},{24,16},{1,9},{9,1},{17,25},{25,17},{2,10},{10... | collective-permute-start | bytes 393224 | tf_op jit(solution)/shard_map/ppermute | solution.py:360
  119.6 6.4 %collective-permute-start.15 = (bf16[256,256]{1,0:T(8,128)(2,1)S(1)}, bf16[256,256]{1,0:T(8,128)(2,1)S(1)}, u32[]{:S(2)}, u32[]{:S(2)}) collective-permute-start(bf16[256,256]{1,0:T(8,128)(2,1)S(1)} %multiply_convert_fusion.refs_0_), channel_id=1, source_target_pairs={{0,16},{8,24},{16,0},{24,8},{1,17},{9,25},{17,1},{25,9},{2,18},{10... | collective-permute-start | bytes 393224 | tf_op jit(solution)/shard_map/ppermute | solution.py:360
  120.7 7.2 %collective-permute-start.16 = (bf16[256,256]{1,0:T(8,128)(2,1)S(1)}, bf16[256,256]{1,0:T(8,128)(2,1)S(1)}, u32[]{:S(2)}, u32[]{:S(2)}) collective-permute-start(bf16[256,256]{1,0:T(8,128)(2,1)S(1)} %multiply_convert_fusion.refs_0_), channel_id=1, source_target_pairs={{0,24},{8,16},{16,8},{24,0},{1,25},{9,17},{17,9},{25,1},{2,26},{10... | collective-permute-start | bytes 393224 | tf_op jit(solution)/shard_map/ppermute | solution.py:360
  121.5 6.4 %copy-start.3 = (bf16[256,256]{1,0:T(8,128)(2,1)}, bf16[256,256]{1,0:T(8,128)(2,1)S(1)}, u32[]{:S(2)}) copy-start(bf16[256,256]{1,0:T(8,128)(2,1)S(1)} %collective-permute-done.14.refs_1_) | copy-start | bytes 393220
  (8 other events, 21.9 us)

commit v13 on v11

--- a/solution.py
+++ b/solution.py
@@ -22,8 +22,8 @@
     return pl.BlockSpec(memory_space=pltpu.SMEM)
 
 
-def params():
-    return pltpu.CompilerParams(vmem_limit_bytes=56 * 2**20)
+def params(mebibytes=56):
+    return pltpu.CompilerParams(vmem_limit_bytes=mebibytes * 2**20)
 
 
 def filter_kernel(place_ref, sig_ref, rim_ref, taps_ref, *refs):
@@ -351,9 +351,26 @@
         in_specs=[index_spec()] + [pl.BlockSpec((rows, width), lambda: (0, 0))] * ways,
         out_specs=pl.BlockSpec(shape, lambda: (0, 0, 0)),
         out_shape=jax.ShapeDtypeStruct(shape, F32),
-        compiler_params=params(),
+        compiler_params=params(63),
         name="place_all",
     )(place, *parts)
+
+
+def write_out(value):
+    def body(in_ref, out_ref):
+        out_ref[...] = in_ref[...]
+
+    spec = pl.BlockSpec((value.shape[0] // 2,) + value.shape[1:], lambda i: (i, 0, 0))
+    return pl.pallas_call(
+        body,
+        grid=(2,),
+        in_specs=[spec],
+        out_specs=spec,
+        out_shape=jax.ShapeDtypeStruct(value.shape, value.dtype),
+        compiler_params=params(),
+        cost_estimate=pl.CostEstimate(flops=0, bytes_accessed=4 * value.size, transcendentals=0),
+        name="write_out",
+    )(value)
 
 
 def swap(value, axis, k):
@@ -396,17 +413,19 @@
         place, features, neighbours.T, live_mask[None], lap_coef[None],
         [w_query, w_key, w_value, w_out],
     )
-    returned = exchange(attended, "contact")
     grads = backward(place, upstream, kept, w_out, tm_count)
     grads = swap_all(grads, "tm")
+    attended, grads[1] = lax.optimization_barrier((attended, grads[1]))
+    returned = exchange(attended, "contact")
     part = sum(piece.astype(F32) for piece in grads).astype(BF16)
-    part, _ = lax.optimization_barrier((part, returned))
     grad_scale = (batch * (slab // width) * tm_count * neighbours.shape[0]) ** (-0.5)
     step = 1
     while step < count:
         both = part.astype(F32) + swap(part, "contact", step).astype(F32)
         step *= 2
         part = lax.optimization_barrier((both * (1.0 if step < count else grad_scale)).astype(BF16))
+    part, returned = lax.optimization_barrier((part, returned))
+    returned = write_out(returned)
     summed = place_all(place, swap_all([part] * tm_count, "tm"))
     if pieces > 1:
         returned = returned.reshape(batch, pieces, contacts_here, span)

time: 128 us -> 139 us (1.086)
  waiting for transfers between devices: 32.5 us -> 44 us
  starting transfers between devices: 48.4 us -> 45.9 us
  Pallas kernels: 40.7 us -> 42.7 us
    ppermute x16, waiting for transfers between devices: 29.7 us -> 41.2 us  [swap(): lax.ppermute(value, axis, [(i, i ^ k) for i in range(lax.axis_size(axis))])]
    ppermute x16, starting transfers between devices: 36.7 us -> 28.9 us  [swap(): lax.ppermute(value, axis, [(i, i ^ k) for i in range(lax.axis_size(axis))])]
    all_to_all x2, starting transfers between devices: 9.33 us -> 14.6 us  [exchange(): return lax.all_to_all(value, axis, split_axis=0, concat_axis=0, tiled=True)]
    pallas_call x0 -> x1, Pallas kernels: none -> 2.04 us  [write_out(): pl.pallas_call(body, grid=(2,), in_specs=[spec], out_specs=spec, out_shap...]
    unnamed x27 -> x28, local copies, waits for them, and re-layouts: 2.91 us -> 2.91 us
  transfers between devices with their start and end apart: 19 -> 19, of which waited for: 11 -> 12; matrix products, arithmetic and copies ran while one was open for 1% -> 1% of each run, Pallas kernels for 26% -> 15%
where the time goes in v13:
time: 139 us
  starting transfers between devices  45.9 us (33%)
  waiting for transfers between devices  44 us (32%)
  Pallas kernels  42.7 us (31%)
  local copies, waits for them, and re-layouts  3.82 us (3%)
  other arithmetic  1.76 us (1%)
    ppermute x16, waiting for transfers between devices, swap(): lax.ppermute(value, axis, [(i, i ^ k) for i in range(lax.axis_size(axis))])  41.2 us
    ppermute x16, starting transfers between devices, swap(): lax.ppermute(value, axis, [(i, i ^ k) for i in range(lax.axis_size(axis))])  28.9 us
    pallas_call x1, Pallas kernels, forward(): pl.pallas_call(functools.partial(forward_kernel, blocks), grid=(groups,),...  18.3 us
    pallas_call x1, Pallas kernels, backward(): pl.pallas_call(functools.partial(backward_kernel, blocks), grid=(groups,)...  15.3 us
    all_to_all x2, starting transfers between devices, exchange(): return lax.all_to_all(value, axis, split_axis=0, concat_axis=0, tiled=True)  14.6 us
    pallas_call x1, Pallas kernels, filter_all(): pl.pallas_call(filter_kernel, grid=(contacts // rows,), in_specs=[index_s...  4.85 us
    unnamed x28, local copies, waits for them, and re-layouts  2.91 us
  transfers between devices with their start and end apart: 19, of which 12 were waited for; matrix products, arithmetic and copies ran while one was open for 1% of the time, Pallas kernels for 15%

profile of v13, /device:TPU:0, one launch (start us, length us, event | category | flops | bytes accessed | tf_op | source)
XLA Modules:
  0.0 139.0 jit_solution(3163512659182471174)
XLA Ops:
  1.5 2.4 %collective-permute-start = (bf16[8,64,128]{2,1,0:T(8,128)(2,1)S(1)}, bf16[8,64,128]{2,1,0:T(8,128)(2,1)S(1)}, u32[]{:S(2)}, u32[]{:S(2)}) collective-permute-start(bf16[8,64,128]{2,1,0:T(8,128)(2,1)S(1)} %slice.3), channel_id=1, source_target_pairs={{0,8},{8,16},{16,24},{1,9},{9,17},{17,25},{2,10},{10,18},{18,26},{... | collective-permute-start | bytes 393224 | tf_op jit(solution)/shard_map/ppermute | solution.py:404
  5.5 4.8 %filter.1 = (bf16[64,1024]{1,0:T(8,128)(2,1)}, bf16[64,1024]{1,0:T(8,128)(2,1)}, bf16[64,1024]{1,0:T(8,128)(2,1)}, bf16[64,1024]{1,0:T(8,128)(2,1)}, bf16[64,102...) custom-call(s32[2]{0:T(128)} %pad_add_fusion.place_ref, ...), custom_call_target="tpu_custom_call" | custom-call | flops 268435456 | bytes 2097152 | tf_op jit(solution)/shard_map/filter/pallas_call | solution.py:72
  10.4 4.5 %collective-permute-start.1 = (bf16[64,1024]{1,0:T(8,128)(2,1)}, bf16[64,1024]{1,0:T(8,128)(2,1)S(1)}, u32[]{:S(2)}, u32[]{:S(2)}) collective-permute-start(bf16[64,1024]{1,0:T(8,128)(2,1)} %get-tuple-element.31), channel_id=1, source_target_pairs={{0,6},{1,7},{2,4},{3,5},{4,2},{5,3},{6,0},{7,1},{8,14},{9,15},{10,... | collective-permute-start | bytes 393224 | tf_op jit(solution)/shard_map/ppermute | solution.py:377
  16.4 3.1 %collective-permute-start.5 = (bf16[64,1024]{1,0:T(8,128)(2,1)}, bf16[64,1024]{1,0:T(8,128)(2,1)S(1)}, u32[]{:S(2)}, u32[]{:S(2)}) collective-permute-start(bf16[64,1024]{1,0:T(8,128)(2,1)} %get-tuple-element.37), channel_id=1, source_target_pairs={{0,3},{1,2},{2,1},{3,0},{4,7},{5,6},{6,5},{7,4},{8,11},{9,10},{10,... | collective-permute-start | bytes 393224 | tf_op jit(solution)/shard_map/ppermute | solution.py:377
  19.6 2.1 %collective-permute-start.6 = (bf16[64,1024]{1,0:T(8,128)(2,1)}, bf16[64,1024]{1,0:T(8,128)(2,1)S(1)}, u32[]{:S(2)}, u32[]{:S(2)}) collective-permute-start(bf16[64,1024]{1,0:T(8,128)(2,1)} %get-tuple-element.38), channel_id=1, source_target_pairs={{0,4},{1,5},{2,6},{3,7},{4,0},{5,1},{6,2},{7,3},{8,12},{9,13},{10,... | collective-permute-start | bytes 393224 | tf_op jit(solution)/shard_map/ppermute | solution.py:377
  22.9 5.0 %collective-permute-start.7 = (bf16[64,1024]{1,0:T(8,128)(2,1)}, bf16[64,1024]{1,0:T(8,128)(2,1)S(1)}, u32[]{:S(2)}, u32[]{:S(2)}) collective-permute-start(bf16[64,1024]{1,0:T(8,128)(2,1)} %get-tuple-element.39), channel_id=1, source_target_pairs={{0,5},{1,4},{2,7},{3,6},{4,1},{5,0},{6,3},{7,2},{8,13},{9,12},{10,... | collective-permute-start | bytes 393224 | tf_op jit(solution)/shard_map/ppermute | solution.py:377
  28.0 4.9 %all-to-all-start = ((bf16[8,64,1024]{2,1,0:T(8,128)(2,1)}), bf16[8,64,1024]{2,1,0:T(8,128)(2,1)S(1)}, u32[]{:S(2)}, u32[]{:S(2)}) async-start(bf16[8,64,1024]{2,1,0:T(8,128)(2,1)} %param.19), calls=%async_computation | async-start | bytes 2097152 | tf_op jit(solution)/shard_map/all_to_all | solution.py:386
  32.9 5.6 %collective-permute-done.7.refs_5_ = bf16[64,1024]{1,0:T(8,128)(2,1)S(1)} collective-permute-done((bf16[64,1024]{1,0:T(8,128)(2,1)}, bf16[64,1024]{1,0:T(8,128)(2,1)S(1)}, u32[]{:S(2)}, u32[]{:S(2)}) %collective-permute-start.7) | collective-permute-done | bytes 131104 | tf_op jit(solution)/shard_map/ppermute | solution.py:377
  39.2 18.3 %forward.1 = (bf16[8,64,1024]{2,1,0:T(8,128)(2,1)}, bf16[512,8192]{1,0:T(8,128)(2,1)}, bf16[512,1024]{1,0:T(8,128)(2,1)}, bf16[512,1024]{1,0:T(8,128)(2,1)}, bf1...) custom-call(s32[2]{0:T(128)} %pad_add_fusion.place_ref, ...), custom_call_target="tpu_custom_call" | custom-call | flops 20000000000 | bytes 10485760 | tf_op jit(solution)/shard_map/forward/pallas_call | solution.py:278
  57.6 2.5 %all-to-all-done.up_ref = bf16[8,64,1024]{2,1,0:T(8,128)(2,1)S(1)} async-done(((bf16[8,64,1024]{2,1,0:T(8,128)(2,1)}), bf16[8,64,1024]{2,1,0:T(8,128)(2,1)S(1)}, u32[]{:S(2)}, u32[]{:S(2)}) %all-to-all-start) | async-done | bytes 1048608 | tf_op jit(solution)/shard_map/all_to_all | solution.py:386
  61.0 15.3 %backward.1 = (bf16[256,256]{1,0:T(8,128)(2,1)}, bf16[256,256]{1,0:T(8,128)(2,1)}, bf16[256,256]{1,0:T(8,128)(2,1)}, bf16[256,256]{1,0:T(8,128)(2,1)}) custom-call(s32[2]{0:T(128)} %pad_add_fusion.place_ref, bf16[256,256]{1,0:T(8,128)(2,1)} %wo_ref.3, bf16[8,64,1024]{2,1,0:T(8,128)(2,1)} %copy-done.1, bf16[512,8192]{1,0:T(8,128)(2,1)} %get-tuple-element.42.prob_ref, ...), custom_call_target="tpu_custom_call" | custom-call | flops 20000000000 | bytes 10485760 | tf_op jit(solution)/shard_map/backward/pallas_call | solution.py:314
  79.2 9.7 %all-to-all-start.1 = ((bf16[8,64,1024]{2,1,0:T(8,128)(2,1)}), bf16[8,64,1024]{2,1,0:T(8,128)(2,1)S(1)}, u32[]{:S(2)}, u32[]{:S(2)}) async-start(bf16[8,64,1024]{2,1,0:T(8,128)(2,1)} %get-tuple-element.57), calls=%async_computation.1 | async-start | bytes 2097152 | tf_op jit(solution)/shard_map/all_to_all | solution.py:386
  88.9 2.7 %collective-permute-start.10 = (bf16[256,256]{1,0:T(8,128)(2,1)}, bf16[256,256]{1,0:T(8,128)(2,1)S(1)}, u32[]{:S(2)}, u32[]{:S(2)}) collective-permute-start(bf16[256,256]{1,0:T(8,128)(2,1)} %get-tuple-element.56), channel_id=1, source_target_pairs={{0,24},{8,16},{16,8},{24,0},{1,25},{9,17},{17,9},{25,1},{2,26},{10... | collective-permute-start | bytes 393224 | tf_op jit(solution)/shard_map/ppermute | solution.py:377
  92.2 3.6 %collective-permute-done.10 = bf16[256,256]{1,0:T(8,128)(2,1)S(1)} collective-permute-done((bf16[256,256]{1,0:T(8,128)(2,1)}, bf16[256,256]{1,0:T(8,128)(2,1)S(1)}, u32[]{:S(2)}, u32[]{:S(2)}) %collective-permute-start.10) | collective-permute-done | bytes 131104 | tf_op jit(solution)/shard_map/ppermute | solution.py:377
  95.8 2.9 %collective-permute-done.9 = bf16[256,256]{1,0:T(8,128)(2,1)S(1)} collective-permute-done((bf16[256,256]{1,0:T(8,128)(2,1)}, bf16[256,256]{1,0:T(8,128)(2,1)S(1)}, u32[]{:S(2)}, u32[]{:S(2)}) %collective-permute-start.9) | collective-permute-done | bytes 131104 | tf_op jit(solution)/shard_map/ppermute | solution.py:377
  101.4 6.5 %collective-permute-done.11 = bf16[256,256]{1,0:T(8,128)(2,1)S(1)} collective-permute-done((bf16[256,256]{1,0:T(8,128)(2,1)S(1)}, bf16[256,256]{1,0:T(8,128)(2,1)S(1)}, u32[]{:S(2)}, u32[]{:S(2)}) %collective-permute-start.11) | collective-permute-done | bytes 131104 | tf_op jit(solution)/shard_map/ppermute | solution.py:377
  108.0 2.7 %collective-permute-start.12 = (bf16[256,256]{1,0:T(8,128)(2,1)S(1)}, bf16[256,256]{1,0:T(8,128)(2,1)S(1)}, u32[]{:S(2)}, u32[]{:S(2)}) collective-permute-start(bf16[256,256]{1,0:T(8,128)(2,1)S(1)} %add_convert_fusion.1), channel_id=1, source_target_pairs={{0,2},{1,3},{2,0},{3,1},{4,6},{5,7},{6,4},{7,5},{8,10},{9,11},{10,... | collective-permute-start | bytes 393224 | tf_op jit(solution)/shard_map/ppermute | solution.py:377
  110.7 7.3 %collective-permute-done.12 = bf16[256,256]{1,0:T(8,128)(2,1)S(1)} collective-permute-done((bf16[256,256]{1,0:T(8,128)(2,1)S(1)}, bf16[256,256]{1,0:T(8,128)(2,1)S(1)}, u32[]{:S(2)}, u32[]{:S(2)}) %collective-permute-start.12) | collective-permute-done | bytes 131104 | tf_op jit(solution)/shard_map/ppermute | solution.py:377
  118.1 8.4 %collective-permute-done.13 = bf16[256,256]{1,0:T(8,128)(2,1)S(1)} collective-permute-done((bf16[256,256]{1,0:T(8,128)(2,1)S(1)}, bf16[256,256]{1,0:T(8,128)(2,1)S(1)}, u32[]{:S(2)}, u32[]{:S(2)}) %collective-permute-start.13) | collective-permute-done | bytes 131104 | tf_op jit(solution)/shard_map/ppermute | solution.py:377
  126.7 2.8 %collective-permute-start.15 = (bf16[256,256]{1,0:T(8,128)(2,1)S(1)}, bf16[256,256]{1,0:T(8,128)(2,1)S(1)}, u32[]{:S(2)}, u32[]{:S(2)}) collective-permute-start(bf16[256,256]{1,0:T(8,128)(2,1)S(1)} %multiply_convert_fusion.refs_0_), channel_id=1, source_target_pairs={{0,16},{8,24},{16,0},{24,8},{1,17},{9,25},{17,1},{25,9},{2,18},{10... | collective-permute-start | bytes 393224 | tf_op jit(solution)/shard_map/ppermute | solution.py:377
  129.6 2.0 %write_out.1 = bf16[8,64,1024]{2,1,0:T(8,128)(2,1)} custom-call(bf16[8,64,1024]{2,1,0:T(8,128)(2,1)} %copy-done), custom_call_target="tpu_custom_call" | custom-call | bytes 2097152 | tf_op jit(solution)/shard_map/write_out/pallas_call | solution.py:364
  131.6 2.2 %collective-permute-done.15.refs_2_ = bf16[256,256]{1,0:T(8,128)(2,1)S(1)} collective-permute-done((bf16[256,256]{1,0:T(8,128)(2,1)S(1)}, bf16[256,256]{1,0:T(8,128)(2,1)S(1)}, u32[]{:S(2)}, u32[]{:S(2)}) %collective-permute-start.15) | collective-permute-done | bytes 131104 | tf_op jit(solution)/shard_map/ppermute | solution.py:377
  133.9 2.3 %collective-permute-done.16.refs_3_ = bf16[256,256]{1,0:T(8,128)(2,1)S(1)} collective-permute-done((bf16[256,256]{1,0:T(8,128)(2,1)S(1)}, bf16[256,256]{1,0:T(8,128)(2,1)S(1)}, u32[]{:S(2)}, u32[]{:S(2)}) %collective-permute-start.16) | collective-permute-done | bytes 131104 | tf_op jit(solution)/shard_map/ppermute | solution.py:377
  136.8 2.1 %place_all.1 = f32[4,256,256]{2,1,0:T(8,128)} custom-call(s32[2]{0:T(128)} %pad_add_fusion.place_ref, bf16[256,256]{1,0:T(8,128)(2,1)} %copy-done.2, bf16[256,256]{1,0:T(8,128)(2,1)} %copy-done.4, bf16[256,256]{1,0:T(8,128)(2,1)} %copy-done.5, bf16[256,256]{1,0:T(8,128)(2,1)} %copy-done.6), custom_call_target="tpu_custom_call" | custom-call | tf_op jit(solution)/shard_map/place_all/pallas_call | solution.py:349
  (53 shorter events, 14.1 us)
Async XLA Ops:
  1.5 3.3 %collective-permute-start = (bf16[8,64,128]{2,1,0:T(8,128)(2,1)S(1)}, bf16[8,64,128]{2,1,0:T(8,128)(2,1)S(1)}, u32[]{:S(2)}, u32[]{:S(2)}) collective-permute-start(bf16[8,64,128]{2,1,0:T(8,128)(2,1)S(1)} %slice.3), channel_id=1, source_target_pairs={{0,8},{8,16},{16,24},{1,9},{9,17},{17,25},{2,10},{10,18},{18,26},{... | collective-permute-start | bytes 393224 | tf_op jit(solution)/shard_map/ppermute | solution.py:404
  10.4 9.2 %collective-permute-start.1 = (bf16[64,1024]{1,0:T(8,128)(2,1)}, bf16[64,1024]{1,0:T(8,128)(2,1)S(1)}, u32[]{:S(2)}, u32[]{:S(2)}) collective-permute-start(bf16[64,1024]{1,0:T(8,128)(2,1)} %get-tuple-element.31), channel_id=1, source_target_pairs={{0,6},{1,7},{2,4},{3,5},{4,2},{5,3},{6,0},{7,1},{8,14},{9,15},{10,... | collective-permute-start | bytes 393224 | tf_op jit(solution)/shard_map/ppermute | solution.py:377
  14.9 8.0 %collective-permute-start.2 = (bf16[64,1024]{1,0:T(8,128)(2,1)}, bf16[64,1024]{1,0:T(8,128)(2,1)S(1)}, u32[]{:S(2)}, u32[]{:S(2)}) collective-permute-start(bf16[64,1024]{1,0:T(8,128)(2,1)} %get-tuple-element.32), channel_id=1, source_target_pairs={{0,7},{1,6},{2,5},{3,4},{4,3},{5,2},{6,1},{7,0},{8,15},{9,14},{10,... | collective-permute-start | bytes 393224 | tf_op jit(solution)/shard_map/ppermute | solution.py:377
  16.1 16.8 %collective-permute-start.3 = (bf16[64,1024]{1,0:T(8,128)(2,1)}, bf16[64,1024]{1,0:T(8,128)(2,1)S(1)}, u32[]{:S(2)}, u32[]{:S(2)}) collective-permute-start(bf16[64,1024]{1,0:T(8,128)(2,1)} %get-tuple-element.35), channel_id=1, source_target_pairs={{0,1},{1,0},{2,3},{3,2},{4,5},{5,4},{6,7},{7,6},{8,9},{9,8},{10,11... | collective-permute-start | bytes 393224 | tf_op jit(solution)/shard_map/ppermute | solution.py:377
  16.4 16.5 %collective-permute-start.4 = (bf16[64,1024]{1,0:T(8,128)(2,1)}, bf16[64,1024]{1,0:T(8,128)(2,1)S(1)}, u32[]{:S(2)}, u32[]{:S(2)}) collective-permute-start(bf16[64,1024]{1,0:T(8,128)(2,1)} %get-tuple-element.36), channel_id=1, source_target_pairs={{0,2},{1,3},{2,0},{3,1},{4,6},{5,7},{6,4},{7,5},{8,10},{9,11},{10,... | collective-permute-start | bytes 393224 | tf_op jit(solution)/shard_map/ppermute | solution.py:377
  16.4 16.5 %collective-permute-start.5 = (bf16[64,1024]{1,0:T(8,128)(2,1)}, bf16[64,1024]{1,0:T(8,128)(2,1)S(1)}, u32[]{:S(2)}, u32[]{:S(2)}) collective-permute-start(bf16[64,1024]{1,0:T(8,128)(2,1)} %get-tuple-element.37), channel_id=1, source_target_pairs={{0,3},{1,2},{2,1},{3,0},{4,7},{5,6},{6,5},{7,4},{8,11},{9,10},{10,... | collective-permute-start | bytes 393224 | tf_op jit(solution)/shard_map/ppermute | solution.py:377
  19.6 19.0 %copy-start.7 = (bf16[64,1024]{1,0:T(8,128)(2,1)}, bf16[64,1024]{1,0:T(8,128)(2,1)S(1)}, u32[]{:S(2)}) copy-start(bf16[64,1024]{1,0:T(8,128)(2,1)S(1)} %collective-permute-done.1.refs_6_) | copy-start | bytes 393220
  19.6 13.4 %collective-permute-start.6 = (bf16[64,1024]{1,0:T(8,128)(2,1)}, bf16[64,1024]{1,0:T(8,128)(2,1)S(1)}, u32[]{:S(2)}, u32[]{:S(2)}) collective-permute-start(bf16[64,1024]{1,0:T(8,128)(2,1)} %get-tuple-element.38), channel_id=1, source_target_pairs={{0,4},{1,5},{2,6},{3,7},{4,0},{5,1},{6,2},{7,3},{8,12},{9,13},{10,... | collective-permute-start | bytes 393224 | tf_op jit(solution)/shard_map/ppermute | solution.py:377
  22.9 15.7 %copy-start.8 = (bf16[64,1024]{1,0:T(8,128)(2,1)}, bf16[64,1024]{1,0:T(8,128)(2,1)S(1)}, u32[]{:S(2)}) copy-start(bf16[64,1024]{1,0:T(8,128)(2,1)S(1)} %collective-permute-done.2.refs_7_) | copy-start | bytes 393220
  22.9 15.6 %collective-permute-start.7 = (bf16[64,1024]{1,0:T(8,128)(2,1)}, bf16[64,1024]{1,0:T(8,128)(2,1)S(1)}, u32[]{:S(2)}, u32[]{:S(2)}) collective-permute-start(bf16[64,1024]{1,0:T(8,128)(2,1)} %get-tuple-element.39), channel_id=1, source_target_pairs={{0,5},{1,4},{2,7},{3,6},{4,1},{5,0},{6,3},{7,2},{8,13},{9,12},{10,... | collective-permute-start | bytes 393224 | tf_op jit(solution)/shard_map/ppermute | solution.py:377
  28.0 32.1 %all-to-all-start = ((bf16[8,64,1024]{2,1,0:T(8,128)(2,1)}), bf16[8,64,1024]{2,1,0:T(8,128)(2,1)S(1)}, u32[]{:S(2)}, u32[]{:S(2)}) async-start(bf16[8,64,1024]{2,1,0:T(8,128)(2,1)} %param.19), calls=%async_computation | async-start | bytes 2097152 | tf_op jit(solution)/shard_map/all_to_all | solution.py:386
  32.9 5.7 %copy-start.9 = (bf16[64,1024]{1,0:T(8,128)(2,1)}, bf16[64,1024]{1,0:T(8,128)(2,1)S(1)}, u32[]{:S(2)}) copy-start(bf16[64,1024]{1,0:T(8,128)(2,1)S(1)} %collective-permute-done.3.refs_1_) | copy-start | bytes 393220
  32.9 5.7 %copy-start.10 = (bf16[64,1024]{1,0:T(8,128)(2,1)}, bf16[64,1024]{1,0:T(8,128)(2,1)S(1)}, u32[]{:S(2)}) copy-start(bf16[64,1024]{1,0:T(8,128)(2,1)S(1)} %collective-permute-done.4.refs_2_) | copy-start | bytes 393220
  76.3 2.8 %collective-permute-start.8 = (bf16[256,256]{1,0:T(8,128)(2,1)}, bf16[256,256]{1,0:T(8,128)(2,1)S(1)}, u32[]{:S(2)}, u32[]{:S(2)}) collective-permute-start(bf16[256,256]{1,0:T(8,128)(2,1)} %get-tuple-element.53), channel_id=1, source_target_pairs={{0,8},{8,0},{16,24},{24,16},{1,9},{9,1},{17,25},{25,17},{2,10},{10... | collective-permute-start | bytes 393224 | tf_op jit(solution)/shard_map/ppermute | solution.py:377
  79.2 47.4 %all-to-all-start.1 = ((bf16[8,64,1024]{2,1,0:T(8,128)(2,1)}), bf16[8,64,1024]{2,1,0:T(8,128)(2,1)S(1)}, u32[]{:S(2)}, u32[]{:S(2)}) async-start(bf16[8,64,1024]{2,1,0:T(8,128)(2,1)} %get-tuple-element.57), calls=%async_computation.1 | async-start | bytes 2097152 | tf_op jit(solution)/shard_map/all_to_all | solution.py:386
  88.9 6.9 %collective-permute-start.10 = (bf16[256,256]{1,0:T(8,128)(2,1)}, bf16[256,256]{1,0:T(8,128)(2,1)S(1)}, u32[]{:S(2)}, u32[]{:S(2)}) collective-permute-start(bf16[256,256]{1,0:T(8,128)(2,1)} %get-tuple-element.56), channel_id=1, source_target_pairs={{0,24},{8,16},{16,8},{24,0},{1,25},{9,17},{17,9},{25,1},{2,26},{10... | collective-permute-start | bytes 393224 | tf_op jit(solution)/shard_map/ppermute | solution.py:377
  91.6 7.1 %collective-permute-start.9 = (bf16[256,256]{1,0:T(8,128)(2,1)}, bf16[256,256]{1,0:T(8,128)(2,1)S(1)}, u32[]{:S(2)}, u32[]{:S(2)}) collective-permute-start(bf16[256,256]{1,0:T(8,128)(2,1)} %get-tuple-element.55), channel_id=1, source_target_pairs={{0,16},{8,24},{16,0},{24,8},{1,17},{9,25},{17,1},{25,9},{2,18},{10... | collective-permute-start | bytes 393224 | tf_op jit(solution)/shard_map/ppermute | solution.py:377
  99.6 8.3 %collective-permute-start.11 = (bf16[256,256]{1,0:T(8,128)(2,1)S(1)}, bf16[256,256]{1,0:T(8,128)(2,1)S(1)}, u32[]{:S(2)}, u32[]{:S(2)}) collective-permute-start(bf16[256,256]{1,0:T(8,128)(2,1)S(1)} %add_convert_fusion.2), channel_id=1, source_target_pairs={{0,1},{1,0},{2,3},{3,2},{4,5},{5,4},{6,7},{7,6},{8,9},{9,8},{10,11... | collective-permute-start | bytes 393224 | tf_op jit(solution)/shard_map/ppermute | solution.py:377
  108.0 10.0 %collective-permute-start.12 = (bf16[256,256]{1,0:T(8,128)(2,1)S(1)}, bf16[256,256]{1,0:T(8,128)(2,1)S(1)}, u32[]{:S(2)}, u32[]{:S(2)}) collective-permute-start(bf16[256,256]{1,0:T(8,128)(2,1)S(1)} %add_convert_fusion.1), channel_id=1, source_target_pairs={{0,2},{1,3},{2,0},{3,1},{4,6},{5,7},{6,4},{7,5},{8,10},{9,11},{10,... | collective-permute-start | bytes 393224 | tf_op jit(solution)/shard_map/ppermute | solution.py:377
  118.0 8.5 %collective-permute-start.13 = (bf16[256,256]{1,0:T(8,128)(2,1)S(1)}, bf16[256,256]{1,0:T(8,128)(2,1)S(1)}, u32[]{:S(2)}, u32[]{:S(2)}) collective-permute-start(bf16[256,256]{1,0:T(8,128)(2,1)S(1)} %add_convert_fusion), channel_id=1, source_target_pairs={{0,4},{1,5},{2,6},{3,7},{4,0},{5,1},{6,2},{7,3},{8,12},{9,13},{10,... | collective-permute-start | bytes 393224 | tf_op jit(solution)/shard_map/ppermute | solution.py:377
  126.5 9.6 %copy-start.2 = (bf16[256,256]{1,0:T(8,128)(2,1)}, bf16[256,256]{1,0:T(8,128)(2,1)S(1)}, u32[]{:S(2)}) copy-start(bf16[256,256]{1,0:T(8,128)(2,1)S(1)} %multiply_convert_fusion.refs_0_) | copy-start | bytes 393220
  126.6 5.0 %collective-permute-start.14 = (bf16[256,256]{1,0:T(8,128)(2,1)S(1)}, bf16[256,256]{1,0:T(8,128)(2,1)S(1)}, u32[]{:S(2)}, u32[]{:S(2)}) collective-permute-start(bf16[256,256]{1,0:T(8,128)(2,1)S(1)} %multiply_convert_fusion.refs_0_), channel_id=1, source_target_pairs={{0,8},{8,0},{16,24},{24,16},{1,9},{9,1},{17,25},{25,17},{2,10},{10... | collective-permute-start | bytes 393224 | tf_op jit(solution)/shard_map/ppermute | solution.py:377
  126.7 7.2 %collective-permute-start.15 = (bf16[256,256]{1,0:T(8,128)(2,1)S(1)}, bf16[256,256]{1,0:T(8,128)(2,1)S(1)}, u32[]{:S(2)}, u32[]{:S(2)}) collective-permute-start(bf16[256,256]{1,0:T(8,128)(2,1)S(1)} %multiply_convert_fusion.refs_0_), channel_id=1, source_target_pairs={{0,16},{8,24},{16,0},{24,8},{1,17},{9,25},{17,1},{25,9},{2,18},{10... | collective-permute-start | bytes 393224 | tf_op jit(solution)/shard_map/ppermute | solution.py:377
  129.5 6.6 %collective-permute-start.16 = (bf16[256,256]{1,0:T(8,128)(2,1)S(1)}, bf16[256,256]{1,0:T(8,128)(2,1)S(1)}, u32[]{:S(2)}, u32[]{:S(2)}) collective-permute-start(bf16[256,256]{1,0:T(8,128)(2,1)S(1)} %multiply_convert_fusion.refs_0_), channel_id=1, source_target_pairs={{0,24},{8,16},{16,8},{24,0},{1,25},{9,17},{17,9},{25,1},{2,26},{10... | collective-permute-start | bytes 393224 | tf_op jit(solution)/shard_map/ppermute | solution.py:377
  (9 other events, 24.1 us)

commit v14 on v13

--- a/solution.py
+++ b/solution.py
@@ -22,11 +22,45 @@
     return pl.BlockSpec(memory_space=pltpu.SMEM)
 
 
-def params(mebibytes=56):
-    return pltpu.CompilerParams(vmem_limit_bytes=mebibytes * 2**20)
-
-
-def filter_kernel(place_ref, sig_ref, rim_ref, taps_ref, *refs):
+def params():
+    return pltpu.CompilerParams(vmem_limit_bytes=56 * 2**20)
+
+
+def table_kernel(taps_ref, out_ref):
+    rows, depth, width = out_ref.shape
+    taps = taps_ref[...].astype(F32)
+    first = lax.broadcasted_iota(jnp.int32, (rows, width), 1) == 0
+    taps = jnp.concatenate(
+        [taps[:, :width], jnp.where(first, taps[:, width : width + 1], 0.0)], axis=1
+    )
+    for row in range(rows):
+        spread = jnp.broadcast_to(taps[row : row + 1, :], (width, depth))
+        rolled = pltpu.roll(spread, 0, 1, stride=1, stride_axis=0).astype(BF16)
+        out_ref[row, :width, :] = rolled[:, width:]
+        out_ref[row, width:, :] = rolled[:, :width]
+
+
+def tables(taps):
+    contacts, count = taps.shape
+    width = count - 1
+    rows = 16
+    return pl.pallas_call(
+        table_kernel,
+        grid=(contacts // rows,),
+        in_specs=[pl.BlockSpec((rows, count), lambda i: (i, 0))],
+        out_specs=pl.BlockSpec((rows, 2 * width, width), lambda i: (i, 0, 0)),
+        out_shape=jax.ShapeDtypeStruct((contacts, 2 * width, width), BF16),
+        compiler_params=params(),
+        cost_estimate=pl.CostEstimate(
+            flops=contacts * width * width * 4,
+            bytes_accessed=contacts * width * width * 4,
+            transcendentals=0,
+        ),
+        name="tables",
+    )(taps)
+
+
+def filter_kernel(place_ref, sig_ref, rim_ref, table_ref, *refs):
     out_refs, kept = refs[:-1], refs[-1]
     batch, rows, slab = sig_ref.shape
     width = rim_ref.shape[2]
@@ -35,21 +69,13 @@
     span = slab // pieces
     signal = jnp.swapaxes(sig_ref[...].astype(F32), 0, 1)
     rim = jnp.swapaxes(rim_ref[...].astype(F32), 0, 1)
-    taps = taps_ref[...].astype(F32)
-    first = lax.broadcasted_iota(jnp.int32, (rows, width), 1) == 0
-    taps = jnp.concatenate(
-        [taps[:, :width], jnp.where(first, taps[:, width : width + 1], 0.0)], axis=1
-    )
     results = []
     for row in range(rows):
         own = [signal[row, :, j * width : (j + 1) * width] for j in range(blocks)]
         current = jnp.concatenate(own, axis=0)
         before = jnp.concatenate([rim[row]] + own[:-1], axis=0)
         window = jnp.concatenate([before, current], axis=1).astype(BF16)
-        spread = jnp.broadcast_to(taps[row : row + 1, :], (width, 2 * width))
-        rolled = pltpu.roll(spread, 0, 1, stride=1, stride_axis=0)
-        table = jnp.concatenate([rolled[:, width:], rolled[:, :width]], axis=0).astype(BF16)
-        product = mm(window, table)
+        product = mm(window, table_ref[row])
         results.append(
             jnp.concatenate(
                 [product[j * batch : (j + 1) * batch] for j in range(blocks)], axis=1
@@ -64,7 +90,7 @@
         out_ref[...] = kept[me ^ k]
 
 
-def filter_all(place, signal, rim, taps, count):
+def filter_all(place, signal, rim, table, count):
     batch, contacts, slab = signal.shape
     width = rim.shape[2]
     rows = 16
@@ -76,7 +102,7 @@
             index_spec(),
             pl.BlockSpec((batch, rows, slab), lambda i: (0, i, 0)),
             pl.BlockSpec((batch, rows, width), lambda i: (0, i, 0)),
-            pl.BlockSpec((rows, taps.shape[1]), lambda i: (i, 0)),
+            pl.BlockSpec((rows, 2 * width, width), lambda i: (i, 0, 0)),
         ],
         out_specs=[pl.BlockSpec((rows, span), lambda i: (i, 0))] * count,
         out_shape=[jax.ShapeDtypeStruct((contacts, span), BF16)] * count,
@@ -88,7 +114,7 @@
             transcendentals=0,
         ),
         name="filter",
-    )(place, signal, rim, taps)
+    )(place, signal, rim, table)
 
 
 def pair_masks(pair):
@@ -351,7 +377,7 @@
         in_specs=[index_spec()] + [pl.BlockSpec((rows, width), lambda: (0, 0))] * ways,
         out_specs=pl.BlockSpec(shape, lambda: (0, 0, 0)),
         out_shape=jax.ShapeDtypeStruct(shape, F32),
-        compiler_params=params(63),
+        compiler_params=params(),
         name="place_all",
     )(place, *parts)
 
@@ -404,7 +430,7 @@
     rim = lax.ppermute(
         signal[:, :, slab - rim_width :], "tm", [(i, i + 1) for i in range(tm_count - 1)]
     )
-    filtered = filter_all(place, signal, rim, fir_taps, count)
+    filtered = filter_all(place, signal, rim, tables(fir_taps), count)
     features = swap_all(filtered, "contact")
     arrived = count - max(2, count // 4)
     features[arrived:], cotangent = lax.optimization_barrier((features[arrived:], cotangent))
@@ -413,19 +439,18 @@
         place, features, neighbours.T, live_mask[None], lap_coef[None],
         [w_query, w_key, w_value, w_out],
     )
+    returned = exchange(attended, "contact")
     grads = backward(place, upstream, kept, w_out, tm_count)
     grads = swap_all(grads, "tm")
-    attended, grads[1] = lax.optimization_barrier((attended, grads[1]))
-    returned = exchange(attended, "contact")
     part = sum(piece.astype(F32) for piece in grads).astype(BF16)
+    part, returned = lax.optimization_barrier((part, returned))
+    returned = write_out(returned)
     grad_scale = (batch * (slab // width) * tm_count * neighbours.shape[0]) ** (-0.5)
     step = 1
     while step < count:
         both = part.astype(F32) + swap(part, "contact", step).astype(F32)
         step *= 2
         part = lax.optimization_barrier((both * (1.0 if step < count else grad_scale)).astype(BF16))
-    part, returned = lax.optimization_barrier((part, returned))
-    returned = write_out(returned)
     summed = place_all(place, swap_all([part] * tm_count, "tm"))
     if pieces > 1:
         returned = returned.reshape(batch, pieces, contacts_here, span)

time: 139 us -> 130 us (0.935)
  waiting for transfers between devices: 44 us -> 31.6 us
  Pallas kernels: 42.7 us -> 46.9 us
    ppermute x16, waiting for transfers between devices: 41.2 us -> 27.9 us  [swap(): lax.ppermute(value, axis, [(i, i ^ k) for i in range(lax.axis_size(axis))])]
    all_to_all x2, starting transfers between devices: 14.6 us -> 8.76 us  [exchange(): return lax.all_to_all(value, axis, split_axis=0, concat_axis=0, tiled=True)]
    ppermute x16, starting transfers between devices: 28.9 us -> 34 us  [swap(): lax.ppermute(value, axis, [(i, i ^ k) for i in range(lax.axis_size(axis))])]
    pallas_call x0 -> x1, Pallas kernels: none -> 4.18 us  [tables(): pl.pallas_call(table_kernel, grid=(contacts // rows,), in_specs=[pl.Block...]
  transfers between devices with their start and end apart: 19 -> 19, of which waited for: 12 -> 9; matrix products, arithmetic and copies ran while one was open for 1% -> 1% of each run, Pallas kernels for 15% -> 31%
where the time goes in v14:
time: 130 us; the launch traced here: 129 us
  Pallas kernels  46.9 us (36%)
  starting transfers between devices  45.1 us (35%)
  waiting for transfers between devices  31.6 us (24%)
  local copies, waits for them, and re-layouts  2.86 us (2%)
  other arithmetic  1.75 us (1%)
    ppermute x16, starting transfers between devices, swap(): lax.ppermute(value, axis, [(i, i ^ k) for i in range(lax.axis_size(axis))])  34 us
    ppermute x16, waiting for transfers between devices, swap(): lax.ppermute(value, axis, [(i, i ^ k) for i in range(lax.axis_size(axis))])  27.9 us
    pallas_call x1, Pallas kernels, forward(): pl.pallas_call(functools.partial(forward_kernel, blocks), grid=(groups,),...  18.3 us
    pallas_call x1, Pallas kernels, backward(): pl.pallas_call(functools.partial(backward_kernel, blocks), grid=(groups,)...  15.3 us
    all_to_all x2, starting transfers between devices, exchange(): return lax.all_to_all(value, axis, split_axis=0, concat_axis=0, tiled=True)  8.76 us
    pallas_call x1, Pallas kernels, filter_all(): pl.pallas_call(filter_kernel, grid=(contacts // rows,), in_specs=[index_s...  4.89 us
    pallas_call x1, Pallas kernels, tables(): pl.pallas_call(table_kernel, grid=(contacts // rows,), in_specs=[pl.Block...  4.18 us
    all_to_all x2, waiting for transfers between devices, exchange(): return lax.all_to_all(value, axis, split_axis=0, concat_axis=0, tiled=True)  3.71 us
  transfers between devices with their start and end apart: 19, of which 9 were waited for; matrix products, arithmetic and copies ran while one was open for 1% of the time, Pallas kernels for 31%

profile of v14, /device:TPU:0, one launch (start us, length us, event | category | flops | bytes accessed | tf_op | source)
XLA Modules:
  0.0 129.1 jit_solution(15157426369181866900)
XLA Ops:
  1.5 2.4 %collective-permute-start = (bf16[8,64,128]{2,1,0:T(8,128)(2,1)S(1)}, bf16[8,64,128]{2,1,0:T(8,128)(2,1)S(1)}, u32[]{:S(2)}, u32[]{:S(2)}) collective-permute-start(bf16[8,64,128]{2,1,0:T(8,128)(2,1)S(1)} %slice.3), channel_id=1, source_target_pairs={{0,8},{8,16},{16,24},{1,9},{9,17},{17,25},{2,10},{10,18},{18,26},{... | collective-permute-start | bytes 393224 | tf_op jit(solution)/shard_map/ppermute | solution.py:430
  3.9 4.2 %tables.1.table_ref = bf16[64,256,128]{2,1,0:T(8,128)(2,1)} custom-call(bf16[64,129]{1,0:T(8,128)(2,1)} %taps_ref.1), custom_call_target="tpu_custom_call" | custom-call | flops 4194304 | bytes 4194304 | tf_op jit(solution)/shard_map/tables/pallas_call | solution.py:47
  9.4 4.9 %filter.1 = (bf16[64,1024]{1,0:T(8,128)(2,1)}, bf16[64,1024]{1,0:T(8,128)(2,1)}, bf16[64,1024]{1,0:T(8,128)(2,1)}, bf16[64,1024]{1,0:T(8,128)(2,1)}, bf16[64,102...) custom-call(s32[2]{0:T(128)} %pad_add_fusion.place_ref, ...), custom_call_target="tpu_custom_call" | custom-call | flops 268435456 | bytes 2097152 | tf_op jit(solution)/shard_map/filter/pallas_call | solution.py:98
  14.3 4.5 %collective-permute-start.1 = (bf16[64,1024]{1,0:T(8,128)(2,1)}, bf16[64,1024]{1,0:T(8,128)(2,1)S(1)}, u32[]{:S(2)}, u32[]{:S(2)}) collective-permute-start(bf16[64,1024]{1,0:T(8,128)(2,1)} %get-tuple-element.29), channel_id=1, source_target_pairs={{0,6},{1,7},{2,4},{3,5},{4,2},{5,3},{6,0},{7,1},{8,14},{9,15},{10,... | collective-permute-start | bytes 393224 | tf_op jit(solution)/shard_map/ppermute | solution.py:403
  20.4 3.1 %collective-permute-start.5 = (bf16[64,1024]{1,0:T(8,128)(2,1)}, bf16[64,1024]{1,0:T(8,128)(2,1)S(1)}, u32[]{:S(2)}, u32[]{:S(2)}) collective-permute-start(bf16[64,1024]{1,0:T(8,128)(2,1)} %get-tuple-element.35), channel_id=1, source_target_pairs={{0,3},{1,2},{2,1},{3,0},{4,7},{5,6},{6,5},{7,4},{8,11},{9,10},{10,... | collective-permute-start | bytes 393224 | tf_op jit(solution)/shard_map/ppermute | solution.py:403
  23.5 5.0 %collective-permute-start.6 = (bf16[64,1024]{1,0:T(8,128)(2,1)}, bf16[64,1024]{1,0:T(8,128)(2,1)S(1)}, u32[]{:S(2)}, u32[]{:S(2)}) collective-permute-start(bf16[64,1024]{1,0:T(8,128)(2,1)} %get-tuple-element.36), channel_id=1, source_target_pairs={{0,4},{1,5},{2,6},{3,7},{4,0},{5,1},{6,2},{7,3},{8,12},{9,13},{10,... | collective-permute-start | bytes 393224 | tf_op jit(solution)/shard_map/ppermute | solution.py:403
  28.5 4.9 %collective-permute-start.7 = (bf16[64,1024]{1,0:T(8,128)(2,1)}, bf16[64,1024]{1,0:T(8,128)(2,1)S(1)}, u32[]{:S(2)}, u32[]{:S(2)}) collective-permute-start(bf16[64,1024]{1,0:T(8,128)(2,1)} %get-tuple-element.37), channel_id=1, source_target_pairs={{0,5},{1,4},{2,7},{3,6},{4,1},{5,0},{6,3},{7,2},{8,13},{9,12},{10,... | collective-permute-start | bytes 393224 | tf_op jit(solution)/shard_map/ppermute | solution.py:403
  33.4 3.6 %all-to-all-start = ((bf16[8,64,1024]{2,1,0:T(8,128)(2,1)}), bf16[8,64,1024]{2,1,0:T(8,128)(2,1)S(1)}, u32[]{:S(2)}, u32[]{:S(2)}) async-start(bf16[8,64,1024]{2,1,0:T(8,128)(2,1)} %param.19), calls=%async_computation | async-start | bytes 2097152 | tf_op jit(solution)/shard_map/all_to_all | solution.py:412
  37.0 6.3 %collective-permute-done.7.refs_5_ = bf16[64,1024]{1,0:T(8,128)(2,1)S(1)} collective-permute-done((bf16[64,1024]{1,0:T(8,128)(2,1)}, bf16[64,1024]{1,0:T(8,128)(2,1)S(1)}, u32[]{:S(2)}, u32[]{:S(2)}) %collective-permute-start.7) | collective-permute-done | bytes 131104 | tf_op jit(solution)/shard_map/ppermute | solution.py:403
  44.0 18.3 %forward.1 = (bf16[8,64,1024]{2,1,0:T(8,128)(2,1)}, bf16[512,8192]{1,0:T(8,128)(2,1)}, bf16[512,1024]{1,0:T(8,128)(2,1)}, bf16[512,1024]{1,0:T(8,128)(2,1)}, bf1...) custom-call(s32[2]{0:T(128)} %pad_add_fusion.place_ref, ...), custom_call_target="tpu_custom_call" | custom-call | flops 20000000000 | bytes 10485760 | tf_op jit(solution)/shard_map/forward/pallas_call | solution.py:304
  62.4 3.7 %all-to-all-done.up_ref = bf16[8,64,1024]{2,1,0:T(8,128)(2,1)S(1)} async-done(((bf16[8,64,1024]{2,1,0:T(8,128)(2,1)}), bf16[8,64,1024]{2,1,0:T(8,128)(2,1)S(1)}, u32[]{:S(2)}, u32[]{:S(2)}) %all-to-all-start) | async-done | bytes 1048608 | tf_op jit(solution)/shard_map/all_to_all | solution.py:412
  66.1 5.2 %all-to-all-start.1 = ((bf16[8,64,1024]{2,1,0:T(8,128)(2,1)}), bf16[8,64,1024]{2,1,0:T(8,128)(2,1)S(1)}, u32[]{:S(2)}, u32[]{:S(2)}) async-start(bf16[8,64,1024]{2,1,0:T(8,128)(2,1)} %get-tuple-element.53), calls=%async_computation.1 | async-start | bytes 2097152 | tf_op jit(solution)/shard_map/all_to_all | solution.py:412
  71.3 15.3 %backward.1 = (bf16[256,256]{1,0:T(8,128)(2,1)}, bf16[256,256]{1,0:T(8,128)(2,1)}, bf16[256,256]{1,0:T(8,128)(2,1)}, bf16[256,256]{1,0:T(8,128)(2,1)}) custom-call(s32[2]{0:T(128)} %pad_add_fusion.place_ref, bf16[256,256]{1,0:T(8,128)(2,1)} %wo_ref.3, bf16[8,64,1024]{2,1,0:T(8,128)(2,1)} %copy-done.1, bf16[512,8192]{1,0:T(8,128)(2,1)} %get-tuple-element.40.prob_ref, ...), custom_call_target="tpu_custom_call" | custom-call | flops 20000000000 | bytes 10485760 | tf_op jit(solution)/shard_map/backward/pallas_call | solution.py:340
  86.7 5.2 %collective-permute-start.8 = (bf16[256,256]{1,0:T(8,128)(2,1)}, bf16[256,256]{1,0:T(8,128)(2,1)S(1)}, u32[]{:S(2)}, u32[]{:S(2)}) collective-permute-start(bf16[256,256]{1,0:T(8,128)(2,1)} %get-tuple-element.50), channel_id=1, source_target_pairs={{0,8},{8,0},{16,24},{24,16},{1,9},{9,1},{17,25},{25,17},{2,10},{10... | collective-permute-start | bytes 393224 | tf_op jit(solution)/shard_map/ppermute | solution.py:403
  93.1 4.7 %collective-permute-done.9 = bf16[256,256]{1,0:T(8,128)(2,1)S(1)} collective-permute-done((bf16[256,256]{1,0:T(8,128)(2,1)}, bf16[256,256]{1,0:T(8,128)(2,1)S(1)}, u32[]{:S(2)}, u32[]{:S(2)}) %collective-permute-start.9) | collective-permute-done | bytes 131104 | tf_op jit(solution)/shard_map/ppermute | solution.py:403
  98.7 2.1 %collective-permute-start.11 = (bf16[256,256]{1,0:T(8,128)(2,1)S(1)}, bf16[256,256]{1,0:T(8,128)(2,1)S(1)}, u32[]{:S(2)}, u32[]{:S(2)}) collective-permute-start(bf16[256,256]{1,0:T(8,128)(2,1)S(1)} %add_convert_fusion.2), channel_id=1, source_target_pairs={{0,1},{1,0},{2,3},{3,2},{4,5},{5,4},{6,7},{7,6},{8,9},{9,8},{10,11... | collective-permute-start | bytes 393224 | tf_op jit(solution)/shard_map/ppermute | solution.py:403
  100.8 3.3 %collective-permute-done.11 = bf16[256,256]{1,0:T(8,128)(2,1)S(1)} collective-permute-done((bf16[256,256]{1,0:T(8,128)(2,1)S(1)}, bf16[256,256]{1,0:T(8,128)(2,1)S(1)}, u32[]{:S(2)}, u32[]{:S(2)}) %collective-permute-start.11) | collective-permute-done | bytes 131104 | tf_op jit(solution)/shard_map/ppermute | solution.py:403
  105.9 3.3 %collective-permute-done.12 = bf16[256,256]{1,0:T(8,128)(2,1)S(1)} collective-permute-done((bf16[256,256]{1,0:T(8,128)(2,1)S(1)}, bf16[256,256]{1,0:T(8,128)(2,1)S(1)}, u32[]{:S(2)}, u32[]{:S(2)}) %collective-permute-start.12) | collective-permute-done | bytes 131104 | tf_op jit(solution)/shard_map/ppermute | solution.py:403
  109.2 2.8 %collective-permute-start.13 = (bf16[256,256]{1,0:T(8,128)(2,1)S(1)}, bf16[256,256]{1,0:T(8,128)(2,1)S(1)}, u32[]{:S(2)}, u32[]{:S(2)}) collective-permute-start(bf16[256,256]{1,0:T(8,128)(2,1)S(1)} %add_convert_fusion), channel_id=1, source_target_pairs={{0,4},{1,5},{2,6},{3,7},{4,0},{5,1},{6,2},{7,3},{8,12},{9,13},{10,... | collective-permute-start | bytes 393224 | tf_op jit(solution)/shard_map/ppermute | solution.py:403
  112.0 4.5 %collective-permute-done.13 = bf16[256,256]{1,0:T(8,128)(2,1)S(1)} collective-permute-done((bf16[256,256]{1,0:T(8,128)(2,1)S(1)}, bf16[256,256]{1,0:T(8,128)(2,1)S(1)}, u32[]{:S(2)}, u32[]{:S(2)}) %collective-permute-start.13) | collective-permute-done | bytes 131104 | tf_op jit(solution)/shard_map/ppermute | solution.py:403
  116.7 3.0 %collective-permute-start.15 = (bf16[256,256]{1,0:T(8,128)(2,1)S(1)}, bf16[256,256]{1,0:T(8,128)(2,1)S(1)}, u32[]{:S(2)}, u32[]{:S(2)}) collective-permute-start(bf16[256,256]{1,0:T(8,128)(2,1)S(1)} %multiply_convert_fusion.refs_0_), channel_id=1, source_target_pairs={{0,16},{8,24},{16,0},{24,8},{1,17},{9,25},{17,1},{25,9},{2,18},{10... | collective-permute-start | bytes 393224 | tf_op jit(solution)/shard_map/ppermute | solution.py:403
  121.8 2.2 %collective-permute-done.15.refs_2_ = bf16[256,256]{1,0:T(8,128)(2,1)S(1)} collective-permute-done((bf16[256,256]{1,0:T(8,128)(2,1)S(1)}, bf16[256,256]{1,0:T(8,128)(2,1)S(1)}, u32[]{:S(2)}, u32[]{:S(2)}) %collective-permute-start.15) | collective-permute-done | bytes 131104 | tf_op jit(solution)/shard_map/ppermute | solution.py:403
  124.0 2.3 %collective-permute-done.16.refs_3_ = bf16[256,256]{1,0:T(8,128)(2,1)S(1)} collective-permute-done((bf16[256,256]{1,0:T(8,128)(2,1)S(1)}, bf16[256,256]{1,0:T(8,128)(2,1)S(1)}, u32[]{:S(2)}, u32[]{:S(2)}) %collective-permute-start.16) | collective-permute-done | bytes 131104 | tf_op jit(solution)/shard_map/ppermute | solution.py:403
  127.0 2.1 %place_all.1 = f32[4,256,256]{2,1,0:T(8,128)} custom-call(s32[2]{0:T(128)} %pad_add_fusion.place_ref, bf16[256,256]{1,0:T(8,128)(2,1)} %copy-done.2, bf16[256,256]{1,0:T(8,128)(2,1)} %copy-done.4, bf16[256,256]{1,0:T(8,128)(2,1)} %copy-done.5, bf16[256,256]{1,0:T(8,128)(2,1)} %copy-done.6), custom_call_target="tpu_custom_call" | custom-call | tf_op jit(solution)/shard_map/place_all/pallas_call | solution.py:375
  (54 shorter events, 11.3 us)
Async XLA Ops:
  1.5 7.2 %collective-permute-start = (bf16[8,64,128]{2,1,0:T(8,128)(2,1)S(1)}, bf16[8,64,128]{2,1,0:T(8,128)(2,1)S(1)}, u32[]{:S(2)}, u32[]{:S(2)}) collective-permute-start(bf16[8,64,128]{2,1,0:T(8,128)(2,1)S(1)} %slice.3), channel_id=1, source_target_pairs={{0,8},{8,16},{16,24},{1,9},{9,17},{17,25},{2,10},{10,18},{18,26},{... | collective-permute-start | bytes 393224 | tf_op jit(solution)/shard_map/ppermute | solution.py:430
  14.3 9.2 %collective-permute-start.1 = (bf16[64,1024]{1,0:T(8,128)(2,1)}, bf16[64,1024]{1,0:T(8,128)(2,1)S(1)}, u32[]{:S(2)}, u32[]{:S(2)}) collective-permute-start(bf16[64,1024]{1,0:T(8,128)(2,1)} %get-tuple-element.29), channel_id=1, source_target_pairs={{0,6},{1,7},{2,4},{3,5},{4,2},{5,3},{6,0},{7,1},{8,14},{9,15},{10,... | collective-permute-start | bytes 393224 | tf_op jit(solution)/shard_map/ppermute | solution.py:403
  18.8 9.7 %collective-permute-start.2 = (bf16[64,1024]{1,0:T(8,128)(2,1)}, bf16[64,1024]{1,0:T(8,128)(2,1)S(1)}, u32[]{:S(2)}, u32[]{:S(2)}) collective-permute-start(bf16[64,1024]{1,0:T(8,128)(2,1)} %get-tuple-element.30), channel_id=1, source_target_pairs={{0,7},{1,6},{2,5},{3,4},{4,3},{5,2},{6,1},{7,0},{8,15},{9,14},{10,... | collective-permute-start | bytes 393224 | tf_op jit(solution)/shard_map/ppermute | solution.py:403
  20.0 17.0 %collective-permute-start.3 = (bf16[64,1024]{1,0:T(8,128)(2,1)}, bf16[64,1024]{1,0:T(8,128)(2,1)S(1)}, u32[]{:S(2)}, u32[]{:S(2)}) collective-permute-start(bf16[64,1024]{1,0:T(8,128)(2,1)} %get-tuple-element.33), channel_id=1, source_target_pairs={{0,1},{1,0},{2,3},{3,2},{4,5},{5,4},{6,7},{7,6},{8,9},{9,8},{10,11... | collective-permute-start | bytes 393224 | tf_op jit(solution)/shard_map/ppermute | solution.py:403
  20.4 16.6 %collective-permute-start.4 = (bf16[64,1024]{1,0:T(8,128)(2,1)}, bf16[64,1024]{1,0:T(8,128)(2,1)S(1)}, u32[]{:S(2)}, u32[]{:S(2)}) collective-permute-start(bf16[64,1024]{1,0:T(8,128)(2,1)} %get-tuple-element.34), channel_id=1, source_target_pairs={{0,2},{1,3},{2,0},{3,1},{4,6},{5,7},{6,4},{7,5},{8,10},{9,11},{10,... | collective-permute-start | bytes 393224 | tf_op jit(solution)/shard_map/ppermute | solution.py:403
  20.4 16.6 %collective-permute-start.5 = (bf16[64,1024]{1,0:T(8,128)(2,1)}, bf16[64,1024]{1,0:T(8,128)(2,1)S(1)}, u32[]{:S(2)}, u32[]{:S(2)}) collective-permute-start(bf16[64,1024]{1,0:T(8,128)(2,1)} %get-tuple-element.35), channel_id=1, source_target_pairs={{0,3},{1,2},{2,1},{3,0},{4,7},{5,6},{6,5},{7,4},{8,11},{9,10},{10,... | collective-permute-start | bytes 393224 | tf_op jit(solution)/shard_map/ppermute | solution.py:403
  23.5 19.9 %copy-start.7 = (bf16[64,1024]{1,0:T(8,128)(2,1)}, bf16[64,1024]{1,0:T(8,128)(2,1)S(1)}, u32[]{:S(2)}) copy-start(bf16[64,1024]{1,0:T(8,128)(2,1)S(1)} %collective-permute-done.1.refs_6_) | copy-start | bytes 393220
  23.5 13.5 %collective-permute-start.6 = (bf16[64,1024]{1,0:T(8,128)(2,1)}, bf16[64,1024]{1,0:T(8,128)(2,1)S(1)}, u32[]{:S(2)}, u32[]{:S(2)}) collective-permute-start(bf16[64,1024]{1,0:T(8,128)(2,1)} %get-tuple-element.36), channel_id=1, source_target_pairs={{0,4},{1,5},{2,6},{3,7},{4,0},{5,1},{6,2},{7,3},{8,12},{9,13},{10,... | collective-permute-start | bytes 393224 | tf_op jit(solution)/shard_map/ppermute | solution.py:403
  28.5 14.9 %copy-start.8 = (bf16[64,1024]{1,0:T(8,128)(2,1)}, bf16[64,1024]{1,0:T(8,128)(2,1)S(1)}, u32[]{:S(2)}) copy-start(bf16[64,1024]{1,0:T(8,128)(2,1)S(1)} %collective-permute-done.2.refs_7_) | copy-start | bytes 393220
  28.5 14.8 %collective-permute-start.7 = (bf16[64,1024]{1,0:T(8,128)(2,1)}, bf16[64,1024]{1,0:T(8,128)(2,1)S(1)}, u32[]{:S(2)}, u32[]{:S(2)}) collective-permute-start(bf16[64,1024]{1,0:T(8,128)(2,1)} %get-tuple-element.37), channel_id=1, source_target_pairs={{0,5},{1,4},{2,7},{3,6},{4,1},{5,0},{6,3},{7,2},{8,13},{9,12},{10,... | collective-permute-start | bytes 393224 | tf_op jit(solution)/shard_map/ppermute | solution.py:403
  33.4 32.7 %all-to-all-start = ((bf16[8,64,1024]{2,1,0:T(8,128)(2,1)}), bf16[8,64,1024]{2,1,0:T(8,128)(2,1)S(1)}, u32[]{:S(2)}, u32[]{:S(2)}) async-start(bf16[8,64,1024]{2,1,0:T(8,128)(2,1)} %param.19), calls=%async_computation | async-start | bytes 2097152 | tf_op jit(solution)/shard_map/all_to_all | solution.py:412
  37.0 6.4 %copy-start.9 = (bf16[64,1024]{1,0:T(8,128)(2,1)}, bf16[64,1024]{1,0:T(8,128)(2,1)S(1)}, u32[]{:S(2)}) copy-start(bf16[64,1024]{1,0:T(8,128)(2,1)S(1)} %collective-permute-done.3.refs_1_) | copy-start | bytes 393220
  66.1 32.6 %all-to-all-start.1 = ((bf16[8,64,1024]{2,1,0:T(8,128)(2,1)}), bf16[8,64,1024]{2,1,0:T(8,128)(2,1)S(1)}, u32[]{:S(2)}, u32[]{:S(2)}) async-start(bf16[8,64,1024]{2,1,0:T(8,128)(2,1)} %get-tuple-element.53), calls=%async_computation.1 | async-start | bytes 2097152 | tf_op jit(solution)/shard_map/all_to_all | solution.py:412
  86.6 5.3 %collective-permute-start.10 = (bf16[256,256]{1,0:T(8,128)(2,1)}, bf16[256,256]{1,0:T(8,128)(2,1)S(1)}, u32[]{:S(2)}, u32[]{:S(2)}) collective-permute-start(bf16[256,256]{1,0:T(8,128)(2,1)} %get-tuple-element.52), channel_id=1, source_target_pairs={{0,24},{8,16},{16,8},{24,0},{1,25},{9,17},{17,9},{25,1},{2,26},{10... | collective-permute-start | bytes 393224 | tf_op jit(solution)/shard_map/ppermute | solution.py:403
  86.7 6.4 %collective-permute-start.8 = (bf16[256,256]{1,0:T(8,128)(2,1)}, bf16[256,256]{1,0:T(8,128)(2,1)S(1)}, u32[]{:S(2)}, u32[]{:S(2)}) collective-permute-start(bf16[256,256]{1,0:T(8,128)(2,1)} %get-tuple-element.50), channel_id=1, source_target_pairs={{0,8},{8,0},{16,24},{24,16},{1,9},{9,1},{17,25},{25,17},{2,10},{10... | collective-permute-start | bytes 393224 | tf_op jit(solution)/shard_map/ppermute | solution.py:403
  91.9 5.9 %collective-permute-start.9 = (bf16[256,256]{1,0:T(8,128)(2,1)}, bf16[256,256]{1,0:T(8,128)(2,1)S(1)}, u32[]{:S(2)}, u32[]{:S(2)}) collective-permute-start(bf16[256,256]{1,0:T(8,128)(2,1)} %get-tuple-element.51), channel_id=1, source_target_pairs={{0,16},{8,24},{16,0},{24,8},{1,17},{9,25},{17,1},{25,9},{2,18},{10... | collective-permute-start | bytes 393224 | tf_op jit(solution)/shard_map/ppermute | solution.py:403
  98.7 21.0 %copy-start = (bf16[8,64,1024]{2,1,0:T(8,128)(2,1)}, bf16[8,64,1024]{2,1,0:T(8,128)(2,1)S(1)}, u32[]{:S(2)}) copy-start(bf16[8,64,1024]{2,1,0:T(8,128)(2,1)S(1)} %all-to-all-done.1.in_ref) | copy-start | bytes 3145732
  98.7 5.4 %collective-permute-start.11 = (bf16[256,256]{1,0:T(8,128)(2,1)S(1)}, bf16[256,256]{1,0:T(8,128)(2,1)S(1)}, u32[]{:S(2)}, u32[]{:S(2)}) collective-permute-start(bf16[256,256]{1,0:T(8,128)(2,1)S(1)} %add_convert_fusion.2), channel_id=1, source_target_pairs={{0,1},{1,0},{2,3},{3,2},{4,5},{5,4},{6,7},{7,6},{8,9},{9,8},{10,11... | collective-permute-start | bytes 393224 | tf_op jit(solution)/shard_map/ppermute | solution.py:403
  104.1 5.0 %collective-permute-start.12 = (bf16[256,256]{1,0:T(8,128)(2,1)S(1)}, bf16[256,256]{1,0:T(8,128)(2,1)S(1)}, u32[]{:S(2)}, u32[]{:S(2)}) collective-permute-start(bf16[256,256]{1,0:T(8,128)(2,1)S(1)} %add_convert_fusion.1), channel_id=1, source_target_pairs={{0,2},{1,3},{2,0},{3,1},{4,6},{5,7},{6,4},{7,5},{8,10},{9,11},{10,... | collective-permute-start | bytes 393224 | tf_op jit(solution)/shard_map/ppermute | solution.py:403
  109.2 7.3 %collective-permute-start.13 = (bf16[256,256]{1,0:T(8,128)(2,1)S(1)}, bf16[256,256]{1,0:T(8,128)(2,1)S(1)}, u32[]{:S(2)}, u32[]{:S(2)}) collective-permute-start(bf16[256,256]{1,0:T(8,128)(2,1)S(1)} %add_convert_fusion), channel_id=1, source_target_pairs={{0,4},{1,5},{2,6},{3,7},{4,0},{5,1},{6,2},{7,3},{8,12},{9,13},{10,... | collective-permute-start | bytes 393224 | tf_op jit(solution)/shard_map/ppermute | solution.py:403
  116.6 9.7 %copy-start.2 = (bf16[256,256]{1,0:T(8,128)(2,1)}, bf16[256,256]{1,0:T(8,128)(2,1)S(1)}, u32[]{:S(2)}) copy-start(bf16[256,256]{1,0:T(8,128)(2,1)S(1)} %multiply_convert_fusion.refs_0_) | copy-start | bytes 393220
  116.6 5.2 %collective-permute-start.14 = (bf16[256,256]{1,0:T(8,128)(2,1)S(1)}, bf16[256,256]{1,0:T(8,128)(2,1)S(1)}, u32[]{:S(2)}, u32[]{:S(2)}) collective-permute-start(bf16[256,256]{1,0:T(8,128)(2,1)S(1)} %multiply_convert_fusion.refs_0_), channel_id=1, source_target_pairs={{0,8},{8,0},{16,24},{24,16},{1,9},{9,1},{17,25},{25,17},{2,10},{10... | collective-permute-start | bytes 393224 | tf_op jit(solution)/shard_map/ppermute | solution.py:403
  116.7 7.3 %collective-permute-start.15 = (bf16[256,256]{1,0:T(8,128)(2,1)S(1)}, bf16[256,256]{1,0:T(8,128)(2,1)S(1)}, u32[]{:S(2)}, u32[]{:S(2)}) collective-permute-start(bf16[256,256]{1,0:T(8,128)(2,1)S(1)} %multiply_convert_fusion.refs_0_), channel_id=1, source_target_pairs={{0,16},{8,24},{16,0},{24,8},{1,17},{9,25},{17,1},{25,9},{2,18},{10... | collective-permute-start | bytes 393224 | tf_op jit(solution)/shard_map/ppermute | solution.py:403
  119.6 6.6 %collective-permute-start.16 = (bf16[256,256]{1,0:T(8,128)(2,1)S(1)}, bf16[256,256]{1,0:T(8,128)(2,1)S(1)}, u32[]{:S(2)}, u32[]{:S(2)}) collective-permute-start(bf16[256,256]{1,0:T(8,128)(2,1)S(1)} %multiply_convert_fusion.refs_0_), channel_id=1, source_target_pairs={{0,24},{8,16},{16,8},{24,0},{1,25},{9,17},{17,9},{25,1},{2,26},{10... | collective-permute-start | bytes 393224 | tf_op jit(solution)/shard_map/ppermute | solution.py:403
  (9 other events, 33.1 us)

commit v15 on v13

--- a/solution.py
+++ b/solution.py
@@ -22,8 +22,8 @@
     return pl.BlockSpec(memory_space=pltpu.SMEM)
 
 
-def params(mebibytes=56):
-    return pltpu.CompilerParams(vmem_limit_bytes=mebibytes * 2**20)
+def params():
+    return pltpu.CompilerParams(vmem_limit_bytes=56 * 2**20)
 
 
 def filter_kernel(place_ref, sig_ref, rim_ref, taps_ref, *refs):
@@ -351,7 +351,7 @@
         in_specs=[index_spec()] + [pl.BlockSpec((rows, width), lambda: (0, 0))] * ways,
         out_specs=pl.BlockSpec(shape, lambda: (0, 0, 0)),
         out_shape=jax.ShapeDtypeStruct(shape, F32),
-        compiler_params=params(63),
+        compiler_params=params(),
         name="place_all",
     )(place, *parts)
 
@@ -413,19 +413,18 @@
         place, features, neighbours.T, live_mask[None], lap_coef[None],
         [w_query, w_key, w_value, w_out],
     )
+    returned = exchange(attended, "contact")
     grads = backward(place, upstream, kept, w_out, tm_count)
     grads = swap_all(grads, "tm")
-    attended, grads[1] = lax.optimization_barrier((attended, grads[1]))
-    returned = exchange(attended, "contact")
     part = sum(piece.astype(F32) for piece in grads).astype(BF16)
+    part, returned = lax.optimization_barrier((part, returned))
+    returned = write_out(returned)
     grad_scale = (batch * (slab // width) * tm_count * neighbours.shape[0]) ** (-0.5)
     step = 1
     while step < count:
         both = part.astype(F32) + swap(part, "contact", step).astype(F32)
         step *= 2
         part = lax.optimization_barrier((both * (1.0 if step < count else grad_scale)).astype(BF16))
-    part, returned = lax.optimization_barrier((part, returned))
-    returned = write_out(returned)
     summed = place_all(place, swap_all([part] * tm_count, "tm"))
     if pieces > 1:
         returned = returned.reshape(batch, pieces, contacts_here, span)

time: 139 us -> 127 us (0.914)
  waiting for transfers between devices: 44 us -> 30.4 us
  starting transfers between devices: 45.9 us -> 48.4 us
    ppermute x16, waiting for transfers between devices: 41.2 us -> 27.6 us  [swap(): lax.ppermute(value, axis, [(i, i ^ k) for i in range(lax.axis_size(axis))])]
    ppermute x16, starting transfers between devices: 28.9 us -> 36.7 us  [swap(): lax.ppermute(value, axis, [(i, i ^ k) for i in range(lax.axis_size(axis))])]
    all_to_all x2, starting transfers between devices: 14.6 us -> 9.31 us  [exchange(): return lax.all_to_all(value, axis, split_axis=0, concat_axis=0, tiled=True)]
  transfers between devices with their start and end apart: 19 -> 19, of which waited for: 12 -> 11; matrix products, arithmetic and copies ran while one was open for 1% -> 1% of each run, Pallas kernels for 15% -> 28%
where the time goes in v15:
time: 127 us
  starting transfers between devices  48.4 us (38%)
  Pallas kernels  42.7 us (34%)
  waiting for transfers between devices  30.4 us (24%)
  local copies, waits for them, and re-layouts  2.86 us (2%)
  other arithmetic  1.75 us (1%)
    ppermute x16, starting transfers between devices, swap(): lax.ppermute(value, axis, [(i, i ^ k) for i in range(lax.axis_size(axis))])  36.7 us
    ppermute x16, waiting for transfers between devices, swap(): lax.ppermute(value, axis, [(i, i ^ k) for i in range(lax.axis_size(axis))])  27.6 us
    pallas_call x1, Pallas kernels, forward(): pl.pallas_call(functools.partial(forward_kernel, blocks), grid=(groups,),...  18.3 us
    pallas_call x1, Pallas kernels, backward(): pl.pallas_call(functools.partial(backward_kernel, blocks), grid=(groups,)...  15.3 us
    all_to_all x2, starting transfers between devices, exchange(): return lax.all_to_all(value, axis, split_axis=0, concat_axis=0, tiled=True)  9.31 us
    pallas_call x1, Pallas kernels, filter_all(): pl.pallas_call(filter_kernel, grid=(contacts // rows,), in_specs=[index_s...  4.85 us
  transfers between devices with their start and end apart: 19, of which 11 were waited for; matrix products, arithmetic and copies ran while one was open for 1% of the time, Pallas kernels for 28%

profile of v15, /device:TPU:0, one launch (start us, length us, event | category | flops | bytes accessed | tf_op | source)
XLA Modules:
  0.0 127.0 jit_solution(17844581753241806115)
XLA Ops:
  1.5 2.4 %collective-permute-start = (bf16[8,64,128]{2,1,0:T(8,128)(2,1)S(1)}, bf16[8,64,128]{2,1,0:T(8,128)(2,1)S(1)}, u32[]{:S(2)}, u32[]{:S(2)}) collective-permute-start(bf16[8,64,128]{2,1,0:T(8,128)(2,1)S(1)} %slice.3), channel_id=1, source_target_pairs={{0,8},{8,16},{16,24},{1,9},{9,17},{17,25},{2,10},{10,18},{18,26},{... | collective-permute-start | bytes 393224 | tf_op jit(solution)/shard_map/ppermute | solution.py:404
  5.5 4.8 %filter.1 = (bf16[64,1024]{1,0:T(8,128)(2,1)}, bf16[64,1024]{1,0:T(8,128)(2,1)}, bf16[64,1024]{1,0:T(8,128)(2,1)}, bf16[64,1024]{1,0:T(8,128)(2,1)}, bf16[64,102...) custom-call(s32[2]{0:T(128)} %pad_add_fusion.place_ref, ...), custom_call_target="tpu_custom_call" | custom-call | flops 268435456 | bytes 2097152 | tf_op jit(solution)/shard_map/filter/pallas_call | solution.py:72
  10.4 4.5 %collective-permute-start.1 = (bf16[64,1024]{1,0:T(8,128)(2,1)}, bf16[64,1024]{1,0:T(8,128)(2,1)S(1)}, u32[]{:S(2)}, u32[]{:S(2)}) collective-permute-start(bf16[64,1024]{1,0:T(8,128)(2,1)} %get-tuple-element.29), channel_id=1, source_target_pairs={{0,6},{1,7},{2,4},{3,5},{4,2},{5,3},{6,0},{7,1},{8,14},{9,15},{10,... | collective-permute-start | bytes 393224 | tf_op jit(solution)/shard_map/ppermute | solution.py:377
  16.4 3.1 %collective-permute-start.5 = (bf16[64,1024]{1,0:T(8,128)(2,1)}, bf16[64,1024]{1,0:T(8,128)(2,1)S(1)}, u32[]{:S(2)}, u32[]{:S(2)}) collective-permute-start(bf16[64,1024]{1,0:T(8,128)(2,1)} %get-tuple-element.35), channel_id=1, source_target_pairs={{0,3},{1,2},{2,1},{3,0},{4,7},{5,6},{6,5},{7,4},{8,11},{9,10},{10,... | collective-permute-start | bytes 393224 | tf_op jit(solution)/shard_map/ppermute | solution.py:377
  19.6 2.1 %collective-permute-start.6 = (bf16[64,1024]{1,0:T(8,128)(2,1)}, bf16[64,1024]{1,0:T(8,128)(2,1)S(1)}, u32[]{:S(2)}, u32[]{:S(2)}) collective-permute-start(bf16[64,1024]{1,0:T(8,128)(2,1)} %get-tuple-element.36), channel_id=1, source_target_pairs={{0,4},{1,5},{2,6},{3,7},{4,0},{5,1},{6,2},{7,3},{8,12},{9,13},{10,... | collective-permute-start | bytes 393224 | tf_op jit(solution)/shard_map/ppermute | solution.py:377
  22.9 5.0 %collective-permute-start.7 = (bf16[64,1024]{1,0:T(8,128)(2,1)}, bf16[64,1024]{1,0:T(8,128)(2,1)S(1)}, u32[]{:S(2)}, u32[]{:S(2)}) collective-permute-start(bf16[64,1024]{1,0:T(8,128)(2,1)} %get-tuple-element.37), channel_id=1, source_target_pairs={{0,5},{1,4},{2,7},{3,6},{4,1},{5,0},{6,3},{7,2},{8,13},{9,12},{10,... | collective-permute-start | bytes 393224 | tf_op jit(solution)/shard_map/ppermute | solution.py:377
  28.0 4.9 %all-to-all-start = ((bf16[8,64,1024]{2,1,0:T(8,128)(2,1)}), bf16[8,64,1024]{2,1,0:T(8,128)(2,1)S(1)}, u32[]{:S(2)}, u32[]{:S(2)}) async-start(bf16[8,64,1024]{2,1,0:T(8,128)(2,1)} %param.19), calls=%async_computation | async-start | bytes 2097152 | tf_op jit(solution)/shard_map/all_to_all | solution.py:386
  32.9 5.6 %collective-permute-done.7.refs_5_ = bf16[64,1024]{1,0:T(8,128)(2,1)S(1)} collective-permute-done((bf16[64,1024]{1,0:T(8,128)(2,1)}, bf16[64,1024]{1,0:T(8,128)(2,1)S(1)}, u32[]{:S(2)}, u32[]{:S(2)}) %collective-permute-start.7) | collective-permute-done | bytes 131104 | tf_op jit(solution)/shard_map/ppermute | solution.py:377
  39.2 18.3 %forward.1 = (bf16[8,64,1024]{2,1,0:T(8,128)(2,1)}, bf16[512,8192]{1,0:T(8,128)(2,1)}, bf16[512,1024]{1,0:T(8,128)(2,1)}, bf16[512,1024]{1,0:T(8,128)(2,1)}, bf1...) custom-call(s32[2]{0:T(128)} %pad_add_fusion.place_ref, ...), custom_call_target="tpu_custom_call" | custom-call | flops 20000000000 | bytes 10485760 | tf_op jit(solution)/shard_map/forward/pallas_call | solution.py:278
  57.6 2.5 %all-to-all-done.up_ref = bf16[8,64,1024]{2,1,0:T(8,128)(2,1)S(1)} async-done(((bf16[8,64,1024]{2,1,0:T(8,128)(2,1)}), bf16[8,64,1024]{2,1,0:T(8,128)(2,1)S(1)}, u32[]{:S(2)}, u32[]{:S(2)}) %all-to-all-start) | async-done | bytes 1048608 | tf_op jit(solution)/shard_map/all_to_all | solution.py:386
  60.1 4.4 %all-to-all-start.1 = ((bf16[8,64,1024]{2,1,0:T(8,128)(2,1)}), bf16[8,64,1024]{2,1,0:T(8,128)(2,1)S(1)}, u32[]{:S(2)}, u32[]{:S(2)}) async-start(bf16[8,64,1024]{2,1,0:T(8,128)(2,1)} %get-tuple-element.53), calls=%async_computation.1 | async-start | bytes 2097152 | tf_op jit(solution)/shard_map/all_to_all | solution.py:386
  64.5 15.3 %backward.1 = (bf16[256,256]{1,0:T(8,128)(2,1)}, bf16[256,256]{1,0:T(8,128)(2,1)}, bf16[256,256]{1,0:T(8,128)(2,1)}, bf16[256,256]{1,0:T(8,128)(2,1)}) custom-call(s32[2]{0:T(128)} %pad_add_fusion.place_ref, bf16[256,256]{1,0:T(8,128)(2,1)} %wo_ref.3, bf16[8,64,1024]{2,1,0:T(8,128)(2,1)} %copy-done.1, bf16[512,8192]{1,0:T(8,128)(2,1)} %get-tuple-element.40.prob_ref, ...), custom_call_target="tpu_custom_call" | custom-call | flops 20000000000 | bytes 10485760 | tf_op jit(solution)/shard_map/backward/pallas_call | solution.py:314
  80.2 9.6 %collective-permute-start.8 = (bf16[256,256]{1,0:T(8,128)(2,1)}, bf16[256,256]{1,0:T(8,128)(2,1)S(1)}, u32[]{:S(2)}, u32[]{:S(2)}) collective-permute-start(bf16[256,256]{1,0:T(8,128)(2,1)} %get-tuple-element.50), channel_id=1, source_target_pairs={{0,8},{8,0},{16,24},{24,16},{1,9},{9,1},{17,25},{25,17},{2,10},{10... | collective-permute-start | bytes 393224 | tf_op jit(solution)/shard_map/ppermute | solution.py:377
  90.9 4.7 %collective-permute-done.9 = bf16[256,256]{1,0:T(8,128)(2,1)S(1)} collective-permute-done((bf16[256,256]{1,0:T(8,128)(2,1)}, bf16[256,256]{1,0:T(8,128)(2,1)S(1)}, u32[]{:S(2)}, u32[]{:S(2)}) %collective-permute-start.9) | collective-permute-done | bytes 131104 | tf_op jit(solution)/shard_map/ppermute | solution.py:377
  96.6 2.1 %collective-permute-start.11 = (bf16[256,256]{1,0:T(8,128)(2,1)S(1)}, bf16[256,256]{1,0:T(8,128)(2,1)S(1)}, u32[]{:S(2)}, u32[]{:S(2)}) collective-permute-start(bf16[256,256]{1,0:T(8,128)(2,1)S(1)} %add_convert_fusion.2), channel_id=1, source_target_pairs={{0,1},{1,0},{2,3},{3,2},{4,5},{5,4},{6,7},{7,6},{8,9},{9,8},{10,11... | collective-permute-start | bytes 393224 | tf_op jit(solution)/shard_map/ppermute | solution.py:377
  98.7 3.0 %collective-permute-done.11 = bf16[256,256]{1,0:T(8,128)(2,1)S(1)} collective-permute-done((bf16[256,256]{1,0:T(8,128)(2,1)S(1)}, bf16[256,256]{1,0:T(8,128)(2,1)S(1)}, u32[]{:S(2)}, u32[]{:S(2)}) %collective-permute-start.11) | collective-permute-done | bytes 131104 | tf_op jit(solution)/shard_map/ppermute | solution.py:377
  103.7 3.0 %collective-permute-done.12 = bf16[256,256]{1,0:T(8,128)(2,1)S(1)} collective-permute-done((bf16[256,256]{1,0:T(8,128)(2,1)S(1)}, bf16[256,256]{1,0:T(8,128)(2,1)S(1)}, u32[]{:S(2)}, u32[]{:S(2)}) %collective-permute-start.12) | collective-permute-done | bytes 131104 | tf_op jit(solution)/shard_map/ppermute | solution.py:377
  106.8 3.1 %collective-permute-start.13 = (bf16[256,256]{1,0:T(8,128)(2,1)S(1)}, bf16[256,256]{1,0:T(8,128)(2,1)S(1)}, u32[]{:S(2)}, u32[]{:S(2)}) collective-permute-start(bf16[256,256]{1,0:T(8,128)(2,1)S(1)} %add_convert_fusion), channel_id=1, source_target_pairs={{0,4},{1,5},{2,6},{3,7},{4,0},{5,1},{6,2},{7,3},{8,12},{9,13},{10,... | collective-permute-start | bytes 393224 | tf_op jit(solution)/shard_map/ppermute | solution.py:377
  109.9 4.4 %collective-permute-done.13 = bf16[256,256]{1,0:T(8,128)(2,1)S(1)} collective-permute-done((bf16[256,256]{1,0:T(8,128)(2,1)S(1)}, bf16[256,256]{1,0:T(8,128)(2,1)S(1)}, u32[]{:S(2)}, u32[]{:S(2)}) %collective-permute-start.13) | collective-permute-done | bytes 131104 | tf_op jit(solution)/shard_map/ppermute | solution.py:377
  114.4 3.1 %collective-permute-start.15 = (bf16[256,256]{1,0:T(8,128)(2,1)S(1)}, bf16[256,256]{1,0:T(8,128)(2,1)S(1)}, u32[]{:S(2)}, u32[]{:S(2)}) collective-permute-start(bf16[256,256]{1,0:T(8,128)(2,1)S(1)} %multiply_convert_fusion.refs_0_), channel_id=1, source_target_pairs={{0,16},{8,24},{16,0},{24,8},{1,17},{9,25},{17,1},{25,9},{2,18},{10... | collective-permute-start | bytes 393224 | tf_op jit(solution)/shard_map/ppermute | solution.py:377
  117.6 2.0 %write_out.1 = bf16[8,64,1024]{2,1,0:T(8,128)(2,1)} custom-call(bf16[8,64,1024]{2,1,0:T(8,128)(2,1)} %copy-done), custom_call_target="tpu_custom_call" | custom-call | bytes 2097152 | tf_op jit(solution)/shard_map/write_out/pallas_call | solution.py:364
  119.6 2.2 %collective-permute-done.15.refs_2_ = bf16[256,256]{1,0:T(8,128)(2,1)S(1)} collective-permute-done((bf16[256,256]{1,0:T(8,128)(2,1)S(1)}, bf16[256,256]{1,0:T(8,128)(2,1)S(1)}, u32[]{:S(2)}, u32[]{:S(2)}) %collective-permute-start.15) | collective-permute-done | bytes 131104 | tf_op jit(solution)/shard_map/ppermute | solution.py:377
  121.9 2.3 %collective-permute-done.16.refs_3_ = bf16[256,256]{1,0:T(8,128)(2,1)S(1)} collective-permute-done((bf16[256,256]{1,0:T(8,128)(2,1)S(1)}, bf16[256,256]{1,0:T(8,128)(2,1)S(1)}, u32[]{:S(2)}, u32[]{:S(2)}) %collective-permute-start.16) | collective-permute-done | bytes 131104 | tf_op jit(solution)/shard_map/ppermute | solution.py:377
  124.8 2.1 %place_all.1 = f32[4,256,256]{2,1,0:T(8,128)} custom-call(s32[2]{0:T(128)} %pad_add_fusion.place_ref, bf16[256,256]{1,0:T(8,128)(2,1)} %copy-done.2, bf16[256,256]{1,0:T(8,128)(2,1)} %copy-done.4, bf16[256,256]{1,0:T(8,128)(2,1)} %copy-done.5, bf16[256,256]{1,0:T(8,128)(2,1)} %copy-done.6), custom_call_target="tpu_custom_call" | custom-call | tf_op jit(solution)/shard_map/place_all/pallas_call | solution.py:349
  (53 shorter events, 11.4 us)
Async XLA Ops:
  1.5 3.3 %collective-permute-start = (bf16[8,64,128]{2,1,0:T(8,128)(2,1)S(1)}, bf16[8,64,128]{2,1,0:T(8,128)(2,1)S(1)}, u32[]{:S(2)}, u32[]{:S(2)}) collective-permute-start(bf16[8,64,128]{2,1,0:T(8,128)(2,1)S(1)} %slice.3), channel_id=1, source_target_pairs={{0,8},{8,16},{16,24},{1,9},{9,17},{17,25},{2,10},{10,18},{18,26},{... | collective-permute-start | bytes 393224 | tf_op jit(solution)/shard_map/ppermute | solution.py:404
  10.4 9.2 %collective-permute-start.1 = (bf16[64,1024]{1,0:T(8,128)(2,1)}, bf16[64,1024]{1,0:T(8,128)(2,1)S(1)}, u32[]{:S(2)}, u32[]{:S(2)}) collective-permute-start(bf16[64,1024]{1,0:T(8,128)(2,1)} %get-tuple-element.29), channel_id=1, source_target_pairs={{0,6},{1,7},{2,4},{3,5},{4,2},{5,3},{6,0},{7,1},{8,14},{9,15},{10,... | collective-permute-start | bytes 393224 | tf_op jit(solution)/shard_map/ppermute | solution.py:377
  14.9 8.0 %collective-permute-start.2 = (bf16[64,1024]{1,0:T(8,128)(2,1)}, bf16[64,1024]{1,0:T(8,128)(2,1)S(1)}, u32[]{:S(2)}, u32[]{:S(2)}) collective-permute-start(bf16[64,1024]{1,0:T(8,128)(2,1)} %get-tuple-element.30), channel_id=1, source_target_pairs={{0,7},{1,6},{2,5},{3,4},{4,3},{5,2},{6,1},{7,0},{8,15},{9,14},{10,... | collective-permute-start | bytes 393224 | tf_op jit(solution)/shard_map/ppermute | solution.py:377
  16.1 16.8 %collective-permute-start.3 = (bf16[64,1024]{1,0:T(8,128)(2,1)}, bf16[64,1024]{1,0:T(8,128)(2,1)S(1)}, u32[]{:S(2)}, u32[]{:S(2)}) collective-permute-start(bf16[64,1024]{1,0:T(8,128)(2,1)} %get-tuple-element.33), channel_id=1, source_target_pairs={{0,1},{1,0},{2,3},{3,2},{4,5},{5,4},{6,7},{7,6},{8,9},{9,8},{10,11... | collective-permute-start | bytes 393224 | tf_op jit(solution)/shard_map/ppermute | solution.py:377
  16.4 16.5 %collective-permute-start.4 = (bf16[64,1024]{1,0:T(8,128)(2,1)}, bf16[64,1024]{1,0:T(8,128)(2,1)S(1)}, u32[]{:S(2)}, u32[]{:S(2)}) collective-permute-start(bf16[64,1024]{1,0:T(8,128)(2,1)} %get-tuple-element.34), channel_id=1, source_target_pairs={{0,2},{1,3},{2,0},{3,1},{4,6},{5,7},{6,4},{7,5},{8,10},{9,11},{10,... | collective-permute-start | bytes 393224 | tf_op jit(solution)/shard_map/ppermute | solution.py:377
  16.4 16.5 %collective-permute-start.5 = (bf16[64,1024]{1,0:T(8,128)(2,1)}, bf16[64,1024]{1,0:T(8,128)(2,1)S(1)}, u32[]{:S(2)}, u32[]{:S(2)}) collective-permute-start(bf16[64,1024]{1,0:T(8,128)(2,1)} %get-tuple-element.35), channel_id=1, source_target_pairs={{0,3},{1,2},{2,1},{3,0},{4,7},{5,6},{6,5},{7,4},{8,11},{9,10},{10,... | collective-permute-start | bytes 393224 | tf_op jit(solution)/shard_map/ppermute | solution.py:377
  19.6 19.0 %copy-start.7 = (bf16[64,1024]{1,0:T(8,128)(2,1)}, bf16[64,1024]{1,0:T(8,128)(2,1)S(1)}, u32[]{:S(2)}) copy-start(bf16[64,1024]{1,0:T(8,128)(2,1)S(1)} %collective-permute-done.1.refs_6_) | copy-start | bytes 393220
  19.6 13.4 %collective-permute-start.6 = (bf16[64,1024]{1,0:T(8,128)(2,1)}, bf16[64,1024]{1,0:T(8,128)(2,1)S(1)}, u32[]{:S(2)}, u32[]{:S(2)}) collective-permute-start(bf16[64,1024]{1,0:T(8,128)(2,1)} %get-tuple-element.36), channel_id=1, source_target_pairs={{0,4},{1,5},{2,6},{3,7},{4,0},{5,1},{6,2},{7,3},{8,12},{9,13},{10,... | collective-permute-start | bytes 393224 | tf_op jit(solution)/shard_map/ppermute | solution.py:377
  22.9 15.7 %copy-start.8 = (bf16[64,1024]{1,0:T(8,128)(2,1)}, bf16[64,1024]{1,0:T(8,128)(2,1)S(1)}, u32[]{:S(2)}) copy-start(bf16[64,1024]{1,0:T(8,128)(2,1)S(1)} %collective-permute-done.2.refs_7_) | copy-start | bytes 393220
  22.9 15.6 %collective-permute-start.7 = (bf16[64,1024]{1,0:T(8,128)(2,1)}, bf16[64,1024]{1,0:T(8,128)(2,1)S(1)}, u32[]{:S(2)}, u32[]{:S(2)}) collective-permute-start(bf16[64,1024]{1,0:T(8,128)(2,1)} %get-tuple-element.37), channel_id=1, source_target_pairs={{0,5},{1,4},{2,7},{3,6},{4,1},{5,0},{6,3},{7,2},{8,13},{9,12},{10,... | collective-permute-start | bytes 393224 | tf_op jit(solution)/shard_map/ppermute | solution.py:377
  28.0 32.1 %all-to-all-start = ((bf16[8,64,1024]{2,1,0:T(8,128)(2,1)}), bf16[8,64,1024]{2,1,0:T(8,128)(2,1)S(1)}, u32[]{:S(2)}, u32[]{:S(2)}) async-start(bf16[8,64,1024]{2,1,0:T(8,128)(2,1)} %param.19), calls=%async_computation | async-start | bytes 2097152 | tf_op jit(solution)/shard_map/all_to_all | solution.py:386
  32.9 5.7 %copy-start.9 = (bf16[64,1024]{1,0:T(8,128)(2,1)}, bf16[64,1024]{1,0:T(8,128)(2,1)S(1)}, u32[]{:S(2)}) copy-start(bf16[64,1024]{1,0:T(8,128)(2,1)S(1)} %collective-permute-done.3.refs_1_) | copy-start | bytes 393220
  60.1 36.5 %all-to-all-start.1 = ((bf16[8,64,1024]{2,1,0:T(8,128)(2,1)}), bf16[8,64,1024]{2,1,0:T(8,128)(2,1)S(1)}, u32[]{:S(2)}, u32[]{:S(2)}) async-start(bf16[8,64,1024]{2,1,0:T(8,128)(2,1)} %get-tuple-element.53), calls=%async_computation.1 | async-start | bytes 2097152 | tf_op jit(solution)/shard_map/all_to_all | solution.py:386
  79.8 10.0 %collective-permute-start.10 = (bf16[256,256]{1,0:T(8,128)(2,1)}, bf16[256,256]{1,0:T(8,128)(2,1)S(1)}, u32[]{:S(2)}, u32[]{:S(2)}) collective-permute-start(bf16[256,256]{1,0:T(8,128)(2,1)} %get-tuple-element.52), channel_id=1, source_target_pairs={{0,24},{8,16},{16,8},{24,0},{1,25},{9,17},{17,9},{25,1},{2,26},{10... | collective-permute-start | bytes 393224 | tf_op jit(solution)/shard_map/ppermute | solution.py:377
  80.2 10.8 %collective-permute-start.8 = (bf16[256,256]{1,0:T(8,128)(2,1)}, bf16[256,256]{1,0:T(8,128)(2,1)S(1)}, u32[]{:S(2)}, u32[]{:S(2)}) collective-permute-start(bf16[256,256]{1,0:T(8,128)(2,1)} %get-tuple-element.50), channel_id=1, source_target_pairs={{0,8},{8,0},{16,24},{24,16},{1,9},{9,1},{17,25},{25,17},{2,10},{10... | collective-permute-start | bytes 393224 | tf_op jit(solution)/shard_map/ppermute | solution.py:377
  89.7 5.9 %collective-permute-start.9 = (bf16[256,256]{1,0:T(8,128)(2,1)}, bf16[256,256]{1,0:T(8,128)(2,1)S(1)}, u32[]{:S(2)}, u32[]{:S(2)}) collective-permute-start(bf16[256,256]{1,0:T(8,128)(2,1)} %get-tuple-element.51), channel_id=1, source_target_pairs={{0,16},{8,24},{16,0},{24,8},{1,17},{9,25},{17,1},{25,9},{2,18},{10... | collective-permute-start | bytes 393224 | tf_op jit(solution)/shard_map/ppermute | solution.py:377
  96.6 21.0 %copy-start = (bf16[8,64,1024]{2,1,0:T(8,128)(2,1)}, bf16[8,64,1024]{2,1,0:T(8,128)(2,1)S(1)}, u32[]{:S(2)}) copy-start(bf16[8,64,1024]{2,1,0:T(8,128)(2,1)S(1)} %all-to-all-done.1.in_ref) | copy-start | bytes 3145732
  96.6 5.1 %collective-permute-start.11 = (bf16[256,256]{1,0:T(8,128)(2,1)S(1)}, bf16[256,256]{1,0:T(8,128)(2,1)S(1)}, u32[]{:S(2)}, u32[]{:S(2)}) collective-permute-start(bf16[256,256]{1,0:T(8,128)(2,1)S(1)} %add_convert_fusion.2), channel_id=1, source_target_pairs={{0,1},{1,0},{2,3},{3,2},{4,5},{5,4},{6,7},{7,6},{8,9},{9,8},{10,11... | collective-permute-start | bytes 393224 | tf_op jit(solution)/shard_map/ppermute | solution.py:377
  101.7 5.0 %collective-permute-start.12 = (bf16[256,256]{1,0:T(8,128)(2,1)S(1)}, bf16[256,256]{1,0:T(8,128)(2,1)S(1)}, u32[]{:S(2)}, u32[]{:S(2)}) collective-permute-start(bf16[256,256]{1,0:T(8,128)(2,1)S(1)} %add_convert_fusion.1), channel_id=1, source_target_pairs={{0,2},{1,3},{2,0},{3,1},{4,6},{5,7},{6,4},{7,5},{8,10},{9,11},{10,... | collective-permute-start | bytes 393224 | tf_op jit(solution)/shard_map/ppermute | solution.py:377
  106.8 7.4 %collective-permute-start.13 = (bf16[256,256]{1,0:T(8,128)(2,1)S(1)}, bf16[256,256]{1,0:T(8,128)(2,1)S(1)}, u32[]{:S(2)}, u32[]{:S(2)}) collective-permute-start(bf16[256,256]{1,0:T(8,128)(2,1)S(1)} %add_convert_fusion), channel_id=1, source_target_pairs={{0,4},{1,5},{2,6},{3,7},{4,0},{5,1},{6,2},{7,3},{8,12},{9,13},{10,... | collective-permute-start | bytes 393224 | tf_op jit(solution)/shard_map/ppermute | solution.py:377
  114.3 9.9 %copy-start.2 = (bf16[256,256]{1,0:T(8,128)(2,1)}, bf16[256,256]{1,0:T(8,128)(2,1)S(1)}, u32[]{:S(2)}) copy-start(bf16[256,256]{1,0:T(8,128)(2,1)S(1)} %multiply_convert_fusion.refs_0_) | copy-start | bytes 393220
  114.3 5.3 %collective-permute-start.14 = (bf16[256,256]{1,0:T(8,128)(2,1)S(1)}, bf16[256,256]{1,0:T(8,128)(2,1)S(1)}, u32[]{:S(2)}, u32[]{:S(2)}) collective-permute-start(bf16[256,256]{1,0:T(8,128)(2,1)S(1)} %multiply_convert_fusion.refs_0_), channel_id=1, source_target_pairs={{0,8},{8,0},{16,24},{24,16},{1,9},{9,1},{17,25},{25,17},{2,10},{10... | collective-permute-start | bytes 393224 | tf_op jit(solution)/shard_map/ppermute | solution.py:377
  114.4 7.5 %collective-permute-start.15 = (bf16[256,256]{1,0:T(8,128)(2,1)S(1)}, bf16[256,256]{1,0:T(8,128)(2,1)S(1)}, u32[]{:S(2)}, u32[]{:S(2)}) collective-permute-start(bf16[256,256]{1,0:T(8,128)(2,1)S(1)} %multiply_convert_fusion.refs_0_), channel_id=1, source_target_pairs={{0,16},{8,24},{16,0},{24,8},{1,17},{9,25},{17,1},{25,9},{2,18},{10... | collective-permute-start | bytes 393224 | tf_op jit(solution)/shard_map/ppermute | solution.py:377
  117.5 6.6 %collective-permute-start.16 = (bf16[256,256]{1,0:T(8,128)(2,1)S(1)}, bf16[256,256]{1,0:T(8,128)(2,1)S(1)}, u32[]{:S(2)}, u32[]{:S(2)}) collective-permute-start(bf16[256,256]{1,0:T(8,128)(2,1)S(1)} %multiply_convert_fusion.refs_0_), channel_id=1, source_target_pairs={{0,24},{8,16},{16,8},{24,0},{1,25},{9,17},{17,9},{25,1},{2,26},{10... | collective-permute-start | bytes 393224 | tf_op jit(solution)/shard_map/ppermute | solution.py:377
  (9 other events, 30.2 us)

commit v16 on v15

--- a/solution.py
+++ b/solution.py
@@ -67,7 +67,7 @@
 def filter_all(place, signal, rim, taps, count):
     batch, contacts, slab = signal.shape
     width = rim.shape[2]
-    rows = 16
+    rows = min(32, contacts)
     span = slab * batch // count
     return pl.pallas_call(
         filter_kernel,
@@ -406,7 +406,7 @@
     )
     filtered = filter_all(place, signal, rim, fir_taps, count)
     features = swap_all(filtered, "contact")
-    arrived = count - max(2, count // 4)
+    arrived = count - max(2, 3 * count // 8)
     features[arrived:], cotangent = lax.optimization_barrier((features[arrived:], cotangent))
     upstream = exchange(cotangent, "contact")
     attended, *kept = forward(

time: 127 us -> 127 us (level)
    all_to_all x2, waiting for transfers between devices: 2.52 us -> 7.81 us  [exchange(): return lax.all_to_all(value, axis, split_axis=0, concat_axis=0, tiled=True)]
    ppermute x16, starting transfers between devices: 36.7 us -> 32.2 us  [swap(): lax.ppermute(value, axis, [(i, i ^ k) for i in range(lax.axis_size(axis))])]
    ppermute x16, waiting for transfers between devices: 27.6 us -> 23.3 us  [swap(): lax.ppermute(value, axis, [(i, i ^ k) for i in range(lax.axis_size(axis))])]
    all_to_all x2, starting transfers between devices: 9.31 us -> 12.9 us  [exchange(): return lax.all_to_all(value, axis, split_axis=0, concat_axis=0, tiled=True)]
  transfers between devices with their start and end apart: 19 -> 19, of which waited for: 11 -> 10; matrix products, arithmetic and copies ran while one was open for 1% -> 1% of each run, Pallas kernels for 28% -> 28%
where the time goes in v16:
time: 127 us
  starting transfers between devices  47.4 us (37%)
  Pallas kernels  42.2 us (33%)
  waiting for transfers between devices  31.4 us (25%)
  local copies, waits for them, and re-layouts  2.96 us (2%)
  other arithmetic  1.75 us (1%)
    ppermute x16, starting transfers between devices, swap(): lax.ppermute(value, axis, [(i, i ^ k) for i in range(lax.axis_size(axis))])  32.2 us
    ppermute x16, waiting for transfers between devices, swap(): lax.ppermute(value, axis, [(i, i ^ k) for i in range(lax.axis_size(axis))])  23.3 us
    pallas_call x1, Pallas kernels, forward(): pl.pallas_call(functools.partial(forward_kernel, blocks), grid=(groups,),...  18.3 us
    pallas_call x1, Pallas kernels, backward(): pl.pallas_call(functools.partial(backward_kernel, blocks), grid=(groups,)...  15.3 us
    all_to_all x2, starting transfers between devices, exchange(): return lax.all_to_all(value, axis, split_axis=0, concat_axis=0, tiled=True)  12.9 us
    all_to_all x2, waiting for transfers between devices, exchange(): return lax.all_to_all(value, axis, split_axis=0, concat_axis=0, tiled=True)  7.81 us
    pallas_call x1, Pallas kernels, filter_all(): pl.pallas_call(filter_kernel, grid=(contacts // rows,), in_specs=[index_s...  4.33 us
  transfers between devices with their start and end apart: 19, of which 10 were waited for; matrix products, arithmetic and copies ran while one was open for 1% of the time, Pallas kernels for 28%

profile of v16, /device:TPU:0, one launch (start us, length us, event | category | flops | bytes accessed | tf_op | source)
XLA Modules:
  0.0 126.5 jit_solution(9139385064838462515)
XLA Ops:
  1.5 2.4 %collective-permute-start = (bf16[8,64,128]{2,1,0:T(8,128)(2,1)S(1)}, bf16[8,64,128]{2,1,0:T(8,128)(2,1)S(1)}, u32[]{:S(2)}, u32[]{:S(2)}) collective-permute-start(bf16[8,64,128]{2,1,0:T(8,128)(2,1)S(1)} %slice.3), channel_id=1, source_target_pairs={{0,8},{8,16},{16,24},{1,9},{9,17},{17,25},{2,10},{10,18},{18,26},{... | collective-permute-start | bytes 393224 | tf_op jit(solution)/shard_map/ppermute | solution.py:404
  5.5 4.3 %filter.1 = (bf16[64,1024]{1,0:T(8,128)(2,1)}, bf16[64,1024]{1,0:T(8,128)(2,1)}, bf16[64,1024]{1,0:T(8,128)(2,1)}, bf16[64,1024]{1,0:T(8,128)(2,1)}, bf16[64,102...) custom-call(s32[2]{0:T(128)} %pad_add_fusion.place_ref, ...), custom_call_target="tpu_custom_call" | custom-call | flops 268435456 | bytes 2097152 | tf_op jit(solution)/shard_map/filter/pallas_call | solution.py:72
  9.9 4.4 %collective-permute-start.1 = (bf16[64,1024]{1,0:T(8,128)(2,1)}, bf16[64,1024]{1,0:T(8,128)(2,1)S(1)}, u32[]{:S(2)}, u32[]{:S(2)}) collective-permute-start(bf16[64,1024]{1,0:T(8,128)(2,1)} %get-tuple-element.30), channel_id=1, source_target_pairs={{0,5},{1,4},{2,7},{3,6},{4,1},{5,0},{6,3},{7,2},{8,13},{9,12},{10,... | collective-permute-start | bytes 393224 | tf_op jit(solution)/shard_map/ppermute | solution.py:377
  15.6 2.4 %collective-permute-start.3 = (bf16[64,1024]{1,0:T(8,128)(2,1)}, bf16[64,1024]{1,0:T(8,128)(2,1)S(1)}, u32[]{:S(2)}, u32[]{:S(2)}) collective-permute-start(bf16[64,1024]{1,0:T(8,128)(2,1)} %get-tuple-element.32), channel_id=1, source_target_pairs={{0,7},{1,6},{2,5},{3,4},{4,3},{5,2},{6,1},{7,0},{8,15},{9,14},{10,... | collective-permute-start | bytes 393224 | tf_op jit(solution)/shard_map/ppermute | solution.py:377
  18.1 1.5 %collective-permute-start.4 = (bf16[64,1024]{1,0:T(8,128)(2,1)}, bf16[64,1024]{1,0:T(8,128)(2,1)S(1)}, u32[]{:S(2)}, u32[]{:S(2)}) collective-permute-start(bf16[64,1024]{1,0:T(8,128)(2,1)} %get-tuple-element.35), channel_id=1, source_target_pairs={{0,1},{1,0},{2,3},{3,2},{4,5},{5,4},{6,7},{7,6},{8,9},{9,8},{10,11... | collective-permute-start | bytes 393224 | tf_op jit(solution)/shard_map/ppermute | solution.py:377
  19.6 8.7 %collective-permute-start.6 = (bf16[64,1024]{1,0:T(8,128)(2,1)}, bf16[64,1024]{1,0:T(8,128)(2,1)S(1)}, u32[]{:S(2)}, u32[]{:S(2)}) collective-permute-start(bf16[64,1024]{1,0:T(8,128)(2,1)} %get-tuple-element.37), channel_id=1, source_target_pairs={{0,3},{1,2},{2,1},{3,0},{4,7},{5,6},{6,5},{7,4},{8,11},{9,10},{10,... | collective-permute-start | bytes 393224 | tf_op jit(solution)/shard_map/ppermute | solution.py:377
  28.3 4.7 %collective-permute-start.7 = (bf16[64,1024]{1,0:T(8,128)(2,1)}, bf16[64,1024]{1,0:T(8,128)(2,1)S(1)}, u32[]{:S(2)}, u32[]{:S(2)}) collective-permute-start(bf16[64,1024]{1,0:T(8,128)(2,1)} %get-tuple-element.38), channel_id=1, source_target_pairs={{0,4},{1,5},{2,6},{3,7},{4,0},{5,1},{6,2},{7,3},{8,12},{9,13},{10,... | collective-permute-start | bytes 393224 | tf_op jit(solution)/shard_map/ppermute | solution.py:377
  33.0 9.2 %all-to-all-start = ((bf16[8,64,1024]{2,1,0:T(8,128)(2,1)}), bf16[8,64,1024]{2,1,0:T(8,128)(2,1)S(1)}, u32[]{:S(2)}, u32[]{:S(2)}) async-start(bf16[8,64,1024]{2,1,0:T(8,128)(2,1)} %param.19), calls=%async_computation | async-start | bytes 2097152 | tf_op jit(solution)/shard_map/all_to_all | solution.py:386
  43.1 18.3 %forward.1 = (bf16[8,64,1024]{2,1,0:T(8,128)(2,1)}, bf16[512,8192]{1,0:T(8,128)(2,1)}, bf16[512,1024]{1,0:T(8,128)(2,1)}, bf16[512,1024]{1,0:T(8,128)(2,1)}, bf1...) custom-call(s32[2]{0:T(128)} %pad_add_fusion.place_ref, ...), custom_call_target="tpu_custom_call" | custom-call | flops 20000000000 | bytes 10485760 | tf_op jit(solution)/shard_map/forward/pallas_call | solution.py:278
  61.4 6.9 %all-to-all-done.up_ref = bf16[8,64,1024]{2,1,0:T(8,128)(2,1)S(1)} async-done(((bf16[8,64,1024]{2,1,0:T(8,128)(2,1)}), bf16[8,64,1024]{2,1,0:T(8,128)(2,1)S(1)}, u32[]{:S(2)}, u32[]{:S(2)}) %all-to-all-start) | async-done | bytes 1048608 | tf_op jit(solution)/shard_map/all_to_all | solution.py:386
  68.3 3.6 %all-to-all-start.1 = ((bf16[8,64,1024]{2,1,0:T(8,128)(2,1)}), bf16[8,64,1024]{2,1,0:T(8,128)(2,1)S(1)}, u32[]{:S(2)}, u32[]{:S(2)}) async-start(bf16[8,64,1024]{2,1,0:T(8,128)(2,1)} %get-tuple-element.55), calls=%async_computation.1 | async-start | bytes 2097152 | tf_op jit(solution)/shard_map/all_to_all | solution.py:386
  71.9 15.3 %backward.1 = (bf16[256,256]{1,0:T(8,128)(2,1)}, bf16[256,256]{1,0:T(8,128)(2,1)}, bf16[256,256]{1,0:T(8,128)(2,1)}, bf16[256,256]{1,0:T(8,128)(2,1)}) custom-call(s32[2]{0:T(128)} %pad_add_fusion.place_ref, bf16[256,256]{1,0:T(8,128)(2,1)} %wo_ref.3, bf16[8,64,1024]{2,1,0:T(8,128)(2,1)} %copy-done.1, bf16[512,8192]{1,0:T(8,128)(2,1)} %get-tuple-element.42.prob_ref, ...), custom_call_target="tpu_custom_call" | custom-call | flops 20000000000 | bytes 10485760 | tf_op jit(solution)/shard_map/backward/pallas_call | solution.py:314
  87.4 2.1 %collective-permute-start.9 = (bf16[256,256]{1,0:T(8,128)(2,1)}, bf16[256,256]{1,0:T(8,128)(2,1)S(1)}, u32[]{:S(2)}, u32[]{:S(2)}) collective-permute-start(bf16[256,256]{1,0:T(8,128)(2,1)} %get-tuple-element.53), channel_id=1, source_target_pairs={{0,16},{8,24},{16,0},{24,8},{1,17},{9,25},{17,1},{25,9},{2,18},{10... | collective-permute-start | bytes 393224 | tf_op jit(solution)/shard_map/ppermute | solution.py:377
  89.5 3.9 %collective-permute-done.10 = bf16[256,256]{1,0:T(8,128)(2,1)S(1)} collective-permute-done((bf16[256,256]{1,0:T(8,128)(2,1)}, bf16[256,256]{1,0:T(8,128)(2,1)S(1)}, u32[]{:S(2)}, u32[]{:S(2)}) %collective-permute-start.10) | collective-permute-done | bytes 131104 | tf_op jit(solution)/shard_map/ppermute | solution.py:377
  93.3 2.6 %collective-permute-done.9 = bf16[256,256]{1,0:T(8,128)(2,1)S(1)} collective-permute-done((bf16[256,256]{1,0:T(8,128)(2,1)}, bf16[256,256]{1,0:T(8,128)(2,1)S(1)}, u32[]{:S(2)}, u32[]{:S(2)}) %collective-permute-start.9) | collective-permute-done | bytes 131104 | tf_op jit(solution)/shard_map/ppermute | solution.py:377
  99.3 3.5 %collective-permute-done.11 = bf16[256,256]{1,0:T(8,128)(2,1)S(1)} collective-permute-done((bf16[256,256]{1,0:T(8,128)(2,1)S(1)}, bf16[256,256]{1,0:T(8,128)(2,1)S(1)}, u32[]{:S(2)}, u32[]{:S(2)}) %collective-permute-start.11) | collective-permute-done | bytes 131104 | tf_op jit(solution)/shard_map/ppermute | solution.py:377
  104.2 3.7 %collective-permute-done.12 = bf16[256,256]{1,0:T(8,128)(2,1)S(1)} collective-permute-done((bf16[256,256]{1,0:T(8,128)(2,1)S(1)}, bf16[256,256]{1,0:T(8,128)(2,1)S(1)}, u32[]{:S(2)}, u32[]{:S(2)}) %collective-permute-start.12) | collective-permute-done | bytes 131104 | tf_op jit(solution)/shard_map/ppermute | solution.py:377
  108.0 2.2 %collective-permute-start.13 = (bf16[256,256]{1,0:T(8,128)(2,1)S(1)}, bf16[256,256]{1,0:T(8,128)(2,1)S(1)}, u32[]{:S(2)}, u32[]{:S(2)}) collective-permute-start(bf16[256,256]{1,0:T(8,128)(2,1)S(1)} %add_convert_fusion), channel_id=1, source_target_pairs={{0,4},{1,5},{2,6},{3,7},{4,0},{5,1},{6,2},{7,3},{8,12},{9,13},{10,... | collective-permute-start | bytes 393224 | tf_op jit(solution)/shard_map/ppermute | solution.py:377
  110.2 5.1 %collective-permute-done.13 = bf16[256,256]{1,0:T(8,128)(2,1)S(1)} collective-permute-done((bf16[256,256]{1,0:T(8,128)(2,1)S(1)}, bf16[256,256]{1,0:T(8,128)(2,1)S(1)}, u32[]{:S(2)}, u32[]{:S(2)}) %collective-permute-start.13) | collective-permute-done | bytes 131104 | tf_op jit(solution)/shard_map/ppermute | solution.py:377
  115.5 1.8 %collective-permute-start.16 = (bf16[256,256]{1,0:T(8,128)(2,1)S(1)}, bf16[256,256]{1,0:T(8,128)(2,1)S(1)}, u32[]{:S(2)}, u32[]{:S(2)}) collective-permute-start(bf16[256,256]{1,0:T(8,128)(2,1)S(1)} %multiply_convert_fusion.refs_0_), channel_id=1, source_target_pairs={{0,24},{8,16},{16,8},{24,0},{1,25},{9,17},{17,9},{25,1},{2,26},{10... | collective-permute-start | bytes 393224 | tf_op jit(solution)/shard_map/ppermute | solution.py:377
  117.3 2.0 %write_out.1 = bf16[8,64,1024]{2,1,0:T(8,128)(2,1)} custom-call(bf16[8,64,1024]{2,1,0:T(8,128)(2,1)} %copy-done), custom_call_target="tpu_custom_call" | custom-call | bytes 2097152 | tf_op jit(solution)/shard_map/write_out/pallas_call | solution.py:364
  119.4 2.5 %collective-permute-done.15.refs_2_ = bf16[256,256]{1,0:T(8,128)(2,1)S(1)} collective-permute-done((bf16[256,256]{1,0:T(8,128)(2,1)S(1)}, bf16[256,256]{1,0:T(8,128)(2,1)S(1)}, u32[]{:S(2)}, u32[]{:S(2)}) %collective-permute-start.15) | collective-permute-done | bytes 131104 | tf_op jit(solution)/shard_map/ppermute | solution.py:377
  121.8 1.9 %collective-permute-done.16.refs_3_ = bf16[256,256]{1,0:T(8,128)(2,1)S(1)} collective-permute-done((bf16[256,256]{1,0:T(8,128)(2,1)S(1)}, bf16[256,256]{1,0:T(8,128)(2,1)S(1)}, u32[]{:S(2)}, u32[]{:S(2)}) %collective-permute-start.16) | collective-permute-done | bytes 131104 | tf_op jit(solution)/shard_map/ppermute | solution.py:377
  124.4 2.1 %place_all.1 = f32[4,256,256]{2,1,0:T(8,128)} custom-call(s32[2]{0:T(128)} %pad_add_fusion.place_ref, bf16[256,256]{1,0:T(8,128)(2,1)} %copy-done.2, bf16[256,256]{1,0:T(8,128)(2,1)} %copy-done.4, bf16[256,256]{1,0:T(8,128)(2,1)} %copy-done.5, bf16[256,256]{1,0:T(8,128)(2,1)} %copy-done.6), custom_call_target="tpu_custom_call" | custom-call | tf_op jit(solution)/shard_map/place_all/pallas_call | solution.py:349
  (53 shorter events, 10.3 us)
Async XLA Ops:
  1.5 3.3 %collective-permute-start = (bf16[8,64,128]{2,1,0:T(8,128)(2,1)S(1)}, bf16[8,64,128]{2,1,0:T(8,128)(2,1)S(1)}, u32[]{:S(2)}, u32[]{:S(2)}) collective-permute-start(bf16[8,64,128]{2,1,0:T(8,128)(2,1)S(1)} %slice.3), channel_id=1, source_target_pairs={{0,8},{8,16},{16,24},{1,9},{9,17},{17,25},{2,10},{10,18},{18,26},{... | collective-permute-start | bytes 393224 | tf_op jit(solution)/shard_map/ppermute | solution.py:404
  9.9 9.7 %collective-permute-start.1 = (bf16[64,1024]{1,0:T(8,128)(2,1)}, bf16[64,1024]{1,0:T(8,128)(2,1)S(1)}, u32[]{:S(2)}, u32[]{:S(2)}) collective-permute-start(bf16[64,1024]{1,0:T(8,128)(2,1)} %get-tuple-element.30), channel_id=1, source_target_pairs={{0,5},{1,4},{2,7},{3,6},{4,1},{5,0},{6,3},{7,2},{8,13},{9,12},{10,... | collective-permute-start | bytes 393224 | tf_op jit(solution)/shard_map/ppermute | solution.py:377
  14.3 14.0 %collective-permute-start.2 = (bf16[64,1024]{1,0:T(8,128)(2,1)}, bf16[64,1024]{1,0:T(8,128)(2,1)S(1)}, u32[]{:S(2)}, u32[]{:S(2)}) collective-permute-start(bf16[64,1024]{1,0:T(8,128)(2,1)} %get-tuple-element.31), channel_id=1, source_target_pairs={{0,6},{1,7},{2,4},{3,5},{4,2},{5,3},{6,0},{7,1},{8,14},{9,15},{10,... | collective-permute-start | bytes 393224 | tf_op jit(solution)/shard_map/ppermute | solution.py:377
  15.6 17.4 %collective-permute-start.3 = (bf16[64,1024]{1,0:T(8,128)(2,1)}, bf16[64,1024]{1,0:T(8,128)(2,1)S(1)}, u32[]{:S(2)}, u32[]{:S(2)}) collective-permute-start(bf16[64,1024]{1,0:T(8,128)(2,1)} %get-tuple-element.32), channel_id=1, source_target_pairs={{0,7},{1,6},{2,5},{3,4},{4,3},{5,2},{6,1},{7,0},{8,15},{9,14},{10,... | collective-permute-start | bytes 393224 | tf_op jit(solution)/shard_map/ppermute | solution.py:377
  18.1 24.2 %collective-permute-start.4 = (bf16[64,1024]{1,0:T(8,128)(2,1)}, bf16[64,1024]{1,0:T(8,128)(2,1)S(1)}, u32[]{:S(2)}, u32[]{:S(2)}) collective-permute-start(bf16[64,1024]{1,0:T(8,128)(2,1)} %get-tuple-element.35), channel_id=1, source_target_pairs={{0,1},{1,0},{2,3},{3,2},{4,5},{5,4},{6,7},{7,6},{8,9},{9,8},{10,11... | collective-permute-start | bytes 393224 | tf_op jit(solution)/shard_map/ppermute | solution.py:377
  19.6 22.7 %collective-permute-start.5 = (bf16[64,1024]{1,0:T(8,128)(2,1)}, bf16[64,1024]{1,0:T(8,128)(2,1)S(1)}, u32[]{:S(2)}, u32[]{:S(2)}) collective-permute-start(bf16[64,1024]{1,0:T(8,128)(2,1)} %get-tuple-element.36), channel_id=1, source_target_pairs={{0,2},{1,3},{2,0},{3,1},{4,6},{5,7},{6,4},{7,5},{8,10},{9,11},{10,... | collective-permute-start | bytes 393224 | tf_op jit(solution)/shard_map/ppermute | solution.py:377
  19.6 22.7 %copy-start.7 = (bf16[64,1024]{1,0:T(8,128)(2,1)}, bf16[64,1024]{1,0:T(8,128)(2,1)S(1)}, u32[]{:S(2)}) copy-start(bf16[64,1024]{1,0:T(8,128)(2,1)S(1)} %collective-permute-done.1.refs_5_) | copy-start | bytes 393220
  19.6 22.7 %collective-permute-start.6 = (bf16[64,1024]{1,0:T(8,128)(2,1)}, bf16[64,1024]{1,0:T(8,128)(2,1)S(1)}, u32[]{:S(2)}, u32[]{:S(2)}) collective-permute-start(bf16[64,1024]{1,0:T(8,128)(2,1)} %get-tuple-element.37), channel_id=1, source_target_pairs={{0,3},{1,2},{2,1},{3,0},{4,7},{5,6},{6,5},{7,4},{8,11},{9,10},{10,... | collective-permute-start | bytes 393224 | tf_op jit(solution)/shard_map/ppermute | solution.py:377
  28.3 14.0 %copy-start.8 = (bf16[64,1024]{1,0:T(8,128)(2,1)}, bf16[64,1024]{1,0:T(8,128)(2,1)S(1)}, u32[]{:S(2)}) copy-start(bf16[64,1024]{1,0:T(8,128)(2,1)S(1)} %collective-permute-done.2.refs_6_) | copy-start | bytes 393220
  28.3 14.0 %collective-permute-start.7 = (bf16[64,1024]{1,0:T(8,128)(2,1)}, bf16[64,1024]{1,0:T(8,128)(2,1)S(1)}, u32[]{:S(2)}, u32[]{:S(2)}) collective-permute-start(bf16[64,1024]{1,0:T(8,128)(2,1)} %get-tuple-element.38), channel_id=1, source_target_pairs={{0,4},{1,5},{2,6},{3,7},{4,0},{5,1},{6,2},{7,3},{8,12},{9,13},{10,... | collective-permute-start | bytes 393224 | tf_op jit(solution)/shard_map/ppermute | solution.py:377
  33.0 9.3 %copy-start.9 = (bf16[64,1024]{1,0:T(8,128)(2,1)}, bf16[64,1024]{1,0:T(8,128)(2,1)S(1)}, u32[]{:S(2)}) copy-start(bf16[64,1024]{1,0:T(8,128)(2,1)S(1)} %collective-permute-done.3.refs_7_) | copy-start | bytes 393220
  33.0 35.3 %all-to-all-start = ((bf16[8,64,1024]{2,1,0:T(8,128)(2,1)}), bf16[8,64,1024]{2,1,0:T(8,128)(2,1)S(1)}, u32[]{:S(2)}, u32[]{:S(2)}) async-start(bf16[8,64,1024]{2,1,0:T(8,128)(2,1)} %param.19), calls=%async_computation | async-start | bytes 2097152 | tf_op jit(solution)/shard_map/all_to_all | solution.py:386
  68.3 29.6 %all-to-all-start.1 = ((bf16[8,64,1024]{2,1,0:T(8,128)(2,1)}), bf16[8,64,1024]{2,1,0:T(8,128)(2,1)S(1)}, u32[]{:S(2)}, u32[]{:S(2)}) async-start(bf16[8,64,1024]{2,1,0:T(8,128)(2,1)} %get-tuple-element.55), calls=%async_computation.1 | async-start | bytes 2097152 | tf_op jit(solution)/shard_map/all_to_all | solution.py:386
  87.3 6.1 %collective-permute-start.10 = (bf16[256,256]{1,0:T(8,128)(2,1)}, bf16[256,256]{1,0:T(8,128)(2,1)S(1)}, u32[]{:S(2)}, u32[]{:S(2)}) collective-permute-start(bf16[256,256]{1,0:T(8,128)(2,1)} %get-tuple-element.54), channel_id=1, source_target_pairs={{0,24},{8,16},{16,8},{24,0},{1,25},{9,17},{17,9},{25,1},{2,26},{10... | collective-permute-start | bytes 393224 | tf_op jit(solution)/shard_map/ppermute | solution.py:377
  87.4 6.0 %collective-permute-start.8 = (bf16[256,256]{1,0:T(8,128)(2,1)}, bf16[256,256]{1,0:T(8,128)(2,1)S(1)}, u32[]{:S(2)}, u32[]{:S(2)}) collective-permute-start(bf16[256,256]{1,0:T(8,128)(2,1)} %get-tuple-element.52), channel_id=1, source_target_pairs={{0,8},{8,0},{16,24},{24,16},{1,9},{9,1},{17,25},{25,17},{2,10},{10... | collective-permute-start | bytes 393224 | tf_op jit(solution)/shard_map/ppermute | solution.py:377
  87.4 8.6 %collective-permute-start.9 = (bf16[256,256]{1,0:T(8,128)(2,1)}, bf16[256,256]{1,0:T(8,128)(2,1)S(1)}, u32[]{:S(2)}, u32[]{:S(2)}) collective-permute-start(bf16[256,256]{1,0:T(8,128)(2,1)} %get-tuple-element.53), channel_id=1, source_target_pairs={{0,16},{8,24},{16,0},{24,8},{1,17},{9,25},{17,1},{25,9},{2,18},{10... | collective-permute-start | bytes 393224 | tf_op jit(solution)/shard_map/ppermute | solution.py:377
  97.9 19.4 %copy-start = (bf16[8,64,1024]{2,1,0:T(8,128)(2,1)}, bf16[8,64,1024]{2,1,0:T(8,128)(2,1)S(1)}, u32[]{:S(2)}) copy-start(bf16[8,64,1024]{2,1,0:T(8,128)(2,1)S(1)} %all-to-all-done.1.in_ref) | copy-start | bytes 3145732
  97.9 5.0 %collective-permute-start.11 = (bf16[256,256]{1,0:T(8,128)(2,1)S(1)}, bf16[256,256]{1,0:T(8,128)(2,1)S(1)}, u32[]{:S(2)}, u32[]{:S(2)}) collective-permute-start(bf16[256,256]{1,0:T(8,128)(2,1)S(1)} %add_convert_fusion.2), channel_id=1, source_target_pairs={{0,1},{1,0},{2,3},{3,2},{4,5},{5,4},{6,7},{7,6},{8,9},{9,8},{10,11... | collective-permute-start | bytes 393224 | tf_op jit(solution)/shard_map/ppermute | solution.py:377
  102.9 5.0 %collective-permute-start.12 = (bf16[256,256]{1,0:T(8,128)(2,1)S(1)}, bf16[256,256]{1,0:T(8,128)(2,1)S(1)}, u32[]{:S(2)}, u32[]{:S(2)}) collective-permute-start(bf16[256,256]{1,0:T(8,128)(2,1)S(1)} %add_convert_fusion.1), channel_id=1, source_target_pairs={{0,2},{1,3},{2,0},{3,1},{4,6},{5,7},{6,4},{7,5},{8,10},{9,11},{10,... | collective-permute-start | bytes 393224 | tf_op jit(solution)/shard_map/ppermute | solution.py:377
  108.0 7.3 %collective-permute-start.13 = (bf16[256,256]{1,0:T(8,128)(2,1)S(1)}, bf16[256,256]{1,0:T(8,128)(2,1)S(1)}, u32[]{:S(2)}, u32[]{:S(2)}) collective-permute-start(bf16[256,256]{1,0:T(8,128)(2,1)S(1)} %add_convert_fusion), channel_id=1, source_target_pairs={{0,4},{1,5},{2,6},{3,7},{4,0},{5,1},{6,2},{7,3},{8,12},{9,13},{10,... | collective-permute-start | bytes 393224 | tf_op jit(solution)/shard_map/ppermute | solution.py:377
  115.4 8.4 %copy-start.2 = (bf16[256,256]{1,0:T(8,128)(2,1)}, bf16[256,256]{1,0:T(8,128)(2,1)S(1)}, u32[]{:S(2)}) copy-start(bf16[256,256]{1,0:T(8,128)(2,1)S(1)} %multiply_convert_fusion.refs_0_) | copy-start | bytes 393220
  115.4 4.0 %collective-permute-start.14 = (bf16[256,256]{1,0:T(8,128)(2,1)S(1)}, bf16[256,256]{1,0:T(8,128)(2,1)S(1)}, u32[]{:S(2)}, u32[]{:S(2)}) collective-permute-start(bf16[256,256]{1,0:T(8,128)(2,1)S(1)} %multiply_convert_fusion.refs_0_), channel_id=1, source_target_pairs={{0,8},{8,0},{16,24},{24,16},{1,9},{9,1},{17,25},{25,17},{2,10},{10... | collective-permute-start | bytes 393224 | tf_op jit(solution)/shard_map/ppermute | solution.py:377
  115.4 6.4 %collective-permute-start.15 = (bf16[256,256]{1,0:T(8,128)(2,1)S(1)}, bf16[256,256]{1,0:T(8,128)(2,1)S(1)}, u32[]{:S(2)}, u32[]{:S(2)}) collective-permute-start(bf16[256,256]{1,0:T(8,128)(2,1)S(1)} %multiply_convert_fusion.refs_0_), channel_id=1, source_target_pairs={{0,16},{8,24},{16,0},{24,8},{1,17},{9,25},{17,1},{25,9},{2,18},{10... | collective-permute-start | bytes 393224 | tf_op jit(solution)/shard_map/ppermute | solution.py:377
  115.5 8.2 %collective-permute-start.16 = (bf16[256,256]{1,0:T(8,128)(2,1)S(1)}, bf16[256,256]{1,0:T(8,128)(2,1)S(1)}, u32[]{:S(2)}, u32[]{:S(2)}) collective-permute-start(bf16[256,256]{1,0:T(8,128)(2,1)S(1)} %multiply_convert_fusion.refs_0_), channel_id=1, source_target_pairs={{0,24},{8,16},{16,8},{24,0},{1,25},{9,17},{17,9},{25,1},{2,26},{10... | collective-permute-start | bytes 393224 | tf_op jit(solution)/shard_map/ppermute | solution.py:377
  (9 other events, 14.0 us)

commit v17 on v16

--- a/solution.py
+++ b/solution.py
@@ -406,7 +406,7 @@
     )
     filtered = filter_all(place, signal, rim, fir_taps, count)
     features = swap_all(filtered, "contact")
-    arrived = count - max(2, 3 * count // 8)
+    arrived = count - max(2, count // 2)
     features[arrived:], cotangent = lax.optimization_barrier((features[arrived:], cotangent))
     upstream = exchange(cotangent, "contact")
     attended, *kept = forward(

time: 127 us -> 130 us (1.024)
  waiting for transfers between devices: 31.4 us -> 33.1 us
    all_to_all x2, starting transfers between devices: 12.9 us -> 14.9 us  [exchange(): return lax.all_to_all(value, axis, split_axis=0, concat_axis=0, tiled=True)]
    ppermute x16, waiting for transfers between devices: 23.3 us -> 25.2 us  [swap(): lax.ppermute(value, axis, [(i, i ^ k) for i in range(lax.axis_size(axis))])]
  transfers between devices with their start and end apart: 19 -> 19, of which waited for: 10 -> 11; matrix products, arithmetic and copies ran while one was open for 1% -> 1% of each run, Pallas kernels for 28% -> 28%
where the time goes in v17:
time: 130 us; the launch traced here: 129 us
  starting transfers between devices  48.5 us (37%)
  Pallas kernels  42.2 us (32%)
  waiting for transfers between devices  33.1 us (25%)
  local copies, waits for them, and re-layouts  2.92 us (2%)
  other arithmetic  1.75 us (1%)
    ppermute x16, starting transfers between devices, swap(): lax.ppermute(value, axis, [(i, i ^ k) for i in range(lax.axis_size(axis))])  31.2 us
    ppermute x16, waiting for transfers between devices, swap(): lax.ppermute(value, axis, [(i, i ^ k) for i in range(lax.axis_size(axis))])  25.2 us
    pallas_call x1, Pallas kernels, forward(): pl.pallas_call(functools.partial(forward_kernel, blocks), grid=(groups,),...  18.3 us
    pallas_call x1, Pallas kernels, backward(): pl.pallas_call(functools.partial(backward_kernel, blocks), grid=(groups,)...  15.3 us
    all_to_all x2, starting transfers between devices, exchange(): return lax.all_to_all(value, axis, split_axis=0, concat_axis=0, tiled=True)  14.9 us
    all_to_all x2, waiting for transfers between devices, exchange(): return lax.all_to_all(value, axis, split_axis=0, concat_axis=0, tiled=True)  7.69 us
    pallas_call x1, Pallas kernels, filter_all(): pl.pallas_call(filter_kernel, grid=(contacts // rows,), in_specs=[index_s...  4.33 us
  transfers between devices with their start and end apart: 19, of which 11 were waited for; matrix products, arithmetic and copies ran while one was open for 1% of the time, Pallas kernels for 28%

profile of v17, /device:TPU:0, one launch (start us, length us, event | category | flops | bytes accessed | tf_op | source)
XLA Modules:
  0.0 129.3 jit_solution(9567391753662756097)
XLA Ops:
  1.5 2.4 %collective-permute-start = (bf16[8,64,128]{2,1,0:T(8,128)(2,1)S(1)}, bf16[8,64,128]{2,1,0:T(8,128)(2,1)S(1)}, u32[]{:S(2)}, u32[]{:S(2)}) collective-permute-start(bf16[8,64,128]{2,1,0:T(8,128)(2,1)S(1)} %slice.3), channel_id=1, source_target_pairs={{0,8},{8,16},{16,24},{1,9},{9,17},{17,25},{2,10},{10,18},{18,26},{... | collective-permute-start | bytes 393224 | tf_op jit(solution)/shard_map/ppermute | solution.py:404
  5.5 4.3 %filter.1 = (bf16[64,1024]{1,0:T(8,128)(2,1)}, bf16[64,1024]{1,0:T(8,128)(2,1)}, bf16[64,1024]{1,0:T(8,128)(2,1)}, bf16[64,1024]{1,0:T(8,128)(2,1)}, bf16[64,102...) custom-call(s32[2]{0:T(128)} %pad_add_fusion.place_ref, ...), custom_call_target="tpu_custom_call" | custom-call | flops 268435456 | bytes 2097152 | tf_op jit(solution)/shard_map/filter/pallas_call | solution.py:72
  9.9 3.5 %collective-permute-start.1 = (bf16[64,1024]{1,0:T(8,128)(2,1)}, bf16[64,1024]{1,0:T(8,128)(2,1)S(1)}, u32[]{:S(2)}, u32[]{:S(2)}) collective-permute-start(bf16[64,1024]{1,0:T(8,128)(2,1)} %get-tuple-element.31), channel_id=1, source_target_pairs={{0,4},{1,5},{2,6},{3,7},{4,0},{5,1},{6,2},{7,3},{8,12},{9,13},{10,... | collective-permute-start | bytes 393224 | tf_op jit(solution)/shard_map/ppermute | solution.py:377
  14.6 3.6 %collective-permute-start.3 = (bf16[64,1024]{1,0:T(8,128)(2,1)}, bf16[64,1024]{1,0:T(8,128)(2,1)S(1)}, u32[]{:S(2)}, u32[]{:S(2)}) collective-permute-start(bf16[64,1024]{1,0:T(8,128)(2,1)} %get-tuple-element.33), channel_id=1, source_target_pairs={{0,6},{1,7},{2,4},{3,5},{4,2},{5,3},{6,0},{7,1},{8,14},{9,15},{10,... | collective-permute-start | bytes 393224 | tf_op jit(solution)/shard_map/ppermute | solution.py:377
  19.9 10.2 %collective-permute-start.6 = (bf16[64,1024]{1,0:T(8,128)(2,1)}, bf16[64,1024]{1,0:T(8,128)(2,1)S(1)}, u32[]{:S(2)}, u32[]{:S(2)}) collective-permute-start(bf16[64,1024]{1,0:T(8,128)(2,1)} %get-tuple-element.38), channel_id=1, source_target_pairs={{0,2},{1,3},{2,0},{3,1},{4,6},{5,7},{6,4},{7,5},{8,10},{9,11},{10,... | collective-permute-start | bytes 393224 | tf_op jit(solution)/shard_map/ppermute | solution.py:377
  30.2 1.9 %collective-permute-done.2.refs_5_ = bf16[64,1024]{1,0:T(8,128)(2,1)S(1)} collective-permute-done((bf16[64,1024]{1,0:T(8,128)(2,1)}, bf16[64,1024]{1,0:T(8,128)(2,1)S(1)}, u32[]{:S(2)}, u32[]{:S(2)}) %collective-permute-start.2) | collective-permute-done | bytes 131104 | tf_op jit(solution)/shard_map/ppermute | solution.py:377
  32.1 1.9 %collective-permute-start.7 = (bf16[64,1024]{1,0:T(8,128)(2,1)}, bf16[64,1024]{1,0:T(8,128)(2,1)S(1)}, u32[]{:S(2)}, u32[]{:S(2)}) collective-permute-start(bf16[64,1024]{1,0:T(8,128)(2,1)} %get-tuple-element.39), channel_id=1, source_target_pairs={{0,3},{1,2},{2,1},{3,0},{4,7},{5,6},{6,5},{7,4},{8,11},{9,10},{10,... | collective-permute-start | bytes 393224 | tf_op jit(solution)/shard_map/ppermute | solution.py:377
  33.9 11.3 %all-to-all-start = ((bf16[8,64,1024]{2,1,0:T(8,128)(2,1)}), bf16[8,64,1024]{2,1,0:T(8,128)(2,1)S(1)}, u32[]{:S(2)}, u32[]{:S(2)}) async-start(bf16[8,64,1024]{2,1,0:T(8,128)(2,1)} %param.19), calls=%async_computation | async-start | bytes 2097152 | tf_op jit(solution)/shard_map/all_to_all | solution.py:386
  46.0 18.3 %forward.1 = (bf16[8,64,1024]{2,1,0:T(8,128)(2,1)}, bf16[512,8192]{1,0:T(8,128)(2,1)}, bf16[512,1024]{1,0:T(8,128)(2,1)}, bf16[512,1024]{1,0:T(8,128)(2,1)}, bf1...) custom-call(s32[2]{0:T(128)} %pad_add_fusion.place_ref, ...), custom_call_target="tpu_custom_call" | custom-call | flops 20000000000 | bytes 10485760 | tf_op jit(solution)/shard_map/forward/pallas_call | solution.py:278
  64.3 6.8 %all-to-all-done.up_ref = bf16[8,64,1024]{2,1,0:T(8,128)(2,1)S(1)} async-done(((bf16[8,64,1024]{2,1,0:T(8,128)(2,1)}), bf16[8,64,1024]{2,1,0:T(8,128)(2,1)S(1)}, u32[]{:S(2)}, u32[]{:S(2)}) %all-to-all-start) | async-done | bytes 1048608 | tf_op jit(solution)/shard_map/all_to_all | solution.py:386
  71.1 3.6 %all-to-all-start.1 = ((bf16[8,64,1024]{2,1,0:T(8,128)(2,1)}), bf16[8,64,1024]{2,1,0:T(8,128)(2,1)S(1)}, u32[]{:S(2)}, u32[]{:S(2)}) async-start(bf16[8,64,1024]{2,1,0:T(8,128)(2,1)} %get-tuple-element.57), calls=%async_computation.1 | async-start | bytes 2097152 | tf_op jit(solution)/shard_map/all_to_all | solution.py:386
  74.8 15.3 %backward.1 = (bf16[256,256]{1,0:T(8,128)(2,1)}, bf16[256,256]{1,0:T(8,128)(2,1)}, bf16[256,256]{1,0:T(8,128)(2,1)}, bf16[256,256]{1,0:T(8,128)(2,1)}) custom-call(s32[2]{0:T(128)} %pad_add_fusion.place_ref, bf16[256,256]{1,0:T(8,128)(2,1)} %wo_ref.3, bf16[8,64,1024]{2,1,0:T(8,128)(2,1)} %copy-done.1, bf16[512,8192]{1,0:T(8,128)(2,1)} %get-tuple-element.44.prob_ref, ...), custom_call_target="tpu_custom_call" | custom-call | flops 20000000000 | bytes 10485760 | tf_op jit(solution)/shard_map/backward/pallas_call | solution.py:314
  90.2 2.1 %collective-permute-start.9 = (bf16[256,256]{1,0:T(8,128)(2,1)}, bf16[256,256]{1,0:T(8,128)(2,1)S(1)}, u32[]{:S(2)}, u32[]{:S(2)}) collective-permute-start(bf16[256,256]{1,0:T(8,128)(2,1)} %get-tuple-element.55), channel_id=1, source_target_pairs={{0,16},{8,24},{16,0},{24,8},{1,17},{9,25},{17,1},{25,9},{2,18},{10... | collective-permute-start | bytes 393224 | tf_op jit(solution)/shard_map/ppermute | solution.py:377
  92.3 3.9 %collective-permute-done.10 = bf16[256,256]{1,0:T(8,128)(2,1)S(1)} collective-permute-done((bf16[256,256]{1,0:T(8,128)(2,1)}, bf16[256,256]{1,0:T(8,128)(2,1)S(1)}, u32[]{:S(2)}, u32[]{:S(2)}) %collective-permute-start.10) | collective-permute-done | bytes 131104 | tf_op jit(solution)/shard_map/ppermute | solution.py:377
  96.2 2.6 %collective-permute-done.9 = bf16[256,256]{1,0:T(8,128)(2,1)S(1)} collective-permute-done((bf16[256,256]{1,0:T(8,128)(2,1)}, bf16[256,256]{1,0:T(8,128)(2,1)S(1)}, u32[]{:S(2)}, u32[]{:S(2)}) %collective-permute-start.9) | collective-permute-done | bytes 131104 | tf_op jit(solution)/shard_map/ppermute | solution.py:377
  102.1 3.5 %collective-permute-done.11 = bf16[256,256]{1,0:T(8,128)(2,1)S(1)} collective-permute-done((bf16[256,256]{1,0:T(8,128)(2,1)S(1)}, bf16[256,256]{1,0:T(8,128)(2,1)S(1)}, u32[]{:S(2)}, u32[]{:S(2)}) %collective-permute-start.11) | collective-permute-done | bytes 131104 | tf_op jit(solution)/shard_map/ppermute | solution.py:377
  107.0 3.7 %collective-permute-done.12 = bf16[256,256]{1,0:T(8,128)(2,1)S(1)} collective-permute-done((bf16[256,256]{1,0:T(8,128)(2,1)S(1)}, bf16[256,256]{1,0:T(8,128)(2,1)S(1)}, u32[]{:S(2)}, u32[]{:S(2)}) %collective-permute-start.12) | collective-permute-done | bytes 131104 | tf_op jit(solution)/shard_map/ppermute | solution.py:377
  110.8 2.2 %collective-permute-start.13 = (bf16[256,256]{1,0:T(8,128)(2,1)S(1)}, bf16[256,256]{1,0:T(8,128)(2,1)S(1)}, u32[]{:S(2)}, u32[]{:S(2)}) collective-permute-start(bf16[256,256]{1,0:T(8,128)(2,1)S(1)} %add_convert_fusion), channel_id=1, source_target_pairs={{0,4},{1,5},{2,6},{3,7},{4,0},{5,1},{6,2},{7,3},{8,12},{9,13},{10,... | collective-permute-start | bytes 393224 | tf_op jit(solution)/shard_map/ppermute | solution.py:377
  113.0 5.1 %collective-permute-done.13 = bf16[256,256]{1,0:T(8,128)(2,1)S(1)} collective-permute-done((bf16[256,256]{1,0:T(8,128)(2,1)S(1)}, bf16[256,256]{1,0:T(8,128)(2,1)S(1)}, u32[]{:S(2)}, u32[]{:S(2)}) %collective-permute-start.13) | collective-permute-done | bytes 131104 | tf_op jit(solution)/shard_map/ppermute | solution.py:377
  118.3 1.8 %collective-permute-start.16 = (bf16[256,256]{1,0:T(8,128)(2,1)S(1)}, bf16[256,256]{1,0:T(8,128)(2,1)S(1)}, u32[]{:S(2)}, u32[]{:S(2)}) collective-permute-start(bf16[256,256]{1,0:T(8,128)(2,1)S(1)} %multiply_convert_fusion.refs_0_), channel_id=1, source_target_pairs={{0,24},{8,16},{16,8},{24,0},{1,25},{9,17},{17,9},{25,1},{2,26},{10... | collective-permute-start | bytes 393224 | tf_op jit(solution)/shard_map/ppermute | solution.py:377
  120.1 2.0 %write_out.1 = bf16[8,64,1024]{2,1,0:T(8,128)(2,1)} custom-call(bf16[8,64,1024]{2,1,0:T(8,128)(2,1)} %copy-done), custom_call_target="tpu_custom_call" | custom-call | bytes 2097152 | tf_op jit(solution)/shard_map/write_out/pallas_call | solution.py:364
  122.2 2.5 %collective-permute-done.15.refs_2_ = bf16[256,256]{1,0:T(8,128)(2,1)S(1)} collective-permute-done((bf16[256,256]{1,0:T(8,128)(2,1)S(1)}, bf16[256,256]{1,0:T(8,128)(2,1)S(1)}, u32[]{:S(2)}, u32[]{:S(2)}) %collective-permute-start.15) | collective-permute-done | bytes 131104 | tf_op jit(solution)/shard_map/ppermute | solution.py:377
  124.6 1.9 %collective-permute-done.16.refs_3_ = bf16[256,256]{1,0:T(8,128)(2,1)S(1)} collective-permute-done((bf16[256,256]{1,0:T(8,128)(2,1)S(1)}, bf16[256,256]{1,0:T(8,128)(2,1)S(1)}, u32[]{:S(2)}, u32[]{:S(2)}) %collective-permute-start.16) | collective-permute-done | bytes 131104 | tf_op jit(solution)/shard_map/ppermute | solution.py:377
  127.2 2.1 %place_all.1 = f32[4,256,256]{2,1,0:T(8,128)} custom-call(s32[2]{0:T(128)} %pad_add_fusion.place_ref, bf16[256,256]{1,0:T(8,128)(2,1)} %copy-done.2, bf16[256,256]{1,0:T(8,128)(2,1)} %copy-done.4, bf16[256,256]{1,0:T(8,128)(2,1)} %copy-done.5, bf16[256,256]{1,0:T(8,128)(2,1)} %copy-done.6), custom_call_target="tpu_custom_call" | custom-call | tf_op jit(solution)/shard_map/place_all/pallas_call | solution.py:349
  (53 shorter events, 11.9 us)
Async XLA Ops:
  1.5 3.3 %collective-permute-start = (bf16[8,64,128]{2,1,0:T(8,128)(2,1)S(1)}, bf16[8,64,128]{2,1,0:T(8,128)(2,1)S(1)}, u32[]{:S(2)}, u32[]{:S(2)}) collective-permute-start(bf16[8,64,128]{2,1,0:T(8,128)(2,1)S(1)} %slice.3), channel_id=1, source_target_pairs={{0,8},{8,16},{16,24},{1,9},{9,17},{17,25},{2,10},{10,18},{18,26},{... | collective-permute-start | bytes 393224 | tf_op jit(solution)/shard_map/ppermute | solution.py:404
  9.9 10.1 %collective-permute-start.1 = (bf16[64,1024]{1,0:T(8,128)(2,1)}, bf16[64,1024]{1,0:T(8,128)(2,1)S(1)}, u32[]{:S(2)}, u32[]{:S(2)}) collective-permute-start(bf16[64,1024]{1,0:T(8,128)(2,1)} %get-tuple-element.31), channel_id=1, source_target_pairs={{0,4},{1,5},{2,6},{3,7},{4,0},{5,1},{6,2},{7,3},{8,12},{9,13},{10,... | collective-permute-start | bytes 393224 | tf_op jit(solution)/shard_map/ppermute | solution.py:377
  13.3 18.7 %collective-permute-start.2 = (bf16[64,1024]{1,0:T(8,128)(2,1)}, bf16[64,1024]{1,0:T(8,128)(2,1)S(1)}, u32[]{:S(2)}, u32[]{:S(2)}) collective-permute-start(bf16[64,1024]{1,0:T(8,128)(2,1)} %get-tuple-element.32), channel_id=1, source_target_pairs={{0,5},{1,4},{2,7},{3,6},{4,1},{5,0},{6,3},{7,2},{8,13},{9,12},{10,... | collective-permute-start | bytes 393224 | tf_op jit(solution)/shard_map/ppermute | solution.py:377
  14.6 19.3 %collective-permute-start.3 = (bf16[64,1024]{1,0:T(8,128)(2,1)}, bf16[64,1024]{1,0:T(8,128)(2,1)S(1)}, u32[]{:S(2)}, u32[]{:S(2)}) collective-permute-start(bf16[64,1024]{1,0:T(8,128)(2,1)} %get-tuple-element.33), channel_id=1, source_target_pairs={{0,6},{1,7},{2,4},{3,5},{4,2},{5,3},{6,0},{7,1},{8,14},{9,15},{10,... | collective-permute-start | bytes 393224 | tf_op jit(solution)/shard_map/ppermute | solution.py:377
  18.2 15.7 %collective-permute-start.4 = (bf16[64,1024]{1,0:T(8,128)(2,1)}, bf16[64,1024]{1,0:T(8,128)(2,1)S(1)}, u32[]{:S(2)}, u32[]{:S(2)}) collective-permute-start(bf16[64,1024]{1,0:T(8,128)(2,1)} %get-tuple-element.34), channel_id=1, source_target_pairs={{0,7},{1,6},{2,5},{3,4},{4,3},{5,2},{6,1},{7,0},{8,15},{9,14},{10,... | collective-permute-start | bytes 393224 | tf_op jit(solution)/shard_map/ppermute | solution.py:377
  18.2 27.0 %collective-permute-start.5 = (bf16[64,1024]{1,0:T(8,128)(2,1)}, bf16[64,1024]{1,0:T(8,128)(2,1)S(1)}, u32[]{:S(2)}, u32[]{:S(2)}) collective-permute-start(bf16[64,1024]{1,0:T(8,128)(2,1)} %get-tuple-element.37), channel_id=1, source_target_pairs={{0,1},{1,0},{2,3},{3,2},{4,5},{5,4},{6,7},{7,6},{8,9},{9,8},{10,11... | collective-permute-start | bytes 393224 | tf_op jit(solution)/shard_map/ppermute | solution.py:377
  19.9 25.4 %copy-start.7 = (bf16[64,1024]{1,0:T(8,128)(2,1)}, bf16[64,1024]{1,0:T(8,128)(2,1)S(1)}, u32[]{:S(2)}) copy-start(bf16[64,1024]{1,0:T(8,128)(2,1)S(1)} %collective-permute-done.1.refs_4_) | copy-start | bytes 393220
  19.9 25.3 %collective-permute-start.6 = (bf16[64,1024]{1,0:T(8,128)(2,1)}, bf16[64,1024]{1,0:T(8,128)(2,1)S(1)}, u32[]{:S(2)}, u32[]{:S(2)}) collective-permute-start(bf16[64,1024]{1,0:T(8,128)(2,1)} %get-tuple-element.38), channel_id=1, source_target_pairs={{0,2},{1,3},{2,0},{3,1},{4,6},{5,7},{6,4},{7,5},{8,10},{9,11},{10,... | collective-permute-start | bytes 393224 | tf_op jit(solution)/shard_map/ppermute | solution.py:377
  32.1 13.2 %copy-start.8 = (bf16[64,1024]{1,0:T(8,128)(2,1)}, bf16[64,1024]{1,0:T(8,128)(2,1)S(1)}, u32[]{:S(2)}) copy-start(bf16[64,1024]{1,0:T(8,128)(2,1)S(1)} %collective-permute-done.2.refs_5_) | copy-start | bytes 393220
  32.1 13.2 %collective-permute-start.7 = (bf16[64,1024]{1,0:T(8,128)(2,1)}, bf16[64,1024]{1,0:T(8,128)(2,1)S(1)}, u32[]{:S(2)}, u32[]{:S(2)}) collective-permute-start(bf16[64,1024]{1,0:T(8,128)(2,1)} %get-tuple-element.39), channel_id=1, source_target_pairs={{0,3},{1,2},{2,1},{3,0},{4,7},{5,6},{6,5},{7,4},{8,11},{9,10},{10,... | collective-permute-start | bytes 393224 | tf_op jit(solution)/shard_map/ppermute | solution.py:377
  33.9 11.4 %copy-start.9 = (bf16[64,1024]{1,0:T(8,128)(2,1)}, bf16[64,1024]{1,0:T(8,128)(2,1)S(1)}, u32[]{:S(2)}) copy-start(bf16[64,1024]{1,0:T(8,128)(2,1)S(1)} %collective-permute-done.3.refs_6_) | copy-start | bytes 393220
  33.9 11.4 %copy-start.10 = (bf16[64,1024]{1,0:T(8,128)(2,1)}, bf16[64,1024]{1,0:T(8,128)(2,1)S(1)}, u32[]{:S(2)}) copy-start(bf16[64,1024]{1,0:T(8,128)(2,1)S(1)} %collective-permute-done.4.refs_7_) | copy-start | bytes 393220
  33.9 37.2 %all-to-all-start = ((bf16[8,64,1024]{2,1,0:T(8,128)(2,1)}), bf16[8,64,1024]{2,1,0:T(8,128)(2,1)S(1)}, u32[]{:S(2)}, u32[]{:S(2)}) async-start(bf16[8,64,1024]{2,1,0:T(8,128)(2,1)} %param.19), calls=%async_computation | async-start | bytes 2097152 | tf_op jit(solution)/shard_map/all_to_all | solution.py:386
  71.1 29.6 %all-to-all-start.1 = ((bf16[8,64,1024]{2,1,0:T(8,128)(2,1)}), bf16[8,64,1024]{2,1,0:T(8,128)(2,1)S(1)}, u32[]{:S(2)}, u32[]{:S(2)}) async-start(bf16[8,64,1024]{2,1,0:T(8,128)(2,1)} %get-tuple-element.57), calls=%async_computation.1 | async-start | bytes 2097152 | tf_op jit(solution)/shard_map/all_to_all | solution.py:386
  90.1 6.1 %collective-permute-start.10 = (bf16[256,256]{1,0:T(8,128)(2,1)}, bf16[256,256]{1,0:T(8,128)(2,1)S(1)}, u32[]{:S(2)}, u32[]{:S(2)}) collective-permute-start(bf16[256,256]{1,0:T(8,128)(2,1)} %get-tuple-element.56), channel_id=1, source_target_pairs={{0,24},{8,16},{16,8},{24,0},{1,25},{9,17},{17,9},{25,1},{2,26},{10... | collective-permute-start | bytes 393224 | tf_op jit(solution)/shard_map/ppermute | solution.py:377
  90.2 6.0 %collective-permute-start.8 = (bf16[256,256]{1,0:T(8,128)(2,1)}, bf16[256,256]{1,0:T(8,128)(2,1)S(1)}, u32[]{:S(2)}, u32[]{:S(2)}) collective-permute-start(bf16[256,256]{1,0:T(8,128)(2,1)} %get-tuple-element.54), channel_id=1, source_target_pairs={{0,8},{8,0},{16,24},{24,16},{1,9},{9,1},{17,25},{25,17},{2,10},{10... | collective-permute-start | bytes 393224 | tf_op jit(solution)/shard_map/ppermute | solution.py:377
  90.2 8.6 %collective-permute-start.9 = (bf16[256,256]{1,0:T(8,128)(2,1)}, bf16[256,256]{1,0:T(8,128)(2,1)S(1)}, u32[]{:S(2)}, u32[]{:S(2)}) collective-permute-start(bf16[256,256]{1,0:T(8,128)(2,1)} %get-tuple-element.55), channel_id=1, source_target_pairs={{0,16},{8,24},{16,0},{24,8},{1,17},{9,25},{17,1},{25,9},{2,18},{10... | collective-permute-start | bytes 393224 | tf_op jit(solution)/shard_map/ppermute | solution.py:377
  100.7 19.4 %copy-start = (bf16[8,64,1024]{2,1,0:T(8,128)(2,1)}, bf16[8,64,1024]{2,1,0:T(8,128)(2,1)S(1)}, u32[]{:S(2)}) copy-start(bf16[8,64,1024]{2,1,0:T(8,128)(2,1)S(1)} %all-to-all-done.1.in_ref) | copy-start | bytes 3145732
  100.7 5.0 %collective-permute-start.11 = (bf16[256,256]{1,0:T(8,128)(2,1)S(1)}, bf16[256,256]{1,0:T(8,128)(2,1)S(1)}, u32[]{:S(2)}, u32[]{:S(2)}) collective-permute-start(bf16[256,256]{1,0:T(8,128)(2,1)S(1)} %add_convert_fusion.2), channel_id=1, source_target_pairs={{0,1},{1,0},{2,3},{3,2},{4,5},{5,4},{6,7},{7,6},{8,9},{9,8},{10,11... | collective-permute-start | bytes 393224 | tf_op jit(solution)/shard_map/ppermute | solution.py:377
  105.7 5.0 %collective-permute-start.12 = (bf16[256,256]{1,0:T(8,128)(2,1)S(1)}, bf16[256,256]{1,0:T(8,128)(2,1)S(1)}, u32[]{:S(2)}, u32[]{:S(2)}) collective-permute-start(bf16[256,256]{1,0:T(8,128)(2,1)S(1)} %add_convert_fusion.1), channel_id=1, source_target_pairs={{0,2},{1,3},{2,0},{3,1},{4,6},{5,7},{6,4},{7,5},{8,10},{9,11},{10,... | collective-permute-start | bytes 393224 | tf_op jit(solution)/shard_map/ppermute | solution.py:377
  110.8 7.3 %collective-permute-start.13 = (bf16[256,256]{1,0:T(8,128)(2,1)S(1)}, bf16[256,256]{1,0:T(8,128)(2,1)S(1)}, u32[]{:S(2)}, u32[]{:S(2)}) collective-permute-start(bf16[256,256]{1,0:T(8,128)(2,1)S(1)} %add_convert_fusion), channel_id=1, source_target_pairs={{0,4},{1,5},{2,6},{3,7},{4,0},{5,1},{6,2},{7,3},{8,12},{9,13},{10,... | collective-permute-start | bytes 393224 | tf_op jit(solution)/shard_map/ppermute | solution.py:377
  118.2 4.0 %collective-permute-start.14 = (bf16[256,256]{1,0:T(8,128)(2,1)S(1)}, bf16[256,256]{1,0:T(8,128)(2,1)S(1)}, u32[]{:S(2)}, u32[]{:S(2)}) collective-permute-start(bf16[256,256]{1,0:T(8,128)(2,1)S(1)} %multiply_convert_fusion.refs_0_), channel_id=1, source_target_pairs={{0,8},{8,0},{16,24},{24,16},{1,9},{9,1},{17,25},{25,17},{2,10},{10... | collective-permute-start | bytes 393224 | tf_op jit(solution)/shard_map/ppermute | solution.py:377
  118.3 6.4 %collective-permute-start.15 = (bf16[256,256]{1,0:T(8,128)(2,1)S(1)}, bf16[256,256]{1,0:T(8,128)(2,1)S(1)}, u32[]{:S(2)}, u32[]{:S(2)}) collective-permute-start(bf16[256,256]{1,0:T(8,128)(2,1)S(1)} %multiply_convert_fusion.refs_0_), channel_id=1, source_target_pairs={{0,16},{8,24},{16,0},{24,8},{1,17},{9,25},{17,1},{25,9},{2,18},{10... | collective-permute-start | bytes 393224 | tf_op jit(solution)/shard_map/ppermute | solution.py:377
  118.3 8.2 %collective-permute-start.16 = (bf16[256,256]{1,0:T(8,128)(2,1)S(1)}, bf16[256,256]{1,0:T(8,128)(2,1)S(1)}, u32[]{:S(2)}, u32[]{:S(2)}) collective-permute-start(bf16[256,256]{1,0:T(8,128)(2,1)S(1)} %multiply_convert_fusion.refs_0_), channel_id=1, source_target_pairs={{0,24},{8,16},{16,8},{24,0},{1,25},{9,17},{17,9},{25,1},{2,26},{10... | collective-permute-start | bytes 393224 | tf_op jit(solution)/shard_map/ppermute | solution.py:377
  (9 other events, 21.6 us)

commit v18 on v16

--- a/solution.py
+++ b/solution.py
@@ -67,7 +67,7 @@
 def filter_all(place, signal, rim, taps, count):
     batch, contacts, slab = signal.shape
     width = rim.shape[2]
-    rows = min(32, contacts)
+    rows = min(64, contacts)
     span = slab * batch // count
     return pl.pallas_call(
         filter_kernel,

time: 127 us -> 127 us (level)
  no operation moved by 1% of the time
where the time goes in v18:
time: 127 us
  starting transfers between devices  47.4 us (37%)
  Pallas kernels  42.3 us (33%)
  waiting for transfers between devices  31.4 us (25%)
  local copies, waits for them, and re-layouts  2.96 us (2%)
  other arithmetic  1.75 us (1%)
    ppermute x16, starting transfers between devices, swap(): lax.ppermute(value, axis, [(i, i ^ k) for i in range(lax.axis_size(axis))])  32.1 us
    ppermute x16, waiting for transfers between devices, swap(): lax.ppermute(value, axis, [(i, i ^ k) for i in range(lax.axis_size(axis))])  23.3 us
    pallas_call x1, Pallas kernels, forward(): pl.pallas_call(functools.partial(forward_kernel, blocks), grid=(groups,),...  18.3 us
    pallas_call x1, Pallas kernels, backward(): pl.pallas_call(functools.partial(backward_kernel, blocks), grid=(groups,)...  15.3 us
    all_to_all x2, starting transfers between devices, exchange(): return lax.all_to_all(value, axis, split_axis=0, concat_axis=0, tiled=True)  12.9 us
    all_to_all x2, waiting for transfers between devices, exchange(): return lax.all_to_all(value, axis, split_axis=0, concat_axis=0, tiled=True)  7.8 us
    pallas_call x1, Pallas kernels, filter_all(): pl.pallas_call(filter_kernel, grid=(contacts // rows,), in_specs=[index_s...  4.47 us
  transfers between devices with their start and end apart: 19, of which 10 were waited for; matrix products, arithmetic and copies ran while one was open for 1% of the time, Pallas kernels for 28%

profile of v18, /device:TPU:0, one launch (start us, length us, event | category | flops | bytes accessed | tf_op | source)
XLA Modules:
  0.0 126.6 jit_solution(18357927555968361977)
XLA Ops:
  1.5 2.4 %collective-permute-start = (bf16[8,64,128]{2,1,0:T(8,128)(2,1)S(1)}, bf16[8,64,128]{2,1,0:T(8,128)(2,1)S(1)}, u32[]{:S(2)}, u32[]{:S(2)}) collective-permute-start(bf16[8,64,128]{2,1,0:T(8,128)(2,1)S(1)} %slice.3), channel_id=1, source_target_pairs={{0,8},{8,16},{16,24},{1,9},{9,17},{17,25},{2,10},{10,18},{18,26},{... | collective-permute-start | bytes 393224 | tf_op jit(solution)/shard_map/ppermute | solution.py:404
  5.5 4.5 %filter.1 = (bf16[64,1024]{1,0:T(8,128)(2,1)}, bf16[64,1024]{1,0:T(8,128)(2,1)}, bf16[64,1024]{1,0:T(8,128)(2,1)}, bf16[64,1024]{1,0:T(8,128)(2,1)}, bf16[64,102...) custom-call(s32[2]{0:T(128)} %pad_add_fusion.place_ref, ...), custom_call_target="tpu_custom_call" | custom-call | flops 268435456 | bytes 2097152 | tf_op jit(solution)/shard_map/filter/pallas_call | solution.py:72
  10.0 4.4 %collective-permute-start.1 = (bf16[64,1024]{1,0:T(8,128)(2,1)}, bf16[64,1024]{1,0:T(8,128)(2,1)S(1)}, u32[]{:S(2)}, u32[]{:S(2)}) collective-permute-start(bf16[64,1024]{1,0:T(8,128)(2,1)} %get-tuple-element.30), channel_id=1, source_target_pairs={{0,5},{1,4},{2,7},{3,6},{4,1},{5,0},{6,3},{7,2},{8,13},{9,12},{10,... | collective-permute-start | bytes 393224 | tf_op jit(solution)/shard_map/ppermute | solution.py:377
  15.7 2.4 %collective-permute-start.3 = (bf16[64,1024]{1,0:T(8,128)(2,1)}, bf16[64,1024]{1,0:T(8,128)(2,1)S(1)}, u32[]{:S(2)}, u32[]{:S(2)}) collective-permute-start(bf16[64,1024]{1,0:T(8,128)(2,1)} %get-tuple-element.32), channel_id=1, source_target_pairs={{0,7},{1,6},{2,5},{3,4},{4,3},{5,2},{6,1},{7,0},{8,15},{9,14},{10,... | collective-permute-start | bytes 393224 | tf_op jit(solution)/shard_map/ppermute | solution.py:377
  18.1 1.5 %collective-permute-start.4 = (bf16[64,1024]{1,0:T(8,128)(2,1)}, bf16[64,1024]{1,0:T(8,128)(2,1)S(1)}, u32[]{:S(2)}, u32[]{:S(2)}) collective-permute-start(bf16[64,1024]{1,0:T(8,128)(2,1)} %get-tuple-element.35), channel_id=1, source_target_pairs={{0,1},{1,0},{2,3},{3,2},{4,5},{5,4},{6,7},{7,6},{8,9},{9,8},{10,11... | collective-permute-start | bytes 393224 | tf_op jit(solution)/shard_map/ppermute | solution.py:377
  19.7 8.7 %collective-permute-start.6 = (bf16[64,1024]{1,0:T(8,128)(2,1)}, bf16[64,1024]{1,0:T(8,128)(2,1)S(1)}, u32[]{:S(2)}, u32[]{:S(2)}) collective-permute-start(bf16[64,1024]{1,0:T(8,128)(2,1)} %get-tuple-element.37), channel_id=1, source_target_pairs={{0,3},{1,2},{2,1},{3,0},{4,7},{5,6},{6,5},{7,4},{8,11},{9,10},{10,... | collective-permute-start | bytes 393224 | tf_op jit(solution)/shard_map/ppermute | solution.py:377
  28.4 4.7 %collective-permute-start.7 = (bf16[64,1024]{1,0:T(8,128)(2,1)}, bf16[64,1024]{1,0:T(8,128)(2,1)S(1)}, u32[]{:S(2)}, u32[]{:S(2)}) collective-permute-start(bf16[64,1024]{1,0:T(8,128)(2,1)} %get-tuple-element.38), channel_id=1, source_target_pairs={{0,4},{1,5},{2,6},{3,7},{4,0},{5,1},{6,2},{7,3},{8,12},{9,13},{10,... | collective-permute-start | bytes 393224 | tf_op jit(solution)/shard_map/ppermute | solution.py:377
  33.1 9.2 %all-to-all-start = ((bf16[8,64,1024]{2,1,0:T(8,128)(2,1)}), bf16[8,64,1024]{2,1,0:T(8,128)(2,1)S(1)}, u32[]{:S(2)}, u32[]{:S(2)}) async-start(bf16[8,64,1024]{2,1,0:T(8,128)(2,1)} %param.19), calls=%async_computation | async-start | bytes 2097152 | tf_op jit(solution)/shard_map/all_to_all | solution.py:386
  43.2 18.3 %forward.1 = (bf16[8,64,1024]{2,1,0:T(8,128)(2,1)}, bf16[512,8192]{1,0:T(8,128)(2,1)}, bf16[512,1024]{1,0:T(8,128)(2,1)}, bf16[512,1024]{1,0:T(8,128)(2,1)}, bf1...) custom-call(s32[2]{0:T(128)} %pad_add_fusion.place_ref, ...), custom_call_target="tpu_custom_call" | custom-call | flops 20000000000 | bytes 10485760 | tf_op jit(solution)/shard_map/forward/pallas_call | solution.py:278
  61.5 6.9 %all-to-all-done.up_ref = bf16[8,64,1024]{2,1,0:T(8,128)(2,1)S(1)} async-done(((bf16[8,64,1024]{2,1,0:T(8,128)(2,1)}), bf16[8,64,1024]{2,1,0:T(8,128)(2,1)S(1)}, u32[]{:S(2)}, u32[]{:S(2)}) %all-to-all-start) | async-done | bytes 1048608 | tf_op jit(solution)/shard_map/all_to_all | solution.py:386
  68.4 3.6 %all-to-all-start.1 = ((bf16[8,64,1024]{2,1,0:T(8,128)(2,1)}), bf16[8,64,1024]{2,1,0:T(8,128)(2,1)S(1)}, u32[]{:S(2)}, u32[]{:S(2)}) async-start(bf16[8,64,1024]{2,1,0:T(8,128)(2,1)} %get-tuple-element.55), calls=%async_computation.1 | async-start | bytes 2097152 | tf_op jit(solution)/shard_map/all_to_all | solution.py:386
  72.0 15.3 %backward.1 = (bf16[256,256]{1,0:T(8,128)(2,1)}, bf16[256,256]{1,0:T(8,128)(2,1)}, bf16[256,256]{1,0:T(8,128)(2,1)}, bf16[256,256]{1,0:T(8,128)(2,1)}) custom-call(s32[2]{0:T(128)} %pad_add_fusion.place_ref, bf16[256,256]{1,0:T(8,128)(2,1)} %wo_ref.3, bf16[8,64,1024]{2,1,0:T(8,128)(2,1)} %copy-done.1, bf16[512,8192]{1,0:T(8,128)(2,1)} %get-tuple-element.42.prob_ref, ...), custom_call_target="tpu_custom_call" | custom-call | flops 20000000000 | bytes 10485760 | tf_op jit(solution)/shard_map/backward/pallas_call | solution.py:314
  87.5 2.1 %collective-permute-start.9 = (bf16[256,256]{1,0:T(8,128)(2,1)}, bf16[256,256]{1,0:T(8,128)(2,1)S(1)}, u32[]{:S(2)}, u32[]{:S(2)}) collective-permute-start(bf16[256,256]{1,0:T(8,128)(2,1)} %get-tuple-element.53), channel_id=1, source_target_pairs={{0,16},{8,24},{16,0},{24,8},{1,17},{9,25},{17,1},{25,9},{2,18},{10... | collective-permute-start | bytes 393224 | tf_op jit(solution)/shard_map/ppermute | solution.py:377
  89.6 3.9 %collective-permute-done.10 = bf16[256,256]{1,0:T(8,128)(2,1)S(1)} collective-permute-done((bf16[256,256]{1,0:T(8,128)(2,1)}, bf16[256,256]{1,0:T(8,128)(2,1)S(1)}, u32[]{:S(2)}, u32[]{:S(2)}) %collective-permute-start.10) | collective-permute-done | bytes 131104 | tf_op jit(solution)/shard_map/ppermute | solution.py:377
  93.4 2.6 %collective-permute-done.9 = bf16[256,256]{1,0:T(8,128)(2,1)S(1)} collective-permute-done((bf16[256,256]{1,0:T(8,128)(2,1)}, bf16[256,256]{1,0:T(8,128)(2,1)S(1)}, u32[]{:S(2)}, u32[]{:S(2)}) %collective-permute-start.9) | collective-permute-done | bytes 131104 | tf_op jit(solution)/shard_map/ppermute | solution.py:377
  99.4 3.5 %collective-permute-done.11 = bf16[256,256]{1,0:T(8,128)(2,1)S(1)} collective-permute-done((bf16[256,256]{1,0:T(8,128)(2,1)S(1)}, bf16[256,256]{1,0:T(8,128)(2,1)S(1)}, u32[]{:S(2)}, u32[]{:S(2)}) %collective-permute-start.11) | collective-permute-done | bytes 131104 | tf_op jit(solution)/shard_map/ppermute | solution.py:377
  104.3 3.7 %collective-permute-done.12 = bf16[256,256]{1,0:T(8,128)(2,1)S(1)} collective-permute-done((bf16[256,256]{1,0:T(8,128)(2,1)S(1)}, bf16[256,256]{1,0:T(8,128)(2,1)S(1)}, u32[]{:S(2)}, u32[]{:S(2)}) %collective-permute-start.12) | collective-permute-done | bytes 131104 | tf_op jit(solution)/shard_map/ppermute | solution.py:377
  108.1 2.2 %collective-permute-start.13 = (bf16[256,256]{1,0:T(8,128)(2,1)S(1)}, bf16[256,256]{1,0:T(8,128)(2,1)S(1)}, u32[]{:S(2)}, u32[]{:S(2)}) collective-permute-start(bf16[256,256]{1,0:T(8,128)(2,1)S(1)} %add_convert_fusion), channel_id=1, source_target_pairs={{0,4},{1,5},{2,6},{3,7},{4,0},{5,1},{6,2},{7,3},{8,12},{9,13},{10,... | collective-permute-start | bytes 393224 | tf_op jit(solution)/shard_map/ppermute | solution.py:377
  110.3 5.1 %collective-permute-done.13 = bf16[256,256]{1,0:T(8,128)(2,1)S(1)} collective-permute-done((bf16[256,256]{1,0:T(8,128)(2,1)S(1)}, bf16[256,256]{1,0:T(8,128)(2,1)S(1)}, u32[]{:S(2)}, u32[]{:S(2)}) %collective-permute-start.13) | collective-permute-done | bytes 131104 | tf_op jit(solution)/shard_map/ppermute | solution.py:377
  115.6 1.8 %collective-permute-start.16 = (bf16[256,256]{1,0:T(8,128)(2,1)S(1)}, bf16[256,256]{1,0:T(8,128)(2,1)S(1)}, u32[]{:S(2)}, u32[]{:S(2)}) collective-permute-start(bf16[256,256]{1,0:T(8,128)(2,1)S(1)} %multiply_convert_fusion.refs_0_), channel_id=1, source_target_pairs={{0,24},{8,16},{16,8},{24,0},{1,25},{9,17},{17,9},{25,1},{2,26},{10... | collective-permute-start | bytes 393224 | tf_op jit(solution)/shard_map/ppermute | solution.py:377
  117.4 2.0 %write_out.1 = bf16[8,64,1024]{2,1,0:T(8,128)(2,1)} custom-call(bf16[8,64,1024]{2,1,0:T(8,128)(2,1)} %copy-done), custom_call_target="tpu_custom_call" | custom-call | bytes 2097152 | tf_op jit(solution)/shard_map/write_out/pallas_call | solution.py:364
  119.4 2.5 %collective-permute-done.15.refs_2_ = bf16[256,256]{1,0:T(8,128)(2,1)S(1)} collective-permute-done((bf16[256,256]{1,0:T(8,128)(2,1)S(1)}, bf16[256,256]{1,0:T(8,128)(2,1)S(1)}, u32[]{:S(2)}, u32[]{:S(2)}) %collective-permute-start.15) | collective-permute-done | bytes 131104 | tf_op jit(solution)/shard_map/ppermute | solution.py:377
  121.9 1.9 %collective-permute-done.16.refs_3_ = bf16[256,256]{1,0:T(8,128)(2,1)S(1)} collective-permute-done((bf16[256,256]{1,0:T(8,128)(2,1)S(1)}, bf16[256,256]{1,0:T(8,128)(2,1)S(1)}, u32[]{:S(2)}, u32[]{:S(2)}) %collective-permute-start.16) | collective-permute-done | bytes 131104 | tf_op jit(solution)/shard_map/ppermute | solution.py:377
  124.5 2.1 %place_all.1 = f32[4,256,256]{2,1,0:T(8,128)} custom-call(s32[2]{0:T(128)} %pad_add_fusion.place_ref, bf16[256,256]{1,0:T(8,128)(2,1)} %copy-done.2, bf16[256,256]{1,0:T(8,128)(2,1)} %copy-done.4, bf16[256,256]{1,0:T(8,128)(2,1)} %copy-done.5, bf16[256,256]{1,0:T(8,128)(2,1)} %copy-done.6), custom_call_target="tpu_custom_call" | custom-call | tf_op jit(solution)/shard_map/place_all/pallas_call | solution.py:349
  (53 shorter events, 10.3 us)
Async XLA Ops:
  1.5 3.3 %collective-permute-start = (bf16[8,64,128]{2,1,0:T(8,128)(2,1)S(1)}, bf16[8,64,128]{2,1,0:T(8,128)(2,1)S(1)}, u32[]{:S(2)}, u32[]{:S(2)}) collective-permute-start(bf16[8,64,128]{2,1,0:T(8,128)(2,1)S(1)} %slice.3), channel_id=1, source_target_pairs={{0,8},{8,16},{16,24},{1,9},{9,17},{17,25},{2,10},{10,18},{18,26},{... | collective-permute-start | bytes 393224 | tf_op jit(solution)/shard_map/ppermute | solution.py:404
  10.0 9.7 %collective-permute-start.1 = (bf16[64,1024]{1,0:T(8,128)(2,1)}, bf16[64,1024]{1,0:T(8,128)(2,1)S(1)}, u32[]{:S(2)}, u32[]{:S(2)}) collective-permute-start(bf16[64,1024]{1,0:T(8,128)(2,1)} %get-tuple-element.30), channel_id=1, source_target_pairs={{0,5},{1,4},{2,7},{3,6},{4,1},{5,0},{6,3},{7,2},{8,13},{9,12},{10,... | collective-permute-start | bytes 393224 | tf_op jit(solution)/shard_map/ppermute | solution.py:377
  14.4 14.0 %collective-permute-start.2 = (bf16[64,1024]{1,0:T(8,128)(2,1)}, bf16[64,1024]{1,0:T(8,128)(2,1)S(1)}, u32[]{:S(2)}, u32[]{:S(2)}) collective-permute-start(bf16[64,1024]{1,0:T(8,128)(2,1)} %get-tuple-element.31), channel_id=1, source_target_pairs={{0,6},{1,7},{2,4},{3,5},{4,2},{5,3},{6,0},{7,1},{8,14},{9,15},{10,... | collective-permute-start | bytes 393224 | tf_op jit(solution)/shard_map/ppermute | solution.py:377
  15.7 17.4 %collective-permute-start.3 = (bf16[64,1024]{1,0:T(8,128)(2,1)}, bf16[64,1024]{1,0:T(8,128)(2,1)S(1)}, u32[]{:S(2)}, u32[]{:S(2)}) collective-permute-start(bf16[64,1024]{1,0:T(8,128)(2,1)} %get-tuple-element.32), channel_id=1, source_target_pairs={{0,7},{1,6},{2,5},{3,4},{4,3},{5,2},{6,1},{7,0},{8,15},{9,14},{10,... | collective-permute-start | bytes 393224 | tf_op jit(solution)/shard_map/ppermute | solution.py:377
  18.1 24.2 %collective-permute-start.4 = (bf16[64,1024]{1,0:T(8,128)(2,1)}, bf16[64,1024]{1,0:T(8,128)(2,1)S(1)}, u32[]{:S(2)}, u32[]{:S(2)}) collective-permute-start(bf16[64,1024]{1,0:T(8,128)(2,1)} %get-tuple-element.35), channel_id=1, source_target_pairs={{0,1},{1,0},{2,3},{3,2},{4,5},{5,4},{6,7},{7,6},{8,9},{9,8},{10,11... | collective-permute-start | bytes 393224 | tf_op jit(solution)/shard_map/ppermute | solution.py:377
  19.7 22.7 %collective-permute-start.5 = (bf16[64,1024]{1,0:T(8,128)(2,1)}, bf16[64,1024]{1,0:T(8,128)(2,1)S(1)}, u32[]{:S(2)}, u32[]{:S(2)}) collective-permute-start(bf16[64,1024]{1,0:T(8,128)(2,1)} %get-tuple-element.36), channel_id=1, source_target_pairs={{0,2},{1,3},{2,0},{3,1},{4,6},{5,7},{6,4},{7,5},{8,10},{9,11},{10,... | collective-permute-start | bytes 393224 | tf_op jit(solution)/shard_map/ppermute | solution.py:377
  19.7 22.7 %copy-start.7 = (bf16[64,1024]{1,0:T(8,128)(2,1)}, bf16[64,1024]{1,0:T(8,128)(2,1)S(1)}, u32[]{:S(2)}) copy-start(bf16[64,1024]{1,0:T(8,128)(2,1)S(1)} %collective-permute-done.1.refs_5_) | copy-start | bytes 393220
  19.7 22.7 %collective-permute-start.6 = (bf16[64,1024]{1,0:T(8,128)(2,1)}, bf16[64,1024]{1,0:T(8,128)(2,1)S(1)}, u32[]{:S(2)}, u32[]{:S(2)}) collective-permute-start(bf16[64,1024]{1,0:T(8,128)(2,1)} %get-tuple-element.37), channel_id=1, source_target_pairs={{0,3},{1,2},{2,1},{3,0},{4,7},{5,6},{6,5},{7,4},{8,11},{9,10},{10,... | collective-permute-start | bytes 393224 | tf_op jit(solution)/shard_map/ppermute | solution.py:377
  28.4 14.0 %copy-start.8 = (bf16[64,1024]{1,0:T(8,128)(2,1)}, bf16[64,1024]{1,0:T(8,128)(2,1)S(1)}, u32[]{:S(2)}) copy-start(bf16[64,1024]{1,0:T(8,128)(2,1)S(1)} %collective-permute-done.2.refs_6_) | copy-start | bytes 393220
  28.4 14.0 %collective-permute-start.7 = (bf16[64,1024]{1,0:T(8,128)(2,1)}, bf16[64,1024]{1,0:T(8,128)(2,1)S(1)}, u32[]{:S(2)}, u32[]{:S(2)}) collective-permute-start(bf16[64,1024]{1,0:T(8,128)(2,1)} %get-tuple-element.38), channel_id=1, source_target_pairs={{0,4},{1,5},{2,6},{3,7},{4,0},{5,1},{6,2},{7,3},{8,12},{9,13},{10,... | collective-permute-start | bytes 393224 | tf_op jit(solution)/shard_map/ppermute | solution.py:377
  33.1 9.3 %copy-start.9 = (bf16[64,1024]{1,0:T(8,128)(2,1)}, bf16[64,1024]{1,0:T(8,128)(2,1)S(1)}, u32[]{:S(2)}) copy-start(bf16[64,1024]{1,0:T(8,128)(2,1)S(1)} %collective-permute-done.3.refs_7_) | copy-start | bytes 393220
  33.1 35.3 %all-to-all-start = ((bf16[8,64,1024]{2,1,0:T(8,128)(2,1)}), bf16[8,64,1024]{2,1,0:T(8,128)(2,1)S(1)}, u32[]{:S(2)}, u32[]{:S(2)}) async-start(bf16[8,64,1024]{2,1,0:T(8,128)(2,1)} %param.19), calls=%async_computation | async-start | bytes 2097152 | tf_op jit(solution)/shard_map/all_to_all | solution.py:386
  68.4 29.6 %all-to-all-start.1 = ((bf16[8,64,1024]{2,1,0:T(8,128)(2,1)}), bf16[8,64,1024]{2,1,0:T(8,128)(2,1)S(1)}, u32[]{:S(2)}, u32[]{:S(2)}) async-start(bf16[8,64,1024]{2,1,0:T(8,128)(2,1)} %get-tuple-element.55), calls=%async_computation.1 | async-start | bytes 2097152 | tf_op jit(solution)/shard_map/all_to_all | solution.py:386
  87.4 6.1 %collective-permute-start.10 = (bf16[256,256]{1,0:T(8,128)(2,1)}, bf16[256,256]{1,0:T(8,128)(2,1)S(1)}, u32[]{:S(2)}, u32[]{:S(2)}) collective-permute-start(bf16[256,256]{1,0:T(8,128)(2,1)} %get-tuple-element.54), channel_id=1, source_target_pairs={{0,24},{8,16},{16,8},{24,0},{1,25},{9,17},{17,9},{25,1},{2,26},{10... | collective-permute-start | bytes 393224 | tf_op jit(solution)/shard_map/ppermute | solution.py:377
  87.4 6.0 %collective-permute-start.8 = (bf16[256,256]{1,0:T(8,128)(2,1)}, bf16[256,256]{1,0:T(8,128)(2,1)S(1)}, u32[]{:S(2)}, u32[]{:S(2)}) collective-permute-start(bf16[256,256]{1,0:T(8,128)(2,1)} %get-tuple-element.52), channel_id=1, source_target_pairs={{0,8},{8,0},{16,24},{24,16},{1,9},{9,1},{17,25},{25,17},{2,10},{10... | collective-permute-start | bytes 393224 | tf_op jit(solution)/shard_map/ppermute | solution.py:377
  87.5 8.6 %collective-permute-start.9 = (bf16[256,256]{1,0:T(8,128)(2,1)}, bf16[256,256]{1,0:T(8,128)(2,1)S(1)}, u32[]{:S(2)}, u32[]{:S(2)}) collective-permute-start(bf16[256,256]{1,0:T(8,128)(2,1)} %get-tuple-element.53), channel_id=1, source_target_pairs={{0,16},{8,24},{16,0},{24,8},{1,17},{9,25},{17,1},{25,9},{2,18},{10... | collective-permute-start | bytes 393224 | tf_op jit(solution)/shard_map/ppermute | solution.py:377
  98.0 19.4 %copy-start = (bf16[8,64,1024]{2,1,0:T(8,128)(2,1)}, bf16[8,64,1024]{2,1,0:T(8,128)(2,1)S(1)}, u32[]{:S(2)}) copy-start(bf16[8,64,1024]{2,1,0:T(8,128)(2,1)S(1)} %all-to-all-done.1.in_ref) | copy-start | bytes 3145732
  98.0 5.0 %collective-permute-start.11 = (bf16[256,256]{1,0:T(8,128)(2,1)S(1)}, bf16[256,256]{1,0:T(8,128)(2,1)S(1)}, u32[]{:S(2)}, u32[]{:S(2)}) collective-permute-start(bf16[256,256]{1,0:T(8,128)(2,1)S(1)} %add_convert_fusion.2), channel_id=1, source_target_pairs={{0,1},{1,0},{2,3},{3,2},{4,5},{5,4},{6,7},{7,6},{8,9},{9,8},{10,11... | collective-permute-start | bytes 393224 | tf_op jit(solution)/shard_map/ppermute | solution.py:377
  103.0 5.0 %collective-permute-start.12 = (bf16[256,256]{1,0:T(8,128)(2,1)S(1)}, bf16[256,256]{1,0:T(8,128)(2,1)S(1)}, u32[]{:S(2)}, u32[]{:S(2)}) collective-permute-start(bf16[256,256]{1,0:T(8,128)(2,1)S(1)} %add_convert_fusion.1), channel_id=1, source_target_pairs={{0,2},{1,3},{2,0},{3,1},{4,6},{5,7},{6,4},{7,5},{8,10},{9,11},{10,... | collective-permute-start | bytes 393224 | tf_op jit(solution)/shard_map/ppermute | solution.py:377
  108.1 7.3 %collective-permute-start.13 = (bf16[256,256]{1,0:T(8,128)(2,1)S(1)}, bf16[256,256]{1,0:T(8,128)(2,1)S(1)}, u32[]{:S(2)}, u32[]{:S(2)}) collective-permute-start(bf16[256,256]{1,0:T(8,128)(2,1)S(1)} %add_convert_fusion), channel_id=1, source_target_pairs={{0,4},{1,5},{2,6},{3,7},{4,0},{5,1},{6,2},{7,3},{8,12},{9,13},{10,... | collective-permute-start | bytes 393224 | tf_op jit(solution)/shard_map/ppermute | solution.py:377
  115.4 8.4 %copy-start.2 = (bf16[256,256]{1,0:T(8,128)(2,1)}, bf16[256,256]{1,0:T(8,128)(2,1)S(1)}, u32[]{:S(2)}) copy-start(bf16[256,256]{1,0:T(8,128)(2,1)S(1)} %multiply_convert_fusion.refs_0_) | copy-start | bytes 393220
  115.4 4.0 %collective-permute-start.14 = (bf16[256,256]{1,0:T(8,128)(2,1)S(1)}, bf16[256,256]{1,0:T(8,128)(2,1)S(1)}, u32[]{:S(2)}, u32[]{:S(2)}) collective-permute-start(bf16[256,256]{1,0:T(8,128)(2,1)S(1)} %multiply_convert_fusion.refs_0_), channel_id=1, source_target_pairs={{0,8},{8,0},{16,24},{24,16},{1,9},{9,1},{17,25},{25,17},{2,10},{10... | collective-permute-start | bytes 393224 | tf_op jit(solution)/shard_map/ppermute | solution.py:377
  115.5 6.4 %collective-permute-start.15 = (bf16[256,256]{1,0:T(8,128)(2,1)S(1)}, bf16[256,256]{1,0:T(8,128)(2,1)S(1)}, u32[]{:S(2)}, u32[]{:S(2)}) collective-permute-start(bf16[256,256]{1,0:T(8,128)(2,1)S(1)} %multiply_convert_fusion.refs_0_), channel_id=1, source_target_pairs={{0,16},{8,24},{16,0},{24,8},{1,17},{9,25},{17,1},{25,9},{2,18},{10... | collective-permute-start | bytes 393224 | tf_op jit(solution)/shard_map/ppermute | solution.py:377
  115.6 8.2 %collective-permute-start.16 = (bf16[256,256]{1,0:T(8,128)(2,1)S(1)}, bf16[256,256]{1,0:T(8,128)(2,1)S(1)}, u32[]{:S(2)}, u32[]{:S(2)}) collective-permute-start(bf16[256,256]{1,0:T(8,128)(2,1)S(1)} %multiply_convert_fusion.refs_0_), channel_id=1, source_target_pairs={{0,24},{8,16},{16,8},{24,0},{1,25},{9,17},{17,9},{25,1},{2,26},{10... | collective-permute-start | bytes 393224 | tf_op jit(solution)/shard_map/ppermute | solution.py:377
  (9 other events, 14.0 us)
